TPU v7x, 32 devices: a whole 2x2x4 slice. The times are simulated.
32 devices in a mesh: grp: 4 (over x, core), blk: 8 (over z, y).
Axes of the slice: x: 2, y: 2, z: 4, core: 2. Of those that a mesh axis runs over, the one named last changes fastest.
Arguments:
- particles: bfloat16 [64, 2, 4000], P(('blk', 'grp')), may hold values from -6 to 6
- ctf_class: int32 [64], P(('blk', 'grp')), may hold values from 0 to 63
- orient_prior: bfloat16 [64, 192], P(('blk', 'grp')), may hold values from -6 to 6
- ctf_curves: float32 [64, 4000], replicated, may hold values from -1 to 1
- noise_weight: float32 [4000], replicated, may hold values from 0.005 to 0.05
- shift_phase: float32 [9, 4000], replicated, may hold values from -3.140625 to 3.140625
- trans_index: int32 [9], replicated, may hold values from 0 to 8, each once
- projections: bfloat16 [256, 2, 4000], P(('grp', 'blk')), may hold values from -1.75 to 1.75
- orient_subset: int32 [256], P(('grp', 'blk')), may hold values from 0 to 191
Outputs:
- scores: float32 [64, 9, 256], P('blk', None, 'grp')
Inputs may be any that keep to these rules, and one draw needn't show every extreme that they name: `trans_index`: each row of shift_phase is named once.
All inputs are finite; a program needn't handle non-finite values.
Results may differ from a plain program's by a relative error of at most 0.00056.
Values may be sent and summed in bfloat16 or wider, within the bound.
No kernel may reach another device: no remote copies, remote signals or barrier semaphores. Data moves between devices by JAX's collectives and lax.ppermute only.
A program may use at most 128 MiB of HBM per device.

v0:
```python
import jax
import jax.numpy as jnp
from jax import lax
from jax.sharding import PartitionSpec as P


def per_device(
    particles,
    ctf_class,
    orient_prior,
    ctf_curves,
    noise_weight,
    shift_phase,
    trans_index,
    projections,
    orient_subset,
):
    highest = lax.Precision.HIGHEST
    classes_count = ctf_curves.shape[0]
    subset_count = orient_prior.shape[1]
    shift_count = shift_phase.shape[0]
    weight_rows = ctf_curves * noise_weight[None, :]

    def class_onehot(classes):
        return (classes[:, None] == jnp.arange(classes_count, dtype=jnp.int32)[None, :]).astype(
            jnp.float32
        )

    curve_local = jnp.dot(class_onehot(ctf_class), weight_rows, precision=highest)
    local_weighted = (particles.astype(jnp.float32) * curve_local[:, None, :]).astype(jnp.bfloat16)
    weighted, classes, prior = (
        lax.all_gather(local_weighted, "grp", axis=0, tiled=True),
        lax.all_gather(ctf_class, "grp", axis=0, tiled=True),
        lax.all_gather(orient_prior, "grp", axis=0, tiled=True),
    )
    onehot_rows = class_onehot(classes)
    prior_wide = prior.astype(jnp.float32)
    pick_shift = (trans_index[:, None] == jnp.arange(shift_count, dtype=jnp.int32)[None, :]).astype(
        jnp.float32
    )
    angle = jnp.dot(pick_shift, shift_phase, precision=highest)
    cos_part = jnp.cos(angle)
    sin_part = jnp.sin(angle)
    curve_sq = ctf_curves * ctf_curves * noise_weight[None, :]
    bank = lax.all_gather(projections, "blk", axis=0, tiled=True)
    subset_ids = lax.all_gather(orient_subset, "blk", axis=0, tiled=True)
    bank_real = bank[:, 0, :].astype(jnp.float32)
    bank_imag = bank[:, 1, :].astype(jnp.float32)
    real_shift = cos_part[:, None, :] * bank_real[None] + sin_part[:, None, :] * bank_imag[None]
    imag_shift = cos_part[:, None, :] * bank_imag[None] - sin_part[:, None, :] * bank_real[None]
    shifted = jnp.stack([real_shift, imag_shift], axis=2).astype(jnp.bfloat16)
    cross = jnp.einsum("nck,tmck->ntm", weighted, shifted, preferred_element_type=jnp.float32)
    power = bank_real * bank_real + bank_imag * bank_imag
    norm_table = jnp.dot(curve_sq, power.T, precision=highest)
    norm_sel = jnp.dot(onehot_rows, norm_table, precision=highest)
    subset_onehot = (
        subset_ids[None, :] == jnp.arange(subset_count, dtype=jnp.int32)[:, None]
    ).astype(jnp.float32)
    prior_term = jnp.dot(prior_wide, subset_onehot, precision=highest)
    return cross - 0.5 * norm_sel[:, None, :] + prior_term[:, None, :]


def solution(mesh):
    placed = (
        P(("blk", "grp"), None, None),
        P(("blk", "grp")),
        P(("blk", "grp"), None),
        P(),
        P(),
        P(),
        P(),
        P(("grp", "blk"), None, None),
        P(("grp", "blk")),
    )
    return jax.shard_map(
        per_device, mesh=mesh, in_specs=placed, out_specs=P("blk", None, "grp"), check_vma=False
    )
```

profile of v0, /device:TPU:0, one launch (start us, length us, event | category | flops | bytes accessed | tf_op | source)
XLA Modules:
  0.0 82.6 jit_solution(14103374313230277708)
XLA Ops:
  0.0 0.0 copy-start
  0.0 1.3 %dynamic-slice.1 = u32[1]{0:T(128)} dynamic-slice(u32[32]{0:T(128)} %constant.14, u32[]{:T(128)S(6)} %add.25), dynamic_slice_sizes={1} | dynamic-slice | bytes 12
  1.9 1.3 %dynamic-slice = u32[1]{0:T(128)} dynamic-slice(u32[32]{0:T(128)} %constant.9, u32[]{:T(128)S(6)} %add.25), dynamic_slice_sizes={1} | dynamic-slice | bytes 12
  4.0 0.9 %dynamic-update-slice.1 = s32[64]{0:T(128)S(1)} dynamic-update-slice(s32[64]{0:T(128)S(1)} %broadcast.68, s32[8]{0:T(128)} %param.17, u32[]{:T(128)} %bitcast.8) | dynamic-update-slice | bytes 68
  4.8 13.1 %all-reduce.1 = s32[64]{0:T(128)S(1)} all-reduce(s32[64]{0:T(128)S(1)} %dynamic-update-slice.1), channel_id=1, replica_groups=mesh['grp'=4,'blk'=8] {'blk'}, use_global_device_ids=true, to_apply=%add.1 | all-reduce | flops 64 | bytes 512
  17.9 0.8 %dynamic-update-slice = s32[8]{0:T(128)S(1)} dynamic-update-slice(s32[8]{0:T(128)S(1)} %broadcast.67, s32[2]{0:T(128)} %param.10, u32[]{:T(128)} %bitcast.5) | dynamic-update-slice | bytes 20
  18.7 4.9 %all-reduce = s32[8]{0:T(128)S(1)} all-reduce(s32[8]{0:T(128)S(1)} %dynamic-update-slice), channel_id=1, replica_groups=mesh['grp'=4,'blk'=8] {'grp'}, use_global_device_ids=true, to_apply=%add | all-reduce | flops 8 | bytes 64
  23.6 5.3 %all-gather = bf16[4,2,192]{2,1,0:T(2,128)(2,1)S(1)} all-gather(bf16[1,2,192]{2,1,0:T(2,128)(2,1)} %bitcast.34), channel_id=1, replica_groups=mesh['grp'=4,'blk'=8] {'grp'}, dimensions={0}, use_global_device_ids=true | all-gather | bytes 3840 | tf_op jit(solution)/shard_map/all_gather | solution.py:34
  28.9 0.1 convolution_bitcast_fusion
  29.0 1.7 %fusion.19 = f32[2,4000]{1,0:T(2,128)S(1)} fusion(f32[64,4000]{1,0:T(8,128)} %param.12, f32[4000]{0:T(1024)} %param.13, s32[2]{0:T(128)} %param.10), kind=kOutput, calls=%fused_computation.17 | convolution fusion | flops 6400128 | bytes 1072008 | tf_op jit(solution)/shard_map/dot_general | solution.py:29
  30.8 0.8 multiply_convert_fusion
  31.6 5.4 %all_gather.15 = bf16[8,2,4000]{2,1,0:T(2,128)(2,1)S(1)} all-gather(bf16[2,2,4000]{2,1,0:T(2,128)(2,1)S(1)} %multiply_convert_fusion), channel_id=1, replica_groups=mesh['grp'=4,'blk'=8] {'grp'}, dimensions={0}, use_global_device_ids=true | all-gather | bytes 160000 | tf_op jit(solution)/shard_map/all_gather | solution.py:32
  37.0 1.0 %copy.14 = bf16[8,2,4000]{2,0,1:T(8,128)(2,1)S(1)} copy(bf16[8,2,4000]{2,1,0:T(2,128)(2,1)} %param.16) | data formatting | bytes 256000 | tf_op args[7]
  38.0 0.0 copy-done
  38.0 1.9 %fusion.37 = (f32[9,4000]{1,0:T(8,128)S(1)}, f32[9,4000]{1,0:T(8,128)S(1)}) fusion(f32[9,4000]{1,0:T(8,128)S(1)} %copy-done, s32[9]{0:T(128)} %param.15), kind=kOutput, calls=%fused_computation.39 | convolution fusion | flops 3888081 | bytes 432036 | tf_op jit(solution)/shard_map/dot_general | solution.py:41
  39.9 33.1 %all_gather.16 = bf16[64,2,4000]{2,0,1:T(8,128)(2,1)S(1)} all-gather(bf16[8,2,4000]{2,0,1:T(8,128)(2,1)S(1)} %copy.14), channel_id=1, replica_groups=mesh['grp'=4,'blk'=8] {'blk'}, dimensions={0}, use_global_device_ids=true | all-gather | bytes 1152000 | tf_op jit(solution)/shard_map/all_gather | solution.py:45
  73.0 2.4 %fusion.13 = f32[64,64]{1,0:T(8,128)S(1)} fusion(f32[64,4000]{1,0:T(8,128)} %param.12, f32[4000]{0:T(1024)} %param.13, bf16[64,2,4000]{2,0,1:T(8,128)(2,1)S(1)} %all_gather.16), kind=kOutput, calls=%fused_computation.11 | convolution fusion | flops 198400000 | bytes 2080384 | tf_op jit(solution)/shard_map/dot_general | solution.py:54
  75.4 0.2 convolution_multiply_fusion
  75.6 0.2 fusion.22
  75.8 2.6 %add_convert_fusion = (bf16[9,64,1,4000]{3,1,2,0:T(8,128)(2,1)S(1)}, bf16[9,64,1,4000]{3,1,2,0:T(8,128)(2,1)S(1)}) fusion(f32[64,4000]{1,0:T(8,128)S(1)} %get-tuple-element.8, f32[9,4000]{1,0:T(8,128)S(1)} %get-tuple-element.10, f32[64,4000]{1,0:T(8,128)S(1)} %get-tuple-element.7, f32[9,4000]{1,0:T(8,128)S(1)} %get-tuple-element.9), kind=kLoop, calls=%fused_computation.5 | loop fusion | flops 18432000 | bytes 11552000 | tf_op jit(solution)/shard_map/convert.2
  78.4 4.2 %fusion.10 = f32[8,9,64]{2,0,1:T(8,128)} fusion(bf16[9,64,1,4000]{3,1,2,0:T(8,128)(2,1)S(1)} %get-tuple-element.6, bf16[9,64,1,4000]{3,1,2,0:T(8,128)(2,1)S(1)} %get-tuple-element.5, bf16[8,2,4000]{2,1,0:T(2,128)(2,1)S(1)} %all_gather.15, f32[8,64]{1,0:T(8,128)S(1)} %convolution_bitcast_fusion, f32[8,64]{1,0:T(8,128)S(1)} %convolution_multiply_fusion), kind=kOutput, calls=%fused_computation.8 | convolution fusion | flops 92169216 | bytes 9366528 | tf_op jit(solution)/shard_map/nck,tmck->ntm/dot_general | solution.py:52
  (3 shorter events, 0.0 us)
Async XLA Ops:
  0.0 38.0 %copy-start = (f32[9,4000]{1,0:T(8,128)S(1)}, f32[9,4000]{1,0:T(8,128)}, u32[]{:S(2)}) copy-start(f32[9,4000]{1,0:T(8,128)} %param.14) | copy-start | bytes 432004
where the time goes:
time: 83 us; the launch traced here: 82.6 us
  blocking collectives  61.8 us (74%)
  matrix products  10.6 us (13%)
  local copies, waits for them, and re-layouts  5.31 us (6%)
  other arithmetic  3.58 us (4%)
  between operations  1.41 us (2%)
    all_gather x1, blocking collectives, per_device(): bank = lax.all_gather(projections, 'blk', axis=0, tiled=True)  33.1 us
    unnamed x2, blocking collectives  18 us
    all_gather x1, blocking collectives, per_device(): lax.all_gather(local_weighted, 'grp', axis=0, tiled=True)  5.43 us
    unnamed x10, local copies, waits for them, and re-layouts  5.31 us
    all_gather x1, blocking collectives, per_device(): lax.all_gather(orient_prior, 'grp', axis=0, tiled=True)  5.27 us
    dot_general x1, matrix products, per_device(): jnp.einsum('nck,tmck->ntm', weighted, shifted, preferred_element_type=jnp...  4.24 us
    another operation x1, other arithmetic  2.56 us
    dot_general x1, matrix products, per_device(): norm_table = jnp.dot(curve_sq, power.T, precision=highest)  2.43 us

commit v1 on v0

v1 whole, which is shorter than its diff:
```python
import jax
import jax.numpy as jnp
from jax import lax
from jax.sharding import PartitionSpec as P


def per_device(
    particles,
    ctf_class,
    orient_prior,
    ctf_curves,
    noise_weight,
    shift_phase,
    trans_index,
    projections,
    orient_subset,
):
    highest = lax.Precision.HIGHEST
    nb, ng = lax.axis_size("blk"), lax.axis_size("grp")
    me = lax.axis_index("blk")
    n_part, n_proj = particles.shape[0], projections.shape[0]
    length = particles.shape[2]
    classes_count = ctf_curves.shape[0]
    subset_count = orient_prior.shape[1]
    chunk = 128 * -(-length // (128 * nb))
    pad = nb * chunk - length

    def chunk_of(rows):
        wide = jnp.pad(rows, ((0, 0), (0, pad)))
        return lax.dynamic_slice(wide, (0, me * chunk), (rows.shape[0], chunk))

    curve = jnp.concatenate(
        [lax.dynamic_slice(ctf_curves, (ctf_class[i], 0), (1, length)) for i in range(n_part)]
    )
    curve = curve * noise_weight[None, :]
    weighted = (particles.astype(jnp.float32) * curve[:, None, :]).astype(jnp.bfloat16)

    small = jnp.concatenate(
        [
            ctf_class.astype(jnp.bfloat16),
            orient_subset.astype(jnp.bfloat16),
            orient_prior.reshape(-1),
        ]
    )
    n_small = small.shape[0]
    n_ext = -(-n_small // (2 * chunk))
    ext = jnp.pad(small, (0, n_ext * 2 * chunk - n_small)).reshape(1, n_ext, 2, chunk)

    rows = jnp.concatenate([projections, weighted], axis=0)
    rows = jnp.pad(rows, ((0, 0), (0, 0), (0, pad)))
    rows = rows.reshape(n_proj + n_part, 2, nb, chunk).transpose(2, 0, 1, 3)
    message = jnp.concatenate([rows, jnp.broadcast_to(ext, (nb, n_ext, 2, chunk))], axis=1)
    recv = lax.all_to_all(message, "blk", 0, 0, tiled=True)
    gath = lax.all_gather(recv[:, n_proj:], "grp", axis=1)

    bank = recv[:, :n_proj].reshape(nb * n_proj, 2, chunk)
    weighted_all = gath[:, :, :n_part].reshape(nb * ng * n_part, 2, chunk)
    small_all = gath[:, :, n_part:].reshape(nb, ng, n_ext * 2 * chunk)[:, :, :n_small]
    classes = small_all[:, :, :n_part].reshape(-1).astype(jnp.int32)
    prior_all = small_all[:, :, n_part + n_proj :].reshape(nb, ng * n_part, subset_count)
    prior = lax.dynamic_index_in_dim(prior_all, me, 0, keepdims=False).astype(jnp.float32)
    own = recv[:, n_proj + n_part :].reshape(nb, n_ext * 2 * chunk)
    subset_ids = own[:, n_part : n_part + n_proj].reshape(-1).astype(jnp.int32)

    angle = chunk_of(shift_phase[trans_index])
    cos_part = jnp.cos(angle)
    sin_part = jnp.sin(angle)
    bank_real = bank[:, 0, :].astype(jnp.float32)
    bank_imag = bank[:, 1, :].astype(jnp.float32)
    real_shift = cos_part[:, None, :] * bank_real[None] + sin_part[:, None, :] * bank_imag[None]
    imag_shift = cos_part[:, None, :] * bank_imag[None] - sin_part[:, None, :] * bank_real[None]
    shifted = jnp.stack([real_shift, imag_shift], axis=2).astype(jnp.bfloat16)
    cross = jnp.einsum("nck,tmck->ntm", weighted_all, shifted, preferred_element_type=jnp.float32)

    curve_sq = chunk_of(ctf_curves)
    curve_sq = curve_sq * curve_sq * chunk_of(noise_weight[None, :])
    power = bank_real * bank_real + bank_imag * bank_imag
    norm_table = jnp.dot(curve_sq, power.T, precision=highest)
    onehot_rows = (
        classes[:, None] == jnp.arange(classes_count, dtype=jnp.int32)[None, :]
    ).astype(jnp.float32)
    norm_sel = jnp.dot(onehot_rows, norm_table, precision=highest)
    subset_onehot = (
        subset_ids[None, :] == jnp.arange(subset_count, dtype=jnp.int32)[:, None]
    ).astype(jnp.float32)
    prior_term = jnp.dot(prior, subset_onehot, precision=highest)
    partial = cross - 0.5 * norm_sel[:, None, :]
    total = lax.psum_scatter(partial, "blk", scatter_dimension=0, tiled=True)
    return total + prior_term[:, None, :]


def solution(mesh):
    placed = (
        P(("blk", "grp"), None, None),
        P(("blk", "grp")),
        P(("blk", "grp"), None),
        P(),
        P(),
        P(),
        P(),
        P(("grp", "blk"), None, None),
        P(("grp", "blk")),
    )
    return jax.shard_map(
        per_device, mesh=mesh, in_specs=placed, out_specs=P("blk", None, "grp"), check_vma=False
    )
```

time: 83 us -> 108 us (1.30)
  waiting for transfers between devices: 0 us -> 63.6 us
  blocking collectives: 61.8 us -> 5.61 us
  between operations: 1.41 us -> 17.4 us
  matrix products: 10.6 us -> 2 us
  starting transfers between devices: 0 us -> 7.31 us
  other arithmetic: 3.58 us -> 5.91 us
    reduce_scatter x0 -> x1, waiting for transfers between devices: none -> 56.9 us  [per_device(): total = lax.psum_scatter(partial, 'blk', scatter_dimension=0, tiled=True)]
    all_gather x3 -> x1, blocking collectives: 43.8 us -> 5.61 us  [per_device(): gath = lax.all_gather(recv[:, n_proj:], 'grp', axis=1)]
    unnamed x2 -> x0, blocking collectives: 18 us -> none
    all_to_all x0 -> x1, starting transfers between devices: none -> 7.27 us  [per_device(): recv = lax.all_to_all(message, 'blk', 0, 0, tiled=True)]
    all_to_all x0 -> x1, waiting for transfers between devices: none -> 6.72 us  [per_device(): recv = lax.all_to_all(message, 'blk', 0, 0, tiled=True)]
    dot_general x4 -> x2, matrix products: 7.96 us -> 1.52 us  [the longest x1 1.38 us: per_device(): jnp.einsum('nck,tmck->ntm', weighted_all, shifted, preferred_element_type...]
    unnamed x10 -> x11, local copies, waits for them, and re-layouts: 5.31 us -> 0.15 us
    another operation x1, other arithmetic: 2.56 us -> 0.31 us
  transfers between devices with their start and end apart: 0 -> 2, of which waited for: 0 -> 2; matrix products, arithmetic and copies ran while one was open for 0% -> 1% of each run, Pallas kernels for 0% -> 0%
where the time goes in v1:
time: 108 us
  waiting for transfers between devices  63.6 us (59%)
  between operations  17.4 us (16%)
  starting transfers between devices  7.31 us (7%)
  other arithmetic  5.91 us (5%)
  local copies, waits for them, and re-layouts  5.7 us (5%)
  blocking collectives  5.61 us (5%)
  matrix products  2 us (2%)
    reduce_scatter x1, waiting for transfers between devices, per_device(): total = lax.psum_scatter(partial, 'blk', scatter_dimension=0, tiled=True)  56.9 us
    all_to_all x1, starting transfers between devices, per_device(): recv = lax.all_to_all(message, 'blk', 0, 0, tiled=True)  7.27 us
    all_to_all x1, waiting for transfers between devices, per_device(): recv = lax.all_to_all(message, 'blk', 0, 0, tiled=True)  6.72 us
    all_gather x1, blocking collectives, per_device(): gath = lax.all_gather(recv[:, n_proj:], 'grp', axis=1)  5.61 us
  transfers between devices with their start and end apart: 2, of which 2 were waited for; matrix products, arithmetic and copies ran while one was open for 1% of the time, Pallas kernels for 0%

profile of v1, /device:TPU:0, one launch (start us, length us, event | category | flops | bytes accessed | tf_op | source)
XLA Modules:
  0.0 107.6 jit_solution(1436261169325031326)
XLA Ops:
  6.5 0.0 copy-start
  6.5 0.0 copy-start.3
  6.5 0.7 convert_element_type.68
  7.3 1.4 %fusion.41 = (s32[1]{0:T(128)}, s32[1]{0:T(128)}) fusion(s32[2]{0:T(128)} %param.10), kind=kLoop, calls=%fused_computation.59 | loop fusion | bytes 16 | tf_op jit(solution)/shard_map/slice | solution.py:33
  11.2 0.7 convert_element_type.69
  11.8 0.8 reshape.105
  12.6 0.1 fusion.36
  14.0 1.0 constant_dynamic-slice_fusion.1
  15.0 0.8 maximum_multiply_fusion
  15.7 0.8 multiply_convert_fusion
  16.5 1.1 fusion.12
  17.6 0.1 reshape.104
  17.8 0.8 copy.32
  18.6 7.3 %all-to-all-start = ((bf16[8,11,2,512]{3,2,1,0:T(2,128)(2,1)}), bf16[8,11,2,512]{3,2,1,0:T(2,128)(2,1)S(1)}, u32[]{:S(2)}, u32[]{:S(2)}) async-start(bf16[8,11,2,512]{3,2,1,0:T(2,128)(2,1)} %copy.32), calls=%async_computation | async-start | bytes 360448 | tf_op jit(solution)/shard_map/all_to_all | solution.py:53
  25.8 0.0 reduce-scatter.2.cloned.1.call-start
  25.9 0.0 copy-done.3
  25.9 0.0 copy-done
  25.9 0.0 copy-start.2
  25.9 0.6 gather_fusion
  26.6 0.1 copy-done.2
  26.7 0.0 copy-start.1
  26.7 0.1 fusion.29
  26.8 6.7 %all-to-all-done = bf16[8,11,2,512]{3,2,1,0:T(2,128)(2,1)S(1)} async-done(((bf16[8,11,2,512]{3,2,1,0:T(2,128)(2,1)}), bf16[8,11,2,512]{3,2,1,0:T(2,128)(2,1)S(1)}, u32[]{:S(2)}, u32[]{:S(2)}) %all-to-all-start) | async-done | bytes 180256 | tf_op jit(solution)/shard_map/all_to_all | solution.py:53
  33.6 5.6 %all-gather = bf16[8,12,2,512]{3,0,2,1:T(8,128)(2,1)S(1)} all-gather(bf16[8,3,2,512]{3,0,2,1:T(8,128)(2,1)S(1)} %copy.33), channel_id=2, replica_groups=mesh['grp'=4,'blk'=8] {'grp'}, dimensions={1}, use_global_device_ids=true | all-gather | bytes 245760 | tf_op jit(solution)/shard_map/all_gather | solution.py:54
  39.3 0.1 slice.55
  39.4 0.0 copy-done.1
  39.4 0.3 fusion.15
  39.7 0.1 copy.34
  39.8 0.1 reshape.125
  39.9 0.1 reshape.113
  40.0 0.2 convolution_multiply_fusion
  40.3 0.3 add_convert_fusion
  40.6 1.4 %fusion.7 = f32[64,9,64]{2,0,1:T(8,128)} fusion(bf16[64,2,512,1]{2,0,1,3:T(8,128)(2,1)S(1)} %reshape.125, bf16[9,64,1,512]{3,1,2,0:T(8,128)(2,1)S(1)} %get-tuple-element.8, bf16[9,64,1,512]{3,1,2,0:T(8,128)(2,1)S(1)} %get-tuple-element.7, f32[64,64]{1,0:T(8,128)S(1)} %convolution_multiply_fusion), kind=kOutput, calls=%fused_computation.8 | convolution fusion | flops 77893632 | bytes 1474560 | tf_op jit(solution)/shard_map/nck,tmck->ntm/dot_general | solution.py:73
  42.0 0.0 reduce-scatter.2.cloned.1.call-update
  42.0 0.1 slice_convert_fusion.1
  42.1 0.1 slice.60
  42.1 0.1 reshape.114
  42.2 0.1 reshape.109
  42.3 0.1 fusion.20
  42.5 56.9 %reduce-scatter.2.cloned.1.call-done = f32[8,9,64]{2,0,1:T(8,128)} async-done(((f32[64,9,64]{2,0,1:T(8,128)}), f32[8,9,64]{2,0,1:T(8,128)}) %reduce-scatter.2.cloned.1.call-update) | async-done | bytes 18448 | tf_op jit(solution)/shard_map/reduce_scatter | solution.py:88
  99.4 1.4 %broadcast_add_fusion = f32[8,9,64]{2,0,1:T(8,128)} fusion(f32[8,9,64]{2,0,1:T(8,128)} %reduce-scatter.2.cloned.1.call-done, f32[8,64]{1,0:T(8,128)S(1)} %fusion.20), kind=kLoop, calls=%fused_computation.35 | loop fusion | flops 4608 | bytes 38912 | tf_op jit(solution)/shard_map/add | solution.py:89
  (17 shorter events, 0.2 us)
Async XLA Ops:
  6.5 19.4 %copy-start = (f32[9,4000]{1,0:T(8,128)S(1)}, f32[9,4000]{1,0:T(8,128)}, u32[]{:S(2)}) copy-start(f32[9,4000]{1,0:T(8,128)} %param.14) | copy-start | bytes 432004
  6.5 19.4 %copy-start.3 = (s32[9]{0:T(128)S(1)}, s32[9]{0:T(128)}, u32[]{:S(2)}) copy-start(s32[9]{0:T(128)} %param.15) | copy-start | bytes 112
  18.6 15.0 %all-to-all-start = ((bf16[8,11,2,512]{3,2,1,0:T(2,128)(2,1)}), bf16[8,11,2,512]{3,2,1,0:T(2,128)(2,1)S(1)}, u32[]{:S(2)}, u32[]{:S(2)}) async-start(bf16[8,11,2,512]{3,2,1,0:T(2,128)(2,1)} %copy.32), calls=%async_computation | async-start | bytes 360448 | tf_op jit(solution)/shard_map/all_to_all | solution.py:53
  25.8 73.5 %reduce-scatter.2.cloned.1.call-start = ((), (), s32[]{:S(2)}) async-start(), calls=%async_computation.2 | async-start | bytes 331776 | tf_op jit(solution)/shard_map/reduce_scatter | solution.py:88
  25.9 0.7 copy-start.2
  26.7 12.8 %copy-start.1 = (f32[64,4000]{1,0:T(8,128)S(1)}, f32[64,4000]{1,0:T(8,128)}, u32[]{:S(2)}) copy-start(f32[64,4000]{1,0:T(8,128)} %param.12) | copy-start | bytes 3072004
Sparse Core Ops, SparseCore 0:
  42.1 57.2 reduce-scatter.1

commit v2 on v0

v2 whole, which is shorter than its diff:
```python
import functools

import jax
import jax.numpy as jnp
from jax import lax
from jax.experimental import pallas as pl
from jax.experimental.pallas import tpu as pltpu
from jax.sharding import PartitionSpec as P

F32 = jnp.float32
BF16 = jnp.bfloat16
HIGHEST = lax.Precision.HIGHEST
NT_DIMS = (((1,), (1,)), ((), ()))
MIB = 1 << 20
ROWS = 8


def _vmem():
    return pl.BlockSpec(memory_space=pltpu.VMEM)


def _smem():
    return pl.BlockSpec(memory_space=pltpu.SMEM)


def _params(mib):
    return pltpu.CompilerParams(vmem_limit_bytes=mib * MIB)


def pack_kernel(
    nz, ny, chunk, class_ref, subset_ref, particles_ref, prior_ref, curves_ref, noise_ref, proj_ref, *rest
):
    banks, parts, (held, sems) = rest[:nz], rest[nz : 2 * nz], rest[2 * nz :]
    n_part, n_proj = particles_ref.shape[0], proj_ref.shape[0]
    length = proj_ref.shape[2]
    z = lax.axis_index("blk") // ny
    copies = []
    for i in range(n_part):
        first = pl.multiple_of(class_ref[i] // ROWS * ROWS, ROWS)
        copy = pltpu.make_async_copy(curves_ref.at[pl.ds(first, ROWS)], held.at[i], sems.at[i])
        copy.start()
        copies.append(copy)

    def piece(values, c):
        width = min(chunk, length - c * chunk)
        values = values[:, c * chunk : c * chunk + width]
        if width < chunk:
            values = jnp.concatenate(
                [values, jnp.zeros((values.shape[0], chunk - width), values.dtype)], axis=1
            )
        return values

    row8 = lax.broadcasted_iota(jnp.int32, (ROWS, chunk), 0)
    lane8 = lax.broadcasted_iota(jnp.int32, (ROWS, chunk), 1)
    ids = jnp.zeros((ROWS, chunk), F32)
    for j in range(n_proj):
        ids = jnp.where(row8 == j, subset_ref[j].astype(F32), ids)

    for c in range(nz):
        real = jnp.zeros((ROWS, chunk), F32)
        imag = jnp.zeros((ROWS, chunk), F32)
        for j in range(n_proj):
            both = piece(proj_ref[j].astype(F32), c)
            real = jnp.where(row8 == j, both[0:1], real)
            imag = jnp.where(row8 == j, both[1:2], imag)
        if c == nz - 1:
            real = jnp.where(lane8 == length - c * chunk, ids, real)
        bank = jnp.concatenate([real, imag], axis=0).astype(BF16)
        for s in range(nz):

            @pl.when((z ^ s) == c)
            def _():
                banks[s][...] = bank

    for copy in copies:
        copy.wait()
    subsets = prior_ref.shape[1]
    prior = prior_ref[...].astype(F32)
    prior = jnp.concatenate([prior, jnp.zeros((n_part, chunk - subsets), F32)], axis=1)
    weighted = []
    for i in range(n_part):
        curve = held[i, pl.ds(class_ref[i] % ROWS, 1), :] * noise_ref[...]
        weighted.append(particles_ref[i].astype(F32) * curve)
    for c in range(nz):
        rows = jnp.zeros((ROWS, chunk), F32)
        for i in range(n_part):
            both = piece(weighted[i], c)
            rows = jnp.where(row8 == i, both[0:1], rows)
            rows = jnp.where(row8 == n_part + i, both[1:2], rows)
            extra = jnp.where(
                lane8 == subsets, class_ref[i].astype(F32), jnp.broadcast_to(prior[i : i + 1], rows.shape)
            )
            rows = jnp.where(row8 == 2 * n_part + i, extra, rows)
        part = rows.astype(BF16)
        for s in range(nz):

            @pl.when((z ^ s) == c)
            def _():
                parts[s][...] = part


def table_kernel(
    nz, ny, chunk, trans_ref, curves_ref, noise_ref, phase_ref, cos_ref, sin_ref, square_ref, angle
):
    z = lax.axis_index("blk") // ny
    length = curves_ref.shape[1]
    angle[...] = jnp.zeros_like(angle)
    square_ref[...] = jnp.zeros_like(square_ref)
    for c in range(nz):
        width = min(chunk, length - c * chunk)
        span = slice(c * chunk, c * chunk + width)

        @pl.when(z == c)
        def _():
            for t in range(phase_ref.shape[0]):
                angle[t : t + 1, :width] = phase_ref[pl.ds(trans_ref[t], 1), span]
            curve = curves_ref[:, span]
            square_ref[:, :width] = curve * curve * noise_ref[:, span]

    cos_ref[...] = jnp.cos(angle[...])
    sin_ref[...] = jnp.sin(angle[...])


def score_kernel(nz, ny, ng, n_part, tail, subsets, cos_ref, sin_ref, square_ref, *rest):
    n_bank = nz * ny
    banks, parts, outs = rest[:n_bank], rest[n_bank : n_bank + ng], rest[n_bank + ng : n_bank + ng + nz]
    real_ref, imag_ref, shifted_ref = rest[n_bank + ng + nz :]
    blk = lax.axis_index("blk")
    z, y, g = blk // ny, blk % ny, lax.axis_index("grp")
    n_proj = banks[0].shape[0] // 2
    chunk = banks[0].shape[1]
    total = n_bank * n_proj
    shifts = cos_ref.shape[0]
    classes_count = square_ref.shape[0]

    for s in range(nz):
        for r in range(ny):
            both = banks[s * ny + r][...].astype(F32)
            where = pl.multiple_of(((z ^ s) * ny + (y ^ r)) * n_proj, n_proj)
            real_ref[pl.ds(where, n_proj), :] = both[:n_proj]
            imag_ref[pl.ds(where, n_proj), :] = both[n_proj:]
    real, imag = real_ref[...], imag_ref[...]

    held = jnp.concatenate([part[...] for part in parts], axis=0)
    count = nz * ng * n_part
    out_row = lax.broadcasted_iota(jnp.int32, (3 * count, held.shape[0]), 0)
    in_row = lax.broadcasted_iota(jnp.int32, (3 * count, held.shape[0]), 1)
    kind, rest_row = out_row // count, out_row % count
    slot, rest_row = rest_row // (ng * n_part), rest_row % (ng * n_part)
    group, i = rest_row // n_part, rest_row % n_part
    source = (group ^ g) * (nz * ROWS) + slot * ROWS + kind * n_part + i
    pick = (in_row == source).astype(F32).astype(BF16)
    ordered = jnp.dot(pick, held, preferred_element_type=F32)
    weighted = jnp.concatenate([ordered[:count], ordered[count : 2 * count]], axis=1).astype(BF16)
    extra = ordered[2 * count :]

    for t in range(shifts):
        cos_part, sin_part = cos_ref[t : t + 1, :], sin_ref[t : t + 1, :]
        rows = slice(t * total, (t + 1) * total)
        shifted_ref[rows, :chunk] = (cos_part * real + sin_part * imag).astype(BF16)
        shifted_ref[rows, chunk:] = (cos_part * imag - sin_part * real).astype(BF16)
    cross = lax.dot_general(weighted, shifted_ref[...], NT_DIMS, preferred_element_type=F32)

    power = real * real + imag * imag
    norm_table = lax.dot_general(
        square_ref[...], power, NT_DIMS, precision=HIGHEST, preferred_element_type=F32
    )
    class_col = lax.broadcasted_iota(jnp.int32, (count, classes_count), 1).astype(F32)
    onehot = (class_col == extra[:, subsets : subsets + 1]).astype(F32)
    norm = jnp.dot(onehot, norm_table, precision=HIGHEST, preferred_element_type=F32)
    subset_col = lax.broadcasted_iota(jnp.int32, (total, subsets), 1).astype(F32)
    subset_hot = (subset_col == real[:, tail : tail + 1]).astype(F32).astype(BF16)
    prior = lax.dot_general(
        extra[:, :subsets].astype(BF16), subset_hot, NT_DIMS, preferred_element_type=F32
    )
    added = jnp.where(z == nz - 1, prior, jnp.zeros_like(prior)) - 0.5 * norm
    added = jnp.concatenate([added] * shifts, axis=1)
    result = cross + added
    dest = ng * n_part
    for s in range(nz):
        outs[s][...] = result[s * dest : (s + 1) * dest]


def sum_kernel(n_proj, *refs):
    *terms, out_ref = refs
    total = terms[0][...]
    for term in terms[1:]:
        total = total + term[...]
    for t in range(out_ref.shape[0]):
        out_ref[t] = total[:, t * n_proj : (t + 1) * n_proj]


def per_device(
    particles,
    ctf_class,
    orient_prior,
    ctf_curves,
    noise_weight,
    shift_phase,
    trans_index,
    projections,
    orient_subset,
):
    nb, ng = lax.axis_size("blk"), lax.axis_size("grp")
    nz = 4
    ny = nb // nz
    n_part, n_proj = particles.shape[0], projections.shape[0]
    length = particles.shape[2]
    shifts = shift_phase.shape[0]
    classes_count = ctf_curves.shape[0]
    subsets = orient_prior.shape[1]
    chunk = 128 * -(-length // (128 * nz))
    tail = length - (nz - 1) * chunk
    noise = noise_weight.reshape(1, length)
    shape = jax.ShapeDtypeStruct

    packed = pl.pallas_call(
        functools.partial(pack_kernel, nz, ny, chunk),
        out_shape=[shape((2 * n_proj, chunk), BF16)] * nz + [shape((ROWS, chunk), BF16)] * nz,
        in_specs=[_smem(), _smem(), _vmem(), _vmem(), pl.BlockSpec(memory_space=pl.ANY), _vmem(), _vmem()],
        out_specs=[_vmem()] * (2 * nz),
        scratch_shapes=[pltpu.VMEM((n_part, ROWS, length), F32), pltpu.SemaphoreType.DMA((n_part,))],
        compiler_params=_params(8),
        name="pack",
    )(ctf_class, orient_subset, particles, orient_prior, ctf_curves, noise, projections)
    banks, parts = packed[:nz], packed[nz:]

    def swap_plane(value, s):
        pairs = [(b, ((b // ny) ^ s) * ny + b % ny) for b in range(nb)]
        return lax.ppermute(value, "blk", pairs)

    def swap_inner(value, r):
        return lax.ppermute(value, "blk", [(b, b // ny * ny + ((b % ny) ^ r)) for b in range(nb)])

    def swap_group(value, r):
        return lax.ppermute(value, "grp", [(g, g ^ r) for g in range(ng)])

    parts = [parts[0]] + [swap_plane(parts[s], s) for s in range(1, nz)]
    banks = [banks[0]] + [swap_plane(banks[s], s) for s in range(1, nz)]
    part = jnp.concatenate(parts, axis=0)
    part_all = [part] + [swap_group(part, r) for r in range(1, ng)]
    bank_all = [
        banks[s] if r == 0 else swap_inner(banks[s], r) for s in range(nz) for r in range(ny)
    ]

    cos_part, sin_part, square = pl.pallas_call(
        functools.partial(table_kernel, nz, ny, chunk),
        out_shape=[shape((shifts, chunk), F32)] * 2 + [shape((classes_count, chunk), F32)],
        in_specs=[_smem(), _vmem(), _vmem(), _vmem()],
        out_specs=[_vmem()] * 3,
        scratch_shapes=[pltpu.VMEM((shifts, chunk), F32)],
        compiler_params=_params(8),
        cost_estimate=pl.CostEstimate(flops=4_000_000, bytes_accessed=2_000_000, transcendentals=0),
        name="tables",
    )(trans_index, ctf_curves, noise, shift_phase)

    count = nz * ng * n_part
    total = nb * n_proj
    outs = pl.pallas_call(
        functools.partial(score_kernel, nz, ny, ng, n_part, tail, subsets),
        out_shape=[shape((ng * n_part, shifts * total), F32)] * nz,
        in_specs=[_vmem()] * (3 + nb + ng),
        out_specs=[_vmem()] * nz,
        scratch_shapes=[
            pltpu.VMEM((total, chunk), F32),
            pltpu.VMEM((total, chunk), F32),
            pltpu.VMEM((shifts * total, 2 * chunk), BF16),
        ],
        compiler_params=_params(32),
        cost_estimate=pl.CostEstimate(
            flops=4 * count * total * shifts * chunk, bytes_accessed=4_000_000, transcendentals=0
        ),
        name="score",
    )(cos_part, sin_part, square, *bank_all, *part_all)
    terms = [outs[0]] + [swap_plane(outs[s], s) for s in range(1, nz)]
    scores = pl.pallas_call(
        functools.partial(sum_kernel, total),
        out_shape=shape((shifts, ng * n_part, total), F32),
        in_specs=[_vmem()] * nz,
        out_specs=_vmem(),
        compiler_params=_params(4),
        name="sum",
    )(*terms)
    return scores.transpose(1, 0, 2)


def solution(mesh):
    placed = (
        P(("blk", "grp"), None, None),
        P(("blk", "grp")),
        P(("blk", "grp"), None),
        P(),
        P(),
        P(),
        P(),
        P(("grp", "blk"), None, None),
        P(("grp", "blk")),
    )
    return jax.shard_map(
        per_device, mesh=mesh, in_specs=placed, out_specs=P("blk", None, "grp"), check_vma=False
    )
```

time: 83 us -> 38.5 us (0.46)
  blocking collectives: 61.8 us -> 0 us
  starting transfers between devices: 0 us -> 20.8 us
  matrix products: 10.6 us -> 0 us
  waiting for transfers between devices: 0 us -> 7.76 us
  Pallas kernels: 0 us -> 4.63 us
  other arithmetic: 3.58 us -> 0 us
  between operations: 1.41 us -> 0.09 us
    all_gather x3 -> x0, blocking collectives: 43.8 us -> none  [the longest x1 33.1 us: per_device(): bank = lax.all_gather(projections, 'blk', axis=0, tiled=True)]
    ppermute x0 -> x16, starting transfers between devices: none -> 20.8 us  [the longest x9 14.5 us: swap_plane(): return lax.ppermute(value, 'blk', pairs)]
    unnamed x2 -> x0, blocking collectives: 18 us -> none
    dot_general x6 -> x0, matrix products: 10.6 us -> none  [the longest x1 4.24 us: per_device(): jnp.einsum('nck,tmck->ntm', weighted, shifted, preferred_element_type=jnp...]
    ppermute x0 -> x16, waiting for transfers between devices: none -> 7.76 us  [the longest x9 5.39 us: swap_plane(): return lax.ppermute(value, 'blk', pairs)]
    pallas_call x0 -> x4, Pallas kernels: none -> 4.63 us  [the longest x1 1.55 us: per_device(): pl.pallas_call(functools.partial(score_kernel, nz, ny, ng, n_part, tail,...]
    another operation x1 -> x0, other arithmetic: 2.56 us -> none
    convert_element_type x2 -> x0, other arithmetic: 1.01 us -> none  [the longest x1 0.8 us: per_device(): (particles.astype(jnp.float32) * curve_local[:, None, :]).astype(jnp.bflo...]
  transfers between devices with their start and end apart: 0 -> 16, of which waited for: 0 -> 5; matrix products, arithmetic and copies ran while one was open for 0% -> 0% of each run, Pallas kernels for 0% -> 3%
where the time goes in v2:
time: 38.5 us; the launch traced here: 38.2 us
  starting transfers between devices  20.8 us (54%)
  waiting for transfers between devices  7.76 us (20%)
  local copies, waits for them, and re-layouts  4.96 us (13%)
  Pallas kernels  4.63 us (12%)
    ppermute x9, starting transfers between devices, swap_plane(): return lax.ppermute(value, 'blk', pairs)  14.5 us
    ppermute x9, waiting for transfers between devices, swap_plane(): return lax.ppermute(value, 'blk', pairs)  5.39 us
    unnamed x25, local copies, waits for them, and re-layouts  4.96 us
    ppermute x4, starting transfers between devices, swap_inner(): lax.ppermute(value, 'blk', [(b, b // ny * ny + (b % ny ^ r)) for b in ran...  4.73 us
    ppermute x4, waiting for transfers between devices, swap_inner(): lax.ppermute(value, 'blk', [(b, b // ny * ny + (b % ny ^ r)) for b in ran...  2.36 us
    ppermute x3, starting transfers between devices, swap_group(): return lax.ppermute(value, 'grp', [(g, g ^ r) for g in range(ng)])  1.57 us
    pallas_call x1, Pallas kernels, per_device(): pl.pallas_call(functools.partial(score_kernel, nz, ny, ng, n_part, tail,...  1.55 us
    pallas_call x1, Pallas kernels, per_device(): pl.pallas_call(functools.partial(pack_kernel, nz, ny, chunk), out_shape=[...  1.36 us
  transfers between devices with their start and end apart: 16, of which 5 were waited for; matrix products, arithmetic and copies ran while one was open for 0% of the time, Pallas kernels for 3%

profile of v2, /device:TPU:0, one launch (start us, length us, event | category | flops | bytes accessed | tf_op | source)
XLA Modules:
  0.0 38.2 jit_solution(12909669454450094725)
XLA Ops:
  0.0 0.0 copy-start.7
  0.0 0.0 copy-start.8
  0.0 0.7 %copy-done.7 = bf16[2,192]{1,0:T(2,128)(2,1)S(1)} copy-done((bf16[2,192]{1,0:T(2,128)(2,1)S(1)}, bf16[2,192]{1,0:T(2,128)(2,1)}, u32[]{:S(2)}) %copy-start.7) | copy-done | bytes 792
  0.7 0.0 copy-done.8
  0.7 0.0 copy-start
  0.7 1.2 %copy-done = f32[64,4000]{1,0:T(8,128)S(1)} copy-done((f32[64,4000]{1,0:T(8,128)S(1)}, f32[64,4000]{1,0:T(8,128)}, u32[]{:S(2)}) %copy-start) | copy-done | bytes 1024024
  1.9 0.0 copy-start.3
  1.9 0.9 %copy-done.3 = bf16[8,2,4000]{2,1,0:T(2,128)(2,1)S(1)} copy-done((bf16[8,2,4000]{2,1,0:T(2,128)(2,1)S(1)}, bf16[8,2,4000]{2,1,0:T(2,128)(2,1)}, u32[]{:S(2)}) %copy-start.3) | copy-done | bytes 128024
  2.8 0.0 copy-start.4
  2.8 0.7 %copy-done.4 = f32[4000]{0:T(1024)S(1)} copy-done((f32[4000]{0:T(1024)S(1)}, f32[4000]{0:T(1024)}, u32[]{:S(2)}) %copy-start.4) | copy-done | bytes 16024
  3.5 0.0 copy-start.6
  3.5 0.8 %copy-done.6 = bf16[2,2,4000]{2,1,0:T(2,128)(2,1)S(1)} copy-done((bf16[2,2,4000]{2,1,0:T(2,128)(2,1)S(1)}, bf16[2,2,4000]{2,1,0:T(2,128)(2,1)}, u32[]{:S(2)}) %copy-start.6) | copy-done | bytes 32024
  4.3 0.0 copy-start.9
  4.3 0.7 %copy-done.9 = s32[8]{0:T(128)S(1)} copy-done((s32[8]{0:T(128)S(1)}, s32[8]{0:T(128)}, u32[]{:S(2)}) %copy-start.9) | copy-done | bytes 56
  4.9 0.0 copy-start.1
  4.9 0.0 copy-start.2
  4.9 1.4 %pack.1 = (bf16[16,1024]{1,0:T(8,128)(2,1)S(1)}, bf16[16,1024]{1,0:T(8,128)(2,1)S(1)}, bf16[16,1024]{1,0:T(8,128)(2,1)S(1)}, bf16[16,1024]{1,0:T(8,128)(2,1)S(1)...) custom-call(s32[2]{0:T(128)S(1)} %copy-done.8, ...), custom_call_target="tpu_custom_call" | custom-call | tf_op jit(solution)/shard_map/pack/pallas_call | solution.py:217
  6.3 3.1 %collective-permute-start.7 = (bf16[8,1024]{1,0:T(8,128)(2,1)S(1)}, bf16[8,1024]{1,0:T(8,128)(2,1)S(1)}, u32[]{:S(2)}, u32[]{:S(2)}) collective-permute-start(bf16[8,1024]{1,0:T(8,128)(2,1)S(1)} %get-tuple-element.28), channel_id=1, source_target_pairs={{0,2},{1,3},{2,0},{3,1},{4,6},{5,7},{6,4},{7,5},{8,10},{9,11},{10,... | collective-permute-start | bytes 49160 | tf_op jit(solution)/shard_map/ppermute | solution.py:230
  9.4 2.6 %collective-permute-start.8 = (bf16[8,1024]{1,0:T(8,128)(2,1)S(1)}, bf16[8,1024]{1,0:T(8,128)(2,1)S(1)}, u32[]{:S(2)}, u32[]{:S(2)}) collective-permute-start(bf16[8,1024]{1,0:T(8,128)(2,1)S(1)} %get-tuple-element.29), channel_id=1, source_target_pairs={{0,4},{1,5},{2,6},{3,7},{4,0},{5,1},{6,2},{7,3},{8,12},{9,13},{10,... | collective-permute-start | bytes 49160 | tf_op jit(solution)/shard_map/ppermute | solution.py:230
  12.0 0.0 collective-permute-start.9
  12.0 0.9 %collective-permute-start.1 = (bf16[16,1024]{1,0:T(8,128)(2,1)S(1)}, bf16[16,1024]{1,0:T(8,128)(2,1)S(1)}, u32[]{:S(2)}, u32[]{:S(2)}) collective-permute-start(bf16[16,1024]{1,0:T(8,128)(2,1)S(1)} %get-tuple-element.24), channel_id=1, source_target_pairs={{0,2},{1,3},{2,0},{3,1},{4,6},{5,7},{6,4},{7,5},{8,10},{9,11},{10,... | collective-permute-start | bytes 98312 | tf_op jit(solution)/shard_map/ppermute | solution.py:230
  12.9 3.5 %collective-permute-start.3 = (bf16[16,1024]{1,0:T(8,128)(2,1)S(1)}, bf16[16,1024]{1,0:T(8,128)(2,1)S(1)}, u32[]{:S(2)}, u32[]{:S(2)}) collective-permute-start(bf16[16,1024]{1,0:T(8,128)(2,1)S(1)} %get-tuple-element.25), channel_id=1, source_target_pairs={{0,4},{1,5},{2,6},{3,7},{4,0},{5,1},{6,2},{7,3},{8,12},{9,13},{10,... | collective-permute-start | bytes 98312 | tf_op jit(solution)/shard_map/ppermute | solution.py:230
  16.4 0.0 collective-permute-done.7
  16.4 0.0 collective-permute-start.5
  16.4 0.0 collective-permute-done.8
  16.4 1.7 %collective-permute-start = (bf16[16,1024]{1,0:T(8,128)(2,1)S(1)}, bf16[16,1024]{1,0:T(8,128)(2,1)S(1)}, u32[]{:S(2)}, u32[]{:S(2)}) collective-permute-start(bf16[16,1024]{1,0:T(8,128)(2,1)S(1)} %get-tuple-element.23.rest_0_), channel_id=1, source_target_pairs={{0,1},{1,0},{2,3},{3,2},{4,5},{5,4},{6,7},{7,6},{8,9},{9,8},{10,11... | collective-permute-start | bytes 98312 | tf_op jit(solution)/shard_map/ppermute | solution.py:233
  18.1 0.0 copy-start.5
  18.1 0.0 copy-start.10
  18.1 0.0 collective-permute-done.9
  18.2 0.1 collective-permute-start.12
  18.2 0.0 collective-permute-done.1.rest_2_
  18.2 1.0 %collective-permute-start.2 = (bf16[16,1024]{1,0:T(8,128)(2,1)S(1)}, bf16[16,1024]{1,0:T(8,128)(2,1)S(1)}, u32[]{:S(2)}, u32[]{:S(2)}) collective-permute-start(bf16[16,1024]{1,0:T(8,128)(2,1)S(1)} %collective-permute-done.1.rest_2_), channel_id=1, source_target_pairs={{0,1},{1,0},{2,3},{3,2},{4,5},{5,4},{6,7},{7,6},{8,9},{9,8},{10,11... | collective-permute-start | bytes 98312 | tf_op jit(solution)/shard_map/ppermute | solution.py:233
  19.2 0.0 collective-permute-done.3.rest_4_
  19.2 1.5 %collective-permute-start.11 = (bf16[32,1024]{1,0:T(8,128)(2,1)S(1)}, bf16[32,1024]{1,0:T(8,128)(2,1)S(1)}, u32[]{:S(2)}, u32[]{:S(2)}) collective-permute-start(bf16[32,1024]{1,0:T(8,128)(2,1)S(1)} %constant_dynamic-update-slice_fusion.rest_8_), channel_id=1, source_target_pairs={{0,16},{8,24},{16,0},{24,8},{1,17},{9,25},{17,1},{25,9},{2,18},{10... | collective-permute-start | bytes 196616 | tf_op jit(solution)/shard_map/ppermute | solution.py:236
  20.7 1.4 %collective-permute-done.5.rest_6_ = bf16[16,1024]{1,0:T(8,128)(2,1)S(1)} collective-permute-done((bf16[16,1024]{1,0:T(8,128)(2,1)S(1)}, bf16[16,1024]{1,0:T(8,128)(2,1)S(1)}, u32[]{:S(2)}, u32[]{:S(2)}) %collective-permute-start.5) | collective-permute-done | bytes 32800 | tf_op jit(solution)/shard_map/ppermute | solution.py:230
  22.1 0.0 collective-permute-start.10
  22.1 0.0 collective-permute-done.rest_1_
  22.1 1.5 %collective-permute-start.4 = (bf16[16,1024]{1,0:T(8,128)(2,1)S(1)}, bf16[16,1024]{1,0:T(8,128)(2,1)S(1)}, u32[]{:S(2)}, u32[]{:S(2)}) collective-permute-start(bf16[16,1024]{1,0:T(8,128)(2,1)S(1)} %collective-permute-done.3.rest_4_), channel_id=1, source_target_pairs={{0,1},{1,0},{2,3},{3,2},{4,5},{5,4},{6,7},{7,6},{8,9},{9,8},{10,11... | collective-permute-start | bytes 98312 | tf_op jit(solution)/shard_map/ppermute | solution.py:233
  23.6 0.0 collective-permute-done.2.rest_3_
  23.6 0.5 %collective-permute-start.6 = (bf16[16,1024]{1,0:T(8,128)(2,1)S(1)}, bf16[16,1024]{1,0:T(8,128)(2,1)S(1)}, u32[]{:S(2)}, u32[]{:S(2)}) collective-permute-start(bf16[16,1024]{1,0:T(8,128)(2,1)S(1)} %collective-permute-done.5.rest_6_), channel_id=1, source_target_pairs={{0,1},{1,0},{2,3},{3,2},{4,5},{5,4},{6,7},{7,6},{8,9},{9,8},{10,11... | collective-permute-start | bytes 98312 | tf_op jit(solution)/shard_map/ppermute | solution.py:233
  24.1 0.0 copy-done.1
  24.1 0.0 copy-done.2
  24.1 0.0 copy-done.5
  24.2 0.0 copy-done.10
  24.2 1.0 %tables.1 = (f32[9,1024]{1,0:T(8,128)S(1)}, f32[9,1024]{1,0:T(8,128)S(1)}, f32[64,1024]{1,0:T(8,128)S(1)}) custom-call(s32[9]{0:T(128)S(1)} %copy-done.10, f32[64,4000]{1,0:T(8,128)S(1)} %copy-done.1, f32[1,4000]{1,0:T(1,128)S(1)} %bitcast.3, f32[9,4000]{1,0:T(8,128)S(1)} %copy-done.2), custom_call_target="tpu_custom_call" | custom-call | flops 4000000 | bytes 2000000 | tf_op jit(solution)/shard_map/tables/pallas_call | solution.py:246
  25.2 0.8 %collective-permute-done.4.rest_5_ = bf16[16,1024]{1,0:T(8,128)(2,1)S(1)} collective-permute-done((bf16[16,1024]{1,0:T(8,128)(2,1)S(1)}, bf16[16,1024]{1,0:T(8,128)(2,1)S(1)}, u32[]{:S(2)}, u32[]{:S(2)}) %collective-permute-start.4) | collective-permute-done | bytes 32800 | tf_op jit(solution)/shard_map/ppermute | solution.py:233
  26.0 1.5 %collective-permute-done.6.rest_7_ = bf16[16,1024]{1,0:T(8,128)(2,1)S(1)} collective-permute-done((bf16[16,1024]{1,0:T(8,128)(2,1)S(1)}, bf16[16,1024]{1,0:T(8,128)(2,1)S(1)}, u32[]{:S(2)}, u32[]{:S(2)}) %collective-permute-start.6) | collective-permute-done | bytes 32800 | tf_op jit(solution)/shard_map/ppermute | solution.py:233
  27.6 0.0 collective-permute-done.12.rest_11_
  27.6 0.0 collective-permute-done.11.rest_10_
  27.6 0.0 collective-permute-done.10.rest_9_
  27.6 1.5 %score.1 = (f32[8,576]{1,0:T(8,128)S(1)}, f32[8,576]{1,0:T(8,128)S(1)}, f32[8,576]{1,0:T(8,128)S(1)}, f32[8,576]{1,0:T(8,128)S(1)}) custom-call(f32[9,1024]{1,0:T(8,128)S(1)} %get-tuple-element.20.cos_ref, f32[9,1024]{1,0:T(8,128)S(1)} %get-tuple-element.21.sin_ref, f32[64,1024]{1,0:T(8,128)S(1)} %get-tuple-element.22.square_ref, ...), custom_call_target="tpu_custom_call" | custom-call | flops 75497472 | bytes 4000000 | tf_op jit(solution)/shard_map/score/pallas_call | solution.py:259
  29.1 0.0 collective-permute-start.13
  29.1 2.8 %collective-permute-start.14 = (f32[8,576]{1,0:T(8,128)S(1)}, f32[8,576]{1,0:T(8,128)S(1)}, u32[]{:S(2)}, u32[]{:S(2)}) collective-permute-start(f32[8,576]{1,0:T(8,128)S(1)} %get-tuple-element.33), channel_id=1, source_target_pairs={{0,4},{1,5},{2,6},{3,7},{4,0},{5,1},{6,2},{7,3},{8,12},{9,13},{10,... | collective-permute-start | bytes 55304 | tf_op jit(solution)/shard_map/ppermute | solution.py:230
  31.9 1.6 %collective-permute-start.15 = (f32[8,576]{1,0:T(8,128)S(1)}, f32[8,576]{1,0:T(8,128)S(1)}, u32[]{:S(2)}, u32[]{:S(2)}) collective-permute-start(f32[8,576]{1,0:T(8,128)S(1)} %get-tuple-element.34), channel_id=1, source_target_pairs={{0,6},{1,7},{2,4},{3,5},{4,2},{5,3},{6,0},{7,1},{8,14},{9,15},{10,... | collective-permute-start | bytes 55304 | tf_op jit(solution)/shard_map/ppermute | solution.py:230
  33.5 0.0 collective-permute-done.13.refs_1_
  33.5 0.5 %collective-permute-done.14.refs_2_ = f32[8,576]{1,0:T(8,128)S(1)} collective-permute-done((f32[8,576]{1,0:T(8,128)S(1)}, f32[8,576]{1,0:T(8,128)S(1)}, u32[]{:S(2)}, u32[]{:S(2)}) %collective-permute-start.14) | collective-permute-done | bytes 18464 | tf_op jit(solution)/shard_map/ppermute | solution.py:230
  34.0 3.5 %collective-permute-done.15.refs_3_ = f32[8,576]{1,0:T(8,128)S(1)} collective-permute-done((f32[8,576]{1,0:T(8,128)S(1)}, f32[8,576]{1,0:T(8,128)S(1)}, u32[]{:S(2)}, u32[]{:S(2)}) %collective-permute-start.15) | collective-permute-done | bytes 18464 | tf_op jit(solution)/shard_map/ppermute | solution.py:230
  37.5 0.7 %sum.1 = f32[9,8,64]{2,1,0:T(8,128)} custom-call(f32[8,576]{1,0:T(8,128)S(1)} %get-tuple-element.31.refs_0_, f32[8,576]{1,0:T(8,128)S(1)} %collective-permute-done.13.refs_1_, f32[8,576]{1,0:T(8,128)S(1)} %collective-permute-done.14.refs_2_, f32[8,576]{1,0:T(8,128)S(1)} %collective-permute-done.15.refs_3_), custom_call_target="tpu_custom_call" | custom-call | tf_op jit(solution)/shard_map/sum/pallas_call | solution.py:276
  (4 shorter events, 0.0 us)
Async XLA Ops:
  0.0 0.7 %copy-start.7 = (bf16[2,192]{1,0:T(2,128)(2,1)S(1)}, bf16[2,192]{1,0:T(2,128)(2,1)}, u32[]{:S(2)}) copy-start(bf16[2,192]{1,0:T(2,128)(2,1)} %prior_ref.1) | copy-start | bytes 2308
  0.0 0.7 %copy-start.8 = (s32[2]{0:T(128)S(1)}, s32[2]{0:T(128)}, u32[]{:S(2)}) copy-start(s32[2]{0:T(128)} %class_ref.1) | copy-start | bytes 28
  0.7 1.2 %copy-start = (f32[64,4000]{1,0:T(8,128)S(1)}, f32[64,4000]{1,0:T(8,128)}, u32[]{:S(2)}) copy-start(f32[64,4000]{1,0:T(8,128)} %curves_ref.3) | copy-start | bytes 3072004
  1.9 0.9 %copy-start.3 = (bf16[8,2,4000]{2,1,0:T(2,128)(2,1)S(1)}, bf16[8,2,4000]{2,1,0:T(2,128)(2,1)}, u32[]{:S(2)}) copy-start(bf16[8,2,4000]{2,1,0:T(2,128)(2,1)} %proj_ref.1) | copy-start | bytes 384004
  2.8 0.7 %copy-start.4 = (f32[4000]{0:T(1024)S(1)}, f32[4000]{0:T(1024)}, u32[]{:S(2)}) copy-start(f32[4000]{0:T(1024)} %param.13) | copy-start | bytes 48004
  3.5 0.8 %copy-start.6 = (bf16[2,2,4000]{2,1,0:T(2,128)(2,1)S(1)}, bf16[2,2,4000]{2,1,0:T(2,128)(2,1)}, u32[]{:S(2)}) copy-start(bf16[2,2,4000]{2,1,0:T(2,128)(2,1)} %particles_ref.1) | copy-start | bytes 96004
  4.3 0.7 %copy-start.9 = (s32[8]{0:T(128)S(1)}, s32[8]{0:T(128)}, u32[]{:S(2)}) copy-start(s32[8]{0:T(128)} %subset_ref.1) | copy-start | bytes 100
  4.9 19.2 %copy-start.1 = (f32[64,4000]{1,0:T(8,128)S(1)}, f32[64,4000]{1,0:T(8,128)}, u32[]{:S(2)}) copy-start(f32[64,4000]{1,0:T(8,128)} %curves_ref.3) | copy-start | bytes 3072004
  4.9 19.2 %copy-start.2 = (f32[9,4000]{1,0:T(8,128)S(1)}, f32[9,4000]{1,0:T(8,128)}, u32[]{:S(2)}) copy-start(f32[9,4000]{1,0:T(8,128)} %phase_ref.1) | copy-start | bytes 432004
  6.3 10.1 %collective-permute-start.7 = (bf16[8,1024]{1,0:T(8,128)(2,1)S(1)}, bf16[8,1024]{1,0:T(8,128)(2,1)S(1)}, u32[]{:S(2)}, u32[]{:S(2)}) collective-permute-start(bf16[8,1024]{1,0:T(8,128)(2,1)S(1)} %get-tuple-element.28), channel_id=1, source_target_pairs={{0,2},{1,3},{2,0},{3,1},{4,6},{5,7},{6,4},{7,5},{8,10},{9,11},{10,... | collective-permute-start | bytes 49160 | tf_op jit(solution)/shard_map/ppermute | solution.py:230
  9.4 7.0 %collective-permute-start.8 = (bf16[8,1024]{1,0:T(8,128)(2,1)S(1)}, bf16[8,1024]{1,0:T(8,128)(2,1)S(1)}, u32[]{:S(2)}, u32[]{:S(2)}) collective-permute-start(bf16[8,1024]{1,0:T(8,128)(2,1)S(1)} %get-tuple-element.29), channel_id=1, source_target_pairs={{0,4},{1,5},{2,6},{3,7},{4,0},{5,1},{6,2},{7,3},{8,12},{9,13},{10,... | collective-permute-start | bytes 49160 | tf_op jit(solution)/shard_map/ppermute | solution.py:230
  12.0 6.1 %collective-permute-start.9 = (bf16[8,1024]{1,0:T(8,128)(2,1)S(1)}, bf16[8,1024]{1,0:T(8,128)(2,1)S(1)}, u32[]{:S(2)}, u32[]{:S(2)}) collective-permute-start(bf16[8,1024]{1,0:T(8,128)(2,1)S(1)} %get-tuple-element.30), channel_id=1, source_target_pairs={{0,6},{1,7},{2,4},{3,5},{4,2},{5,3},{6,0},{7,1},{8,14},{9,15},{10,... | collective-permute-start | bytes 49160 | tf_op jit(solution)/shard_map/ppermute | solution.py:230
  12.0 6.2 %collective-permute-start.1 = (bf16[16,1024]{1,0:T(8,128)(2,1)S(1)}, bf16[16,1024]{1,0:T(8,128)(2,1)S(1)}, u32[]{:S(2)}, u32[]{:S(2)}) collective-permute-start(bf16[16,1024]{1,0:T(8,128)(2,1)S(1)} %get-tuple-element.24), channel_id=1, source_target_pairs={{0,2},{1,3},{2,0},{3,1},{4,6},{5,7},{6,4},{7,5},{8,10},{9,11},{10,... | collective-permute-start | bytes 98312 | tf_op jit(solution)/shard_map/ppermute | solution.py:230
  12.9 6.3 %collective-permute-start.3 = (bf16[16,1024]{1,0:T(8,128)(2,1)S(1)}, bf16[16,1024]{1,0:T(8,128)(2,1)S(1)}, u32[]{:S(2)}, u32[]{:S(2)}) collective-permute-start(bf16[16,1024]{1,0:T(8,128)(2,1)S(1)} %get-tuple-element.25), channel_id=1, source_target_pairs={{0,4},{1,5},{2,6},{3,7},{4,0},{5,1},{6,2},{7,3},{8,12},{9,13},{10,... | collective-permute-start | bytes 98312 | tf_op jit(solution)/shard_map/ppermute | solution.py:230
  16.4 5.7 %collective-permute-start.5 = (bf16[16,1024]{1,0:T(8,128)(2,1)S(1)}, bf16[16,1024]{1,0:T(8,128)(2,1)S(1)}, u32[]{:S(2)}, u32[]{:S(2)}) collective-permute-start(bf16[16,1024]{1,0:T(8,128)(2,1)S(1)} %get-tuple-element.26), channel_id=1, source_target_pairs={{0,6},{1,7},{2,4},{3,5},{4,2},{5,3},{6,0},{7,1},{8,14},{9,15},{10,... | collective-permute-start | bytes 98312 | tf_op jit(solution)/shard_map/ppermute | solution.py:230
  16.4 5.7 %collective-permute-start = (bf16[16,1024]{1,0:T(8,128)(2,1)S(1)}, bf16[16,1024]{1,0:T(8,128)(2,1)S(1)}, u32[]{:S(2)}, u32[]{:S(2)}) collective-permute-start(bf16[16,1024]{1,0:T(8,128)(2,1)S(1)} %get-tuple-element.23.rest_0_), channel_id=1, source_target_pairs={{0,1},{1,0},{2,3},{3,2},{4,5},{5,4},{6,7},{7,6},{8,9},{9,8},{10,11... | collective-permute-start | bytes 98312 | tf_op jit(solution)/shard_map/ppermute | solution.py:233
  18.1 6.0 %copy-start.5 = (f32[4000]{0:T(1024)S(1)}, f32[4000]{0:T(1024)}, u32[]{:S(2)}) copy-start(f32[4000]{0:T(1024)} %param.13) | copy-start | bytes 48004
  18.1 6.0 %copy-start.10 = (s32[9]{0:T(128)S(1)}, s32[9]{0:T(128)}, u32[]{:S(2)}) copy-start(s32[9]{0:T(128)} %trans_ref.1) | copy-start | bytes 112
  18.2 9.4 %collective-permute-start.12 = (bf16[32,1024]{1,0:T(8,128)(2,1)S(1)}, bf16[32,1024]{1,0:T(8,128)(2,1)S(1)}, u32[]{:S(2)}, u32[]{:S(2)}) collective-permute-start(bf16[32,1024]{1,0:T(8,128)(2,1)S(1)} %constant_dynamic-update-slice_fusion.rest_8_), channel_id=1, source_target_pairs={{0,24},{8,16},{16,8},{24,0},{1,25},{9,17},{17,9},{25,1},{2,26},{10... | collective-permute-start | bytes 196616 | tf_op jit(solution)/shard_map/ppermute | solution.py:236
  18.2 5.4 %collective-permute-start.2 = (bf16[16,1024]{1,0:T(8,128)(2,1)S(1)}, bf16[16,1024]{1,0:T(8,128)(2,1)S(1)}, u32[]{:S(2)}, u32[]{:S(2)}) collective-permute-start(bf16[16,1024]{1,0:T(8,128)(2,1)S(1)} %collective-permute-done.1.rest_2_), channel_id=1, source_target_pairs={{0,1},{1,0},{2,3},{3,2},{4,5},{5,4},{6,7},{7,6},{8,9},{9,8},{10,11... | collective-permute-start | bytes 98312 | tf_op jit(solution)/shard_map/ppermute | solution.py:233
  19.2 8.3 %collective-permute-start.11 = (bf16[32,1024]{1,0:T(8,128)(2,1)S(1)}, bf16[32,1024]{1,0:T(8,128)(2,1)S(1)}, u32[]{:S(2)}, u32[]{:S(2)}) collective-permute-start(bf16[32,1024]{1,0:T(8,128)(2,1)S(1)} %constant_dynamic-update-slice_fusion.rest_8_), channel_id=1, source_target_pairs={{0,16},{8,24},{16,0},{24,8},{1,17},{9,25},{17,1},{25,9},{2,18},{10... | collective-permute-start | bytes 196616 | tf_op jit(solution)/shard_map/ppermute | solution.py:236
  22.1 5.5 %collective-permute-start.10 = (bf16[32,1024]{1,0:T(8,128)(2,1)S(1)}, bf16[32,1024]{1,0:T(8,128)(2,1)S(1)}, u32[]{:S(2)}, u32[]{:S(2)}) collective-permute-start(bf16[32,1024]{1,0:T(8,128)(2,1)S(1)} %constant_dynamic-update-slice_fusion.rest_8_), channel_id=1, source_target_pairs={{0,8},{8,0},{16,24},{24,16},{1,9},{9,1},{17,25},{25,17},{2,10},{10... | collective-permute-start | bytes 196616 | tf_op jit(solution)/shard_map/ppermute | solution.py:236
  22.1 3.9 %collective-permute-start.4 = (bf16[16,1024]{1,0:T(8,128)(2,1)S(1)}, bf16[16,1024]{1,0:T(8,128)(2,1)S(1)}, u32[]{:S(2)}, u32[]{:S(2)}) collective-permute-start(bf16[16,1024]{1,0:T(8,128)(2,1)S(1)} %collective-permute-done.3.rest_4_), channel_id=1, source_target_pairs={{0,1},{1,0},{2,3},{3,2},{4,5},{5,4},{6,7},{7,6},{8,9},{9,8},{10,11... | collective-permute-start | bytes 98312 | tf_op jit(solution)/shard_map/ppermute | solution.py:233
  23.6 3.9 %collective-permute-start.6 = (bf16[16,1024]{1,0:T(8,128)(2,1)S(1)}, bf16[16,1024]{1,0:T(8,128)(2,1)S(1)}, u32[]{:S(2)}, u32[]{:S(2)}) collective-permute-start(bf16[16,1024]{1,0:T(8,128)(2,1)S(1)} %collective-permute-done.5.rest_6_), channel_id=1, source_target_pairs={{0,1},{1,0},{2,3},{3,2},{4,5},{5,4},{6,7},{7,6},{8,9},{9,8},{10,11... | collective-permute-start | bytes 98312 | tf_op jit(solution)/shard_map/ppermute | solution.py:233
  29.1 4.4 %collective-permute-start.13 = (f32[8,576]{1,0:T(8,128)S(1)}, f32[8,576]{1,0:T(8,128)S(1)}, u32[]{:S(2)}, u32[]{:S(2)}) collective-permute-start(f32[8,576]{1,0:T(8,128)S(1)} %get-tuple-element.32), channel_id=1, source_target_pairs={{0,2},{1,3},{2,0},{3,1},{4,6},{5,7},{6,4},{7,5},{8,10},{9,11},{10,... | collective-permute-start | bytes 55304 | tf_op jit(solution)/shard_map/ppermute | solution.py:230
  29.1 4.9 %collective-permute-start.14 = (f32[8,576]{1,0:T(8,128)S(1)}, f32[8,576]{1,0:T(8,128)S(1)}, u32[]{:S(2)}, u32[]{:S(2)}) collective-permute-start(f32[8,576]{1,0:T(8,128)S(1)} %get-tuple-element.33), channel_id=1, source_target_pairs={{0,4},{1,5},{2,6},{3,7},{4,0},{5,1},{6,2},{7,3},{8,12},{9,13},{10,... | collective-permute-start | bytes 55304 | tf_op jit(solution)/shard_map/ppermute | solution.py:230
  31.9 5.6 %collective-permute-start.15 = (f32[8,576]{1,0:T(8,128)S(1)}, f32[8,576]{1,0:T(8,128)S(1)}, u32[]{:S(2)}, u32[]{:S(2)}) collective-permute-start(f32[8,576]{1,0:T(8,128)S(1)} %get-tuple-element.34), channel_id=1, source_target_pairs={{0,6},{1,7},{2,4},{3,5},{4,2},{5,3},{6,0},{7,1},{8,14},{9,15},{10,... | collective-permute-start | bytes 55304 | tf_op jit(solution)/shard_map/ppermute | solution.py:230

commit v3 on v2

v3 whole, which is shorter than its diff:
```python
import functools

import jax
import jax.numpy as jnp
from jax import lax
from jax.experimental import pallas as pl
from jax.experimental.pallas import tpu as pltpu
from jax.sharding import PartitionSpec as P

F32 = jnp.float32
BF16 = jnp.bfloat16
HIGHEST = lax.Precision.HIGHEST
NT_DIMS = (((1,), (1,)), ((), ()))
MIB = 1 << 20
ROWS = 8


def _vmem():
    return pl.BlockSpec(memory_space=pltpu.VMEM)


def _smem():
    return pl.BlockSpec(memory_space=pltpu.SMEM)


def _params(mib):
    return pltpu.CompilerParams(vmem_limit_bytes=mib * MIB)


def pack_kernel(
    half,
    chunk,
    class_hbm,
    subset_hbm,
    particles_hbm,
    prior_hbm,
    curves_hbm,
    noise_hbm,
    proj_hbm,
    bank_keep,
    part_keep,
    send,
    class_ref,
    subset_ref,
    particles_ref,
    prior_ref,
    curves_ref,
    noise_ref,
    proj_ref,
    sems,
):
    pairs = [
        (proj_hbm, proj_ref),
        (subset_hbm, subset_ref),
        (class_hbm, class_ref),
        (curves_hbm, curves_ref),
        (particles_hbm, particles_ref),
        (noise_hbm, noise_ref),
        (prior_hbm, prior_ref),
    ]
    copies = [pltpu.make_async_copy(a, b, sems.at[n]) for n, (a, b) in enumerate(pairs)]
    for copy in copies:
        copy.start()
    n_part, n_proj = particles_ref.shape[0], proj_ref.shape[0]
    length = proj_ref.shape[2]
    mine = lax.axis_index("blk") // half

    def piece(values, c):
        width = min(chunk, length - c * chunk)
        values = values[:, c * chunk : c * chunk + width]
        if width < chunk:
            values = jnp.concatenate(
                [values, jnp.zeros((values.shape[0], chunk - width), values.dtype)], axis=1
            )
        return values

    row8 = lax.broadcasted_iota(jnp.int32, (ROWS, chunk), 0)
    lane8 = lax.broadcasted_iota(jnp.int32, (ROWS, chunk), 1)
    for copy in copies[:2]:
        copy.wait()
    for c in range(2):
        real = jnp.zeros((ROWS, chunk), F32)
        imag = jnp.zeros((ROWS, chunk), F32)
        for j in range(n_proj):
            both = piece(proj_ref[j].astype(F32), c)
            real = jnp.where(row8 == j, both[0:1], real)
            imag = jnp.where(row8 == j, both[1:2], imag)
        if c == 1:
            for j in range(n_proj):
                place = (row8 == j) & (lane8 == length - chunk)
                real = jnp.where(place, subset_ref[j].astype(F32), real)
        bank = jnp.concatenate([real, imag], axis=0).astype(BF16)

        @pl.when(mine == c)
        def _():
            bank_keep[...] = bank

        @pl.when(mine != c)
        def _():
            send[: 2 * n_proj] = bank

    for copy in copies[2:]:
        copy.wait()
    subsets = prior_ref.shape[1]
    prior = prior_ref[...].astype(F32)
    prior = jnp.concatenate([prior, jnp.zeros((n_part, chunk - subsets), F32)], axis=1)
    weighted = []
    for i in range(n_part):
        curve = curves_ref[pl.ds(class_ref[i], 1), :] * noise_ref[...]
        weighted.append(particles_ref[i].astype(F32) * curve)
    for c in range(2):
        rows = jnp.zeros((ROWS, chunk), F32)
        for i in range(n_part):
            both = piece(weighted[i], c)
            rows = jnp.where(row8 == i, both[0:1], rows)
            rows = jnp.where(row8 == n_part + i, both[1:2], rows)
            extra = jnp.where(
                lane8 == subsets, class_ref[i].astype(F32), jnp.broadcast_to(prior[i : i + 1], rows.shape)
            )
            rows = jnp.where(row8 == 2 * n_part + i, extra, rows)
        part = rows.astype(BF16)

        @pl.when(mine == c)
        def _():
            part_keep[...] = part

        @pl.when(mine != c)
        def _():
            send[2 * n_proj :] = part


def table_kernel(
    half, chunk, trans_ref, curves_ref, noise_ref, phase_ref, cos_ref, sin_ref, square_ref, angle
):
    mine = lax.axis_index("blk") // half
    length = curves_ref.shape[1]
    angle[...] = jnp.zeros_like(angle)
    square_ref[...] = jnp.zeros_like(square_ref)
    for c in range(2):
        width = min(chunk, length - c * chunk)
        span = slice(c * chunk, c * chunk + width)

        @pl.when(mine == c)
        def _():
            for t in range(phase_ref.shape[0]):
                angle[t : t + 1, :width] = phase_ref[pl.ds(trans_ref[t], 1), span]
            curve = curves_ref[:, span]
            square_ref[:, :width] = curve * curve * noise_ref[:, span]

    cos_ref[...] = jnp.cos(angle[...])
    sin_ref[...] = jnp.sin(angle[...])


def score_kernel(half, offsets, groups, n_part, tail, subsets, cos_ref, sin_ref, square_ref, *rest):
    n_bank, n_held = len(offsets), len(groups)
    banks, parts, outs = rest[:n_bank], rest[n_bank : n_bank + n_held], rest[n_bank + n_held :][:2]
    real_ref, imag_ref, shifted_ref = rest[n_bank + n_held + 2 :]
    blk, g = lax.axis_index("blk"), lax.axis_index("grp")
    ng = sum(len(group) for group in groups)
    total, chunk = real_ref.shape
    n_proj = total // (2 * half)
    shifts = cos_ref.shape[0]
    classes_count = square_ref.shape[0]

    for bank, offs in zip(banks, offsets):
        for n, offset in enumerate(offs):
            both = bank[2 * n_proj * n : 2 * n_proj * (n + 1)].astype(F32)
            where = pl.multiple_of((blk ^ offset) * n_proj, n_proj)
            real_ref[pl.ds(where, n_proj), :] = both[:n_proj]
            imag_ref[pl.ds(where, n_proj), :] = both[n_proj:]
    real, imag = real_ref[...], imag_ref[...]

    held = jnp.concatenate([part[...] for part in parts], axis=0)
    count = 2 * ng * n_part
    out_row = lax.broadcasted_iota(jnp.int32, (3 * count, held.shape[0]), 0)
    in_row = lax.broadcasted_iota(jnp.int32, (3 * count, held.shape[0]), 1)
    kind, rest_row = out_row // count, out_row % count
    slot, rest_row = rest_row // (ng * n_part), rest_row % (ng * n_part)
    group, i = rest_row // n_part, rest_row % n_part
    source = (group ^ g) * (2 * ROWS) + slot * ROWS + kind * n_part + i
    pick = (in_row == source).astype(F32).astype(BF16)
    ordered = jnp.dot(pick, held, preferred_element_type=F32)
    weighted = jnp.concatenate([ordered[:count], ordered[count : 2 * count]], axis=1).astype(BF16)
    extra = ordered[2 * count :]

    for t in range(shifts):
        cos_part, sin_part = cos_ref[t : t + 1, :], sin_ref[t : t + 1, :]
        rows = slice(t * total, (t + 1) * total)
        shifted_ref[rows, :chunk] = (cos_part * real + sin_part * imag).astype(BF16)
        shifted_ref[rows, chunk:] = (cos_part * imag - sin_part * real).astype(BF16)
    cross = lax.dot_general(weighted, shifted_ref[...], NT_DIMS, preferred_element_type=F32)

    power = real * real + imag * imag
    norm_table = lax.dot_general(
        square_ref[...], power, NT_DIMS, precision=HIGHEST, preferred_element_type=F32
    )
    class_col = lax.broadcasted_iota(jnp.int32, (count, classes_count), 1).astype(F32)
    onehot = (class_col == extra[:, subsets : subsets + 1]).astype(F32)
    norm = jnp.dot(onehot, norm_table, precision=HIGHEST, preferred_element_type=F32)
    subset_col = lax.broadcasted_iota(jnp.int32, (total, subsets), 1).astype(F32)
    subset_hot = (subset_col == real[:, tail : tail + 1]).astype(F32).astype(BF16)
    prior = lax.dot_general(
        extra[:, :subsets].astype(BF16), subset_hot, NT_DIMS, preferred_element_type=F32
    )
    added = jnp.where(blk // half == 1, prior, jnp.zeros_like(prior)) - 0.5 * norm
    added = jnp.concatenate([added] * shifts, axis=1)
    result = cross + added
    dest = ng * n_part
    for s in range(2):
        outs[s][...] = result[s * dest : (s + 1) * dest]


def sum_kernel(n_proj, *refs):
    *terms, out_ref = refs
    total = terms[0][...]
    for term in terms[1:]:
        total = total + term[...]
    for t in range(out_ref.shape[0]):
        out_ref[t] = total[:, t * n_proj : (t + 1) * n_proj]


def per_device(
    particles,
    ctf_class,
    orient_prior,
    ctf_curves,
    noise_weight,
    shift_phase,
    trans_index,
    projections,
    orient_subset,
):
    nb, ng = lax.axis_size("blk"), lax.axis_size("grp")
    half = nb // 2
    n_part, n_proj = particles.shape[0], projections.shape[0]
    length = particles.shape[2]
    shifts = shift_phase.shape[0]
    classes_count = ctf_curves.shape[0]
    subsets = orient_prior.shape[1]
    chunk = 128 * -(-length // 256)
    tail = length - chunk
    noise = noise_weight.reshape(1, length)
    shape = jax.ShapeDtypeStruct

    bank_keep, part_keep, send = pl.pallas_call(
        functools.partial(pack_kernel, half, chunk),
        out_shape=[
            shape((2 * n_proj, chunk), BF16),
            shape((ROWS, chunk), BF16),
            shape((2 * n_proj + ROWS, chunk), BF16),
        ],
        in_specs=[pl.BlockSpec(memory_space=pl.ANY)] * 7,
        out_specs=[_vmem()] * 3,
        scratch_shapes=[
            pltpu.SMEM(ctf_class.shape, jnp.int32),
            pltpu.SMEM(orient_subset.shape, jnp.int32),
            pltpu.VMEM(particles.shape, BF16),
            pltpu.VMEM(orient_prior.shape, BF16),
            pltpu.VMEM(ctf_curves.shape, F32),
            pltpu.VMEM(noise.shape, F32),
            pltpu.VMEM(projections.shape, BF16),
            pltpu.SemaphoreType.DMA((7,)),
        ],
        compiler_params=_params(56),
        name="pack",
    )(ctf_class, orient_subset, particles, orient_prior, ctf_curves, noise, projections)

    def swap(value, axis, bit):
        size = lax.axis_size(axis)
        return lax.ppermute(value, axis, [(i, i ^ bit) for i in range(size)])

    def doubled(first, axis, bits, offsets):
        pieces, held = [first], [offsets]
        for bit in bits:
            whole = pieces[0] if len(pieces) == 1 else jnp.concatenate(pieces, axis=0)
            all_offsets = [offset for offs in held for offset in offs]
            pieces, held = [whole], [all_offsets]
            pieces.append(swap(whole, axis, bit))
            held.append([offset ^ bit for offset in all_offsets])
        return pieces, held

    recv = swap(send, "blk", half)
    bank = jnp.concatenate([bank_keep, recv[: 2 * n_proj]], axis=0)
    part = jnp.concatenate([part_keep, recv[2 * n_proj :]], axis=0)
    blk_bits = [1 << n for n in range(half.bit_length() - 2, -1, -1)]
    grp_bits = [1 << n for n in range(ng.bit_length() - 1)]
    banks, offsets = doubled(bank, "blk", blk_bits, [0, half])
    parts, groups = doubled(part, "grp", grp_bits, [0])

    cos_part, sin_part, square = pl.pallas_call(
        functools.partial(table_kernel, half, chunk),
        out_shape=[shape((shifts, chunk), F32)] * 2 + [shape((classes_count, chunk), F32)],
        in_specs=[_smem(), _vmem(), _vmem(), _vmem()],
        out_specs=[_vmem()] * 3,
        scratch_shapes=[pltpu.VMEM((shifts, chunk), F32)],
        compiler_params=_params(8),
        cost_estimate=pl.CostEstimate(flops=4_000_000, bytes_accessed=2_000_000, transcendentals=0),
        name="tables",
    )(trans_index, ctf_curves, noise, shift_phase)

    count = 2 * ng * n_part
    total = nb * n_proj
    keep, give = pl.pallas_call(
        functools.partial(score_kernel, half, offsets, groups, n_part, tail, subsets),
        out_shape=[shape((ng * n_part, shifts * total), F32)] * 2,
        in_specs=[_vmem()] * (3 + len(banks) + len(parts)),
        out_specs=[_vmem()] * 2,
        scratch_shapes=[
            pltpu.VMEM((total, chunk), F32),
            pltpu.VMEM((total, chunk), F32),
            pltpu.VMEM((shifts * total, 2 * chunk), BF16),
        ],
        compiler_params=_params(40),
        cost_estimate=pl.CostEstimate(
            flops=4 * count * total * shifts * chunk, bytes_accessed=4_000_000, transcendentals=0
        ),
        name="score",
    )(cos_part, sin_part, square, *banks, *parts)
    scores = pl.pallas_call(
        functools.partial(sum_kernel, total),
        out_shape=shape((shifts, ng * n_part, total), F32),
        in_specs=[_vmem()] * 2,
        out_specs=_vmem(),
        compiler_params=_params(4),
        name="sum",
    )(keep, swap(give, "blk", half))
    return scores.transpose(1, 0, 2)


def solution(mesh):
    placed = (
        P(("blk", "grp"), None, None),
        P(("blk", "grp")),
        P(("blk", "grp"), None),
        P(),
        P(),
        P(),
        P(),
        P(("grp", "blk"), None, None),
        P(("grp", "blk")),
    )
    return jax.shard_map(
        per_device, mesh=mesh, in_specs=placed, out_specs=P("blk", None, "grp"), check_vma=False
    )
```

time: 38.5 us -> 32.5 us (0.84)
  starting transfers between devices: 20.8 us -> 12.2 us
  waiting for transfers between devices: 7.76 us -> 12.9 us
  local copies, waits for them, and re-layouts: 4.96 us -> 0.04 us
  Pallas kernels: 4.63 us -> 7.13 us
    ppermute x16 -> x6, starting transfers between devices: 20.8 us -> 12.2 us  [swap(): return lax.ppermute(value, axis, [(i, i ^ bit) for i in range(size)])]
    ppermute x16 -> x6, waiting for transfers between devices: 7.76 us -> 12.9 us  [swap(): return lax.ppermute(value, axis, [(i, i ^ bit) for i in range(size)])]
    unnamed x25 -> x12, local copies, waits for them, and re-layouts: 4.96 us -> 0.03 us
    pallas_call x3, Pallas kernels: 3.94 us -> 6.44 us  [the longest x1 2.76 us: per_device(): pl.pallas_call(functools.partial(score_kernel, half, offsets, groups, n_p...]
  transfers between devices with their start and end apart: 16 -> 6, of which waited for: 5 -> 4; matrix products, arithmetic and copies ran while one was open for 0% -> 0% of each run, Pallas kernels for 3% -> 5%
where the time goes in v3:
time: 32.5 us; the launch traced here: 32.4 us
  waiting for transfers between devices  12.9 us (40%)
  starting transfers between devices  12.2 us (38%)
  Pallas kernels  7.13 us (22%)
    ppermute x6, waiting for transfers between devices, swap(): return lax.ppermute(value, axis, [(i, i ^ bit) for i in range(size)])  12.9 us
    ppermute x6, starting transfers between devices, swap(): return lax.ppermute(value, axis, [(i, i ^ bit) for i in range(size)])  12.2 us
    pallas_call x1, Pallas kernels, per_device(): pl.pallas_call(functools.partial(score_kernel, half, offsets, groups, n_p...  2.76 us
    pallas_call x1, Pallas kernels, per_device(): pl.pallas_call(functools.partial(pack_kernel, half, chunk), out_shape=[sh...  2.2 us
    pallas_call x1, Pallas kernels, per_device(): pl.pallas_call(functools.partial(table_kernel, half, chunk), out_shape=[s...  1.48 us
    pallas_call x1, Pallas kernels, per_device(): pl.pallas_call(functools.partial(sum_kernel, total), out_shape=shape((shi...  0.69 us
  transfers between devices with their start and end apart: 6, of which 4 were waited for; matrix products, arithmetic and copies ran while one was open for 0% of the time, Pallas kernels for 5%

profile of v3, /device:TPU:0, one launch (start us, length us, event | category | flops | bytes accessed | tf_op | source)
XLA Modules:
  0.0 32.4 jit_solution(2642451972931574192)
XLA Ops:
  0.0 0.0 copy-start
  0.0 2.2 %pack.1 = (bf16[16,2048]{1,0:T(8,128)(2,1)}, bf16[8,2048]{1,0:T(8,128)(2,1)}, bf16[24,2048]{1,0:T(8,128)(2,1)}) custom-call(s32[2]{0:T(128)} %class_hbm.1, s32[8]{0:T(128)} %subset_hbm.1, bf16[2,2,4000]{2,1,0:T(2,128)(2,1)} %particles_hbm.1, bf16[2,192]{1,0:T(2,128)(2,1)} %prior_hbm.1, f32[64,4000]{1,0:T(8,128)} %curves_hbm.1, f32[1,4000]{1,0:T(1,128)} %bitcast.2, ...), custom_call_target="tpu_custom_call" | custom-call | tf_op jit(solution)/shard_map/pack/pallas_call | solution.py:245
  2.2 0.0 copy-start.4
  2.2 4.1 %collective-permute-start = (bf16[24,2048]{1,0:T(8,128)(2,1)}, bf16[24,2048]{1,0:T(8,128)(2,1)S(1)}, u32[]{:S(2)}, u32[]{:S(2)}) collective-permute-start(bf16[24,2048]{1,0:T(8,128)(2,1)} %get-tuple-element.17), channel_id=1, source_target_pairs={{0,4},{1,5},{2,6},{3,7},{4,0},{5,1},{6,2},{7,3},{8,12},{9,13},{10,... | collective-permute-start | bytes 294920 | tf_op jit(solution)/shard_map/ppermute | solution.py:270
  6.3 5.1 %collective-permute-done = bf16[24,2048]{1,0:T(8,128)(2,1)S(1)} collective-permute-done((bf16[24,2048]{1,0:T(8,128)(2,1)}, bf16[24,2048]{1,0:T(8,128)(2,1)S(1)}, u32[]{:S(2)}, u32[]{:S(2)}) %collective-permute-start) | collective-permute-done | bytes 98336 | tf_op jit(solution)/shard_map/ppermute | solution.py:270
  11.4 0.0 copy-done.4
  11.5 0.0 copy-start.5
  11.5 0.9 %collective-permute-start.1 = (bf16[32,2048]{1,0:T(8,128)(2,1)S(1)}, bf16[32,2048]{1,0:T(8,128)(2,1)S(1)}, u32[]{:S(2)}, u32[]{:S(2)}) collective-permute-start(bf16[32,2048]{1,0:T(8,128)(2,1)S(1)} %pad_maximum_fusion.1), channel_id=1, source_target_pairs={{0,2},{1,3},{2,0},{3,1},{4,6},{5,7},{6,4},{7,5},{8,10},{9,11},{10,... | collective-permute-start | bytes 393224 | tf_op jit(solution)/shard_map/ppermute | solution.py:270
  12.4 0.0 copy-done.5
  12.4 0.1 collective-permute-start.3
  12.5 4.1 %collective-permute-done.1 = bf16[32,2048]{1,0:T(8,128)(2,1)S(1)} collective-permute-done((bf16[32,2048]{1,0:T(8,128)(2,1)S(1)}, bf16[32,2048]{1,0:T(8,128)(2,1)S(1)}, u32[]{:S(2)}, u32[]{:S(2)}) %collective-permute-start.1) | collective-permute-done | bytes 131104 | tf_op jit(solution)/shard_map/ppermute | solution.py:270
  16.5 0.0 copy-start.2
  16.5 0.0 copy-start.3
  16.5 0.0 copy-start.1
  16.6 1.6 %collective-permute-start.2 = (bf16[64,2048]{1,0:T(8,128)(2,1)S(1)}, bf16[64,2048]{1,0:T(8,128)(2,1)S(1)}, u32[]{:S(2)}, u32[]{:S(2)}) collective-permute-start(bf16[64,2048]{1,0:T(8,128)(2,1)S(1)} %pad_maximum_fusion.rest_0_), channel_id=1, source_target_pairs={{0,1},{1,0},{2,3},{3,2},{4,5},{5,4},{6,7},{7,6},{8,9},{9,8},{10,11... | collective-permute-start | bytes 786440 | tf_op jit(solution)/shard_map/ppermute | solution.py:270
  18.2 0.0 collective-permute-done.3
  18.2 1.6 %collective-permute-start.4 = (bf16[32,2048]{1,0:T(8,128)(2,1)S(1)}, bf16[32,2048]{1,0:T(8,128)(2,1)S(1)}, u32[]{:S(2)}, u32[]{:S(2)}) collective-permute-start(bf16[32,2048]{1,0:T(8,128)(2,1)S(1)} %pad_maximum_fusion.2.rest_2_), channel_id=1, source_target_pairs={{0,16},{8,24},{16,0},{24,8},{1,17},{9,25},{17,1},{25,9},{2,18},{10... | collective-permute-start | bytes 393224 | tf_op jit(solution)/shard_map/ppermute | solution.py:270
  19.8 0.0 copy-done
  19.8 0.0 copy-done.2
  19.8 0.0 copy-done.3
  19.8 0.0 copy-done.1
  19.8 1.5 %tables.1 = (f32[9,2048]{1,0:T(8,128)S(1)}, f32[9,2048]{1,0:T(8,128)S(1)}, f32[64,2048]{1,0:T(8,128)S(1)}) custom-call(s32[9]{0:T(128)S(1)} %copy-done.3, f32[64,4000]{1,0:T(8,128)S(1)} %copy-done, f32[1,4000]{1,0:T(1,128)S(1)} %bitcast.3, f32[9,4000]{1,0:T(8,128)S(1)} %copy-done.1), custom_call_target="tpu_custom_call" | custom-call | flops 4000000 | bytes 2000000 | tf_op jit(solution)/shard_map/tables/pallas_call | solution.py:290
  21.3 2.0 %collective-permute-done.4.rest_3_ = bf16[32,2048]{1,0:T(8,128)(2,1)S(1)} collective-permute-done((bf16[32,2048]{1,0:T(8,128)(2,1)S(1)}, bf16[32,2048]{1,0:T(8,128)(2,1)S(1)}, u32[]{:S(2)}, u32[]{:S(2)}) %collective-permute-start.4) | collective-permute-done | bytes 131104 | tf_op jit(solution)/shard_map/ppermute | solution.py:270
  23.2 0.0 collective-permute-done.2.rest_1_
  23.2 2.8 %score.1 = (f32[8,576]{1,0:T(8,128)S(1)}, f32[8,576]{1,0:T(8,128)S(1)}) custom-call(f32[9,2048]{1,0:T(8,128)S(1)} %get-tuple-element.13.cos_ref, f32[9,2048]{1,0:T(8,128)S(1)} %get-tuple-element.14.sin_ref, f32[64,2048]{1,0:T(8,128)S(1)} %get-tuple-element.15.square_ref, bf16[64,2048]{1,0:T(8,128)(2,1)S(1)} %pad_maximum_fusion.rest_0_, ...), custom_call_target="tpu_custom_call" | custom-call | flops 75497472 | bytes 4000000 | tf_op jit(solution)/shard_map/score/pallas_call | solution.py:303
  26.0 3.9 %collective-permute-start.5 = (f32[8,576]{1,0:T(8,128)S(1)}, f32[8,576]{1,0:T(8,128)S(1)}, u32[]{:S(2)}, u32[]{:S(2)}) collective-permute-start(f32[8,576]{1,0:T(8,128)S(1)} %get-tuple-element.20), channel_id=1, source_target_pairs={{0,4},{1,5},{2,6},{3,7},{4,0},{5,1},{6,2},{7,3},{8,12},{9,13},{10,... | collective-permute-start | bytes 55304 | tf_op jit(solution)/shard_map/ppermute | solution.py:270
  29.9 1.8 %collective-permute-done.5.refs_1_ = f32[8,576]{1,0:T(8,128)S(1)} collective-permute-done((f32[8,576]{1,0:T(8,128)S(1)}, f32[8,576]{1,0:T(8,128)S(1)}, u32[]{:S(2)}, u32[]{:S(2)}) %collective-permute-start.5) | collective-permute-done | bytes 18464 | tf_op jit(solution)/shard_map/ppermute | solution.py:270
  31.7 0.7 %sum.1 = f32[9,8,64]{2,1,0:T(8,128)} custom-call(f32[8,576]{1,0:T(8,128)S(1)} %get-tuple-element.19.refs_0_, f32[8,576]{1,0:T(8,128)S(1)} %collective-permute-done.5.refs_1_), custom_call_target="tpu_custom_call" | custom-call | tf_op jit(solution)/shard_map/sum/pallas_call | solution.py:319
  (6 shorter events, 0.1 us)
Async XLA Ops:
  0.0 19.8 %copy-start = (f32[64,4000]{1,0:T(8,128)S(1)}, f32[64,4000]{1,0:T(8,128)}, u32[]{:S(2)}) copy-start(f32[64,4000]{1,0:T(8,128)} %curves_hbm.1) | copy-start | bytes 3072004
  2.2 9.2 %copy-start.4 = (bf16[16,2048]{1,0:T(8,128)(2,1)S(1)}, bf16[16,2048]{1,0:T(8,128)(2,1)}, u32[]{:S(2)}) copy-start(bf16[16,2048]{1,0:T(8,128)(2,1)} %get-tuple-element.16) | copy-start | bytes 196612
  2.2 9.2 %collective-permute-start = (bf16[24,2048]{1,0:T(8,128)(2,1)}, bf16[24,2048]{1,0:T(8,128)(2,1)S(1)}, u32[]{:S(2)}, u32[]{:S(2)}) collective-permute-start(bf16[24,2048]{1,0:T(8,128)(2,1)} %get-tuple-element.17), channel_id=1, source_target_pairs={{0,4},{1,5},{2,6},{3,7},{4,0},{5,1},{6,2},{7,3},{8,12},{9,13},{10,... | collective-permute-start | bytes 294920 | tf_op jit(solution)/shard_map/ppermute | solution.py:270
  11.5 0.9 %copy-start.5 = (bf16[8,2048]{1,0:T(8,128)(2,1)S(1)}, bf16[8,2048]{1,0:T(8,128)(2,1)}, u32[]{:S(2)}) copy-start(bf16[8,2048]{1,0:T(8,128)(2,1)} %get-tuple-element.18) | copy-start | bytes 98308
  11.5 5.0 %collective-permute-start.1 = (bf16[32,2048]{1,0:T(8,128)(2,1)S(1)}, bf16[32,2048]{1,0:T(8,128)(2,1)S(1)}, u32[]{:S(2)}, u32[]{:S(2)}) collective-permute-start(bf16[32,2048]{1,0:T(8,128)(2,1)S(1)} %pad_maximum_fusion.1), channel_id=1, source_target_pairs={{0,2},{1,3},{2,0},{3,1},{4,6},{5,7},{6,4},{7,5},{8,10},{9,11},{10,... | collective-permute-start | bytes 393224 | tf_op jit(solution)/shard_map/ppermute | solution.py:270
  12.4 5.8 %collective-permute-start.3 = (bf16[16,2048]{1,0:T(8,128)(2,1)S(1)}, bf16[16,2048]{1,0:T(8,128)(2,1)S(1)}, u32[]{:S(2)}, u32[]{:S(2)}) collective-permute-start(bf16[16,2048]{1,0:T(8,128)(2,1)S(1)} %pad_maximum_fusion.3), channel_id=1, source_target_pairs={{0,8},{8,0},{16,24},{24,16},{1,9},{9,1},{17,25},{25,17},{2,10},{10... | collective-permute-start | bytes 196616 | tf_op jit(solution)/shard_map/ppermute | solution.py:270
  16.5 3.3 %copy-start.2 = (f32[4000]{0:T(1024)S(1)}, f32[4000]{0:T(1024)}, u32[]{:S(2)}) copy-start(f32[4000]{0:T(1024)} %param.13) | copy-start | bytes 48004
  16.5 3.3 %copy-start.3 = (s32[9]{0:T(128)S(1)}, s32[9]{0:T(128)}, u32[]{:S(2)}) copy-start(s32[9]{0:T(128)} %trans_ref.1) | copy-start | bytes 112
  16.5 3.2 %copy-start.1 = (f32[9,4000]{1,0:T(8,128)S(1)}, f32[9,4000]{1,0:T(8,128)}, u32[]{:S(2)}) copy-start(f32[9,4000]{1,0:T(8,128)} %phase_ref.1) | copy-start | bytes 432004
  16.6 6.7 %collective-permute-start.2 = (bf16[64,2048]{1,0:T(8,128)(2,1)S(1)}, bf16[64,2048]{1,0:T(8,128)(2,1)S(1)}, u32[]{:S(2)}, u32[]{:S(2)}) collective-permute-start(bf16[64,2048]{1,0:T(8,128)(2,1)S(1)} %pad_maximum_fusion.rest_0_), channel_id=1, source_target_pairs={{0,1},{1,0},{2,3},{3,2},{4,5},{5,4},{6,7},{7,6},{8,9},{9,8},{10,11... | collective-permute-start | bytes 786440 | tf_op jit(solution)/shard_map/ppermute | solution.py:270
  18.2 5.0 %collective-permute-start.4 = (bf16[32,2048]{1,0:T(8,128)(2,1)S(1)}, bf16[32,2048]{1,0:T(8,128)(2,1)S(1)}, u32[]{:S(2)}, u32[]{:S(2)}) collective-permute-start(bf16[32,2048]{1,0:T(8,128)(2,1)S(1)} %pad_maximum_fusion.2.rest_2_), channel_id=1, source_target_pairs={{0,16},{8,24},{16,0},{24,8},{1,17},{9,25},{17,1},{25,9},{2,18},{10... | collective-permute-start | bytes 393224 | tf_op jit(solution)/shard_map/ppermute | solution.py:270
  26.0 5.7 %collective-permute-start.5 = (f32[8,576]{1,0:T(8,128)S(1)}, f32[8,576]{1,0:T(8,128)S(1)}, u32[]{:S(2)}, u32[]{:S(2)}) collective-permute-start(f32[8,576]{1,0:T(8,128)S(1)} %get-tuple-element.20), channel_id=1, source_target_pairs={{0,4},{1,5},{2,6},{3,7},{4,0},{5,1},{6,2},{7,3},{8,12},{9,13},{10,... | collective-permute-start | bytes 55304 | tf_op jit(solution)/shard_map/ppermute | solution.py:270

commit v4 on v3

v4 whole, which is shorter than its diff:
```python
import functools

import jax
import jax.numpy as jnp
from jax import lax
from jax.experimental import pallas as pl
from jax.experimental.pallas import tpu as pltpu
from jax.sharding import PartitionSpec as P

F32 = jnp.float32
BF16 = jnp.bfloat16
HIGHEST = lax.Precision.HIGHEST
NT_DIMS = (((1,), (1,)), ((), ()))
MIB = 1 << 20


def _vmem():
    return pl.BlockSpec(memory_space=pltpu.VMEM)


def _smem():
    return pl.BlockSpec(memory_space=pltpu.SMEM)


def _params(mib):
    return pltpu.CompilerParams(vmem_limit_bytes=mib * MIB)


def pack_kernel(
    class_hbm,
    subset_hbm,
    particles_hbm,
    prior_hbm,
    curves_hbm,
    noise_hbm,
    proj_hbm,
    bank_ref,
    part_ref,
    class_ref,
    subset_ref,
    particles_ref,
    prior_ref,
    curves_ref,
    noise_ref,
    proj_ref,
    sems,
):
    pairs = [
        (proj_hbm, proj_ref),
        (subset_hbm, subset_ref),
        (class_hbm, class_ref),
        (curves_hbm, curves_ref),
        (particles_hbm, particles_ref),
        (noise_hbm, noise_ref),
        (prior_hbm, prior_ref),
    ]
    copies = [pltpu.make_async_copy(a, b, sems.at[n]) for n, (a, b) in enumerate(pairs)]
    for copy in copies:
        copy.start()
    n_part, n_proj = particles_ref.shape[0], proj_ref.shape[0]
    length = proj_ref.shape[2]
    wide = bank_ref.shape[1]

    def padded(values, width):
        zeros = jnp.zeros((values.shape[0], width - values.shape[1]), values.dtype)
        return jnp.concatenate([values, zeros], axis=1)

    row = lax.broadcasted_iota(jnp.int32, (n_proj, wide), 0)
    lane = lax.broadcasted_iota(jnp.int32, (n_proj, wide), 1)
    for copy in copies[:2]:
        copy.wait()
    real = jnp.zeros((n_proj, wide), F32)
    imag = jnp.zeros((n_proj, wide), F32)
    for j in range(n_proj):
        both = padded(proj_ref[j].astype(F32), wide)
        real = jnp.where(row == j, both[0:1], real)
        imag = jnp.where(row == j, both[1:2], imag)
    for j in range(n_proj):
        real = jnp.where((row == j) & (lane == length), subset_ref[j].astype(F32), real)
    bank_ref[...] = jnp.concatenate([real, imag], axis=0).astype(BF16)

    for copy in copies[2:]:
        copy.wait()
    subsets = prior_ref.shape[1]
    extra = part_ref.shape[1] - wide
    row = lax.broadcasted_iota(jnp.int32, (2 * n_part, wide), 0)
    row_extra = lax.broadcasted_iota(jnp.int32, (2 * n_part, extra), 0)
    lane_extra = lax.broadcasted_iota(jnp.int32, (2 * n_part, extra), 1)
    prior = padded(prior_ref[...].astype(F32), extra)
    rows = jnp.zeros((2 * n_part, wide), F32)
    rows_extra = jnp.zeros((2 * n_part, extra), F32)
    for i in range(n_part):
        curve = curves_ref[pl.ds(class_ref[i], 1), :] * noise_ref[...]
        both = padded(particles_ref[i].astype(F32) * curve, wide)
        rows = jnp.where(row == i, both[0:1], rows)
        rows = jnp.where(row == n_part + i, both[1:2], rows)
        small = jnp.where(
            lane_extra == subsets,
            class_ref[i].astype(F32),
            jnp.broadcast_to(prior[i : i + 1], rows_extra.shape),
        )
        rows_extra = jnp.where(row_extra == i, small, rows_extra)
    part_ref[:, :wide] = rows.astype(BF16)
    part_ref[:, wide:] = rows_extra.astype(BF16)


def sine_cosine(x):
    turns = jnp.floor(x * 0.6366197723675814 + 0.5)
    r = ((x - turns * 1.5703125) - turns * 4.837512969970703125e-4) - turns * 7.549789954891882e-8
    z = r * r
    sine = r + r * z * (-1.6666654611e-1 + z * (8.3321608736e-3 - z * 1.9515295891e-4))
    cosine = 1.0 - 0.5 * z + z * z * (
        4.166664568298827e-2 + z * (-1.388731625493765e-3 + z * 2.443315711809948e-5)
    )
    quarter = turns.astype(jnp.int32) & 3
    swapped = (quarter & 1) == 1
    first, second = jnp.where(swapped, cosine, sine), jnp.where(swapped, sine, cosine)
    first = jnp.where(quarter >= 2, -first, first)
    second = jnp.where((quarter == 1) | (quarter == 2), -second, second)
    return first, second


def split_terms(values):
    high = values.astype(BF16)
    low = (values - high.astype(F32)).astype(BF16)
    return jnp.concatenate([high, low], axis=0)


def table_kernel(trans_ref, curves_ref, noise_ref, phase_ref, cos_ref, sin_ref, square_ref, angle):
    length = curves_ref.shape[1]
    wide = cos_ref.shape[1]
    for t in range(phase_ref.shape[0]):
        angle[t : t + 1, :] = phase_ref[pl.ds(trans_ref[t], 1), :]
    zeros = jnp.zeros((cos_ref.shape[0], wide - length), F32)
    sine, cosine = sine_cosine(angle[...])
    cos_ref[...] = jnp.concatenate([cosine, zeros], axis=1)
    sin_ref[...] = jnp.concatenate([sine, zeros], axis=1)
    curve = curves_ref[...]
    square = split_terms(curve * curve * noise_ref[...])
    square_ref[...] = jnp.concatenate(
        [square, jnp.zeros((square.shape[0], wide - length), BF16)], axis=1
    )


def score_kernel(
    half, offsets, n_parts, bits, n_part, n_proj, length, subsets, cos_ref, sin_ref, square_ref, *rest
):
    n_bank = len(offsets)
    banks, parts, outs = rest[:n_bank], rest[n_bank : n_bank + n_parts], rest[n_bank + n_parts :][:2]
    real_ref, imag_ref, shifted_ref = rest[n_bank + n_parts + 2 :]
    blk, g = lax.axis_index("blk"), lax.axis_index("grp")
    ng = 1 << len(bits)
    total, wide = real_ref.shape
    shifts = cos_ref.shape[0]
    classes_count = square_ref.shape[0] // 2

    for bank, offs in zip(banks, offsets):
        for n, offset in enumerate(offs):
            both = bank[2 * n_proj * n : 2 * n_proj * (n + 1)].astype(F32)
            where = pl.multiple_of((blk % half ^ offset) * n_proj, n_proj)
            real_ref[pl.ds(where, n_proj), :] = both[:n_proj]
            imag_ref[pl.ds(where, n_proj), :] = both[n_proj:]
    real, imag = real_ref[...], imag_ref[...]

    held = jnp.concatenate([part[...] for part in parts], axis=0)
    count = 2 * ng * n_part
    out_row = lax.broadcasted_iota(jnp.int32, (2 * count, held.shape[0]), 0)
    in_row = lax.broadcasted_iota(jnp.int32, (2 * count, held.shape[0]), 1)
    kind, rest_row = out_row // count, out_row % count
    source, rest_row = rest_row // (ng * n_part), rest_row % (ng * n_part)
    away, i = rest_row // n_part ^ g, rest_row % n_part
    for n, bit in enumerate(bits):
        source += jnp.where(away & bit != 0, 2 << n, 0)
    pick = (in_row == source * (2 * n_part) + kind * n_part + i).astype(F32).astype(BF16)
    ordered = jnp.dot(pick, held, preferred_element_type=F32)
    weighted = jnp.concatenate([ordered[:count, :wide], ordered[count:, :wide]], axis=1).astype(BF16)
    prior_rows = ordered[:count, wide : wide + subsets].astype(BF16)
    class_rows = ordered[:count, wide + subsets : wide + subsets + 1]

    for t in range(shifts):
        cos_part, sin_part = cos_ref[t : t + 1, :], sin_ref[t : t + 1, :]
        rows = slice(t * total, (t + 1) * total)
        shifted_ref[rows, :wide] = (cos_part * real + sin_part * imag).astype(BF16)
        shifted_ref[rows, wide:] = (cos_part * imag - sin_part * real).astype(BF16)
    cross = lax.dot_general(weighted, shifted_ref[...], NT_DIMS, preferred_element_type=F32)

    power = split_terms(real * real + imag * imag)
    table = lax.dot_general(square_ref[...], power, NT_DIMS, preferred_element_type=F32)
    table = table[:classes_count, total:] + table[classes_count:, :total] + table[:classes_count, :total]
    class_col = lax.broadcasted_iota(jnp.int32, (count, classes_count), 1).astype(F32)
    onehot = (class_col == class_rows).astype(F32)
    norm = jnp.dot(onehot, table, precision=HIGHEST, preferred_element_type=F32)
    subset_col = lax.broadcasted_iota(jnp.int32, (total, subsets), 1).astype(F32)
    subset_hot = (subset_col == real[:, length : length + 1]).astype(F32).astype(BF16)
    prior = lax.dot_general(prior_rows, subset_hot, NT_DIMS, preferred_element_type=F32)
    result = cross + jnp.concatenate([prior - 0.5 * norm] * shifts, axis=1)
    dest = ng * n_part
    for s in range(2):
        outs[s][...] = result[s * dest : (s + 1) * dest]


def place_kernel(half, keep_ref, recv_ref, out_ref):
    first = lax.axis_index("blk") < half
    low = jnp.where(first, keep_ref[...], recv_ref[...])
    high = jnp.where(first, recv_ref[...], keep_ref[...])
    shifts, _, width = out_ref.shape
    width = width // 2
    for t in range(shifts):
        span = slice(t * width, (t + 1) * width)
        out_ref[t] = jnp.concatenate([low[:, span], high[:, span]], axis=1)


def per_device(
    particles,
    ctf_class,
    orient_prior,
    ctf_curves,
    noise_weight,
    shift_phase,
    trans_index,
    projections,
    orient_subset,
):
    nb, ng = lax.axis_size("blk"), lax.axis_size("grp")
    half = nb // 2
    n_part, n_proj = particles.shape[0], projections.shape[0]
    length = particles.shape[2]
    shifts = shift_phase.shape[0]
    classes_count = ctf_curves.shape[0]
    subsets = orient_prior.shape[1]
    wide = 128 * (length // 128 + 1)
    extra = 128 * (subsets // 128 + 1)
    noise = noise_weight.reshape(1, length)
    shape = jax.ShapeDtypeStruct

    bank, part = pl.pallas_call(
        pack_kernel,
        out_shape=[shape((2 * n_proj, wide), BF16), shape((2 * n_part, wide + extra), BF16)],
        in_specs=[pl.BlockSpec(memory_space=pl.ANY)] * 7,
        out_specs=[_vmem()] * 2,
        scratch_shapes=[
            pltpu.SMEM(ctf_class.shape, jnp.int32),
            pltpu.SMEM(orient_subset.shape, jnp.int32),
            pltpu.VMEM(particles.shape, BF16),
            pltpu.VMEM(orient_prior.shape, BF16),
            pltpu.VMEM(ctf_curves.shape, F32),
            pltpu.VMEM(noise.shape, F32),
            pltpu.VMEM(projections.shape, BF16),
            pltpu.SemaphoreType.DMA((7,)),
        ],
        compiler_params=_params(56),
        name="pack",
    )(ctf_class, orient_subset, particles, orient_prior, ctf_curves, noise, projections)

    def swap(value, axis, bit):
        size = lax.axis_size(axis)
        return lax.ppermute(value, axis, [(i, i ^ bit) for i in range(size)])

    def doubled(pieces, offsets, axis, bits):
        held = offsets
        for bit in bits:
            whole = pieces[0] if len(pieces) == 1 else jnp.concatenate(pieces, axis=0)
            all_offsets = [offset for offs in held for offset in offs]
            pieces = [whole, swap(whole, axis, bit)]
            held = [all_offsets, [offset ^ bit for offset in all_offsets]]
        return pieces, held

    blk_bits = [1 << n for n in range(half.bit_length() - 2, -1, -1)]
    grp_bits = [1 << n for n in range(ng.bit_length() - 2, -1, -1)]
    banks, offsets = doubled([bank], [[0]], "blk", blk_bits)
    parts, _ = doubled([part, swap(part, "blk", half)], [[0], [0]], "grp", grp_bits)

    cos_part, sin_part, square = pl.pallas_call(
        table_kernel,
        out_shape=[shape((shifts, wide), F32)] * 2 + [shape((2 * classes_count, wide), BF16)],
        in_specs=[_smem(), _vmem(), _vmem(), _vmem()],
        out_specs=[_vmem()] * 3,
        scratch_shapes=[pltpu.VMEM((shifts, length), F32)],
        compiler_params=_params(8),
        cost_estimate=pl.CostEstimate(flops=4_000_000, bytes_accessed=2_000_000, transcendentals=0),
        name="tables",
    )(trans_index, ctf_curves, noise, shift_phase)

    count = 2 * ng * n_part
    total = half * n_proj
    keep, give = pl.pallas_call(
        functools.partial(
            score_kernel, half, offsets, len(parts), grp_bits, n_part, n_proj, length, subsets
        ),
        out_shape=[shape((ng * n_part, shifts * total), F32)] * 2,
        in_specs=[_vmem()] * (3 + len(banks) + len(parts)),
        out_specs=[_vmem()] * 2,
        scratch_shapes=[
            pltpu.VMEM((total, wide), F32),
            pltpu.VMEM((total, wide), F32),
            pltpu.VMEM((shifts * total, 2 * wide), BF16),
        ],
        compiler_params=_params(44),
        cost_estimate=pl.CostEstimate(
            flops=4 * count * total * shifts * wide, bytes_accessed=4_000_000, transcendentals=0
        ),
        name="score",
    )(cos_part, sin_part, square, *banks, *parts)
    scores = pl.pallas_call(
        functools.partial(place_kernel, half),
        out_shape=shape((shifts, ng * n_part, 2 * total), F32),
        in_specs=[_vmem()] * 2,
        out_specs=_vmem(),
        compiler_params=_params(4),
        name="place",
    )(keep, swap(give, "blk", half))
    return scores.transpose(1, 0, 2)


def solution(mesh):
    placed = (
        P(("blk", "grp"), None, None),
        P(("blk", "grp")),
        P(("blk", "grp"), None),
        P(),
        P(),
        P(),
        P(),
        P(("grp", "blk"), None, None),
        P(("grp", "blk")),
    )
    return jax.shard_map(
        per_device, mesh=mesh, in_specs=placed, out_specs=P("blk", None, "grp"), check_vma=False
    )
```

time: 32.5 us -> 26.9 us (0.83)
  waiting for transfers between devices: 12.9 us -> 8.5 us
  starting transfers between devices: 12.2 us -> 10.1 us
  local copies, waits for them, and re-layouts: 0.04 us -> 0.98 us
    ppermute x6, waiting for transfers between devices: 12.9 us -> 8.5 us  [swap(): return lax.ppermute(value, axis, [(i, i ^ bit) for i in range(size)])]
    ppermute x6, starting transfers between devices: 12.2 us -> 10.1 us  [swap(): return lax.ppermute(value, axis, [(i, i ^ bit) for i in range(size)])]
    unnamed x12 -> x11, local copies, waits for them, and re-layouts: 0.03 us -> 0.97 us
  transfers between devices with their start and end apart: 6 -> 6, of which waited for: 4 -> 4; matrix products, arithmetic and copies ran while one was open for 0% -> 4% of each run, Pallas kernels for 5% -> 6%
where the time goes in v4:
time: 26.9 us; the launch traced here: 26.7 us
  starting transfers between devices  10.1 us (38%)
  waiting for transfers between devices  8.5 us (32%)
  Pallas kernels  6.88 us (26%)
  local copies, waits for them, and re-layouts  0.98 us (4%)
    ppermute x6, starting transfers between devices, swap(): return lax.ppermute(value, axis, [(i, i ^ bit) for i in range(size)])  10.1 us
    ppermute x6, waiting for transfers between devices, swap(): return lax.ppermute(value, axis, [(i, i ^ bit) for i in range(size)])  8.5 us
    pallas_call x1, Pallas kernels, per_device(): pl.pallas_call(functools.partial(score_kernel, half, offsets, len(parts),...  2.53 us
    pallas_call x1, Pallas kernels, per_device(): pl.pallas_call(pack_kernel, out_shape=[shape((2 * n_proj, wide), BF16), s...  2.14 us
    pallas_call x1, Pallas kernels, per_device(): pl.pallas_call(table_kernel, out_shape=[shape((shifts, wide), F32)] * 2 +...  1.51 us
    unnamed x11, local copies, waits for them, and re-layouts  0.97 us
    pallas_call x1, Pallas kernels, per_device(): pl.pallas_call(functools.partial(place_kernel, half), out_shape=shape((sh...  0.7 us
  transfers between devices with their start and end apart: 6, of which 4 were waited for; matrix products, arithmetic and copies ran while one was open for 4% of the time, Pallas kernels for 6%

profile of v4, /device:TPU:0, one launch (start us, length us, event | category | flops | bytes accessed | tf_op | source)
XLA Modules:
  0.0 26.7 jit_solution(18415567592557776647)
XLA Ops:
  0.0 0.0 copy-start
  0.0 2.1 %pack.1 = (bf16[16,4096]{1,0:T(8,128)(2,1)}, bf16[4,4352]{1,0:T(4,128)(2,1)}) custom-call(s32[2]{0:T(128)} %class_hbm.1, s32[8]{0:T(128)} %subset_hbm.1, bf16[2,2,4000]{2,1,0:T(2,128)(2,1)} %particles_hbm.1, bf16[2,192]{1,0:T(2,128)(2,1)} %prior_hbm.1, f32[64,4000]{1,0:T(8,128)} %curves_hbm.1, f32[1,4000]{1,0:T(1,128)} %bitcast.2, bf16[8,2,4000]{2,1,0:T(2,128)(2,1)} %proj_hbm.1), custom_call_target="tpu_custom_call" | custom-call | tf_op jit(solution)/shard_map/pack/pallas_call | solution.py:236
  2.2 4.1 %collective-permute-start.2 = (bf16[4,4352]{1,0:T(4,128)(2,1)}, bf16[4,4352]{1,0:T(4,128)(2,1)S(1)}, u32[]{:S(2)}, u32[]{:S(2)}) collective-permute-start(bf16[4,4352]{1,0:T(4,128)(2,1)} %get-tuple-element.16), channel_id=1, source_target_pairs={{0,4},{1,5},{2,6},{3,7},{4,0},{5,1},{6,2},{7,3},{8,12},{9,13},{10,... | collective-permute-start | bytes 104456 | tf_op jit(solution)/shard_map/ppermute | solution.py:257
  6.3 0.0 copy-start.4
  6.3 1.6 %collective-permute-start = (bf16[16,4096]{1,0:T(8,128)(2,1)}, bf16[16,4096]{1,0:T(8,128)(2,1)S(1)}, u32[]{:S(2)}, u32[]{:S(2)}) collective-permute-start(bf16[16,4096]{1,0:T(8,128)(2,1)} %get-tuple-element.15), channel_id=1, source_target_pairs={{0,2},{1,3},{2,0},{3,1},{4,6},{5,7},{6,4},{7,5},{8,10},{9,11},{10,... | collective-permute-start | bytes 393224 | tf_op jit(solution)/shard_map/ppermute | solution.py:257
  7.8 0.9 %constant_dynamic-update-slice_fusion.1 = bf16[32,4096]{1,0:T(8,128)(2,1)S(1)} fusion(bf16[16,4096]{1,0:T(8,128)(2,1)} %get-tuple-element.15), kind=kLoop, calls=%fused_computation.3 | loop fusion | bytes 262144
  8.8 0.1 collective-permute-done.2
  8.9 0.0 copy-done.4
  8.9 0.0 copy-start.1
  8.9 1.7 %collective-permute-start.3 = (bf16[8,4352]{1,0:T(8,128)(2,1)S(1)}, bf16[8,4352]{1,0:T(8,128)(2,1)S(1)}, u32[]{:S(2)}, u32[]{:S(2)}) collective-permute-start(bf16[8,4352]{1,0:T(8,128)(2,1)S(1)} %pad_maximum_fusion.1), channel_id=1, source_target_pairs={{0,16},{8,24},{16,0},{24,8},{1,17},{9,25},{17,1},{25,9},{2,18},{10... | collective-permute-start | bytes 208904 | tf_op jit(solution)/shard_map/ppermute | solution.py:257
  10.6 0.9 %collective-permute-done = bf16[16,4096]{1,0:T(8,128)(2,1)S(1)} collective-permute-done((bf16[16,4096]{1,0:T(8,128)(2,1)}, bf16[16,4096]{1,0:T(8,128)(2,1)S(1)}, u32[]{:S(2)}, u32[]{:S(2)}) %collective-permute-start) | collective-permute-done | bytes 131104 | tf_op jit(solution)/shard_map/ppermute | solution.py:257
  11.5 0.0 copy-start.2
  11.5 0.0 copy-start.3
  11.5 1.9 %collective-permute-start.1 = (bf16[32,4096]{1,0:T(8,128)(2,1)S(1)}, bf16[32,4096]{1,0:T(8,128)(2,1)S(1)}, u32[]{:S(2)}, u32[]{:S(2)}) collective-permute-start(bf16[32,4096]{1,0:T(8,128)(2,1)S(1)} %constant_dynamic-update-slice_fusion.rest_0_), channel_id=1, source_target_pairs={{0,1},{1,0},{2,3},{3,2},{4,5},{5,4},{6,7},{7,6},{8,9},{9,8},{10,11... | collective-permute-start | bytes 786440 | tf_op jit(solution)/shard_map/ppermute | solution.py:257
  13.4 0.0 collective-permute-done.3
  13.4 0.1 pad_maximum_fusion.rest_2_
  13.5 0.1 collective-permute-start.4
  13.5 0.0 copy-done
  13.6 0.0 copy-done.1
  13.6 0.0 copy-done.2
  13.6 0.0 copy-done.3
  13.6 1.5 %tables.1 = (f32[9,4096]{1,0:T(8,128)S(1)}, f32[9,4096]{1,0:T(8,128)S(1)}, bf16[128,4096]{1,0:T(8,128)(2,1)S(1)}) custom-call(s32[9]{0:T(128)S(1)} %copy-done.3, f32[64,4000]{1,0:T(8,128)S(1)} %copy-done, f32[1,4000]{1,0:T(1,128)S(1)} %bitcast.3, f32[9,4000]{1,0:T(8,128)S(1)} %copy-done.1), custom_call_target="tpu_custom_call" | custom-call | flops 4000000 | bytes 2000000 | tf_op jit(solution)/shard_map/tables/pallas_call | solution.py:273
  15.1 0.0 collective-permute-done.4.rest_3_
  15.1 3.8 %collective-permute-done.1.rest_1_ = bf16[32,4096]{1,0:T(8,128)(2,1)S(1)} collective-permute-done((bf16[32,4096]{1,0:T(8,128)(2,1)S(1)}, bf16[32,4096]{1,0:T(8,128)(2,1)S(1)}, u32[]{:S(2)}, u32[]{:S(2)}) %collective-permute-start.1) | collective-permute-done | bytes 262176 | tf_op jit(solution)/shard_map/ppermute | solution.py:257
  18.9 2.5 %score.1 = (f32[8,288]{1,0:T(8,128)S(1)}, f32[8,288]{1,0:T(8,128)S(1)}) custom-call(f32[9,4096]{1,0:T(8,128)S(1)} %get-tuple-element.12.cos_ref, f32[9,4096]{1,0:T(8,128)S(1)} %get-tuple-element.13.sin_ref, bf16[128,4096]{1,0:T(8,128)(2,1)S(1)} %get-tuple-element.14.square_ref, bf16[32,4096]{1,0:T(8,128)(2,1)S(1)} %constant_dynamic-update-slice_fusion.rest_0_, ...), custom_call_target="tpu_custom_call" | custom-call | flops 75497472 | bytes 4000000 | tf_op jit(solution)/shard_map/score/pallas_call | solution.py:286
  21.4 0.8 %collective-permute-start.5 = (f32[8,288]{1,0:T(8,128)S(1)}, f32[8,288]{1,0:T(8,128)S(1)}, u32[]{:S(2)}, u32[]{:S(2)}) collective-permute-start(f32[8,288]{1,0:T(8,128)S(1)} %get-tuple-element.18), channel_id=1, source_target_pairs={{0,4},{1,5},{2,6},{3,7},{4,0},{5,1},{6,2},{7,3},{8,12},{9,13},{10,... | collective-permute-start | bytes 27656 | tf_op jit(solution)/shard_map/ppermute | solution.py:257
  22.2 3.8 %collective-permute-done.5.recv_ref = f32[8,288]{1,0:T(8,128)S(1)} collective-permute-done((f32[8,288]{1,0:T(8,128)S(1)}, f32[8,288]{1,0:T(8,128)S(1)}, u32[]{:S(2)}, u32[]{:S(2)}) %collective-permute-start.5) | collective-permute-done | bytes 9248 | tf_op jit(solution)/shard_map/ppermute | solution.py:257
  26.0 0.7 %place.1 = f32[9,8,64]{2,1,0:T(8,128)} custom-call(f32[8,288]{1,0:T(8,128)S(1)} %get-tuple-element.17.keep_ref, f32[8,288]{1,0:T(8,128)S(1)} %collective-permute-done.5.recv_ref), custom_call_target="tpu_custom_call" | custom-call | tf_op jit(solution)/shard_map/place/pallas_call | solution.py:304
  (2 shorter events, 0.0 us)
Async XLA Ops:
  0.0 13.5 %copy-start = (f32[64,4000]{1,0:T(8,128)S(1)}, f32[64,4000]{1,0:T(8,128)}, u32[]{:S(2)}) copy-start(f32[64,4000]{1,0:T(8,128)} %curves_hbm.1) | copy-start | bytes 3072004
  2.2 6.7 %collective-permute-start.2 = (bf16[4,4352]{1,0:T(4,128)(2,1)}, bf16[4,4352]{1,0:T(4,128)(2,1)S(1)}, u32[]{:S(2)}, u32[]{:S(2)}) collective-permute-start(bf16[4,4352]{1,0:T(4,128)(2,1)} %get-tuple-element.16), channel_id=1, source_target_pairs={{0,4},{1,5},{2,6},{3,7},{4,0},{5,1},{6,2},{7,3},{8,12},{9,13},{10,... | collective-permute-start | bytes 104456 | tf_op jit(solution)/shard_map/ppermute | solution.py:257
  6.3 2.6 %copy-start.4 = (bf16[4,4352]{1,0:T(4,128)(2,1)S(1)}, bf16[4,4352]{1,0:T(4,128)(2,1)}, u32[]{:S(2)}) copy-start(bf16[4,4352]{1,0:T(4,128)(2,1)} %get-tuple-element.16) | copy-start | bytes 104452
  6.3 5.2 %collective-permute-start = (bf16[16,4096]{1,0:T(8,128)(2,1)}, bf16[16,4096]{1,0:T(8,128)(2,1)S(1)}, u32[]{:S(2)}, u32[]{:S(2)}) collective-permute-start(bf16[16,4096]{1,0:T(8,128)(2,1)} %get-tuple-element.15), channel_id=1, source_target_pairs={{0,2},{1,3},{2,0},{3,1},{4,6},{5,7},{6,4},{7,5},{8,10},{9,11},{10,... | collective-permute-start | bytes 393224 | tf_op jit(solution)/shard_map/ppermute | solution.py:257
  8.9 4.6 %copy-start.1 = (f32[9,4000]{1,0:T(8,128)S(1)}, f32[9,4000]{1,0:T(8,128)}, u32[]{:S(2)}) copy-start(f32[9,4000]{1,0:T(8,128)} %phase_ref.1) | copy-start | bytes 432004
  8.9 4.5 %collective-permute-start.3 = (bf16[8,4352]{1,0:T(8,128)(2,1)S(1)}, bf16[8,4352]{1,0:T(8,128)(2,1)S(1)}, u32[]{:S(2)}, u32[]{:S(2)}) collective-permute-start(bf16[8,4352]{1,0:T(8,128)(2,1)S(1)} %pad_maximum_fusion.1), channel_id=1, source_target_pairs={{0,16},{8,24},{16,0},{24,8},{1,17},{9,25},{17,1},{25,9},{2,18},{10... | collective-permute-start | bytes 208904 | tf_op jit(solution)/shard_map/ppermute | solution.py:257
  11.5 2.1 %copy-start.2 = (f32[4000]{0:T(1024)S(1)}, f32[4000]{0:T(1024)}, u32[]{:S(2)}) copy-start(f32[4000]{0:T(1024)} %param.13) | copy-start | bytes 48004
  11.5 2.1 %copy-start.3 = (s32[9]{0:T(128)S(1)}, s32[9]{0:T(128)}, u32[]{:S(2)}) copy-start(s32[9]{0:T(128)} %trans_ref.1) | copy-start | bytes 112
  11.5 7.3 %collective-permute-start.1 = (bf16[32,4096]{1,0:T(8,128)(2,1)S(1)}, bf16[32,4096]{1,0:T(8,128)(2,1)S(1)}, u32[]{:S(2)}, u32[]{:S(2)}) collective-permute-start(bf16[32,4096]{1,0:T(8,128)(2,1)S(1)} %constant_dynamic-update-slice_fusion.rest_0_), channel_id=1, source_target_pairs={{0,1},{1,0},{2,3},{3,2},{4,5},{5,4},{6,7},{7,6},{8,9},{9,8},{10,11... | collective-permute-start | bytes 786440 | tf_op jit(solution)/shard_map/ppermute | solution.py:257
  13.5 1.6 %collective-permute-start.4 = (bf16[16,4352]{1,0:T(8,128)(2,1)S(1)}, bf16[16,4352]{1,0:T(8,128)(2,1)S(1)}, u32[]{:S(2)}, u32[]{:S(2)}) collective-permute-start(bf16[16,4352]{1,0:T(8,128)(2,1)S(1)} %pad_maximum_fusion.rest_2_), channel_id=1, source_target_pairs={{0,8},{8,0},{16,24},{24,16},{1,9},{9,1},{17,25},{25,17},{2,10},{10... | collective-permute-start | bytes 417800 | tf_op jit(solution)/shard_map/ppermute | solution.py:257
  21.4 4.6 %collective-permute-start.5 = (f32[8,288]{1,0:T(8,128)S(1)}, f32[8,288]{1,0:T(8,128)S(1)}, u32[]{:S(2)}, u32[]{:S(2)}) collective-permute-start(f32[8,288]{1,0:T(8,128)S(1)} %get-tuple-element.18), channel_id=1, source_target_pairs={{0,4},{1,5},{2,6},{3,7},{4,0},{5,1},{6,2},{7,3},{8,12},{9,13},{10,... | collective-permute-start | bytes 27656 | tf_op jit(solution)/shard_map/ppermute | solution.py:257

commit v5 on v4

--- a/solution.py
+++ b/solution.py
@@ -143,13 +143,12 @@
 
 
 def score_kernel(
-    half, offsets, n_parts, bits, n_part, n_proj, length, subsets, cos_ref, sin_ref, square_ref, *rest
+    half, offsets, n_parts, ng, n_part, n_proj, length, subsets, cos_ref, sin_ref, square_ref, *rest
 ):
     n_bank = len(offsets)
     banks, parts, outs = rest[:n_bank], rest[n_bank : n_bank + n_parts], rest[n_bank + n_parts :][:2]
     real_ref, imag_ref, shifted_ref = rest[n_bank + n_parts + 2 :]
-    blk, g = lax.axis_index("blk"), lax.axis_index("grp")
-    ng = 1 << len(bits)
+    blk = lax.axis_index("blk")
     total, wide = real_ref.shape
     shifts = cos_ref.shape[0]
     classes_count = square_ref.shape[0] // 2
@@ -167,10 +166,8 @@
     out_row = lax.broadcasted_iota(jnp.int32, (2 * count, held.shape[0]), 0)
     in_row = lax.broadcasted_iota(jnp.int32, (2 * count, held.shape[0]), 1)
     kind, rest_row = out_row // count, out_row % count
-    source, rest_row = rest_row // (ng * n_part), rest_row % (ng * n_part)
-    away, i = rest_row // n_part ^ g, rest_row % n_part
-    for n, bit in enumerate(bits):
-        source += jnp.where(away & bit != 0, 2 << n, 0)
+    source, rest_row = rest_row // (ng * n_part) ^ blk // half, rest_row % (ng * n_part)
+    source, i = source * ng + rest_row // n_part, rest_row % n_part
     pick = (in_row == source * (2 * n_part) + kind * n_part + i).astype(F32).astype(BF16)
     ordered = jnp.dot(pick, held, preferred_element_type=F32)
     weighted = jnp.concatenate([ordered[:count, :wide], ordered[count:, :wide]], axis=1).astype(BF16)
@@ -236,7 +233,7 @@
     bank, part = pl.pallas_call(
         pack_kernel,
         out_shape=[shape((2 * n_proj, wide), BF16), shape((2 * n_part, wide + extra), BF16)],
-        in_specs=[pl.BlockSpec(memory_space=pl.ANY)] * 7,
+        in_specs=[pl.BlockSpec(memory_space=pltpu.HBM)] * 7,
         out_specs=[_vmem()] * 2,
         scratch_shapes=[
             pltpu.SMEM(ctf_class.shape, jnp.int32),
@@ -248,7 +245,7 @@
             pltpu.VMEM(projections.shape, BF16),
             pltpu.SemaphoreType.DMA((7,)),
         ],
-        compiler_params=_params(56),
+        compiler_params=_params(16),
         name="pack",
     )(ctf_class, orient_subset, particles, orient_prior, ctf_curves, noise, projections)
 
@@ -266,9 +263,13 @@
         return pieces, held
 
     blk_bits = [1 << n for n in range(half.bit_length() - 2, -1, -1)]
-    grp_bits = [1 << n for n in range(ng.bit_length() - 2, -1, -1)]
     banks, offsets = doubled([bank], [[0]], "blk", blk_bits)
-    parts, _ = doubled([part, swap(part, "blk", half)], [[0], [0]], "grp", grp_bits)
+    members = [
+        [b * ng + g for b in (low, low + half) for g in range(ng)] for low in range(half)
+    ]
+    parts = [
+        lax.all_gather(part, ("blk", "grp"), axis_index_groups=members, axis=0, tiled=True)
+    ]
 
     cos_part, sin_part, square = pl.pallas_call(
         table_kernel,
@@ -285,7 +286,7 @@
     total = half * n_proj
     keep, give = pl.pallas_call(
         functools.partial(
-            score_kernel, half, offsets, len(parts), grp_bits, n_part, n_proj, length, subsets
+            score_kernel, half, offsets, len(parts), ng, n_part, n_proj, length, subsets
         ),
         out_shape=[shape((ng * n_part, shifts * total), F32)] * 2,
         in_specs=[_vmem()] * (3 + len(banks) + len(parts)),

time: 26.9 us -> 39.5 us (1.47)
  blocking collectives: 0 us -> 14.5 us
  local copies, waits for them, and re-layouts: 0.98 us -> 5.9 us
  starting transfers between devices: 10.1 us -> 7.02 us
  waiting for transfers between devices: 8.5 us -> 5.91 us
  Pallas kernels: 6.88 us -> 5.77 us
    all_gather x0 -> x1, blocking collectives: none -> 14.5 us  [per_device(): lax.all_gather(part, ('blk', 'grp'), axis_index_groups=members, axis=0, t...]
    unnamed x11 -> x24, local copies, waits for them, and re-layouts: 0.97 us -> 5.89 us
    ppermute x6 -> x3, starting transfers between devices: 10.1 us -> 7.02 us  [swap(): return lax.ppermute(value, axis, [(i, i ^ bit) for i in range(size)])]
    ppermute x6 -> x3, waiting for transfers between devices: 8.5 us -> 5.91 us  [swap(): return lax.ppermute(value, axis, [(i, i ^ bit) for i in range(size)])]
    pallas_call x1, Pallas kernels: 2.14 us -> 1.05 us  [per_device(): pl.pallas_call(pack_kernel, out_shape=[shape((2 * n_proj, wide), BF16), s...]
  transfers between devices with their start and end apart: 6 -> 3, of which waited for: 4 -> 2; matrix products, arithmetic and copies ran while one was open for 4% -> 0% of each run, Pallas kernels for 6% -> 4%
where the time goes in v5:
time: 39.5 us; the launch traced here: 39.2 us
  blocking collectives  14.5 us (37%)
  starting transfers between devices  7.02 us (18%)
  waiting for transfers between devices  5.91 us (15%)
  local copies, waits for them, and re-layouts  5.9 us (15%)
  Pallas kernels  5.77 us (15%)
    all_gather x1, blocking collectives, per_device(): lax.all_gather(part, ('blk', 'grp'), axis_index_groups=members, axis=0, t...  14.5 us
    ppermute x3, starting transfers between devices, swap(): return lax.ppermute(value, axis, [(i, i ^ bit) for i in range(size)])  7.02 us
    ppermute x3, waiting for transfers between devices, swap(): return lax.ppermute(value, axis, [(i, i ^ bit) for i in range(size)])  5.91 us
    unnamed x24, local copies, waits for them, and re-layouts  5.89 us
    pallas_call x1, Pallas kernels, per_device(): pl.pallas_call(functools.partial(score_kernel, half, offsets, len(parts),...  2.52 us
    pallas_call x1, Pallas kernels, per_device(): pl.pallas_call(table_kernel, out_shape=[shape((shifts, wide), F32)] * 2 +...  1.51 us
    pallas_call x1, Pallas kernels, per_device(): pl.pallas_call(pack_kernel, out_shape=[shape((2 * n_proj, wide), BF16), s...  1.05 us
  transfers between devices with their start and end apart: 3, of which 2 were waited for; matrix products, arithmetic and copies ran while one was open for 0% of the time, Pallas kernels for 4%

profile of v5, /device:TPU:0, one launch (start us, length us, event | category | flops | bytes accessed | tf_op | source)
XLA Modules:
  0.0 39.2 jit_solution(10783905606794899847)
XLA Ops:
  0.0 0.0 copy-start.7
  0.0 0.0 copy-start.8
  0.0 0.7 %copy-done.7 = bf16[2,192]{1,0:T(2,128)(2,1)S(1)} copy-done((bf16[2,192]{1,0:T(2,128)(2,1)S(1)}, bf16[2,192]{1,0:T(2,128)(2,1)}, u32[]{:S(2)}) %copy-start.7) | copy-done | bytes 792
  0.7 0.0 copy-done.8
  0.7 0.0 copy-start
  0.7 1.2 %copy-done = f32[64,4000]{1,0:T(8,128)S(1)} copy-done((f32[64,4000]{1,0:T(8,128)S(1)}, f32[64,4000]{1,0:T(8,128)}, u32[]{:S(2)}) %copy-start) | copy-done | bytes 1024024
  1.9 0.0 copy-start.3
  1.9 0.9 %copy-done.3 = bf16[8,2,4000]{2,1,0:T(2,128)(2,1)S(1)} copy-done((bf16[8,2,4000]{2,1,0:T(2,128)(2,1)S(1)}, bf16[8,2,4000]{2,1,0:T(2,128)(2,1)}, u32[]{:S(2)}) %copy-start.3) | copy-done | bytes 128024
  2.8 0.0 copy-start.4
  2.8 0.7 %copy-done.4 = f32[4000]{0:T(1024)S(1)} copy-done((f32[4000]{0:T(1024)S(1)}, f32[4000]{0:T(1024)}, u32[]{:S(2)}) %copy-start.4) | copy-done | bytes 16024
  3.5 0.0 copy-start.6
  3.5 0.8 %copy-done.6 = bf16[2,2,4000]{2,1,0:T(2,128)(2,1)S(1)} copy-done((bf16[2,2,4000]{2,1,0:T(2,128)(2,1)S(1)}, bf16[2,2,4000]{2,1,0:T(2,128)(2,1)}, u32[]{:S(2)}) %copy-start.6) | copy-done | bytes 32024
  4.3 0.0 copy-start.9
  4.3 0.7 %copy-done.9 = s32[8]{0:T(128)S(1)} copy-done((s32[8]{0:T(128)S(1)}, s32[8]{0:T(128)}, u32[]{:S(2)}) %copy-start.9) | copy-done | bytes 56
  4.9 0.0 copy-start.1
  4.9 1.0 %pack.1 = (bf16[16,4096]{1,0:T(8,128)(2,1)S(1)}, bf16[4,4352]{1,0:T(4,128)(2,1)S(1)}) custom-call(s32[2]{0:T(128)S(1)} %copy-done.8, s32[8]{0:T(128)S(1)} %copy-done.9, bf16[2,2,4000]{2,1,0:T(2,128)(2,1)S(1)} %copy-done.6, bf16[2,192]{1,0:T(2,128)(2,1)S(1)} %copy-done.7, f32[64,4000]{1,0:T(8,128)S(1)} %copy-done, f32[1,4000]{1,0:T(1,128)S(1)} %bitcast.3, ...), custom_call_target="tpu_custom_call" | custom-call | tf_op jit(solution)/shard_map/pack/pallas_call | solution.py:233
  6.0 3.1 %collective-permute-start = (bf16[16,4096]{1,0:T(8,128)(2,1)S(1)}, bf16[16,4096]{1,0:T(8,128)(2,1)S(1)}, u32[]{:S(2)}, u32[]{:S(2)}) collective-permute-start(bf16[16,4096]{1,0:T(8,128)(2,1)S(1)} %get-tuple-element.15), channel_id=1, source_target_pairs={{0,2},{1,3},{2,0},{3,1},{4,6},{5,7},{6,4},{7,5},{8,10},{9,11},{10,... | collective-permute-start | bytes 393224 | tf_op jit(solution)/shard_map/ppermute | solution.py:254
  9.1 3.5 %collective-permute-done = bf16[16,4096]{1,0:T(8,128)(2,1)S(1)} collective-permute-done((bf16[16,4096]{1,0:T(8,128)(2,1)S(1)}, bf16[16,4096]{1,0:T(8,128)(2,1)S(1)}, u32[]{:S(2)}, u32[]{:S(2)}) %collective-permute-start) | collective-permute-done | bytes 131104 | tf_op jit(solution)/shard_map/ppermute | solution.py:254
  12.6 1.7 %collective-permute-start.1 = (bf16[32,4096]{1,0:T(8,128)(2,1)S(1)}, bf16[32,4096]{1,0:T(8,128)(2,1)S(1)}, u32[]{:S(2)}, u32[]{:S(2)}) collective-permute-start(bf16[32,4096]{1,0:T(8,128)(2,1)S(1)} %constant_dynamic-update-slice_fusion.rest_0_), channel_id=1, source_target_pairs={{0,1},{1,0},{2,3},{3,2},{4,5},{5,4},{6,7},{7,6},{8,9},{9,8},{10,11... | collective-permute-start | bytes 786440 | tf_op jit(solution)/shard_map/ppermute | solution.py:254
  14.3 14.5 %all-gather = bf16[8,4,4352]{2,1,0:T(4,128)(2,1)S(1)} all-gather(bf16[1,4,4352]{2,1,0:T(4,128)(2,1)S(1)} %bitcast.5), channel_id=1, replica_groups={{0,8,16,24,4,12,20,28},{1,9,17,25,5,13,21,29},{2,10,18,26,6,14,22,30},{..., dimensions={0}, use_global_device_ids=true | all-gather | bytes 313344 | tf_op jit(solution)/shard_map/all_gather | solution.py:271
  28.9 0.0 copy-start.2
  28.9 0.0 copy-start.5
  28.9 0.0 copy-start.10
  28.9 0.1 reshape.5.rest_2_
  29.0 0.0 copy-done.1
  29.0 0.9 %copy-done.2 = f32[9,4000]{1,0:T(8,128)S(1)} copy-done((f32[9,4000]{1,0:T(8,128)S(1)}, f32[9,4000]{1,0:T(8,128)}, u32[]{:S(2)}) %copy-start.2) | copy-done | bytes 144024
  29.8 0.0 copy-done.5
  29.8 0.0 copy-done.10
  29.8 1.5 %tables.1 = (f32[9,4096]{1,0:T(8,128)S(1)}, f32[9,4096]{1,0:T(8,128)S(1)}, bf16[128,4096]{1,0:T(8,128)(2,1)S(1)}) custom-call(s32[9]{0:T(128)S(1)} %copy-done.10, f32[64,4000]{1,0:T(8,128)S(1)} %copy-done.1, f32[1,4000]{1,0:T(1,128)S(1)} %bitcast.4, f32[9,4000]{1,0:T(8,128)S(1)} %copy-done.2), custom_call_target="tpu_custom_call" | custom-call | flops 4000000 | bytes 2000000 | tf_op jit(solution)/shard_map/tables/pallas_call | solution.py:274
  31.4 0.0 collective-permute-done.1.rest_1_
  31.4 2.5 %score.1 = (f32[8,288]{1,0:T(8,128)S(1)}, f32[8,288]{1,0:T(8,128)S(1)}) custom-call(f32[9,4096]{1,0:T(8,128)S(1)} %get-tuple-element.12.cos_ref, f32[9,4096]{1,0:T(8,128)S(1)} %get-tuple-element.13.sin_ref, bf16[128,4096]{1,0:T(8,128)(2,1)S(1)} %get-tuple-element.14.square_ref, bf16[32,4096]{1,0:T(8,128)(2,1)S(1)} %constant_dynamic-update-slice_fusion.rest_0_, ...), custom_call_target="tpu_custom_call" | custom-call | flops 75497472 | bytes 4000000 | tf_op jit(solution)/shard_map/score/pallas_call | solution.py:287
  33.9 2.2 %collective-permute-start.2 = (f32[8,288]{1,0:T(8,128)S(1)}, f32[8,288]{1,0:T(8,128)S(1)}, u32[]{:S(2)}, u32[]{:S(2)}) collective-permute-start(f32[8,288]{1,0:T(8,128)S(1)} %get-tuple-element.18), channel_id=1, source_target_pairs={{0,4},{1,5},{2,6},{3,7},{4,0},{5,1},{6,2},{7,3},{8,12},{9,13},{10,... | collective-permute-start | bytes 27656 | tf_op jit(solution)/shard_map/ppermute | solution.py:254
  36.1 2.4 %collective-permute-done.2.recv_ref = f32[8,288]{1,0:T(8,128)S(1)} collective-permute-done((f32[8,288]{1,0:T(8,128)S(1)}, f32[8,288]{1,0:T(8,128)S(1)}, u32[]{:S(2)}, u32[]{:S(2)}) %collective-permute-start.2) | collective-permute-done | bytes 9248 | tf_op jit(solution)/shard_map/ppermute | solution.py:254
  38.5 0.7 %place.1 = f32[9,8,64]{2,1,0:T(8,128)} custom-call(f32[8,288]{1,0:T(8,128)S(1)} %get-tuple-element.17.keep_ref, f32[8,288]{1,0:T(8,128)S(1)} %collective-permute-done.2.recv_ref), custom_call_target="tpu_custom_call" | custom-call | tf_op jit(solution)/shard_map/place/pallas_call | solution.py:305
  (2 shorter events, 0.0 us)
Async XLA Ops:
  0.0 0.7 %copy-start.7 = (bf16[2,192]{1,0:T(2,128)(2,1)S(1)}, bf16[2,192]{1,0:T(2,128)(2,1)}, u32[]{:S(2)}) copy-start(bf16[2,192]{1,0:T(2,128)(2,1)} %prior_hbm.1) | copy-start | bytes 2308
  0.0 0.7 %copy-start.8 = (s32[2]{0:T(128)S(1)}, s32[2]{0:T(128)}, u32[]{:S(2)}) copy-start(s32[2]{0:T(128)} %class_hbm.1) | copy-start | bytes 28
  0.7 1.2 %copy-start = (f32[64,4000]{1,0:T(8,128)S(1)}, f32[64,4000]{1,0:T(8,128)}, u32[]{:S(2)}) copy-start(f32[64,4000]{1,0:T(8,128)} %curves_hbm.1) | copy-start | bytes 3072004
  1.9 0.9 %copy-start.3 = (bf16[8,2,4000]{2,1,0:T(2,128)(2,1)S(1)}, bf16[8,2,4000]{2,1,0:T(2,128)(2,1)}, u32[]{:S(2)}) copy-start(bf16[8,2,4000]{2,1,0:T(2,128)(2,1)} %proj_hbm.1) | copy-start | bytes 384004
  2.8 0.7 %copy-start.4 = (f32[4000]{0:T(1024)S(1)}, f32[4000]{0:T(1024)}, u32[]{:S(2)}) copy-start(f32[4000]{0:T(1024)} %param.13) | copy-start | bytes 48004
  3.5 0.8 %copy-start.6 = (bf16[2,2,4000]{2,1,0:T(2,128)(2,1)S(1)}, bf16[2,2,4000]{2,1,0:T(2,128)(2,1)}, u32[]{:S(2)}) copy-start(bf16[2,2,4000]{2,1,0:T(2,128)(2,1)} %particles_hbm.1) | copy-start | bytes 96004
  4.3 0.7 %copy-start.9 = (s32[8]{0:T(128)S(1)}, s32[8]{0:T(128)}, u32[]{:S(2)}) copy-start(s32[8]{0:T(128)} %subset_hbm.1) | copy-start | bytes 100
  4.9 24.0 %copy-start.1 = (f32[64,4000]{1,0:T(8,128)S(1)}, f32[64,4000]{1,0:T(8,128)}, u32[]{:S(2)}) copy-start(f32[64,4000]{1,0:T(8,128)} %curves_hbm.1) | copy-start | bytes 3072004
  6.0 6.6 %collective-permute-start = (bf16[16,4096]{1,0:T(8,128)(2,1)S(1)}, bf16[16,4096]{1,0:T(8,128)(2,1)S(1)}, u32[]{:S(2)}, u32[]{:S(2)}) collective-permute-start(bf16[16,4096]{1,0:T(8,128)(2,1)S(1)} %get-tuple-element.15), channel_id=1, source_target_pairs={{0,2},{1,3},{2,0},{3,1},{4,6},{5,7},{6,4},{7,5},{8,10},{9,11},{10,... | collective-permute-start | bytes 393224 | tf_op jit(solution)/shard_map/ppermute | solution.py:254
  12.6 18.8 %collective-permute-start.1 = (bf16[32,4096]{1,0:T(8,128)(2,1)S(1)}, bf16[32,4096]{1,0:T(8,128)(2,1)S(1)}, u32[]{:S(2)}, u32[]{:S(2)}) collective-permute-start(bf16[32,4096]{1,0:T(8,128)(2,1)S(1)} %constant_dynamic-update-slice_fusion.rest_0_), channel_id=1, source_target_pairs={{0,1},{1,0},{2,3},{3,2},{4,5},{5,4},{6,7},{7,6},{8,9},{9,8},{10,11... | collective-permute-start | bytes 786440 | tf_op jit(solution)/shard_map/ppermute | solution.py:254
  28.9 0.9 %copy-start.2 = (f32[9,4000]{1,0:T(8,128)S(1)}, f32[9,4000]{1,0:T(8,128)}, u32[]{:S(2)}) copy-start(f32[9,4000]{1,0:T(8,128)} %phase_ref.1) | copy-start | bytes 432004
  28.9 1.0 %copy-start.5 = (f32[4000]{0:T(1024)S(1)}, f32[4000]{0:T(1024)}, u32[]{:S(2)}) copy-start(f32[4000]{0:T(1024)} %param.13) | copy-start | bytes 48004
  28.9 1.0 %copy-start.10 = (s32[9]{0:T(128)S(1)}, s32[9]{0:T(128)}, u32[]{:S(2)}) copy-start(s32[9]{0:T(128)} %trans_ref.1) | copy-start | bytes 112
  33.9 4.6 %collective-permute-start.2 = (f32[8,288]{1,0:T(8,128)S(1)}, f32[8,288]{1,0:T(8,128)S(1)}, u32[]{:S(2)}, u32[]{:S(2)}) collective-permute-start(f32[8,288]{1,0:T(8,128)S(1)} %get-tuple-element.18), channel_id=1, source_target_pairs={{0,4},{1,5},{2,6},{3,7},{4,0},{5,1},{6,2},{7,3},{8,12},{9,13},{10,... | collective-permute-start | bytes 27656 | tf_op jit(solution)/shard_map/ppermute | solution.py:254

commit v6 on v4

--- a/solution.py
+++ b/solution.py
@@ -16,10 +16,6 @@
 
 def _vmem():
     return pl.BlockSpec(memory_space=pltpu.VMEM)
-
-
-def _smem():
-    return pl.BlockSpec(memory_space=pltpu.SMEM)
 
 
 def _params(mib):
@@ -34,14 +30,19 @@
     curves_hbm,
     noise_hbm,
     proj_hbm,
+    phase_hbm,
+    trans_hbm,
     bank_ref,
     part_ref,
+    curves_ref,
+    noise_ref,
+    angle_ref,
     class_ref,
     subset_ref,
+    trans_ref,
     particles_ref,
     prior_ref,
-    curves_ref,
-    noise_ref,
+    phase_ref,
     proj_ref,
     sems,
 ):
@@ -53,6 +54,8 @@
         (particles_hbm, particles_ref),
         (noise_hbm, noise_ref),
         (prior_hbm, prior_ref),
+        (trans_hbm, trans_ref),
+        (phase_hbm, phase_ref),
     ]
     copies = [pltpu.make_async_copy(a, b, sems.at[n]) for n, (a, b) in enumerate(pairs)]
     for copy in copies:
@@ -75,8 +78,12 @@
         both = padded(proj_ref[j].astype(F32), wide)
         real = jnp.where(row == j, both[0:1], real)
         imag = jnp.where(row == j, both[1:2], imag)
+    last = slice(wide - 128, wide)
+    ends = real[:, last]
     for j in range(n_proj):
-        real = jnp.where((row == j) & (lane == length), subset_ref[j].astype(F32), real)
+        here = (row[:, last] == j) & (lane[:, last] == length)
+        ends = jnp.where(here, subset_ref[j].astype(F32), ends)
+    real = jnp.concatenate([real[:, : wide - 128], ends], axis=1)
     bank_ref[...] = jnp.concatenate([real, imag], axis=0).astype(BF16)
 
     for copy in copies[2:]:
@@ -102,6 +109,8 @@
         rows_extra = jnp.where(row_extra == i, small, rows_extra)
     part_ref[:, :wide] = rows.astype(BF16)
     part_ref[:, wide:] = rows_extra.astype(BF16)
+    for t in range(phase_ref.shape[0]):
+        angle_ref[t : t + 1, :] = phase_ref[pl.ds(trans_ref[t], 1), :]
 
 
 def sine_cosine(x):
@@ -126,13 +135,11 @@
     return jnp.concatenate([high, low], axis=0)
 
 
-def table_kernel(trans_ref, curves_ref, noise_ref, phase_ref, cos_ref, sin_ref, square_ref, angle):
+def table_kernel(curves_ref, noise_ref, angle_ref, cos_ref, sin_ref, square_ref):
     length = curves_ref.shape[1]
     wide = cos_ref.shape[1]
-    for t in range(phase_ref.shape[0]):
-        angle[t : t + 1, :] = phase_ref[pl.ds(trans_ref[t], 1), :]
     zeros = jnp.zeros((cos_ref.shape[0], wide - length), F32)
-    sine, cosine = sine_cosine(angle[...])
+    sine, cosine = sine_cosine(angle_ref[...])
     cos_ref[...] = jnp.concatenate([cosine, zeros], axis=1)
     sin_ref[...] = jnp.concatenate([sine, zeros], axis=1)
     curve = curves_ref[...]
@@ -142,25 +149,58 @@
     )
 
 
+def shift_rows(shifted_ref, cos_ref, sin_ref, real, imag, offset, total):
+    n_proj, wide = real.shape
+    for t in range(cos_ref.shape[0]):
+        cos_part, sin_part = cos_ref[t : t + 1, :], sin_ref[t : t + 1, :]
+        rows = slice(t * total + offset * n_proj, t * total + (offset + 1) * n_proj)
+        shifted_ref[rows, :wide] = (cos_part * real + sin_part * imag).astype(BF16)
+        shifted_ref[rows, wide:] = (cos_part * imag - sin_part * real).astype(BF16)
+
+
+def norm_of(square_ref, powers):
+    power = jnp.concatenate(powers, axis=0)
+    count, classes_count = power.shape[0], square_ref.shape[0] // 2
+    table = lax.dot_general(
+        square_ref[...], split_terms(power), NT_DIMS, preferred_element_type=F32
+    )
+    return (
+        table[:classes_count, count:] + table[classes_count:, :count] + table[:classes_count, :count]
+    )
+
+
+def shift_kernel(offsets, total, cos_ref, sin_ref, square_ref, *rest):
+    banks, (shifted_ref, norm_ref) = rest[: len(offsets)], rest[len(offsets) :]
+    powers = []
+    for bank, offs in zip(banks, offsets):
+        n_proj = bank.shape[0] // (2 * len(offs))
+        for n, offset in enumerate(offs):
+            both = bank[2 * n_proj * n : 2 * n_proj * (n + 1)].astype(F32)
+            real, imag = both[:n_proj], both[n_proj:]
+            shift_rows(shifted_ref, cos_ref, sin_ref, real, imag, offset, total)
+            powers.append(real * real + imag * imag)
+    norm_ref[...] = norm_of(square_ref, powers)
+
+
 def score_kernel(
-    half, offsets, n_parts, bits, n_part, n_proj, length, subsets, cos_ref, sin_ref, square_ref, *rest
+    half, offsets, n_parts, bits, n_part, n_proj, length, subsets, shifted_in, cos_ref, sin_ref, square_ref, norm_ref, *rest
 ):
     n_bank = len(offsets)
     banks, parts, outs = rest[:n_bank], rest[n_bank : n_bank + n_parts], rest[n_bank + n_parts :][:2]
-    real_ref, imag_ref, shifted_ref = rest[n_bank + n_parts + 2 :]
-    blk, g = lax.axis_index("blk"), lax.axis_index("grp")
+    shifted_ref = rest[n_bank + n_parts + 2]
+    g = lax.axis_index("grp")
     ng = 1 << len(bits)
-    total, wide = real_ref.shape
+    total, wide = half * n_proj, cos_ref.shape[1]
     shifts = cos_ref.shape[0]
     classes_count = square_ref.shape[0] // 2
 
-    for bank, offs in zip(banks, offsets):
-        for n, offset in enumerate(offs):
-            both = bank[2 * n_proj * n : 2 * n_proj * (n + 1)].astype(F32)
-            where = pl.multiple_of((blk % half ^ offset) * n_proj, n_proj)
-            real_ref[pl.ds(where, n_proj), :] = both[:n_proj]
-            imag_ref[pl.ds(where, n_proj), :] = both[n_proj:]
-    real, imag = real_ref[...], imag_ref[...]
+    powers = []
+    for n, offset in enumerate(offsets[-1]):
+        both = banks[-1][2 * n_proj * n : 2 * n_proj * (n + 1)].astype(F32)
+        real, imag = both[:n_proj], both[n_proj:]
+        shift_rows(shifted_ref, cos_ref, sin_ref, real, imag, offset, total)
+        powers.append(real * real + imag * imag)
+    norm_last = norm_of(square_ref, powers)
 
     held = jnp.concatenate([part[...] for part in parts], axis=0)
     count = 2 * ng * n_part
@@ -176,33 +216,60 @@
     weighted = jnp.concatenate([ordered[:count, :wide], ordered[count:, :wide]], axis=1).astype(BF16)
     prior_rows = ordered[:count, wide : wide + subsets].astype(BF16)
     class_rows = ordered[:count, wide + subsets : wide + subsets + 1]
-
-    for t in range(shifts):
-        cos_part, sin_part = cos_ref[t : t + 1, :], sin_ref[t : t + 1, :]
-        rows = slice(t * total, (t + 1) * total)
-        shifted_ref[rows, :wide] = (cos_part * real + sin_part * imag).astype(BF16)
-        shifted_ref[rows, wide:] = (cos_part * imag - sin_part * real).astype(BF16)
     cross = lax.dot_general(weighted, shifted_ref[...], NT_DIMS, preferred_element_type=F32)
 
-    power = split_terms(real * real + imag * imag)
-    table = lax.dot_general(square_ref[...], power, NT_DIMS, preferred_element_type=F32)
-    table = table[:classes_count, total:] + table[classes_count:, :total] + table[:classes_count, :total]
+    order = [offset for offs in offsets for offset in offs]
+    first = len(order) - len(offsets[-1])
+    norms, ids = {}, {}
+    ids_at = length // 128 * 128
+    for n, offset in enumerate(order):
+        table, m = (norm_ref, n) if n < first else (norm_last, n - first)
+        norms[offset] = table[:, m * n_proj : (m + 1) * n_proj]
+    for bank, offs in zip(banks, offsets):
+        for n, offset in enumerate(offs):
+            rows = bank[2 * n_proj * n : 2 * n_proj * (n + 1), ids_at : ids_at + 128].astype(F32)
+            ids[offset] = rows[:n_proj]
+    table = jnp.concatenate([norms[offset] for offset in range(half)], axis=1)
+    id_rows = jnp.concatenate([ids[offset] for offset in range(half)], axis=0)
+    id_rows = id_rows[:, length - ids_at : length - ids_at + 1]
     class_col = lax.broadcasted_iota(jnp.int32, (count, classes_count), 1).astype(F32)
     onehot = (class_col == class_rows).astype(F32)
     norm = jnp.dot(onehot, table, precision=HIGHEST, preferred_element_type=F32)
     subset_col = lax.broadcasted_iota(jnp.int32, (total, subsets), 1).astype(F32)
-    subset_hot = (subset_col == real[:, length : length + 1]).astype(F32).astype(BF16)
+    subset_hot = (subset_col == id_rows).astype(F32).astype(BF16)
     prior = lax.dot_general(prior_rows, subset_hot, NT_DIMS, preferred_element_type=F32)
     result = cross + jnp.concatenate([prior - 0.5 * norm] * shifts, axis=1)
     dest = ng * n_part
+    lanes = outs[0].shape[1]
     for s in range(2):
-        outs[s][...] = result[s * dest : (s + 1) * dest]
-
-
-def place_kernel(half, keep_ref, recv_ref, out_ref):
-    first = lax.axis_index("blk") < half
+        rows = result[s * dest : (s + 1) * dest]
+        if rows.shape[1] < lanes:
+            zeros = jnp.zeros((dest, lanes - rows.shape[1]), F32)
+            rows = jnp.concatenate([rows, zeros], axis=1)
+        outs[s][...] = rows
+
+
+def place_kernel(half, n_proj, keep_ref, recv_ref, out_ref):
+    blk = lax.axis_index("blk")
+    first = blk < half
     low = jnp.where(first, keep_ref[...], recv_ref[...])
     high = jnp.where(first, recv_ref[...], keep_ref[...])
+    lanes = low.shape[1]
+    lane = lax.broadcasted_iota(jnp.int32, low.shape, 1)
+
+    def exchanged(values):
+        bit = 1
+        while bit < half:
+            step = bit * n_proj
+            upper = (lane & step) != 0
+            other = jnp.where(
+                upper, pltpu.roll(values, step, 1), pltpu.roll(values, lanes - step, 1)
+            )
+            values = jnp.where((blk & bit) != 0, other, values)
+            bit *= 2
+        return values
+
+    low, high = exchanged(low), exchanged(high)
     shifts, _, width = out_ref.shape
     width = width // 2
     for t in range(shifts):
@@ -233,76 +300,120 @@
     noise = noise_weight.reshape(1, length)
     shape = jax.ShapeDtypeStruct
 
-    bank, part = pl.pallas_call(
+    def vmem_out(dims, dtype):
+        return pltpu.VMEM(dims, dtype)
+
+    operands = (
+        ctf_class,
+        orient_subset,
+        particles,
+        orient_prior,
+        ctf_curves,
+        noise,
+        projections,
+        shift_phase,
+        trans_index,
+    )
+    bank, part, curves, noise, angle = pl.pallas_call(
         pack_kernel,
-        out_shape=[shape((2 * n_proj, wide), BF16), shape((2 * n_part, wide + extra), BF16)],
-        in_specs=[pl.BlockSpec(memory_space=pl.ANY)] * 7,
-        out_specs=[_vmem()] * 2,
+        out_shape=[
+            vmem_out((2 * n_proj, wide), BF16),
+            vmem_out((2 * n_part, wide + extra), BF16),
+            vmem_out(ctf_curves.shape, F32),
+            vmem_out(noise.shape, F32),
+            vmem_out(shift_phase.shape, F32),
+        ],
+        in_specs=[pl.BlockSpec(memory_space=pltpu.HBM)] * len(operands),
+        out_specs=[_vmem()] * 5,
         scratch_shapes=[
             pltpu.SMEM(ctf_class.shape, jnp.int32),
             pltpu.SMEM(orient_subset.shape, jnp.int32),
+            pltpu.SMEM(trans_index.shape, jnp.int32),
             pltpu.VMEM(particles.shape, BF16),
             pltpu.VMEM(orient_prior.shape, BF16),
-            pltpu.VMEM(ctf_curves.shape, F32),
-            pltpu.VMEM(noise.shape, F32),
+            pltpu.VMEM(shift_phase.shape, F32),
             pltpu.VMEM(projections.shape, BF16),
-            pltpu.SemaphoreType.DMA((7,)),
+            pltpu.SemaphoreType.DMA((len(operands),)),
         ],
-        compiler_params=_params(56),
+        compiler_params=_params(16),
         name="pack",
-    )(ctf_class, orient_subset, particles, orient_prior, ctf_curves, noise, projections)
+    )(*[pltpu.with_memory_space_constraint(operand, pltpu.HBM) for operand in operands])
 
     def swap(value, axis, bit):
         size = lax.axis_size(axis)
         return lax.ppermute(value, axis, [(i, i ^ bit) for i in range(size)])
 
-    def doubled(pieces, offsets, axis, bits):
-        held = offsets
+    def joined(pieces):
+        return pieces[0] if len(pieces) == 1 else jnp.concatenate(pieces, axis=0)
+
+    def doubled(pieces, axis, bits):
         for bit in bits:
-            whole = pieces[0] if len(pieces) == 1 else jnp.concatenate(pieces, axis=0)
-            all_offsets = [offset for offs in held for offset in offs]
+            whole = joined(pieces)
             pieces = [whole, swap(whole, axis, bit)]
-            held = [all_offsets, [offset ^ bit for offset in all_offsets]]
-        return pieces, held
-
-    blk_bits = [1 << n for n in range(half.bit_length() - 2, -1, -1)]
+        return pieces
+
     grp_bits = [1 << n for n in range(ng.bit_length() - 2, -1, -1)]
-    banks, offsets = doubled([bank], [[0]], "blk", blk_bits)
-    parts, _ = doubled([part, swap(part, "blk", half)], [[0], [0]], "grp", grp_bits)
+    parts = doubled([part, swap(part, "blk", half)], "grp", grp_bits)
+
+    near = swap(bank, "blk", 1)
+    planes, far_offsets = [bank], [0]
+    for n in range(half.bit_length() - 2, 0, -1):
+        planes.append(swap(joined(planes), "blk", 1 << n))
+        far_offsets += [offset ^ (1 << n) for offset in far_offsets]
+    far, far_offsets = joined(planes[1:]), far_offsets[1:]
+    last = swap(far, "blk", 1)
+    banks = [bank, near, far, last]
+    offsets = [[0], [1], far_offsets, [offset ^ 1 for offset in far_offsets]]
 
     cos_part, sin_part, square = pl.pallas_call(
         table_kernel,
-        out_shape=[shape((shifts, wide), F32)] * 2 + [shape((2 * classes_count, wide), BF16)],
-        in_specs=[_smem(), _vmem(), _vmem(), _vmem()],
+        out_shape=[
+            vmem_out((shifts, wide), F32),
+            vmem_out((shifts, wide), F32),
+            vmem_out((2 * classes_count, wide), BF16),
+        ],
+        in_specs=[_vmem()] * 3,
         out_specs=[_vmem()] * 3,
-        scratch_shapes=[pltpu.VMEM((shifts, length), F32)],
         compiler_params=_params(8),
         cost_estimate=pl.CostEstimate(flops=4_000_000, bytes_accessed=2_000_000, transcendentals=0),
         name="tables",
-    )(trans_index, ctf_curves, noise, shift_phase)
+    )(curves, noise, angle)
 
     count = 2 * ng * n_part
     total = half * n_proj
-    keep, give = pl.pallas_call(
+    early = total - len(far_offsets) * n_proj
+    shifted, norm = pl.pallas_call(
+        functools.partial(shift_kernel, offsets[:3], total),
+        out_shape=[
+            vmem_out((shifts * total, 2 * wide), BF16),
+            vmem_out((classes_count, early), F32),
+        ],
+        in_specs=[_vmem()] * 6,
+        out_specs=[_vmem()] * 2,
+        compiler_params=_params(8),
+        cost_estimate=pl.CostEstimate(
+            flops=6 * early * shifts * wide, bytes_accessed=4_000_000, transcendentals=0
+        ),
+        name="shift",
+    )(cos_part, sin_part, square, *banks[:3])
+    lanes = 128 * -(-shifts * total // 128)
+    keep, give, _ = pl.pallas_call(
         functools.partial(
             score_kernel, half, offsets, len(parts), grp_bits, n_part, n_proj, length, subsets
         ),
-        out_shape=[shape((ng * n_part, shifts * total), F32)] * 2,
-        in_specs=[_vmem()] * (3 + len(banks) + len(parts)),
-        out_specs=[_vmem()] * 2,
-        scratch_shapes=[
-            pltpu.VMEM((total, wide), F32),
-            pltpu.VMEM((total, wide), F32),
-            pltpu.VMEM((shifts * total, 2 * wide), BF16),
-        ],
-        compiler_params=_params(44),
+        out_shape=[vmem_out((ng * n_part, lanes), F32)] * 2
+        + [vmem_out((shifts * total, 2 * wide), BF16)],
+        in_specs=[_vmem()] * (5 + len(banks) + len(parts)),
+        out_specs=[_vmem()] * 3,
+        input_output_aliases={0: 2},
+        compiler_params=_params(8),
         cost_estimate=pl.CostEstimate(
             flops=4 * count * total * shifts * wide, bytes_accessed=4_000_000, transcendentals=0
         ),
         name="score",
-    )(cos_part, sin_part, square, *banks, *parts)
+    )(shifted, cos_part, sin_part, square, norm, *banks, *parts)
     scores = pl.pallas_call(
-        functools.partial(place_kernel, half),
+        functools.partial(place_kernel, half, n_proj),
         out_shape=shape((shifts, ng * n_part, 2 * total), F32),
         in_specs=[_vmem()] * 2,
         out_specs=_vmem(),

time: 26.9 us -> 29.2 us (1.086)
  starting transfers between devices: 10.1 us -> 13.2 us
  local copies, waits for them, and re-layouts: 0.98 us -> 0 us
    ppermute x6 -> x7, starting transfers between devices: 10.1 us -> 13.2 us  [swap(): return lax.ppermute(value, axis, [(i, i ^ bit) for i in range(size)])]
    unnamed x11 -> x0, local copies, waits for them, and re-layouts: 0.97 us -> none
    pallas_call x3 -> x4, Pallas kernels: 4.35 us -> 4.71 us  [the longest x1 1.69 us: per_device(): pl.pallas_call(functools.partial(shift_kernel, offsets[:3], total), out_s...]
    ppermute x6 -> x7, waiting for transfers between devices: 8.5 us -> 8.72 us  [swap(): return lax.ppermute(value, axis, [(i, i ^ bit) for i in range(size)])]
  transfers between devices with their start and end apart: 6 -> 7, of which waited for: 4 -> 6; matrix products, arithmetic and copies ran while one was open for 4% -> 0% of each run, Pallas kernels for 6% -> 8%
where the time goes in v6:
time: 29.2 us; the launch traced here: 29 us
  starting transfers between devices  13.2 us (45%)
  waiting for transfers between devices  8.72 us (30%)
  Pallas kernels  6.99 us (24%)
    ppermute x7, starting transfers between devices, swap(): return lax.ppermute(value, axis, [(i, i ^ bit) for i in range(size)])  13.2 us
    ppermute x7, waiting for transfers between devices, swap(): return lax.ppermute(value, axis, [(i, i ^ bit) for i in range(size)])  8.72 us
    pallas_call x1, Pallas kernels, per_device(): pl.pallas_call(functools.partial(score_kernel, half, offsets, len(parts),...  2.28 us
    pallas_call x1, Pallas kernels, per_device(): pl.pallas_call(functools.partial(shift_kernel, offsets[:3], total), out_s...  1.69 us
    pallas_call x1, Pallas kernels, per_device(): pl.pallas_call(pack_kernel, out_shape=[vmem_out((2 * n_proj, wide), BF16)...  1.58 us
    pallas_call x1, Pallas kernels, per_device(): pl.pallas_call(functools.partial(place_kernel, half, n_proj), out_shape=s...  0.86 us
    pallas_call x1, Pallas kernels, per_device(): pl.pallas_call(table_kernel, out_shape=[vmem_out((shifts, wide), F32), vm...  0.58 us
  transfers between devices with their start and end apart: 7, of which 6 were waited for; matrix products, arithmetic and copies ran while one was open for 0% of the time, Pallas kernels for 8%

profile of v6, /device:TPU:0, one launch (start us, length us, event | category | flops | bytes accessed | tf_op | source)
XLA Modules:
  0.0 29.0 jit_solution(8881523330200099641)
XLA Ops:
  0.0 1.6 %pack.1 = (bf16[16,4096]{1,0:T(8,128)(2,1)S(1)}, bf16[4,4352]{1,0:T(4,128)(2,1)S(1)}, f32[64,4000]{1,0:T(8,128)S(1)}, f32[1,4000]{1,0:T(1,128)S(1)}, f32[9,4000]{1,0:T(8,128)S(1)}) custom-call(s32[2]{0:T(128)} %class_hbm.1, s32[8]{0:T(128)} %subset_hbm.1, bf16[2,2,4000]{2,1,0:T(2,128)(2,1)} %particles_hbm.1, bf16[2,192]{1,0:T(2,128)(2,1)} %prior_hbm.1, ...), custom_call_target="tpu_custom_call" | custom-call | tf_op jit(solution)/shard_map/pack/pallas_call | solution.py:317
  1.6 4.1 %collective-permute-start.3 = (bf16[4,4352]{1,0:T(4,128)(2,1)S(1)}, bf16[4,4352]{1,0:T(4,128)(2,1)S(1)}, u32[]{:S(2)}, u32[]{:S(2)}) collective-permute-start(bf16[4,4352]{1,0:T(4,128)(2,1)S(1)} %get-tuple-element.26), channel_id=1, source_target_pairs={{0,4},{1,5},{2,6},{3,7},{4,0},{5,1},{6,2},{7,3},{8,12},{9,13},{10,... | collective-permute-start | bytes 104456 | tf_op jit(solution)/shard_map/ppermute | solution.py:344
  5.7 2.3 %collective-permute-done.3 = bf16[4,4352]{1,0:T(4,128)(2,1)S(1)} collective-permute-done((bf16[4,4352]{1,0:T(4,128)(2,1)S(1)}, bf16[4,4352]{1,0:T(4,128)(2,1)S(1)}, u32[]{:S(2)}, u32[]{:S(2)}) %collective-permute-start.3) | collective-permute-done | bytes 34848 | tf_op jit(solution)/shard_map/ppermute | solution.py:344
  8.0 1.8 %collective-permute-start.4 = (bf16[8,4352]{1,0:T(8,128)(2,1)S(1)}, bf16[8,4352]{1,0:T(8,128)(2,1)S(1)}, u32[]{:S(2)}, u32[]{:S(2)}) collective-permute-start(bf16[8,4352]{1,0:T(8,128)(2,1)S(1)} %pad_maximum_fusion.1), channel_id=1, source_target_pairs={{0,16},{8,24},{16,0},{24,8},{1,17},{9,25},{17,1},{25,9},{2,18},{10... | collective-permute-start | bytes 208904 | tf_op jit(solution)/shard_map/ppermute | solution.py:344
  9.8 1.3 %collective-permute-start.1 = (bf16[16,4096]{1,0:T(8,128)(2,1)S(1)}, bf16[16,4096]{1,0:T(8,128)(2,1)S(1)}, u32[]{:S(2)}, u32[]{:S(2)}) collective-permute-start(bf16[16,4096]{1,0:T(8,128)(2,1)S(1)} %get-tuple-element.23.rest_0_), channel_id=1, source_target_pairs={{0,2},{1,3},{2,0},{3,1},{4,6},{5,7},{6,4},{7,5},{8,10},{9,11},{10,... | collective-permute-start | bytes 393224 | tf_op jit(solution)/shard_map/ppermute | solution.py:344
  11.1 1.3 %collective-permute-done.4 = bf16[8,4352]{1,0:T(8,128)(2,1)S(1)} collective-permute-done((bf16[8,4352]{1,0:T(8,128)(2,1)S(1)}, bf16[8,4352]{1,0:T(8,128)(2,1)S(1)}, u32[]{:S(2)}, u32[]{:S(2)}) %collective-permute-start.4) | collective-permute-done | bytes 69664 | tf_op jit(solution)/shard_map/ppermute | solution.py:344
  12.4 0.1 pad_maximum_fusion.rest_4_
  12.5 0.1 collective-permute-start.5
  12.5 1.8 %collective-permute-start = (bf16[16,4096]{1,0:T(8,128)(2,1)S(1)}, bf16[16,4096]{1,0:T(8,128)(2,1)S(1)}, u32[]{:S(2)}, u32[]{:S(2)}) collective-permute-start(bf16[16,4096]{1,0:T(8,128)(2,1)S(1)} %get-tuple-element.23.rest_0_), channel_id=1, source_target_pairs={{0,1},{1,0},{2,3},{3,2},{4,5},{5,4},{6,7},{7,6},{8,9},{9,8},{10,11... | collective-permute-start | bytes 393224 | tf_op jit(solution)/shard_map/ppermute | solution.py:344
  14.3 0.4 %collective-permute-done.1.rest_2_ = bf16[16,4096]{1,0:T(8,128)(2,1)S(1)} collective-permute-done((bf16[16,4096]{1,0:T(8,128)(2,1)S(1)}, bf16[16,4096]{1,0:T(8,128)(2,1)S(1)}, u32[]{:S(2)}, u32[]{:S(2)}) %collective-permute-start.1) | collective-permute-done | bytes 131104 | tf_op jit(solution)/shard_map/ppermute | solution.py:344
  14.8 1.5 %collective-permute-start.2 = (bf16[16,4096]{1,0:T(8,128)(2,1)S(1)}, bf16[16,4096]{1,0:T(8,128)(2,1)S(1)}, u32[]{:S(2)}, u32[]{:S(2)}) collective-permute-start(bf16[16,4096]{1,0:T(8,128)(2,1)S(1)} %collective-permute-done.1.rest_2_), channel_id=1, source_target_pairs={{0,1},{1,0},{2,3},{3,2},{4,5},{5,4},{6,7},{7,6},{8,9},{9,8},{10,11... | collective-permute-start | bytes 393224 | tf_op jit(solution)/shard_map/ppermute | solution.py:344
  16.3 0.6 %tables.1 = (f32[9,4096]{1,0:T(8,128)S(1)}, f32[9,4096]{1,0:T(8,128)S(1)}, bf16[128,4096]{1,0:T(8,128)(2,1)S(1)}) custom-call(f32[64,4000]{1,0:T(8,128)S(1)} %get-tuple-element.17.curves_ref, f32[1,4000]{1,0:T(1,128)S(1)} %get-tuple-element.18.noise_ref, f32[9,4000]{1,0:T(8,128)S(1)} %get-tuple-element.19.angle_ref), custom_call_target="tpu_custom_call" | custom-call | flops 4000000 | bytes 2000000 | tf_op jit(solution)/shard_map/tables/pallas_call | solution.py:368
  16.9 2.0 %collective-permute-done.rest_1_ = bf16[16,4096]{1,0:T(8,128)(2,1)S(1)} collective-permute-done((bf16[16,4096]{1,0:T(8,128)(2,1)S(1)}, bf16[16,4096]{1,0:T(8,128)(2,1)S(1)}, u32[]{:S(2)}, u32[]{:S(2)}) %collective-permute-start) | collective-permute-done | bytes 131104 | tf_op jit(solution)/shard_map/ppermute | solution.py:344
  18.9 1.7 %shift.1 = (bf16[288,8192]{1,0:T(8,128)(2,1)S(1)}, f32[64,24]{1,0:T(8,128)S(1)}) custom-call(f32[9,4096]{1,0:T(8,128)S(1)} %get-tuple-element.20.cos_ref, f32[9,4096]{1,0:T(8,128)S(1)} %get-tuple-element.21.sin_ref, bf16[128,4096]{1,0:T(8,128)(2,1)S(1)} %get-tuple-element.22.square_ref, bf16[16,4096]{1,0:T(8,128)(2,1)S(1)} %get-tuple-element.23.rest_0_, ...), custom_call_target="tpu_custom_call" | custom-call | flops 5308416 | bytes 4000000 | tf_op jit(solution)/shard_map/shift/pallas_call | solution.py:385
  20.6 0.0 collective-permute-done.5.rest_5_
  20.6 0.7 %collective-permute-done.2.rest_3_ = bf16[16,4096]{1,0:T(8,128)(2,1)S(1)} collective-permute-done((bf16[16,4096]{1,0:T(8,128)(2,1)S(1)}, bf16[16,4096]{1,0:T(8,128)(2,1)S(1)}, u32[]{:S(2)}, u32[]{:S(2)}) %collective-permute-start.2) | collective-permute-done | bytes 131104 | tf_op jit(solution)/shard_map/ppermute | solution.py:344
  21.3 2.3 %score.1 = (f32[8,384]{1,0:T(8,128)S(1)}, f32[8,384]{1,0:T(8,128)S(1)}, bf16[288,8192]{1,0:T(8,128)(2,1)S(1)}) custom-call(bf16[288,8192]{1,0:T(8,128)(2,1)S(1)} %get-tuple-element.24.shifted_in, f32[9,4096]{1,0:T(8,128)S(1)} %get-tuple-element.20.cos_ref, f32[9,4096]{1,0:T(8,128)S(1)} %get-tuple-element.21.sin_ref, ...), custom_call_target="tpu_custom_call", output_to_operand_aliasing={{2}: (0, {})} | custom-call | flops 75497472 | bytes 4000000 | tf_op jit(solution)/shard_map/score/pallas_call | solution.py:400
  23.5 2.6 %collective-permute-start.6 = (f32[8,384]{1,0:T(8,128)S(1)}, f32[8,384]{1,0:T(8,128)S(1)}, u32[]{:S(2)}, u32[]{:S(2)}) collective-permute-start(f32[8,384]{1,0:T(8,128)S(1)} %get-tuple-element.28), channel_id=1, source_target_pairs={{0,4},{1,5},{2,6},{3,7},{4,0},{5,1},{6,2},{7,3},{8,12},{9,13},{10,... | collective-permute-start | bytes 36872 | tf_op jit(solution)/shard_map/ppermute | solution.py:344
  26.2 2.0 %collective-permute-done.6.recv_ref = f32[8,384]{1,0:T(8,128)S(1)} collective-permute-done((f32[8,384]{1,0:T(8,128)S(1)}, f32[8,384]{1,0:T(8,128)S(1)}, u32[]{:S(2)}, u32[]{:S(2)}) %collective-permute-start.6) | collective-permute-done | bytes 12320 | tf_op jit(solution)/shard_map/ppermute | solution.py:344
  28.2 0.9 %place.1 = f32[9,8,64]{2,1,0:T(8,128)} custom-call(f32[8,384]{1,0:T(8,128)S(1)} %get-tuple-element.27.keep_ref, f32[8,384]{1,0:T(8,128)S(1)} %collective-permute-done.6.recv_ref), custom_call_target="tpu_custom_call" | custom-call | tf_op jit(solution)/shard_map/place/pallas_call | solution.py:415
  (1 shorter events, 0.0 us)
Async XLA Ops:
  1.6 6.4 %collective-permute-start.3 = (bf16[4,4352]{1,0:T(4,128)(2,1)S(1)}, bf16[4,4352]{1,0:T(4,128)(2,1)S(1)}, u32[]{:S(2)}, u32[]{:S(2)}) collective-permute-start(bf16[4,4352]{1,0:T(4,128)(2,1)S(1)} %get-tuple-element.26), channel_id=1, source_target_pairs={{0,4},{1,5},{2,6},{3,7},{4,0},{5,1},{6,2},{7,3},{8,12},{9,13},{10,... | collective-permute-start | bytes 104456 | tf_op jit(solution)/shard_map/ppermute | solution.py:344
  8.0 4.4 %collective-permute-start.4 = (bf16[8,4352]{1,0:T(8,128)(2,1)S(1)}, bf16[8,4352]{1,0:T(8,128)(2,1)S(1)}, u32[]{:S(2)}, u32[]{:S(2)}) collective-permute-start(bf16[8,4352]{1,0:T(8,128)(2,1)S(1)} %pad_maximum_fusion.1), channel_id=1, source_target_pairs={{0,16},{8,24},{16,0},{24,8},{1,17},{9,25},{17,1},{25,9},{2,18},{10... | collective-permute-start | bytes 208904 | tf_op jit(solution)/shard_map/ppermute | solution.py:344
  9.8 5.0 %collective-permute-start.1 = (bf16[16,4096]{1,0:T(8,128)(2,1)S(1)}, bf16[16,4096]{1,0:T(8,128)(2,1)S(1)}, u32[]{:S(2)}, u32[]{:S(2)}) collective-permute-start(bf16[16,4096]{1,0:T(8,128)(2,1)S(1)} %get-tuple-element.23.rest_0_), channel_id=1, source_target_pairs={{0,2},{1,3},{2,0},{3,1},{4,6},{5,7},{6,4},{7,5},{8,10},{9,11},{10,... | collective-permute-start | bytes 393224 | tf_op jit(solution)/shard_map/ppermute | solution.py:344
  12.5 8.1 %collective-permute-start.5 = (bf16[16,4352]{1,0:T(8,128)(2,1)S(1)}, bf16[16,4352]{1,0:T(8,128)(2,1)S(1)}, u32[]{:S(2)}, u32[]{:S(2)}) collective-permute-start(bf16[16,4352]{1,0:T(8,128)(2,1)S(1)} %pad_maximum_fusion.rest_4_), channel_id=1, source_target_pairs={{0,8},{8,0},{16,24},{24,16},{1,9},{9,1},{17,25},{25,17},{2,10},{10... | collective-permute-start | bytes 417800 | tf_op jit(solution)/shard_map/ppermute | solution.py:344
  12.5 6.4 %collective-permute-start = (bf16[16,4096]{1,0:T(8,128)(2,1)S(1)}, bf16[16,4096]{1,0:T(8,128)(2,1)S(1)}, u32[]{:S(2)}, u32[]{:S(2)}) collective-permute-start(bf16[16,4096]{1,0:T(8,128)(2,1)S(1)} %get-tuple-element.23.rest_0_), channel_id=1, source_target_pairs={{0,1},{1,0},{2,3},{3,2},{4,5},{5,4},{6,7},{7,6},{8,9},{9,8},{10,11... | collective-permute-start | bytes 393224 | tf_op jit(solution)/shard_map/ppermute | solution.py:344
  14.8 6.5 %collective-permute-start.2 = (bf16[16,4096]{1,0:T(8,128)(2,1)S(1)}, bf16[16,4096]{1,0:T(8,128)(2,1)S(1)}, u32[]{:S(2)}, u32[]{:S(2)}) collective-permute-start(bf16[16,4096]{1,0:T(8,128)(2,1)S(1)} %collective-permute-done.1.rest_2_), channel_id=1, source_target_pairs={{0,1},{1,0},{2,3},{3,2},{4,5},{5,4},{6,7},{7,6},{8,9},{9,8},{10,11... | collective-permute-start | bytes 393224 | tf_op jit(solution)/shard_map/ppermute | solution.py:344
  23.5 4.6 %collective-permute-start.6 = (f32[8,384]{1,0:T(8,128)S(1)}, f32[8,384]{1,0:T(8,128)S(1)}, u32[]{:S(2)}, u32[]{:S(2)}) collective-permute-start(f32[8,384]{1,0:T(8,128)S(1)} %get-tuple-element.28), channel_id=1, source_target_pairs={{0,4},{1,5},{2,6},{3,7},{4,0},{5,1},{6,2},{7,3},{8,12},{9,13},{10,... | collective-permute-start | bytes 36872 | tf_op jit(solution)/shard_map/ppermute | solution.py:344

commit v7 on v6

--- a/solution.py
+++ b/solution.py
@@ -149,11 +149,12 @@
     )
 
 
-def shift_rows(shifted_ref, cos_ref, sin_ref, real, imag, offset, total):
+def shift_rows(shifted_ref, cos_ref, sin_ref, real, imag, at):
     n_proj, wide = real.shape
-    for t in range(cos_ref.shape[0]):
+    shifts = cos_ref.shape[0]
+    for t in range(shifts):
         cos_part, sin_part = cos_ref[t : t + 1, :], sin_ref[t : t + 1, :]
-        rows = slice(t * total + offset * n_proj, t * total + (offset + 1) * n_proj)
+        rows = slice((at * shifts + t) * n_proj, (at * shifts + t + 1) * n_proj)
         shifted_ref[rows, :wide] = (cos_part * real + sin_part * imag).astype(BF16)
         shifted_ref[rows, wide:] = (cos_part * imag - sin_part * real).astype(BF16)
 
@@ -169,112 +170,143 @@
     )
 
 
-def shift_kernel(offsets, total, cos_ref, sin_ref, square_ref, *rest):
-    banks, (shifted_ref, norm_ref) = rest[: len(offsets)], rest[len(offsets) :]
+def shift_bank(banks, shifted_ref, cos_ref, sin_ref, square_ref, n_proj):
     powers = []
-    for bank, offs in zip(banks, offsets):
-        n_proj = bank.shape[0] // (2 * len(offs))
-        for n, offset in enumerate(offs):
+    for bank in banks:
+        for n in range(bank.shape[0] // (2 * n_proj)):
             both = bank[2 * n_proj * n : 2 * n_proj * (n + 1)].astype(F32)
             real, imag = both[:n_proj], both[n_proj:]
-            shift_rows(shifted_ref, cos_ref, sin_ref, real, imag, offset, total)
+            shift_rows(shifted_ref, cos_ref, sin_ref, real, imag, len(powers))
             powers.append(real * real + imag * imag)
-    norm_ref[...] = norm_of(square_ref, powers)
-
-
-def score_kernel(
-    half, offsets, n_parts, bits, n_part, n_proj, length, subsets, shifted_in, cos_ref, sin_ref, square_ref, norm_ref, *rest
+    return norm_of(square_ref, powers)
+
+
+def shift_kernel(n_proj, cos_ref, sin_ref, square_ref, *rest):
+    *banks, shifted_ref, norm_ref = rest
+    norm_ref[...] = shift_bank(banks, shifted_ref, cos_ref, sin_ref, square_ref, n_proj)
+
+
+def join_kernel(n_parts, *refs):
+    parts, out_ref = refs[:n_parts], refs[-1]
+    at = 0
+    for part in parts:
+        out_ref[at : at + part.shape[0], :] = part[...]
+        at += part.shape[0]
+
+
+def added_rows(extra, table, banks, n_proj, length, subsets):
+    ids_at = length // 128 * 128
+    ids = []
+    for bank in banks:
+        for n in range(bank.shape[0] // (2 * n_proj)):
+            rows = bank[2 * n_proj * n : 2 * n_proj * (n + 1), ids_at : ids_at + 128].astype(F32)
+            ids.append(rows[:n_proj])
+    ids = jnp.concatenate(ids, axis=0)[:, length - ids_at : length - ids_at + 1]
+    count, classes_count = extra.shape[0], table.shape[0]
+    class_col = lax.broadcasted_iota(jnp.int32, (count, classes_count), 1).astype(F32)
+    onehot = (class_col == extra[:, subsets : subsets + 1]).astype(F32)
+    norm = jnp.dot(onehot, table, precision=HIGHEST, preferred_element_type=F32)
+    subset_col = lax.broadcasted_iota(jnp.int32, (ids.shape[0], subsets), 1).astype(F32)
+    subset_hot = (subset_col == ids).astype(F32).astype(BF16)
+    prior = lax.dot_general(
+        extra[:, :subsets].astype(BF16), subset_hot, NT_DIMS, preferred_element_type=F32
+    )
+    return prior - 0.5 * norm
+
+
+def score_rows(weighted, shifted, added, n_proj):
+    cross = lax.dot_general(weighted, shifted, NT_DIMS, preferred_element_type=F32)
+    pieces = added.shape[1] // n_proj
+    width = cross.shape[1] // pieces
+    rows = []
+    for n in range(pieces):
+        rows += [cross[:, n * width : (n + 1) * width], added[:, n * n_proj : (n + 1) * n_proj]]
+    return jnp.concatenate(rows, axis=1)
+
+
+def early_kernel(
+    n_parts, ng, half_weight, weights, n_part, n_proj, length, subsets, shifted_ref, norm_ref, *rest
 ):
-    n_bank = len(offsets)
-    banks, parts, outs = rest[:n_bank], rest[n_bank : n_bank + n_parts], rest[n_bank + n_parts :][:2]
-    shifted_ref = rest[n_bank + n_parts + 2]
+    parts, (*banks, weighted_ref, extra_ref, rows_ref) = rest[:n_parts], rest[n_parts:]
     g = lax.axis_index("grp")
-    ng = 1 << len(bits)
-    total, wide = half * n_proj, cos_ref.shape[1]
-    shifts = cos_ref.shape[0]
-    classes_count = square_ref.shape[0] // 2
-
-    powers = []
-    for n, offset in enumerate(offsets[-1]):
-        both = banks[-1][2 * n_proj * n : 2 * n_proj * (n + 1)].astype(F32)
-        real, imag = both[:n_proj], both[n_proj:]
-        shift_rows(shifted_ref, cos_ref, sin_ref, real, imag, offset, total)
-        powers.append(real * real + imag * imag)
-    norm_last = norm_of(square_ref, powers)
+    wide = weighted_ref.shape[1] // 2
 
     held = jnp.concatenate([part[...] for part in parts], axis=0)
     count = 2 * ng * n_part
     out_row = lax.broadcasted_iota(jnp.int32, (2 * count, held.shape[0]), 0)
     in_row = lax.broadcasted_iota(jnp.int32, (2 * count, held.shape[0]), 1)
     kind, rest_row = out_row // count, out_row % count
-    source, rest_row = rest_row // (ng * n_part), rest_row % (ng * n_part)
+    source, rest_row = rest_row // (ng * n_part) * half_weight, rest_row % (ng * n_part)
     away, i = rest_row // n_part ^ g, rest_row % n_part
-    for n, bit in enumerate(bits):
-        source += jnp.where(away & bit != 0, 2 << n, 0)
+    for bit, weight in weights:
+        source += jnp.where(away & bit != 0, weight, 0)
     pick = (in_row == source * (2 * n_part) + kind * n_part + i).astype(F32).astype(BF16)
     ordered = jnp.dot(pick, held, preferred_element_type=F32)
-    weighted = jnp.concatenate([ordered[:count, :wide], ordered[count:, :wide]], axis=1).astype(BF16)
-    prior_rows = ordered[:count, wide : wide + subsets].astype(BF16)
-    class_rows = ordered[:count, wide + subsets : wide + subsets + 1]
-    cross = lax.dot_general(weighted, shifted_ref[...], NT_DIMS, preferred_element_type=F32)
-
-    order = [offset for offs in offsets for offset in offs]
-    first = len(order) - len(offsets[-1])
-    norms, ids = {}, {}
-    ids_at = length // 128 * 128
-    for n, offset in enumerate(order):
-        table, m = (norm_ref, n) if n < first else (norm_last, n - first)
-        norms[offset] = table[:, m * n_proj : (m + 1) * n_proj]
-    for bank, offs in zip(banks, offsets):
-        for n, offset in enumerate(offs):
-            rows = bank[2 * n_proj * n : 2 * n_proj * (n + 1), ids_at : ids_at + 128].astype(F32)
-            ids[offset] = rows[:n_proj]
-    table = jnp.concatenate([norms[offset] for offset in range(half)], axis=1)
-    id_rows = jnp.concatenate([ids[offset] for offset in range(half)], axis=0)
-    id_rows = id_rows[:, length - ids_at : length - ids_at + 1]
-    class_col = lax.broadcasted_iota(jnp.int32, (count, classes_count), 1).astype(F32)
-    onehot = (class_col == class_rows).astype(F32)
-    norm = jnp.dot(onehot, table, precision=HIGHEST, preferred_element_type=F32)
-    subset_col = lax.broadcasted_iota(jnp.int32, (total, subsets), 1).astype(F32)
-    subset_hot = (subset_col == id_rows).astype(F32).astype(BF16)
-    prior = lax.dot_general(prior_rows, subset_hot, NT_DIMS, preferred_element_type=F32)
-    result = cross + jnp.concatenate([prior - 0.5 * norm] * shifts, axis=1)
-    dest = ng * n_part
-    lanes = outs[0].shape[1]
-    for s in range(2):
-        rows = result[s * dest : (s + 1) * dest]
-        if rows.shape[1] < lanes:
-            zeros = jnp.zeros((dest, lanes - rows.shape[1]), F32)
-            rows = jnp.concatenate([rows, zeros], axis=1)
-        outs[s][...] = rows
-
-
-def place_kernel(half, n_proj, keep_ref, recv_ref, out_ref):
+    weighted_ref[:, :wide] = ordered[:count, :wide].astype(BF16)
+    weighted_ref[:, wide:] = ordered[count:, :wide].astype(BF16)
+    extra = ordered[:count, wide:]
+    extra_ref[...] = extra
+    added = added_rows(extra, norm_ref[...], banks, n_proj, length, subsets)
+    rows_ref[...] = score_rows(weighted_ref[...], shifted_ref[...], added, n_proj)
+
+
+def final_kernel(
+    n_proj, length, subsets, weighted_ref, extra_ref, rows_ref, cos_ref, sin_ref, square_ref, last_ref, *rest
+):
+    *outs, shifted_ref = rest
+    table = shift_bank([last_ref], shifted_ref, cos_ref, sin_ref, square_ref, n_proj)
+    added = added_rows(extra_ref[...], table, [last_ref], n_proj, length, subsets)
+    rows = score_rows(weighted_ref[...], shifted_ref[...], added, n_proj)
+    rows = jnp.concatenate([rows_ref[...], rows], axis=1)
+    dest, lanes = outs[0].shape
+    if rows.shape[1] < lanes:
+        zeros = jnp.zeros((rows.shape[0], lanes - rows.shape[1]), F32)
+        rows = jnp.concatenate([rows, zeros], axis=1)
+    for s, out in enumerate(outs):
+        out[...] = rows[s * dest : (s + 1) * dest]
+
+
+def place_kernel(half, n_proj, order, keep_ref, recv_ref, out_ref):
     blk = lax.axis_index("blk")
     first = blk < half
     low = jnp.where(first, keep_ref[...], recv_ref[...])
     high = jnp.where(first, recv_ref[...], keep_ref[...])
-    lanes = low.shape[1]
-    lane = lax.broadcasted_iota(jnp.int32, low.shape, 1)
+    shifts = out_ref.shape[0]
+    width = (shifts + 1) * n_proj
+
+    def by_shift(values):
+        found = {offset: values[:, n * width : (n + 1) * width] for n, offset in enumerate(order)}
+        lined = []
+        for t in range(shifts + 1):
+            span = slice(t * n_proj, (t + 1) * n_proj)
+            lined += [found[offset][:, span] for offset in range(half)]
+        return jnp.concatenate(lined, axis=1)
 
     def exchanged(values):
+        total = (shifts + 1) * half * n_proj
+        lanes = 128 * -(-total // 128)
+        if lanes > total:
+            zeros = jnp.zeros((values.shape[0], lanes - total), F32)
+            values = jnp.concatenate([values, zeros], axis=1)
+        lane = lax.broadcasted_iota(jnp.int32, values.shape, 1)
         bit = 1
         while bit < half:
             step = bit * n_proj
-            upper = (lane & step) != 0
             other = jnp.where(
-                upper, pltpu.roll(values, step, 1), pltpu.roll(values, lanes - step, 1)
+                (lane & step) != 0, pltpu.roll(values, step, 1), pltpu.roll(values, lanes - step, 1)
             )
             values = jnp.where((blk & bit) != 0, other, values)
             bit *= 2
         return values
 
-    low, high = exchanged(low), exchanged(high)
-    shifts, _, width = out_ref.shape
-    width = width // 2
+    low, high = exchanged(by_shift(low)), exchanged(by_shift(high))
+    span = half * n_proj
+    lined = [
+        jnp.concatenate([low[:, t * span : (t + 1) * span], high[:, t * span : (t + 1) * span]], axis=1)
+        for t in range(shifts + 1)
+    ]
     for t in range(shifts):
-        span = slice(t * width, (t + 1) * width)
-        out_ref[t] = jnp.concatenate([low[:, span], high[:, span]], axis=1)
+        out_ref[t] = lined[t] + lined[shifts]
 
 
 def per_device(
@@ -343,27 +375,30 @@
         size = lax.axis_size(axis)
         return lax.ppermute(value, axis, [(i, i ^ bit) for i in range(size)])
 
+    def swap_both(value, blk_bit, grp_bit):
+        pairs = [
+            (g * nb + b, (g ^ grp_bit) * nb + (b ^ blk_bit)) for g in range(ng) for b in range(nb)
+        ]
+        return lax.ppermute(value, ("grp", "blk"), pairs)
+
     def joined(pieces):
         return pieces[0] if len(pieces) == 1 else jnp.concatenate(pieces, axis=0)
 
-    def doubled(pieces, axis, bits):
-        for bit in bits:
-            whole = joined(pieces)
-            pieces = [whole, swap(whole, axis, bit)]
-        return pieces
-
-    grp_bits = [1 << n for n in range(ng.bit_length() - 2, -1, -1)]
-    parts = doubled([part, swap(part, "blk", half)], "grp", grp_bits)
-
-    near = swap(bank, "blk", 1)
     planes, far_offsets = [bank], [0]
     for n in range(half.bit_length() - 2, 0, -1):
         planes.append(swap(joined(planes), "blk", 1 << n))
         far_offsets += [offset ^ (1 << n) for offset in far_offsets]
     far, far_offsets = joined(planes[1:]), far_offsets[1:]
-    last = swap(far, "blk", 1)
-    banks = [bank, near, far, last]
-    offsets = [[0], [1], far_offsets, [offset ^ 1 for offset in far_offsets]]
+    near = swap(bank, "blk", 1)
+
+    weights, weight = [], 1
+    for n in range(ng.bit_length() - 2, 1, -1):
+        part = joined([part, swap(part, "grp", 1 << n)])
+        weights.append((1 << n, weight))
+        weight *= 2
+    half_weight = weight
+    weights += [(2, 2 * weight), (1, 4 * weight)]
+    parts = [part, swap(part, "blk", half), swap(part, "grp", 2), swap_both(part, half, 2)]
 
     cos_part, sin_part, square = pl.pallas_call(
         table_kernel,
@@ -379,13 +414,26 @@
         name="tables",
     )(curves, noise, angle)
 
+    any_space = pl.BlockSpec(memory_space=pl.ANY)
+    part = pl.pallas_call(
+        functools.partial(join_kernel, len(parts)),
+        out_shape=vmem_out((sum(piece.shape[0] for piece in parts), part.shape[1]), BF16),
+        in_specs=[_vmem()] * len(parts) + [any_space] * 3,
+        out_specs=_vmem(),
+        compiler_params=_params(4),
+        name="join",
+    )(*parts, near, far, cos_part)
+    parts = [part, swap(part, "grp", 1)]
+    last = swap(far, "blk", 1)
+    order = [0, 1] + far_offsets + [offset ^ 1 for offset in far_offsets]
+
     count = 2 * ng * n_part
-    total = half * n_proj
-    early = total - len(far_offsets) * n_proj
+    early = (2 + len(far_offsets)) * n_proj
+    late = len(far_offsets) * n_proj
     shifted, norm = pl.pallas_call(
-        functools.partial(shift_kernel, offsets[:3], total),
+        functools.partial(shift_kernel, n_proj),
         out_shape=[
-            vmem_out((shifts * total, 2 * wide), BF16),
+            vmem_out((shifts * early, 2 * wide), BF16),
             vmem_out((classes_count, early), F32),
         ],
         in_specs=[_vmem()] * 6,
@@ -395,26 +443,40 @@
             flops=6 * early * shifts * wide, bytes_accessed=4_000_000, transcendentals=0
         ),
         name="shift",
-    )(cos_part, sin_part, square, *banks[:3])
-    lanes = 128 * -(-shifts * total // 128)
-    keep, give, _ = pl.pallas_call(
+    )(cos_part, sin_part, square, bank, near, far)
+    weighted, extra_rows, rows = pl.pallas_call(
         functools.partial(
-            score_kernel, half, offsets, len(parts), grp_bits, n_part, n_proj, length, subsets
+            early_kernel, len(parts), ng, half_weight, weights, n_part, n_proj, length, subsets
         ),
-        out_shape=[vmem_out((ng * n_part, lanes), F32)] * 2
-        + [vmem_out((shifts * total, 2 * wide), BF16)],
-        in_specs=[_vmem()] * (5 + len(banks) + len(parts)),
+        out_shape=[
+            vmem_out((count, 2 * wide), BF16),
+            vmem_out((count, extra), F32),
+            vmem_out((count, (shifts + 1) * early), F32),
+        ],
+        in_specs=[_vmem()] * (5 + len(parts)),
         out_specs=[_vmem()] * 3,
-        input_output_aliases={0: 2},
         compiler_params=_params(8),
         cost_estimate=pl.CostEstimate(
-            flops=4 * count * total * shifts * wide, bytes_accessed=4_000_000, transcendentals=0
+            flops=4 * count * early * shifts * wide, bytes_accessed=4_000_000, transcendentals=0
         ),
-        name="score",
-    )(shifted, cos_part, sin_part, square, norm, *banks, *parts)
+        name="early",
+    )(shifted, norm, *parts, bank, near, far)
+    lanes = 128 * -(-(shifts + 1) * half * n_proj // 128)
+    keep, give = pl.pallas_call(
+        functools.partial(final_kernel, n_proj, length, subsets),
+        out_shape=[vmem_out((ng * n_part, lanes), F32)] * 2,
+        in_specs=[_vmem()] * 7,
+        out_specs=[_vmem()] * 2,
+        scratch_shapes=[pltpu.VMEM((shifts * late, 2 * wide), BF16)],
+        compiler_params=_params(24),
+        cost_estimate=pl.CostEstimate(
+            flops=4 * count * late * shifts * wide, bytes_accessed=4_000_000, transcendentals=0
+        ),
+        name="final",
+    )(weighted, extra_rows, rows, cos_part, sin_part, square, last)
     scores = pl.pallas_call(
-        functools.partial(place_kernel, half, n_proj),
-        out_shape=shape((shifts, ng * n_part, 2 * total), F32),
+        functools.partial(place_kernel, half, n_proj, order),
+        out_shape=shape((shifts, ng * n_part, nb * n_proj), F32),
         in_specs=[_vmem()] * 2,
         out_specs=_vmem(),
         compiler_params=_params(4),

time: 29.2 us -> 29.7 us (1.017)
  starting transfers between devices: 13.2 us -> 9.74 us
  waiting for transfers between devices: 8.72 us -> 11.8 us
  Pallas kernels: 6.99 us -> 7.98 us
    ppermute x7, starting transfers between devices: 13.2 us -> 9.43 us  [swap(): return lax.ppermute(value, axis, [(i, i ^ bit) for i in range(size)])]
    ppermute x0 -> x1, waiting for transfers between devices: none -> 3.55 us  [swap_both(): return lax.ppermute(value, ('grp', 'blk'), pairs)]
    pallas_call x3 -> x5, Pallas kernels: 4.83 us -> 5.82 us  [the longest x1 1.69 us: per_device(): pl.pallas_call(functools.partial(shift_kernel, n_proj), out_shape=[vmem_o...]
    ppermute x7, waiting for transfers between devices: 8.72 us -> 8.22 us  [swap(): return lax.ppermute(value, axis, [(i, i ^ bit) for i in range(size)])]
    ppermute x0 -> x1, starting transfers between devices: none -> 0.31 us  [swap_both(): return lax.ppermute(value, ('grp', 'blk'), pairs)]
  transfers between devices with their start and end apart: 7 -> 8, of which waited for: 6 -> 5; matrix products, arithmetic and copies ran while one was open for 0% -> 0% of each run, Pallas kernels for 8% -> 13%
where the time goes in v7:
time: 29.7 us; the launch traced here: 29.5 us
  waiting for transfers between devices  11.8 us (40%)
  starting transfers between devices  9.74 us (33%)
  Pallas kernels  7.98 us (27%)
    ppermute x7, starting transfers between devices, swap(): return lax.ppermute(value, axis, [(i, i ^ bit) for i in range(size)])  9.43 us
    ppermute x7, waiting for transfers between devices, swap(): return lax.ppermute(value, axis, [(i, i ^ bit) for i in range(size)])  8.22 us
    ppermute x1, waiting for transfers between devices, swap_both(): return lax.ppermute(value, ('grp', 'blk'), pairs)  3.55 us
    pallas_call x1, Pallas kernels, per_device(): pl.pallas_call(functools.partial(shift_kernel, n_proj), out_shape=[vmem_o...  1.69 us
    pallas_call x1, Pallas kernels, per_device(): pl.pallas_call(functools.partial(final_kernel, n_proj, length, subsets),...  1.62 us
    pallas_call x1, Pallas kernels, per_device(): pl.pallas_call(pack_kernel, out_shape=[vmem_out((2 * n_proj, wide), BF16)...  1.58 us
    pallas_call x1, Pallas kernels, per_device(): pl.pallas_call(functools.partial(early_kernel, len(parts), ng, half_weigh...  1.49 us
    pallas_call x1, Pallas kernels, per_device(): pl.pallas_call(functools.partial(place_kernel, half, n_proj, order), out_...  0.99 us
  transfers between devices with their start and end apart: 8, of which 5 were waited for; matrix products, arithmetic and copies ran while one was open for 0% of the time, Pallas kernels for 13%

profile of v7, /device:TPU:0, one launch (start us, length us, event | category | flops | bytes accessed | tf_op | source)
XLA Modules:
  0.0 29.5 jit_solution(17843734311945597216)
XLA Ops:
  0.0 1.6 %pack.1 = (bf16[16,4096]{1,0:T(8,128)(2,1)S(1)}, bf16[4,4352]{1,0:T(4,128)(2,1)S(1)}, f32[64,4000]{1,0:T(8,128)S(1)}, f32[1,4000]{1,0:T(1,128)S(1)}, f32[9,4000]{1,0:T(8,128)S(1)}) custom-call(s32[2]{0:T(128)} %class_hbm.1, s32[8]{0:T(128)} %subset_hbm.1, bf16[2,2,4000]{2,1,0:T(2,128)(2,1)} %particles_hbm.1, bf16[2,192]{1,0:T(2,128)(2,1)} %prior_hbm.1, ...), custom_call_target="tpu_custom_call" | custom-call | tf_op jit(solution)/shard_map/pack/pallas_call | solution.py:349
  1.6 3.1 %collective-permute-start.1 = (bf16[16,4096]{1,0:T(8,128)(2,1)S(1)}, bf16[16,4096]{1,0:T(8,128)(2,1)S(1)}, u32[]{:S(2)}, u32[]{:S(2)}) collective-permute-start(bf16[16,4096]{1,0:T(8,128)(2,1)S(1)} %get-tuple-element.26.rest_0_.rest_2_), channel_id=1, source_target_pairs={{0,2},{1,3},{2,0},{3,1},{4,6},{5,7},{6,4},{7,5},{8,10},{9,11},{10,... | collective-permute-start | bytes 393224 | tf_op jit(solution)/shard_map/ppermute | solution.py:376
  4.7 1.5 %collective-permute-start = (bf16[16,4096]{1,0:T(8,128)(2,1)S(1)}, bf16[16,4096]{1,0:T(8,128)(2,1)S(1)}, u32[]{:S(2)}, u32[]{:S(2)}) collective-permute-start(bf16[16,4096]{1,0:T(8,128)(2,1)S(1)} %get-tuple-element.26.rest_0_.rest_2_), channel_id=1, source_target_pairs={{0,1},{1,0},{2,3},{3,2},{4,5},{5,4},{6,7},{7,6},{8,9},{9,8},{10,11... | collective-permute-start | bytes 393224 | tf_op jit(solution)/shard_map/ppermute | solution.py:376
  6.2 2.6 %collective-permute-start.2 = (bf16[4,4352]{1,0:T(4,128)(2,1)S(1)}, bf16[4,4352]{1,0:T(4,128)(2,1)S(1)}, u32[]{:S(2)}, u32[]{:S(2)}) collective-permute-start(bf16[4,4352]{1,0:T(4,128)(2,1)S(1)} %get-tuple-element.29.refs_0_), channel_id=1, source_target_pairs={{0,4},{1,5},{2,6},{3,7},{4,0},{5,1},{6,2},{7,3},{8,12},{9,13},{10,... | collective-permute-start | bytes 104456 | tf_op jit(solution)/shard_map/ppermute | solution.py:376
  8.8 1.5 %collective-permute-start.3 = (bf16[4,4352]{1,0:T(4,128)(2,1)S(1)}, bf16[4,4352]{1,0:T(4,128)(2,1)S(1)}, u32[]{:S(2)}, u32[]{:S(2)}) collective-permute-start(bf16[4,4352]{1,0:T(4,128)(2,1)S(1)} %get-tuple-element.29.refs_0_), channel_id=1, source_target_pairs={{0,16},{8,24},{16,0},{24,8},{1,17},{9,25},{17,1},{25,9},{2,18},{10... | collective-permute-start | bytes 104456 | tf_op jit(solution)/shard_map/ppermute | solution.py:376
  10.3 0.3 %collective-permute-start.4 = (bf16[4,4352]{1,0:T(4,128)(2,1)S(1)}, bf16[4,4352]{1,0:T(4,128)(2,1)S(1)}, u32[]{:S(2)}, u32[]{:S(2)}) collective-permute-start(bf16[4,4352]{1,0:T(4,128)(2,1)S(1)} %get-tuple-element.29.refs_0_), channel_id=1, source_target_pairs={{0,20},{1,21},{2,22},{3,23},{4,16},{5,17},{6,18},{7,19},{8,28},{9,... | collective-permute-start | bytes 104456 | tf_op jit(solution)/shard_map/ppermute | solution.py:382
  10.6 0.6 %tables.1 = (f32[9,4096]{1,0:T(8,128)S(1)}, f32[9,4096]{1,0:T(8,128)S(1)}, bf16[128,4096]{1,0:T(8,128)(2,1)S(1)}) custom-call(f32[64,4000]{1,0:T(8,128)S(1)} %get-tuple-element.20.curves_ref, f32[1,4000]{1,0:T(1,128)S(1)} %get-tuple-element.21.noise_ref, f32[9,4000]{1,0:T(8,128)S(1)} %get-tuple-element.22.angle_ref), custom_call_target="tpu_custom_call" | custom-call | flops 4000000 | bytes 2000000 | tf_op jit(solution)/shard_map/tables/pallas_call | solution.py:403
  11.2 0.2 collective-permute-done.2.refs_1_
  11.4 1.3 %collective-permute-done.3.refs_2_ = bf16[4,4352]{1,0:T(4,128)(2,1)S(1)} collective-permute-done((bf16[4,4352]{1,0:T(4,128)(2,1)S(1)}, bf16[4,4352]{1,0:T(4,128)(2,1)S(1)}, u32[]{:S(2)}, u32[]{:S(2)}) %collective-permute-start.3) | collective-permute-done | bytes 34848 | tf_op jit(solution)/shard_map/ppermute | solution.py:376
  12.7 3.5 %collective-permute-done.4.refs_3_ = bf16[4,4352]{1,0:T(4,128)(2,1)S(1)} collective-permute-done((bf16[4,4352]{1,0:T(4,128)(2,1)S(1)}, bf16[4,4352]{1,0:T(4,128)(2,1)S(1)}, u32[]{:S(2)}, u32[]{:S(2)}) %collective-permute-start.4) | collective-permute-done | bytes 34848 | tf_op jit(solution)/shard_map/ppermute | solution.py:382
  16.3 0.0 collective-permute-done.1.rest_2_.refs_5_.rest_4_
  16.3 0.0 collective-permute-done.rest_1_.refs_4_.rest_3_
  16.3 0.1 collective-permute-start.5
  16.4 0.6 %collective-permute-start.6 = (bf16[16,4096]{1,0:T(8,128)(2,1)S(1)}, bf16[16,4096]{1,0:T(8,128)(2,1)S(1)}, u32[]{:S(2)}, u32[]{:S(2)}) collective-permute-start(bf16[16,4096]{1,0:T(8,128)(2,1)S(1)} %collective-permute-done.1.rest_2_.refs_5_.rest_4_), channel_id=1, source_target_pairs={{0,1},{1,0},{2,3},{3,2},{4,5},{5,4},{6,7},{7,6},{8,9},{9,8},{10,11... | collective-permute-start | bytes 393224 | tf_op jit(solution)/shard_map/ppermute | solution.py:376
  17.0 1.7 %shift.1 = (bf16[216,8192]{1,0:T(8,128)(2,1)S(1)}, f32[64,24]{1,0:T(8,128)S(1)}) custom-call(f32[9,4096]{1,0:T(8,128)S(1)} %get-tuple-element.23.cos_ref.refs_6_, f32[9,4096]{1,0:T(8,128)S(1)} %get-tuple-element.24.sin_ref, bf16[128,4096]{1,0:T(8,128)(2,1)S(1)} %get-tuple-element.25.square_ref, bf16[16,4096]{1,0:T(8,128)(2,1)S(1)} %get-tuple-element.26.rest_0_.rest_2_, ...), custom_call_target="tpu_custom_call" | custom-call | flops 5308416 | bytes 4000000 | tf_op jit(solution)/shard_map/shift/pallas_call | solution.py:433
  18.7 0.0 collective-permute-done.5.rest_1_
  18.7 1.5 %early.1 = (bf16[16,8192]{1,0:T(8,128)(2,1)S(1)}, f32[16,256]{1,0:T(8,128)S(1)}, f32[16,240]{1,0:T(8,128)S(1)}) custom-call(bf16[216,8192]{1,0:T(8,128)(2,1)S(1)} %get-tuple-element.27.shifted_ref, f32[64,24]{1,0:T(8,128)S(1)} %get-tuple-element.28.norm_ref, bf16[16,4352]{1,0:T(8,128)(2,1)S(1)} %join.1.rest_0_, ...), custom_call_target="tpu_custom_call" | custom-call | flops 56623104 | bytes 4000000 | tf_op jit(solution)/shard_map/early/pallas_call | solution.py:447
  20.2 2.2 %collective-permute-done.6.last_ref = bf16[16,4096]{1,0:T(8,128)(2,1)S(1)} collective-permute-done((bf16[16,4096]{1,0:T(8,128)(2,1)S(1)}, bf16[16,4096]{1,0:T(8,128)(2,1)S(1)}, u32[]{:S(2)}, u32[]{:S(2)}) %collective-permute-start.6) | collective-permute-done | bytes 131104 | tf_op jit(solution)/shard_map/ppermute | solution.py:376
  22.3 1.6 %final.1 = (f32[8,384]{1,0:T(8,128)S(1)}, f32[8,384]{1,0:T(8,128)S(1)}) custom-call(bf16[16,8192]{1,0:T(8,128)(2,1)S(1)} %get-tuple-element.30.weighted_ref, f32[16,256]{1,0:T(8,128)S(1)} %get-tuple-element.31.extra_ref, f32[16,240]{1,0:T(8,128)S(1)} %get-tuple-element.32.rows_ref, f32[9,4096]{1,0:T(8,128)S(1)} %get-tuple-element.23.cos_ref.refs_6_, ...), custom_call_target="tpu_custom_call" | custom-call | flops 18874368 | bytes 4000000 | tf_op jit(solution)/shard_map/final/pallas_call | solution.py:465
  23.9 0.1 collective-permute-start.7
  24.0 4.5 %collective-permute-done.7.recv_ref = f32[8,384]{1,0:T(8,128)S(1)} collective-permute-done((f32[8,384]{1,0:T(8,128)S(1)}, f32[8,384]{1,0:T(8,128)S(1)}, u32[]{:S(2)}, u32[]{:S(2)}) %collective-permute-start.7) | collective-permute-done | bytes 12320 | tf_op jit(solution)/shard_map/ppermute | solution.py:376
  28.5 1.0 %place.1 = f32[9,8,64]{2,1,0:T(8,128)} custom-call(f32[8,384]{1,0:T(8,128)S(1)} %get-tuple-element.33.keep_ref, f32[8,384]{1,0:T(8,128)S(1)} %collective-permute-done.7.recv_ref), custom_call_target="tpu_custom_call" | custom-call | tf_op jit(solution)/shard_map/place/pallas_call | solution.py:477
  (1 shorter events, 0.0 us)
Async XLA Ops:
  1.6 14.7 %collective-permute-start.1 = (bf16[16,4096]{1,0:T(8,128)(2,1)S(1)}, bf16[16,4096]{1,0:T(8,128)(2,1)S(1)}, u32[]{:S(2)}, u32[]{:S(2)}) collective-permute-start(bf16[16,4096]{1,0:T(8,128)(2,1)S(1)} %get-tuple-element.26.rest_0_.rest_2_), channel_id=1, source_target_pairs={{0,2},{1,3},{2,0},{3,1},{4,6},{5,7},{6,4},{7,5},{8,10},{9,11},{10,... | collective-permute-start | bytes 393224 | tf_op jit(solution)/shard_map/ppermute | solution.py:376
  4.7 11.6 %collective-permute-start = (bf16[16,4096]{1,0:T(8,128)(2,1)S(1)}, bf16[16,4096]{1,0:T(8,128)(2,1)S(1)}, u32[]{:S(2)}, u32[]{:S(2)}) collective-permute-start(bf16[16,4096]{1,0:T(8,128)(2,1)S(1)} %get-tuple-element.26.rest_0_.rest_2_), channel_id=1, source_target_pairs={{0,1},{1,0},{2,3},{3,2},{4,5},{5,4},{6,7},{7,6},{8,9},{9,8},{10,11... | collective-permute-start | bytes 393224 | tf_op jit(solution)/shard_map/ppermute | solution.py:376
  6.2 5.2 %collective-permute-start.2 = (bf16[4,4352]{1,0:T(4,128)(2,1)S(1)}, bf16[4,4352]{1,0:T(4,128)(2,1)S(1)}, u32[]{:S(2)}, u32[]{:S(2)}) collective-permute-start(bf16[4,4352]{1,0:T(4,128)(2,1)S(1)} %get-tuple-element.29.refs_0_), channel_id=1, source_target_pairs={{0,4},{1,5},{2,6},{3,7},{4,0},{5,1},{6,2},{7,3},{8,12},{9,13},{10,... | collective-permute-start | bytes 104456 | tf_op jit(solution)/shard_map/ppermute | solution.py:376
  8.8 3.9 %collective-permute-start.3 = (bf16[4,4352]{1,0:T(4,128)(2,1)S(1)}, bf16[4,4352]{1,0:T(4,128)(2,1)S(1)}, u32[]{:S(2)}, u32[]{:S(2)}) collective-permute-start(bf16[4,4352]{1,0:T(4,128)(2,1)S(1)} %get-tuple-element.29.refs_0_), channel_id=1, source_target_pairs={{0,16},{8,24},{16,0},{24,8},{1,17},{9,25},{17,1},{25,9},{2,18},{10... | collective-permute-start | bytes 104456 | tf_op jit(solution)/shard_map/ppermute | solution.py:376
  10.3 6.0 %collective-permute-start.4 = (bf16[4,4352]{1,0:T(4,128)(2,1)S(1)}, bf16[4,4352]{1,0:T(4,128)(2,1)S(1)}, u32[]{:S(2)}, u32[]{:S(2)}) collective-permute-start(bf16[4,4352]{1,0:T(4,128)(2,1)S(1)} %get-tuple-element.29.refs_0_), channel_id=1, source_target_pairs={{0,20},{1,21},{2,22},{3,23},{4,16},{5,17},{6,18},{7,19},{8,28},{9,... | collective-permute-start | bytes 104456 | tf_op jit(solution)/shard_map/ppermute | solution.py:382
  16.3 2.3 %collective-permute-start.5 = (bf16[16,4352]{1,0:T(8,128)(2,1)S(1)}, bf16[16,4352]{1,0:T(8,128)(2,1)S(1)}, u32[]{:S(2)}, u32[]{:S(2)}) collective-permute-start(bf16[16,4352]{1,0:T(8,128)(2,1)S(1)} %join.1.rest_0_), channel_id=1, source_target_pairs={{0,8},{8,0},{16,24},{24,16},{1,9},{9,1},{17,25},{25,17},{2,10},{10... | collective-permute-start | bytes 417800 | tf_op jit(solution)/shard_map/ppermute | solution.py:376
  16.4 5.9 %collective-permute-start.6 = (bf16[16,4096]{1,0:T(8,128)(2,1)S(1)}, bf16[16,4096]{1,0:T(8,128)(2,1)S(1)}, u32[]{:S(2)}, u32[]{:S(2)}) collective-permute-start(bf16[16,4096]{1,0:T(8,128)(2,1)S(1)} %collective-permute-done.1.rest_2_.refs_5_.rest_4_), channel_id=1, source_target_pairs={{0,1},{1,0},{2,3},{3,2},{4,5},{5,4},{6,7},{7,6},{8,9},{9,8},{10,11... | collective-permute-start | bytes 393224 | tf_op jit(solution)/shard_map/ppermute | solution.py:376
  23.9 4.6 %collective-permute-start.7 = (f32[8,384]{1,0:T(8,128)S(1)}, f32[8,384]{1,0:T(8,128)S(1)}, u32[]{:S(2)}, u32[]{:S(2)}) collective-permute-start(f32[8,384]{1,0:T(8,128)S(1)} %get-tuple-element.34), channel_id=1, source_target_pairs={{0,4},{1,5},{2,6},{3,7},{4,0},{5,1},{6,2},{7,3},{8,12},{9,13},{10,... | collective-permute-start | bytes 36872 | tf_op jit(solution)/shard_map/ppermute | solution.py:376

commit v8 on v7

--- a/solution.py
+++ b/solution.py
@@ -186,14 +186,6 @@
     norm_ref[...] = shift_bank(banks, shifted_ref, cos_ref, sin_ref, square_ref, n_proj)
 
 
-def join_kernel(n_parts, *refs):
-    parts, out_ref = refs[:n_parts], refs[-1]
-    at = 0
-    for part in parts:
-        out_ref[at : at + part.shape[0], :] = part[...]
-        at += part.shape[0]
-
-
 def added_rows(extra, table, banks, n_proj, length, subsets):
     ids_at = length // 128 * 128
     ids = []
@@ -225,7 +217,7 @@
 
 
 def early_kernel(
-    n_parts, ng, half_weight, weights, n_part, n_proj, length, subsets, shifted_ref, norm_ref, *rest
+    n_parts, ng, weights, n_part, n_proj, length, subsets, shifted_ref, norm_ref, *rest
 ):
     parts, (*banks, weighted_ref, extra_ref, rows_ref) = rest[:n_parts], rest[n_parts:]
     g = lax.axis_index("grp")
@@ -236,7 +228,7 @@
     out_row = lax.broadcasted_iota(jnp.int32, (2 * count, held.shape[0]), 0)
     in_row = lax.broadcasted_iota(jnp.int32, (2 * count, held.shape[0]), 1)
     kind, rest_row = out_row // count, out_row % count
-    source, rest_row = rest_row // (ng * n_part) * half_weight, rest_row % (ng * n_part)
+    source, rest_row = rest_row // (ng * n_part), rest_row % (ng * n_part)
     away, i = rest_row // n_part ^ g, rest_row % n_part
     for bit, weight in weights:
         source += jnp.where(away & bit != 0, weight, 0)
@@ -375,30 +367,21 @@
         size = lax.axis_size(axis)
         return lax.ppermute(value, axis, [(i, i ^ bit) for i in range(size)])
 
-    def swap_both(value, blk_bit, grp_bit):
-        pairs = [
-            (g * nb + b, (g ^ grp_bit) * nb + (b ^ blk_bit)) for g in range(ng) for b in range(nb)
-        ]
-        return lax.ppermute(value, ("grp", "blk"), pairs)
-
     def joined(pieces):
         return pieces[0] if len(pieces) == 1 else jnp.concatenate(pieces, axis=0)
 
-    planes, far_offsets = [bank], [0]
+    parts, weights = [part, swap(part, "blk", half)], []
+    for n in range(ng.bit_length() - 2, -1, -1):
+        part = joined(parts)
+        parts = [part, swap(part, "grp", 1 << n)]
+        weights.append((1 << n, 2 << len(weights)))
+
+    planes, early_order = [bank], [0]
     for n in range(half.bit_length() - 2, 0, -1):
         planes.append(swap(joined(planes), "blk", 1 << n))
-        far_offsets += [offset ^ (1 << n) for offset in far_offsets]
-    far, far_offsets = joined(planes[1:]), far_offsets[1:]
-    near = swap(bank, "blk", 1)
-
-    weights, weight = [], 1
-    for n in range(ng.bit_length() - 2, 1, -1):
-        part = joined([part, swap(part, "grp", 1 << n)])
-        weights.append((1 << n, weight))
-        weight *= 2
-    half_weight = weight
-    weights += [(2, 2 * weight), (1, 4 * weight)]
-    parts = [part, swap(part, "blk", half), swap(part, "grp", 2), swap_both(part, half, 2)]
+        early_order += [offset ^ (1 << n) for offset in early_order]
+    last = swap(joined(planes), "blk", 1)
+    order = early_order + [offset ^ 1 for offset in early_order]
 
     cos_part, sin_part, square = pl.pallas_call(
         table_kernel,
@@ -414,53 +397,39 @@
         name="tables",
     )(curves, noise, angle)
 
-    any_space = pl.BlockSpec(memory_space=pl.ANY)
-    part = pl.pallas_call(
-        functools.partial(join_kernel, len(parts)),
-        out_shape=vmem_out((sum(piece.shape[0] for piece in parts), part.shape[1]), BF16),
-        in_specs=[_vmem()] * len(parts) + [any_space] * 3,
-        out_specs=_vmem(),
-        compiler_params=_params(4),
-        name="join",
-    )(*parts, near, far, cos_part)
-    parts = [part, swap(part, "grp", 1)]
-    last = swap(far, "blk", 1)
-    order = [0, 1] + far_offsets + [offset ^ 1 for offset in far_offsets]
-
     count = 2 * ng * n_part
-    early = (2 + len(far_offsets)) * n_proj
-    late = len(far_offsets) * n_proj
+    early = late = len(early_order) * n_proj
     shifted, norm = pl.pallas_call(
         functools.partial(shift_kernel, n_proj),
         out_shape=[
             vmem_out((shifts * early, 2 * wide), BF16),
             vmem_out((classes_count, early), F32),
         ],
-        in_specs=[_vmem()] * 6,
+        in_specs=[_vmem()] * (3 + len(planes)),
         out_specs=[_vmem()] * 2,
         compiler_params=_params(8),
         cost_estimate=pl.CostEstimate(
             flops=6 * early * shifts * wide, bytes_accessed=4_000_000, transcendentals=0
         ),
         name="shift",
-    )(cos_part, sin_part, square, bank, near, far)
+    )(cos_part, sin_part, square, *planes)
     weighted, extra_rows, rows = pl.pallas_call(
         functools.partial(
-            early_kernel, len(parts), ng, half_weight, weights, n_part, n_proj, length, subsets
+            early_kernel, len(parts), ng, weights, n_part, n_proj, length, subsets
         ),
         out_shape=[
             vmem_out((count, 2 * wide), BF16),
             vmem_out((count, extra), F32),
             vmem_out((count, (shifts + 1) * early), F32),
         ],
-        in_specs=[_vmem()] * (5 + len(parts)),
+        in_specs=[_vmem()] * (2 + len(parts) + len(planes)),
         out_specs=[_vmem()] * 3,
         compiler_params=_params(8),
         cost_estimate=pl.CostEstimate(
             flops=4 * count * early * shifts * wide, bytes_accessed=4_000_000, transcendentals=0
         ),
         name="early",
-    )(shifted, norm, *parts, bank, near, far)
+    )(shifted, norm, *parts, *planes)
     lanes = 128 * -(-(shifts + 1) * half * n_proj // 128)
     keep, give = pl.pallas_call(
         functools.partial(final_kernel, n_proj, length, subsets),

time: 29.7 us -> 25.8 us (0.87)
  waiting for transfers between devices: 11.8 us -> 8 us
  Pallas kernels: 7.98 us -> 7.33 us
  starting transfers between devices: 9.74 us -> 10.1 us
    ppermute x1 -> x0, waiting for transfers between devices: 3.55 us -> none  [swap_both(): return lax.ppermute(value, ('grp', 'blk'), pairs)]
    ppermute x7 -> x6, starting transfers between devices: 9.43 us -> 10.1 us  [swap(): return lax.ppermute(value, axis, [(i, i ^ bit) for i in range(size)])]
    pallas_call x1, Pallas kernels: 1.69 us -> 1.19 us  [per_device(): pl.pallas_call(functools.partial(shift_kernel, n_proj), out_shape=[vmem_o...]
    pallas_call x2 -> x1, Pallas kernels: 1.53 us -> 1.03 us  [per_device(): pl.pallas_call(functools.partial(early_kernel, len(parts), ng, weights, n...]
    pallas_call x1, Pallas kernels: 1.62 us -> 1.96 us  [per_device(): pl.pallas_call(functools.partial(final_kernel, n_proj, length, subsets),...]
    ppermute x1 -> x0, starting transfers between devices: 0.31 us -> none  [swap_both(): return lax.ppermute(value, ('grp', 'blk'), pairs)]
    ppermute x7 -> x6, waiting for transfers between devices: 8.22 us -> 8 us  [swap(): return lax.ppermute(value, axis, [(i, i ^ bit) for i in range(size)])]
  transfers between devices with their start and end apart: 8 -> 6, of which waited for: 5 -> 4; matrix products, arithmetic and copies ran while one was open for 0% -> 0% of each run, Pallas kernels for 13% -> 11%
where the time goes in v8:
time: 25.8 us; the launch traced here: 25.6 us
  starting transfers between devices  10.1 us (39%)
  waiting for transfers between devices  8 us (31%)
  Pallas kernels  7.33 us (28%)
    ppermute x6, starting transfers between devices, swap(): return lax.ppermute(value, axis, [(i, i ^ bit) for i in range(size)])  10.1 us
    ppermute x6, waiting for transfers between devices, swap(): return lax.ppermute(value, axis, [(i, i ^ bit) for i in range(size)])  8 us
    pallas_call x1, Pallas kernels, per_device(): pl.pallas_call(functools.partial(final_kernel, n_proj, length, subsets),...  1.96 us
    pallas_call x1, Pallas kernels, per_device(): pl.pallas_call(pack_kernel, out_shape=[vmem_out((2 * n_proj, wide), BF16)...  1.58 us
    pallas_call x1, Pallas kernels, per_device(): pl.pallas_call(functools.partial(shift_kernel, n_proj), out_shape=[vmem_o...  1.19 us
    pallas_call x1, Pallas kernels, per_device(): pl.pallas_call(functools.partial(early_kernel, len(parts), ng, weights, n...  1.03 us
    pallas_call x1, Pallas kernels, per_device(): pl.pallas_call(functools.partial(place_kernel, half, n_proj, order), out_...  0.98 us
    pallas_call x1, Pallas kernels, per_device(): pl.pallas_call(table_kernel, out_shape=[vmem_out((shifts, wide), F32), vm...  0.59 us
  transfers between devices with their start and end apart: 6, of which 4 were waited for; matrix products, arithmetic and copies ran while one was open for 0% of the time, Pallas kernels for 11%

profile of v8, /device:TPU:0, one launch (start us, length us, event | category | flops | bytes accessed | tf_op | source)
XLA Modules:
  0.0 25.6 jit_solution(18193188841413752506)
XLA Ops:
  0.0 1.6 %pack.1 = (bf16[16,4096]{1,0:T(8,128)(2,1)S(1)}, bf16[4,4352]{1,0:T(4,128)(2,1)S(1)}, f32[64,4000]{1,0:T(8,128)S(1)}, f32[1,4000]{1,0:T(1,128)S(1)}, f32[9,4000]{1,0:T(8,128)S(1)}) custom-call(s32[2]{0:T(128)} %class_hbm.1, s32[8]{0:T(128)} %subset_hbm.1, bf16[2,2,4000]{2,1,0:T(2,128)(2,1)} %particles_hbm.1, bf16[2,192]{1,0:T(2,128)(2,1)} %prior_hbm.1, ...), custom_call_target="tpu_custom_call" | custom-call | tf_op jit(solution)/shard_map/pack/pallas_call | solution.py:341
  1.6 4.1 %collective-permute-start.1 = (bf16[4,4352]{1,0:T(4,128)(2,1)S(1)}, bf16[4,4352]{1,0:T(4,128)(2,1)S(1)}, u32[]{:S(2)}, u32[]{:S(2)}) collective-permute-start(bf16[4,4352]{1,0:T(4,128)(2,1)S(1)} %get-tuple-element.29), channel_id=1, source_target_pairs={{0,4},{1,5},{2,6},{3,7},{4,0},{5,1},{6,2},{7,3},{8,12},{9,13},{10,... | collective-permute-start | bytes 104456 | tf_op jit(solution)/shard_map/ppermute | solution.py:368
  5.7 1.6 %collective-permute-start = (bf16[16,4096]{1,0:T(8,128)(2,1)S(1)}, bf16[16,4096]{1,0:T(8,128)(2,1)S(1)}, u32[]{:S(2)}, u32[]{:S(2)}) collective-permute-start(bf16[16,4096]{1,0:T(8,128)(2,1)S(1)} %get-tuple-element.26.rest_0_.rest_2_), channel_id=1, source_target_pairs={{0,2},{1,3},{2,0},{3,1},{4,6},{5,7},{6,4},{7,5},{8,10},{9,11},{10,... | collective-permute-start | bytes 393224 | tf_op jit(solution)/shard_map/ppermute | solution.py:368
  7.3 0.8 %collective-permute-done.1 = bf16[4,4352]{1,0:T(4,128)(2,1)S(1)} collective-permute-done((bf16[4,4352]{1,0:T(4,128)(2,1)S(1)}, bf16[4,4352]{1,0:T(4,128)(2,1)S(1)}, u32[]{:S(2)}, u32[]{:S(2)}) %collective-permute-start.1) | collective-permute-done | bytes 34848 | tf_op jit(solution)/shard_map/ppermute | solution.py:368
  8.1 1.7 %collective-permute-start.2 = (bf16[8,4352]{1,0:T(8,128)(2,1)S(1)}, bf16[8,4352]{1,0:T(8,128)(2,1)S(1)}, u32[]{:S(2)}, u32[]{:S(2)}) collective-permute-start(bf16[8,4352]{1,0:T(8,128)(2,1)S(1)} %pad_maximum_fusion.2), channel_id=1, source_target_pairs={{0,16},{8,24},{16,0},{24,8},{1,17},{9,25},{17,1},{25,9},{2,18},{10... | collective-permute-start | bytes 208904 | tf_op jit(solution)/shard_map/ppermute | solution.py:368
  9.8 0.9 %collective-permute-done.rest_1_.rest_3_ = bf16[16,4096]{1,0:T(8,128)(2,1)S(1)} collective-permute-done((bf16[16,4096]{1,0:T(8,128)(2,1)S(1)}, bf16[16,4096]{1,0:T(8,128)(2,1)S(1)}, u32[]{:S(2)}, u32[]{:S(2)}) %collective-permute-start) | collective-permute-done | bytes 131104 | tf_op jit(solution)/shard_map/ppermute | solution.py:368
  10.7 1.9 %collective-permute-start.4 = (bf16[32,4096]{1,0:T(8,128)(2,1)S(1)}, bf16[32,4096]{1,0:T(8,128)(2,1)S(1)}, u32[]{:S(2)}, u32[]{:S(2)}) collective-permute-start(bf16[32,4096]{1,0:T(8,128)(2,1)S(1)} %pad_maximum_fusion), channel_id=1, source_target_pairs={{0,1},{1,0},{2,3},{3,2},{4,5},{5,4},{6,7},{7,6},{8,9},{9,8},{10,11... | collective-permute-start | bytes 786440 | tf_op jit(solution)/shard_map/ppermute | solution.py:368
  12.6 0.0 collective-permute-done.2
  12.6 0.1 pad_maximum_fusion.1.rest_0_
  12.7 0.1 collective-permute-start.3
  12.8 0.6 %tables.1 = (f32[9,4096]{1,0:T(8,128)S(1)}, f32[9,4096]{1,0:T(8,128)S(1)}, bf16[128,4096]{1,0:T(8,128)(2,1)S(1)}) custom-call(f32[64,4000]{1,0:T(8,128)S(1)} %get-tuple-element.20.curves_ref, f32[1,4000]{1,0:T(1,128)S(1)} %get-tuple-element.21.noise_ref, f32[9,4000]{1,0:T(8,128)S(1)} %get-tuple-element.22.angle_ref), custom_call_target="tpu_custom_call" | custom-call | flops 4000000 | bytes 2000000 | tf_op jit(solution)/shard_map/tables/pallas_call | solution.py:386
  13.3 1.2 %shift.1 = (bf16[144,8192]{1,0:T(8,128)(2,1)S(1)}, f32[64,16]{1,0:T(8,128)S(1)}) custom-call(f32[9,4096]{1,0:T(8,128)S(1)} %get-tuple-element.23.cos_ref, f32[9,4096]{1,0:T(8,128)S(1)} %get-tuple-element.24.sin_ref, bf16[128,4096]{1,0:T(8,128)(2,1)S(1)} %get-tuple-element.25.square_ref, bf16[16,4096]{1,0:T(8,128)(2,1)S(1)} %get-tuple-element.26.rest_0_.rest_2_, ...), custom_call_target="tpu_custom_call" | custom-call | flops 3538944 | bytes 4000000 | tf_op jit(solution)/shard_map/shift/pallas_call | solution.py:402
  14.5 0.0 collective-permute-done.3.rest_1_
  14.5 1.0 %early.1 = (bf16[16,8192]{1,0:T(8,128)(2,1)S(1)}, f32[16,256]{1,0:T(8,128)S(1)}, f32[16,160]{1,0:T(8,128)S(1)}) custom-call(bf16[144,8192]{1,0:T(8,128)(2,1)S(1)} %get-tuple-element.27.shifted_ref, f32[64,16]{1,0:T(8,128)S(1)} %get-tuple-element.28.norm_ref, bf16[16,4352]{1,0:T(8,128)(2,1)S(1)} %pad_maximum_fusion.1.rest_0_, ...), custom_call_target="tpu_custom_call" | custom-call | flops 37748736 | bytes 4000000 | tf_op jit(solution)/shard_map/early/pallas_call | solution.py:416
  15.6 2.5 %collective-permute-done.4.last_ref = bf16[32,4096]{1,0:T(8,128)(2,1)S(1)} collective-permute-done((bf16[32,4096]{1,0:T(8,128)(2,1)S(1)}, bf16[32,4096]{1,0:T(8,128)(2,1)S(1)}, u32[]{:S(2)}, u32[]{:S(2)}) %collective-permute-start.4) | collective-permute-done | bytes 262176 | tf_op jit(solution)/shard_map/ppermute | solution.py:368
  18.1 2.0 %final.1 = (f32[8,384]{1,0:T(8,128)S(1)}, f32[8,384]{1,0:T(8,128)S(1)}) custom-call(bf16[16,8192]{1,0:T(8,128)(2,1)S(1)} %get-tuple-element.30.weighted_ref, f32[16,256]{1,0:T(8,128)S(1)} %get-tuple-element.31.extra_ref, f32[16,160]{1,0:T(8,128)S(1)} %get-tuple-element.32.rows_ref, f32[9,4096]{1,0:T(8,128)S(1)} %get-tuple-element.23.cos_ref, ...), custom_call_target="tpu_custom_call" | custom-call | flops 37748736 | bytes 4000000 | tf_op jit(solution)/shard_map/final/pallas_call | solution.py:434
  20.0 0.8 %collective-permute-start.5 = (f32[8,384]{1,0:T(8,128)S(1)}, f32[8,384]{1,0:T(8,128)S(1)}, u32[]{:S(2)}, u32[]{:S(2)}) collective-permute-start(f32[8,384]{1,0:T(8,128)S(1)} %get-tuple-element.34), channel_id=1, source_target_pairs={{0,4},{1,5},{2,6},{3,7},{4,0},{5,1},{6,2},{7,3},{8,12},{9,13},{10,... | collective-permute-start | bytes 36872 | tf_op jit(solution)/shard_map/ppermute | solution.py:368
  20.9 3.8 %collective-permute-done.5.recv_ref = f32[8,384]{1,0:T(8,128)S(1)} collective-permute-done((f32[8,384]{1,0:T(8,128)S(1)}, f32[8,384]{1,0:T(8,128)S(1)}, u32[]{:S(2)}, u32[]{:S(2)}) %collective-permute-start.5) | collective-permute-done | bytes 12320 | tf_op jit(solution)/shard_map/ppermute | solution.py:368
  24.7 1.0 %place.1 = f32[9,8,64]{2,1,0:T(8,128)} custom-call(f32[8,384]{1,0:T(8,128)S(1)} %get-tuple-element.33.keep_ref, f32[8,384]{1,0:T(8,128)S(1)} %collective-permute-done.5.recv_ref), custom_call_target="tpu_custom_call" | custom-call | tf_op jit(solution)/shard_map/place/pallas_call | solution.py:446
  (2 shorter events, 0.1 us)
Async XLA Ops:
  1.6 6.5 %collective-permute-start.1 = (bf16[4,4352]{1,0:T(4,128)(2,1)S(1)}, bf16[4,4352]{1,0:T(4,128)(2,1)S(1)}, u32[]{:S(2)}, u32[]{:S(2)}) collective-permute-start(bf16[4,4352]{1,0:T(4,128)(2,1)S(1)} %get-tuple-element.29), channel_id=1, source_target_pairs={{0,4},{1,5},{2,6},{3,7},{4,0},{5,1},{6,2},{7,3},{8,12},{9,13},{10,... | collective-permute-start | bytes 104456 | tf_op jit(solution)/shard_map/ppermute | solution.py:368
  5.7 5.0 %collective-permute-start = (bf16[16,4096]{1,0:T(8,128)(2,1)S(1)}, bf16[16,4096]{1,0:T(8,128)(2,1)S(1)}, u32[]{:S(2)}, u32[]{:S(2)}) collective-permute-start(bf16[16,4096]{1,0:T(8,128)(2,1)S(1)} %get-tuple-element.26.rest_0_.rest_2_), channel_id=1, source_target_pairs={{0,2},{1,3},{2,0},{3,1},{4,6},{5,7},{6,4},{7,5},{8,10},{9,11},{10,... | collective-permute-start | bytes 393224 | tf_op jit(solution)/shard_map/ppermute | solution.py:368
  8.1 4.5 %collective-permute-start.2 = (bf16[8,4352]{1,0:T(8,128)(2,1)S(1)}, bf16[8,4352]{1,0:T(8,128)(2,1)S(1)}, u32[]{:S(2)}, u32[]{:S(2)}) collective-permute-start(bf16[8,4352]{1,0:T(8,128)(2,1)S(1)} %pad_maximum_fusion.2), channel_id=1, source_target_pairs={{0,16},{8,24},{16,0},{24,8},{1,17},{9,25},{17,1},{25,9},{2,18},{10... | collective-permute-start | bytes 208904 | tf_op jit(solution)/shard_map/ppermute | solution.py:368
  10.7 7.3 %collective-permute-start.4 = (bf16[32,4096]{1,0:T(8,128)(2,1)S(1)}, bf16[32,4096]{1,0:T(8,128)(2,1)S(1)}, u32[]{:S(2)}, u32[]{:S(2)}) collective-permute-start(bf16[32,4096]{1,0:T(8,128)(2,1)S(1)} %pad_maximum_fusion), channel_id=1, source_target_pairs={{0,1},{1,0},{2,3},{3,2},{4,5},{5,4},{6,7},{7,6},{8,9},{9,8},{10,11... | collective-permute-start | bytes 786440 | tf_op jit(solution)/shard_map/ppermute | solution.py:368
  12.7 1.9 %collective-permute-start.3 = (bf16[16,4352]{1,0:T(8,128)(2,1)S(1)}, bf16[16,4352]{1,0:T(8,128)(2,1)S(1)}, u32[]{:S(2)}, u32[]{:S(2)}) collective-permute-start(bf16[16,4352]{1,0:T(8,128)(2,1)S(1)} %pad_maximum_fusion.1.rest_0_), channel_id=1, source_target_pairs={{0,8},{8,0},{16,24},{24,16},{1,9},{9,1},{17,25},{25,17},{2,10},{10... | collective-permute-start | bytes 417800 | tf_op jit(solution)/shard_map/ppermute | solution.py:368
  20.0 4.6 %collective-permute-start.5 = (f32[8,384]{1,0:T(8,128)S(1)}, f32[8,384]{1,0:T(8,128)S(1)}, u32[]{:S(2)}, u32[]{:S(2)}) collective-permute-start(f32[8,384]{1,0:T(8,128)S(1)} %get-tuple-element.34), channel_id=1, source_target_pairs={{0,4},{1,5},{2,6},{3,7},{4,0},{5,1},{6,2},{7,3},{8,12},{9,13},{10,... | collective-permute-start | bytes 36872 | tf_op jit(solution)/shard_map/ppermute | solution.py:368

commit v9 on v8

--- a/solution.py
+++ b/solution.py
@@ -376,12 +376,13 @@
         parts = [part, swap(part, "grp", 1 << n)]
         weights.append((1 << n, 2 << len(weights)))
 
-    planes, early_order = [bank], [0]
-    for n in range(half.bit_length() - 2, 0, -1):
-        planes.append(swap(joined(planes), "blk", 1 << n))
-        early_order += [offset ^ (1 << n) for offset in early_order]
-    last = swap(joined(planes), "blk", 1)
-    order = early_order + [offset ^ 1 for offset in early_order]
+    planes, early_order, bit = [bank], [0], 1
+    while 2 * bit < half:
+        planes.append(swap(joined(planes), "blk", bit))
+        early_order += [offset ^ bit for offset in early_order]
+        bit *= 2
+    last = swap(joined(planes), "blk", bit)
+    order = early_order + [offset ^ bit for offset in early_order]
 
     cos_part, sin_part, square = pl.pallas_call(
         table_kernel,

time: 25.8 us -> 25.1 us (0.973)
  waiting for transfers between devices: 8 us -> 6.75 us
  starting transfers between devices: 10.1 us -> 10.7 us
    ppermute x6, waiting for transfers between devices: 8 us -> 6.75 us  [swap(): return lax.ppermute(value, axis, [(i, i ^ bit) for i in range(size)])]
    ppermute x6, starting transfers between devices: 10.1 us -> 10.7 us  [swap(): return lax.ppermute(value, axis, [(i, i ^ bit) for i in range(size)])]
  transfers between devices with their start and end apart: 6 -> 6, of which waited for: 4 -> 5; matrix products, arithmetic and copies ran while one was open for 0% -> 0% of each run, Pallas kernels for 11% -> 11%
where the time goes in v9:
time: 25.1 us; the launch traced here: 24.9 us
  starting transfers between devices  10.7 us (43%)
  Pallas kernels  7.33 us (29%)
  waiting for transfers between devices  6.75 us (27%)
    ppermute x6, starting transfers between devices, swap(): return lax.ppermute(value, axis, [(i, i ^ bit) for i in range(size)])  10.7 us
    ppermute x6, waiting for transfers between devices, swap(): return lax.ppermute(value, axis, [(i, i ^ bit) for i in range(size)])  6.75 us
    pallas_call x1, Pallas kernels, per_device(): pl.pallas_call(functools.partial(final_kernel, n_proj, length, subsets),...  1.96 us
    pallas_call x1, Pallas kernels, per_device(): pl.pallas_call(pack_kernel, out_shape=[vmem_out((2 * n_proj, wide), BF16)...  1.58 us
    pallas_call x1, Pallas kernels, per_device(): pl.pallas_call(functools.partial(shift_kernel, n_proj), out_shape=[vmem_o...  1.18 us
    pallas_call x1, Pallas kernels, per_device(): pl.pallas_call(functools.partial(early_kernel, len(parts), ng, weights, n...  1.03 us
    pallas_call x1, Pallas kernels, per_device(): pl.pallas_call(functools.partial(place_kernel, half, n_proj, order), out_...  0.99 us
    pallas_call x1, Pallas kernels, per_device(): pl.pallas_call(table_kernel, out_shape=[vmem_out((shifts, wide), F32), vm...  0.59 us
  transfers between devices with their start and end apart: 6, of which 5 were waited for; matrix products, arithmetic and copies ran while one was open for 0% of the time, Pallas kernels for 11%

profile of v9, /device:TPU:0, one launch (start us, length us, event | category | flops | bytes accessed | tf_op | source)
XLA Modules:
  0.0 24.9 jit_solution(7845803110113940721)
XLA Ops:
  0.0 1.6 %pack.1 = (bf16[16,4096]{1,0:T(8,128)(2,1)S(1)}, bf16[4,4352]{1,0:T(4,128)(2,1)S(1)}, f32[64,4000]{1,0:T(8,128)S(1)}, f32[1,4000]{1,0:T(1,128)S(1)}, f32[9,4000]{1,0:T(8,128)S(1)}) custom-call(s32[2]{0:T(128)} %class_hbm.1, s32[8]{0:T(128)} %subset_hbm.1, bf16[2,2,4000]{2,1,0:T(2,128)(2,1)} %particles_hbm.1, bf16[2,192]{1,0:T(2,128)(2,1)} %prior_hbm.1, ...), custom_call_target="tpu_custom_call" | custom-call | tf_op jit(solution)/shard_map/pack/pallas_call | solution.py:341
  1.6 4.1 %collective-permute-start.1 = (bf16[4,4352]{1,0:T(4,128)(2,1)S(1)}, bf16[4,4352]{1,0:T(4,128)(2,1)S(1)}, u32[]{:S(2)}, u32[]{:S(2)}) collective-permute-start(bf16[4,4352]{1,0:T(4,128)(2,1)S(1)} %get-tuple-element.29), channel_id=1, source_target_pairs={{0,4},{1,5},{2,6},{3,7},{4,0},{5,1},{6,2},{7,3},{8,12},{9,13},{10,... | collective-permute-start | bytes 104456 | tf_op jit(solution)/shard_map/ppermute | solution.py:368
  5.7 1.5 %collective-permute-start = (bf16[16,4096]{1,0:T(8,128)(2,1)S(1)}, bf16[16,4096]{1,0:T(8,128)(2,1)S(1)}, u32[]{:S(2)}, u32[]{:S(2)}) collective-permute-start(bf16[16,4096]{1,0:T(8,128)(2,1)S(1)} %get-tuple-element.26.rest_0_.rest_2_), channel_id=1, source_target_pairs={{0,1},{1,0},{2,3},{3,2},{4,5},{5,4},{6,7},{7,6},{8,9},{9,8},{10,11... | collective-permute-start | bytes 393224 | tf_op jit(solution)/shard_map/ppermute | solution.py:368
  7.2 0.8 %collective-permute-done.1 = bf16[4,4352]{1,0:T(4,128)(2,1)S(1)} collective-permute-done((bf16[4,4352]{1,0:T(4,128)(2,1)S(1)}, bf16[4,4352]{1,0:T(4,128)(2,1)S(1)}, u32[]{:S(2)}, u32[]{:S(2)}) %collective-permute-start.1) | collective-permute-done | bytes 34848 | tf_op jit(solution)/shard_map/ppermute | solution.py:368
  8.0 1.8 %collective-permute-start.2 = (bf16[8,4352]{1,0:T(8,128)(2,1)S(1)}, bf16[8,4352]{1,0:T(8,128)(2,1)S(1)}, u32[]{:S(2)}, u32[]{:S(2)}) collective-permute-start(bf16[8,4352]{1,0:T(8,128)(2,1)S(1)} %pad_maximum_fusion.2), channel_id=1, source_target_pairs={{0,16},{8,24},{16,0},{24,8},{1,17},{9,25},{17,1},{25,9},{2,18},{10... | collective-permute-start | bytes 208904 | tf_op jit(solution)/shard_map/ppermute | solution.py:368
  9.8 0.9 %collective-permute-done.rest_1_.rest_3_ = bf16[16,4096]{1,0:T(8,128)(2,1)S(1)} collective-permute-done((bf16[16,4096]{1,0:T(8,128)(2,1)S(1)}, bf16[16,4096]{1,0:T(8,128)(2,1)S(1)}, u32[]{:S(2)}, u32[]{:S(2)}) %collective-permute-start) | collective-permute-done | bytes 131104 | tf_op jit(solution)/shard_map/ppermute | solution.py:368
  10.7 1.6 %collective-permute-start.4 = (bf16[32,4096]{1,0:T(8,128)(2,1)S(1)}, bf16[32,4096]{1,0:T(8,128)(2,1)S(1)}, u32[]{:S(2)}, u32[]{:S(2)}) collective-permute-start(bf16[32,4096]{1,0:T(8,128)(2,1)S(1)} %pad_maximum_fusion), channel_id=1, source_target_pairs={{0,2},{1,3},{2,0},{3,1},{4,6},{5,7},{6,4},{7,5},{8,10},{9,11},{10,... | collective-permute-start | bytes 786440 | tf_op jit(solution)/shard_map/ppermute | solution.py:368
  12.3 0.1 collective-permute-done.2
  12.4 0.1 pad_maximum_fusion.1.rest_0_
  12.5 0.1 collective-permute-start.3
  12.5 0.6 %tables.1 = (f32[9,4096]{1,0:T(8,128)S(1)}, f32[9,4096]{1,0:T(8,128)S(1)}, bf16[128,4096]{1,0:T(8,128)(2,1)S(1)}) custom-call(f32[64,4000]{1,0:T(8,128)S(1)} %get-tuple-element.20.curves_ref, f32[1,4000]{1,0:T(1,128)S(1)} %get-tuple-element.21.noise_ref, f32[9,4000]{1,0:T(8,128)S(1)} %get-tuple-element.22.angle_ref), custom_call_target="tpu_custom_call" | custom-call | flops 4000000 | bytes 2000000 | tf_op jit(solution)/shard_map/tables/pallas_call | solution.py:387
  13.1 1.2 %shift.1 = (bf16[144,8192]{1,0:T(8,128)(2,1)S(1)}, f32[64,16]{1,0:T(8,128)S(1)}) custom-call(f32[9,4096]{1,0:T(8,128)S(1)} %get-tuple-element.23.cos_ref, f32[9,4096]{1,0:T(8,128)S(1)} %get-tuple-element.24.sin_ref, bf16[128,4096]{1,0:T(8,128)(2,1)S(1)} %get-tuple-element.25.square_ref, bf16[16,4096]{1,0:T(8,128)(2,1)S(1)} %get-tuple-element.26.rest_0_.rest_2_, ...), custom_call_target="tpu_custom_call" | custom-call | flops 3538944 | bytes 4000000 | tf_op jit(solution)/shard_map/shift/pallas_call | solution.py:403
  14.3 0.0 collective-permute-done.3.rest_1_
  14.3 1.0 %early.1 = (bf16[16,8192]{1,0:T(8,128)(2,1)S(1)}, f32[16,256]{1,0:T(8,128)S(1)}, f32[16,160]{1,0:T(8,128)S(1)}) custom-call(bf16[144,8192]{1,0:T(8,128)(2,1)S(1)} %get-tuple-element.27.shifted_ref, f32[64,16]{1,0:T(8,128)S(1)} %get-tuple-element.28.norm_ref, bf16[16,4352]{1,0:T(8,128)(2,1)S(1)} %pad_maximum_fusion.1.rest_0_, ...), custom_call_target="tpu_custom_call" | custom-call | flops 37748736 | bytes 4000000 | tf_op jit(solution)/shard_map/early/pallas_call | solution.py:417
  15.4 2.0 %collective-permute-done.4.last_ref = bf16[32,4096]{1,0:T(8,128)(2,1)S(1)} collective-permute-done((bf16[32,4096]{1,0:T(8,128)(2,1)S(1)}, bf16[32,4096]{1,0:T(8,128)(2,1)S(1)}, u32[]{:S(2)}, u32[]{:S(2)}) %collective-permute-start.4) | collective-permute-done | bytes 262176 | tf_op jit(solution)/shard_map/ppermute | solution.py:368
  17.4 2.0 %final.1 = (f32[8,384]{1,0:T(8,128)S(1)}, f32[8,384]{1,0:T(8,128)S(1)}) custom-call(bf16[16,8192]{1,0:T(8,128)(2,1)S(1)} %get-tuple-element.30.weighted_ref, f32[16,256]{1,0:T(8,128)S(1)} %get-tuple-element.31.extra_ref, f32[16,160]{1,0:T(8,128)S(1)} %get-tuple-element.32.rows_ref, f32[9,4096]{1,0:T(8,128)S(1)} %get-tuple-element.23.cos_ref, ...), custom_call_target="tpu_custom_call" | custom-call | flops 37748736 | bytes 4000000 | tf_op jit(solution)/shard_map/final/pallas_call | solution.py:435
  19.3 1.6 %collective-permute-start.5 = (f32[8,384]{1,0:T(8,128)S(1)}, f32[8,384]{1,0:T(8,128)S(1)}, u32[]{:S(2)}, u32[]{:S(2)}) collective-permute-start(f32[8,384]{1,0:T(8,128)S(1)} %get-tuple-element.34), channel_id=1, source_target_pairs={{0,4},{1,5},{2,6},{3,7},{4,0},{5,1},{6,2},{7,3},{8,12},{9,13},{10,... | collective-permute-start | bytes 36872 | tf_op jit(solution)/shard_map/ppermute | solution.py:368
  20.9 3.0 %collective-permute-done.5.recv_ref = f32[8,384]{1,0:T(8,128)S(1)} collective-permute-done((f32[8,384]{1,0:T(8,128)S(1)}, f32[8,384]{1,0:T(8,128)S(1)}, u32[]{:S(2)}, u32[]{:S(2)}) %collective-permute-start.5) | collective-permute-done | bytes 12320 | tf_op jit(solution)/shard_map/ppermute | solution.py:368
  24.0 1.0 %place.1 = f32[9,8,64]{2,1,0:T(8,128)} custom-call(f32[8,384]{1,0:T(8,128)S(1)} %get-tuple-element.33.keep_ref, f32[8,384]{1,0:T(8,128)S(1)} %collective-permute-done.5.recv_ref), custom_call_target="tpu_custom_call" | custom-call | tf_op jit(solution)/shard_map/place/pallas_call | solution.py:447
  (2 shorter events, 0.1 us)
Async XLA Ops:
  1.6 6.4 %collective-permute-start.1 = (bf16[4,4352]{1,0:T(4,128)(2,1)S(1)}, bf16[4,4352]{1,0:T(4,128)(2,1)S(1)}, u32[]{:S(2)}, u32[]{:S(2)}) collective-permute-start(bf16[4,4352]{1,0:T(4,128)(2,1)S(1)} %get-tuple-element.29), channel_id=1, source_target_pairs={{0,4},{1,5},{2,6},{3,7},{4,0},{5,1},{6,2},{7,3},{8,12},{9,13},{10,... | collective-permute-start | bytes 104456 | tf_op jit(solution)/shard_map/ppermute | solution.py:368
  5.7 5.0 %collective-permute-start = (bf16[16,4096]{1,0:T(8,128)(2,1)S(1)}, bf16[16,4096]{1,0:T(8,128)(2,1)S(1)}, u32[]{:S(2)}, u32[]{:S(2)}) collective-permute-start(bf16[16,4096]{1,0:T(8,128)(2,1)S(1)} %get-tuple-element.26.rest_0_.rest_2_), channel_id=1, source_target_pairs={{0,1},{1,0},{2,3},{3,2},{4,5},{5,4},{6,7},{7,6},{8,9},{9,8},{10,11... | collective-permute-start | bytes 393224 | tf_op jit(solution)/shard_map/ppermute | solution.py:368
  8.0 4.4 %collective-permute-start.2 = (bf16[8,4352]{1,0:T(8,128)(2,1)S(1)}, bf16[8,4352]{1,0:T(8,128)(2,1)S(1)}, u32[]{:S(2)}, u32[]{:S(2)}) collective-permute-start(bf16[8,4352]{1,0:T(8,128)(2,1)S(1)} %pad_maximum_fusion.2), channel_id=1, source_target_pairs={{0,16},{8,24},{16,0},{24,8},{1,17},{9,25},{17,1},{25,9},{2,18},{10... | collective-permute-start | bytes 208904 | tf_op jit(solution)/shard_map/ppermute | solution.py:368
  10.7 6.7 %collective-permute-start.4 = (bf16[32,4096]{1,0:T(8,128)(2,1)S(1)}, bf16[32,4096]{1,0:T(8,128)(2,1)S(1)}, u32[]{:S(2)}, u32[]{:S(2)}) collective-permute-start(bf16[32,4096]{1,0:T(8,128)(2,1)S(1)} %pad_maximum_fusion), channel_id=1, source_target_pairs={{0,2},{1,3},{2,0},{3,1},{4,6},{5,7},{6,4},{7,5},{8,10},{9,11},{10,... | collective-permute-start | bytes 786440 | tf_op jit(solution)/shard_map/ppermute | solution.py:368
  12.5 1.9 %collective-permute-start.3 = (bf16[16,4352]{1,0:T(8,128)(2,1)S(1)}, bf16[16,4352]{1,0:T(8,128)(2,1)S(1)}, u32[]{:S(2)}, u32[]{:S(2)}) collective-permute-start(bf16[16,4352]{1,0:T(8,128)(2,1)S(1)} %pad_maximum_fusion.1.rest_0_), channel_id=1, source_target_pairs={{0,8},{8,0},{16,24},{24,16},{1,9},{9,1},{17,25},{25,17},{2,10},{10... | collective-permute-start | bytes 417800 | tf_op jit(solution)/shard_map/ppermute | solution.py:368
  19.3 4.6 %collective-permute-start.5 = (f32[8,384]{1,0:T(8,128)S(1)}, f32[8,384]{1,0:T(8,128)S(1)}, u32[]{:S(2)}, u32[]{:S(2)}) collective-permute-start(f32[8,384]{1,0:T(8,128)S(1)} %get-tuple-element.34), channel_id=1, source_target_pairs={{0,4},{1,5},{2,6},{3,7},{4,0},{5,1},{6,2},{7,3},{8,12},{9,13},{10,... | collective-permute-start | bytes 36872 | tf_op jit(solution)/shard_map/ppermute | solution.py:368

commit v10 on v9

--- a/solution.py
+++ b/solution.py
@@ -149,41 +149,61 @@
     )
 
 
-def shift_rows(shifted_ref, cos_ref, sin_ref, real, imag, at):
-    n_proj, wide = real.shape
-    shifts = cos_ref.shape[0]
-    for t in range(shifts):
-        cos_part, sin_part = cos_ref[t : t + 1, :], sin_ref[t : t + 1, :]
-        rows = slice((at * shifts + t) * n_proj, (at * shifts + t + 1) * n_proj)
-        shifted_ref[rows, :wide] = (cos_part * real + sin_part * imag).astype(BF16)
-        shifted_ref[rows, wide:] = (cos_part * imag - sin_part * real).astype(BF16)
-
-
-def norm_of(square_ref, powers):
-    power = jnp.concatenate(powers, axis=0)
-    count, classes_count = power.shape[0], square_ref.shape[0] // 2
-    table = lax.dot_general(
-        square_ref[...], split_terms(power), NT_DIMS, preferred_element_type=F32
-    )
-    return (
+def score_pieces(weighted_ref, banks, cos_ref, sin_ref, square_ref, n_proj):
+    shifts, wide = cos_ref.shape
+    classes_count = square_ref.shape[0] // 2
+    step = 256 if wide % 256 == 0 else 128
+    cross, table = None, None
+    for at in range(0, wide, step):
+        span = slice(at, at + step)
+        reals, imags = [], []
+        for bank in banks:
+            for first in range(0, bank.shape[0], 2 * n_proj):
+                both = bank[first : first + 2 * n_proj, span].astype(F32)
+                reals.append(both[:n_proj])
+                imags.append(both[n_proj:])
+        real, imag = jnp.concatenate(reals, axis=0), jnp.concatenate(imags, axis=0)
+        real_rows, imag_rows = [], []
+        for t in range(shifts):
+            cos_part, sin_part = cos_ref[t : t + 1, span], sin_ref[t : t + 1, span]
+            real_rows.append((cos_part * real + sin_part * imag).astype(BF16))
+            imag_rows.append((cos_part * imag - sin_part * real).astype(BF16))
+        terms = lax.dot_general(
+            weighted_ref[:, span],
+            jnp.concatenate(real_rows, axis=0),
+            NT_DIMS,
+            preferred_element_type=F32,
+        ) + lax.dot_general(
+            weighted_ref[:, wide + at : wide + at + step],
+            jnp.concatenate(imag_rows, axis=0),
+            NT_DIMS,
+            preferred_element_type=F32,
+        )
+        power = split_terms(real * real + imag * imag)
+        norms = lax.dot_general(
+            square_ref[:, span], power, NT_DIMS, preferred_element_type=F32
+        )
+        cross = terms if cross is None else cross + terms
+        table = norms if table is None else table + norms
+    count = table.shape[1] // 2
+    table = (
         table[:classes_count, count:] + table[classes_count:, :count] + table[:classes_count, :count]
     )
-
-
-def shift_bank(banks, shifted_ref, cos_ref, sin_ref, square_ref, n_proj):
-    powers = []
-    for bank in banks:
-        for n in range(bank.shape[0] // (2 * n_proj)):
-            both = bank[2 * n_proj * n : 2 * n_proj * (n + 1)].astype(F32)
-            real, imag = both[:n_proj], both[n_proj:]
-            shift_rows(shifted_ref, cos_ref, sin_ref, real, imag, len(powers))
-            powers.append(real * real + imag * imag)
-    return norm_of(square_ref, powers)
-
-
-def shift_kernel(n_proj, cos_ref, sin_ref, square_ref, *rest):
-    *banks, shifted_ref, norm_ref = rest
-    norm_ref[...] = shift_bank(banks, shifted_ref, cos_ref, sin_ref, square_ref, n_proj)
+    return cross, table
+
+
+def in_lanes(values, blk, bits, n_proj, lanes):
+    if values.shape[1] < lanes:
+        zeros = jnp.zeros((values.shape[0], lanes - values.shape[1]), F32)
+        values = jnp.concatenate([values, zeros], axis=1)
+    lane = lax.broadcasted_iota(jnp.int32, values.shape, 1)
+    for bit in bits:
+        step = bit * n_proj
+        other = jnp.where(
+            (lane & step) != 0, pltpu.roll(values, step, 1), pltpu.roll(values, lanes - step, 1)
+        )
+        values = jnp.where((blk & bit) != 0, other, values)
+    return values
 
 
 def added_rows(extra, table, banks, n_proj, length, subsets):
@@ -206,21 +226,11 @@
     return prior - 0.5 * norm
 
 
-def score_rows(weighted, shifted, added, n_proj):
-    cross = lax.dot_general(weighted, shifted, NT_DIMS, preferred_element_type=F32)
-    pieces = added.shape[1] // n_proj
-    width = cross.shape[1] // pieces
-    rows = []
-    for n in range(pieces):
-        rows += [cross[:, n * width : (n + 1) * width], added[:, n * n_proj : (n + 1) * n_proj]]
-    return jnp.concatenate(rows, axis=1)
-
-
 def early_kernel(
-    n_parts, ng, weights, n_part, n_proj, length, subsets, shifted_ref, norm_ref, *rest
+    n_parts, ng, weights, bits, n_part, n_proj, length, subsets, cos_ref, sin_ref, square_ref, *rest
 ):
     parts, (*banks, weighted_ref, extra_ref, rows_ref) = rest[:n_parts], rest[n_parts:]
-    g = lax.axis_index("grp")
+    blk, g = lax.axis_index("blk"), lax.axis_index("grp")
     wide = weighted_ref.shape[1] // 2
 
     held = jnp.concatenate([part[...] for part in parts], axis=0)
@@ -238,67 +248,44 @@
     weighted_ref[:, wide:] = ordered[count:, :wide].astype(BF16)
     extra = ordered[:count, wide:]
     extra_ref[...] = extra
-    added = added_rows(extra, norm_ref[...], banks, n_proj, length, subsets)
-    rows_ref[...] = score_rows(weighted_ref[...], shifted_ref[...], added, n_proj)
+    cross, table = score_pieces(weighted_ref, banks, cos_ref, sin_ref, square_ref, n_proj)
+    added = added_rows(extra, table, banks, n_proj, length, subsets)
+    rows = jnp.concatenate([cross, added], axis=1)
+    rows_ref[...] = in_lanes(rows, blk, bits, n_proj, rows_ref.shape[1])
 
 
 def final_kernel(
-    n_proj, length, subsets, weighted_ref, extra_ref, rows_ref, cos_ref, sin_ref, square_ref, last_ref, *rest
+    bits, n_proj, length, subsets, weighted_ref, extra_ref, rows_ref, cos_ref, sin_ref, square_ref, last_ref, *outs
 ):
-    *outs, shifted_ref = rest
-    table = shift_bank([last_ref], shifted_ref, cos_ref, sin_ref, square_ref, n_proj)
+    blk = lax.axis_index("blk")
+    cross, table = score_pieces(weighted_ref, [last_ref], cos_ref, sin_ref, square_ref, n_proj)
     added = added_rows(extra_ref[...], table, [last_ref], n_proj, length, subsets)
-    rows = score_rows(weighted_ref[...], shifted_ref[...], added, n_proj)
-    rows = jnp.concatenate([rows_ref[...], rows], axis=1)
-    dest, lanes = outs[0].shape
-    if rows.shape[1] < lanes:
-        zeros = jnp.zeros((rows.shape[0], lanes - rows.shape[1]), F32)
-        rows = jnp.concatenate([rows, zeros], axis=1)
+    rows = jnp.concatenate([cross, added], axis=1)
+    dest, lanes = outs[0].shape[0], rows_ref.shape[1]
+    rows = in_lanes(rows, blk, bits, n_proj, lanes)
     for s, out in enumerate(outs):
-        out[...] = rows[s * dest : (s + 1) * dest]
-
-
-def place_kernel(half, n_proj, order, keep_ref, recv_ref, out_ref):
+        out[:, :lanes] = rows_ref[s * dest : (s + 1) * dest, :]
+        out[:, lanes:] = rows[s * dest : (s + 1) * dest]
+
+
+def place_kernel(half, keep_ref, recv_ref, out_ref):
     blk = lax.axis_index("blk")
-    first = blk < half
-    low = jnp.where(first, keep_ref[...], recv_ref[...])
-    high = jnp.where(first, recv_ref[...], keep_ref[...])
-    shifts = out_ref.shape[0]
-    width = (shifts + 1) * n_proj
-
-    def by_shift(values):
-        found = {offset: values[:, n * width : (n + 1) * width] for n, offset in enumerate(order)}
-        lined = []
-        for t in range(shifts + 1):
-            span = slice(t * n_proj, (t + 1) * n_proj)
-            lined += [found[offset][:, span] for offset in range(half)]
-        return jnp.concatenate(lined, axis=1)
-
-    def exchanged(values):
-        total = (shifts + 1) * half * n_proj
-        lanes = 128 * -(-total // 128)
-        if lanes > total:
-            zeros = jnp.zeros((values.shape[0], lanes - total), F32)
-            values = jnp.concatenate([values, zeros], axis=1)
-        lane = lax.broadcasted_iota(jnp.int32, values.shape, 1)
-        bit = 1
-        while bit < half:
-            step = bit * n_proj
-            other = jnp.where(
-                (lane & step) != 0, pltpu.roll(values, step, 1), pltpu.roll(values, lanes - step, 1)
-            )
-            values = jnp.where((blk & bit) != 0, other, values)
-            bit *= 2
-        return values
-
-    low, high = exchanged(by_shift(low)), exchanged(by_shift(high))
-    span = half * n_proj
-    lined = [
-        jnp.concatenate([low[:, t * span : (t + 1) * span], high[:, t * span : (t + 1) * span]], axis=1)
-        for t in range(shifts + 1)
-    ]
+    own_first, early_first = blk < half, (blk & (half // 2)) == 0
+    keep, recv = keep_ref[...], recv_ref[...]
+    lanes = keep.shape[1] // 2
+    parts = []
+    for values in (jnp.where(own_first, keep, recv), jnp.where(own_first, recv, keep)):
+        early, late = values[:, :lanes], values[:, lanes:]
+        parts += [jnp.where(early_first, early, late), jnp.where(early_first, late, early)]
+    shifts, _, width = out_ref.shape
+    width = width // 4
+
+    def line(t):
+        return jnp.concatenate([part[:, t * width : (t + 1) * width] for part in parts], axis=1)
+
+    added = line(shifts)
     for t in range(shifts):
-        out_ref[t] = lined[t] + lined[shifts]
+        out_ref[t] = line(t) + added
 
 
 def per_device(
@@ -370,19 +357,12 @@
     def joined(pieces):
         return pieces[0] if len(pieces) == 1 else jnp.concatenate(pieces, axis=0)
 
-    parts, weights = [part, swap(part, "blk", half)], []
-    for n in range(ng.bit_length() - 2, -1, -1):
-        part = joined(parts)
-        parts = [part, swap(part, "grp", 1 << n)]
-        weights.append((1 << n, 2 << len(weights)))
-
-    planes, early_order, bit = [bank], [0], 1
+    across = swap(part, "blk", half)
+    planes, bit = [bank], 1
     while 2 * bit < half:
         planes.append(swap(joined(planes), "blk", bit))
-        early_order += [offset ^ bit for offset in early_order]
         bit *= 2
     last = swap(joined(planes), "blk", bit)
-    order = early_order + [offset ^ bit for offset in early_order]
 
     cos_part, sin_part, square = pl.pallas_call(
         table_kernel,
@@ -398,54 +378,47 @@
         name="tables",
     )(curves, noise, angle)
 
+    across, planes[-1], cos_part = lax.optimization_barrier((across, planes[-1], cos_part))
+    parts, weights = [part, across], []
+    for n in range(ng.bit_length() - 2, -1, -1):
+        part = joined(parts)
+        parts = [part, swap(part, "grp", 1 << n)]
+        weights.append((1 << n, 2 << len(weights)))
+
     count = 2 * ng * n_part
-    early = late = len(early_order) * n_proj
-    shifted, norm = pl.pallas_call(
-        functools.partial(shift_kernel, n_proj),
-        out_shape=[
-            vmem_out((shifts * early, 2 * wide), BF16),
-            vmem_out((classes_count, early), F32),
-        ],
-        in_specs=[_vmem()] * (3 + len(planes)),
-        out_specs=[_vmem()] * 2,
-        compiler_params=_params(8),
-        cost_estimate=pl.CostEstimate(
-            flops=6 * early * shifts * wide, bytes_accessed=4_000_000, transcendentals=0
-        ),
-        name="shift",
-    )(cos_part, sin_part, square, *planes)
+    early = half // 2 * n_proj
+    lanes = 128 * -(-(shifts + 1) * early // 128)
+    bits = [1 << n for n in range(half.bit_length() - 2)]
     weighted, extra_rows, rows = pl.pallas_call(
         functools.partial(
-            early_kernel, len(parts), ng, weights, n_part, n_proj, length, subsets
+            early_kernel, len(parts), ng, weights, bits, n_part, n_proj, length, subsets
         ),
         out_shape=[
             vmem_out((count, 2 * wide), BF16),
             vmem_out((count, extra), F32),
-            vmem_out((count, (shifts + 1) * early), F32),
+            vmem_out((count, lanes), F32),
         ],
-        in_specs=[_vmem()] * (2 + len(parts) + len(planes)),
+        in_specs=[_vmem()] * (3 + len(parts) + len(planes)),
         out_specs=[_vmem()] * 3,
-        compiler_params=_params(8),
+        compiler_params=_params(16),
         cost_estimate=pl.CostEstimate(
             flops=4 * count * early * shifts * wide, bytes_accessed=4_000_000, transcendentals=0
         ),
         name="early",
-    )(shifted, norm, *parts, *planes)
-    lanes = 128 * -(-(shifts + 1) * half * n_proj // 128)
+    )(cos_part, sin_part, square, *parts, *planes)
     keep, give = pl.pallas_call(
-        functools.partial(final_kernel, n_proj, length, subsets),
-        out_shape=[vmem_out((ng * n_part, lanes), F32)] * 2,
+        functools.partial(final_kernel, bits, n_proj, length, subsets),
+        out_shape=[vmem_out((ng * n_part, 2 * lanes), F32)] * 2,
         in_specs=[_vmem()] * 7,
         out_specs=[_vmem()] * 2,
-        scratch_shapes=[pltpu.VMEM((shifts * late, 2 * wide), BF16)],
-        compiler_params=_params(24),
+        compiler_params=_params(16),
         cost_estimate=pl.CostEstimate(
-            flops=4 * count * late * shifts * wide, bytes_accessed=4_000_000, transcendentals=0
+            flops=4 * count * early * shifts * wide, bytes_accessed=4_000_000, transcendentals=0
         ),
         name="final",
     )(weighted, extra_rows, rows, cos_part, sin_part, square, last)
     scores = pl.pallas_call(
-        functools.partial(place_kernel, half, n_proj, order),
+        functools.partial(place_kernel, half),
         out_shape=shape((shifts, ng * n_part, nb * n_proj), F32),
         in_specs=[_vmem()] * 2,
         out_specs=_vmem(),

time: 25.1 us -> 24.5 us (0.976)
  Pallas kernels: 7.33 us -> 5.81 us
  starting transfers between devices: 10.7 us -> 11.6 us
    pallas_call x4 -> x3, Pallas kernels: 5.17 us -> 3.65 us  [the longest x1 1.52 us: per_device(): pl.pallas_call(functools.partial(early_kernel, len(parts), ng, weights, b...]
    ppermute x6, starting transfers between devices: 10.7 us -> 11.6 us  [swap(): return lax.ppermute(value, axis, [(i, i ^ bit) for i in range(size)])]
  transfers between devices with their start and end apart: 6 -> 6, of which waited for: 5 -> 5; matrix products, arithmetic and copies ran while one was open for 0% -> 0% of each run, Pallas kernels for 11% -> 9%
where the time goes in v10:
time: 24.5 us; the launch traced here: 24.3 us
  starting transfers between devices  11.6 us (47%)
  waiting for transfers between devices  6.78 us (28%)
  Pallas kernels  5.81 us (24%)
    ppermute x6, starting transfers between devices, swap(): return lax.ppermute(value, axis, [(i, i ^ bit) for i in range(size)])  11.6 us
    ppermute x6, waiting for transfers between devices, swap(): return lax.ppermute(value, axis, [(i, i ^ bit) for i in range(size)])  6.78 us
    pallas_call x1, Pallas kernels, per_device(): pl.pallas_call(pack_kernel, out_shape=[vmem_out((2 * n_proj, wide), BF16)...  1.58 us
    pallas_call x1, Pallas kernels, per_device(): pl.pallas_call(functools.partial(early_kernel, len(parts), ng, weights, b...  1.52 us
    pallas_call x1, Pallas kernels, per_device(): pl.pallas_call(functools.partial(final_kernel, bits, n_proj, length, subs...  1.4 us
    pallas_call x1, Pallas kernels, per_device(): pl.pallas_call(functools.partial(place_kernel, half), out_shape=shape((sh...  0.72 us
    pallas_call x1, Pallas kernels, per_device(): pl.pallas_call(table_kernel, out_shape=[vmem_out((shifts, wide), F32), vm...  0.59 us
  transfers between devices with their start and end apart: 6, of which 5 were waited for; matrix products, arithmetic and copies ran while one was open for 0% of the time, Pallas kernels for 9%

profile of v10, /device:TPU:0, one launch (start us, length us, event | category | flops | bytes accessed | tf_op | source)
XLA Modules:
  0.0 24.3 jit_solution(7845012592752114155)
XLA Ops:
  0.0 1.6 %pack.1 = (bf16[16,4096]{1,0:T(8,128)(2,1)S(1)}, bf16[4,4352]{1,0:T(4,128)(2,1)S(1)}, f32[64,4000]{1,0:T(8,128)S(1)}, f32[1,4000]{1,0:T(1,128)S(1)}, f32[9,4000]{1,0:T(8,128)S(1)}) custom-call(s32[2]{0:T(128)} %class_hbm.1, s32[8]{0:T(128)} %subset_hbm.1, bf16[2,2,4000]{2,1,0:T(2,128)(2,1)} %particles_hbm.1, bf16[2,192]{1,0:T(2,128)(2,1)} %prior_hbm.1, ...), custom_call_target="tpu_custom_call" | custom-call | tf_op jit(solution)/shard_map/pack/pallas_call | solution.py:328
  1.6 3.0 %collective-permute-start.1 = (bf16[16,4096]{1,0:T(8,128)(2,1)S(1)}, bf16[16,4096]{1,0:T(8,128)(2,1)S(1)}, u32[]{:S(2)}, u32[]{:S(2)}) collective-permute-start(bf16[16,4096]{1,0:T(8,128)(2,1)S(1)} %get-tuple-element.22.rest_2_), channel_id=1, source_target_pairs={{0,1},{1,0},{2,3},{3,2},{4,5},{5,4},{6,7},{7,6},{8,9},{9,8},{10,11... | collective-permute-start | bytes 393224 | tf_op jit(solution)/shard_map/ppermute | solution.py:355
  4.6 2.6 %collective-permute-start = (bf16[4,4352]{1,0:T(4,128)(2,1)S(1)}, bf16[4,4352]{1,0:T(4,128)(2,1)S(1)}, u32[]{:S(2)}, u32[]{:S(2)}) collective-permute-start(bf16[4,4352]{1,0:T(4,128)(2,1)S(1)} %get-tuple-element.21), channel_id=1, source_target_pairs={{0,4},{1,5},{2,6},{3,7},{4,0},{5,1},{6,2},{7,3},{8,12},{9,13},{10,... | collective-permute-start | bytes 104456 | tf_op jit(solution)/shard_map/ppermute | solution.py:355
  7.2 0.6 %tables.1 = (f32[9,4096]{1,0:T(8,128)S(1)}, f32[9,4096]{1,0:T(8,128)S(1)}, bf16[128,4096]{1,0:T(8,128)(2,1)S(1)}) custom-call(f32[64,4000]{1,0:T(8,128)S(1)} %get-tuple-element.23.curves_ref, f32[1,4000]{1,0:T(1,128)S(1)} %get-tuple-element.24.noise_ref, f32[9,4000]{1,0:T(8,128)S(1)} %get-tuple-element.25.angle_ref), custom_call_target="tpu_custom_call" | custom-call | flops 4000000 | bytes 2000000 | tf_op jit(solution)/shard_map/tables/pallas_call | solution.py:367
  7.8 1.7 %collective-permute-done = bf16[4,4352]{1,0:T(4,128)(2,1)S(1)} collective-permute-done((bf16[4,4352]{1,0:T(4,128)(2,1)S(1)}, bf16[4,4352]{1,0:T(4,128)(2,1)S(1)}, u32[]{:S(2)}, u32[]{:S(2)}) %collective-permute-start) | collective-permute-done | bytes 34848 | tf_op jit(solution)/shard_map/ppermute | solution.py:355
  9.5 0.0 collective-permute-done.1.rest_3_
  9.5 1.6 %collective-permute-start.2 = (bf16[8,4352]{1,0:T(8,128)(2,1)S(1)}, bf16[8,4352]{1,0:T(8,128)(2,1)S(1)}, u32[]{:S(2)}, u32[]{:S(2)}) collective-permute-start(bf16[8,4352]{1,0:T(8,128)(2,1)S(1)} %pad_maximum_fusion.2), channel_id=1, source_target_pairs={{0,16},{8,24},{16,0},{24,8},{1,17},{9,25},{17,1},{25,9},{2,18},{10... | collective-permute-start | bytes 208904 | tf_op jit(solution)/shard_map/ppermute | solution.py:355
  11.1 1.6 %collective-permute-start.4 = (bf16[32,4096]{1,0:T(8,128)(2,1)S(1)}, bf16[32,4096]{1,0:T(8,128)(2,1)S(1)}, u32[]{:S(2)}, u32[]{:S(2)}) collective-permute-start(bf16[32,4096]{1,0:T(8,128)(2,1)S(1)} %pad_maximum_fusion), channel_id=1, source_target_pairs={{0,2},{1,3},{2,0},{3,1},{4,6},{5,7},{6,4},{7,5},{8,10},{9,11},{10,... | collective-permute-start | bytes 786440 | tf_op jit(solution)/shard_map/ppermute | solution.py:355
  12.7 1.2 %collective-permute-done.2 = bf16[8,4352]{1,0:T(8,128)(2,1)S(1)} collective-permute-done((bf16[8,4352]{1,0:T(8,128)(2,1)S(1)}, bf16[8,4352]{1,0:T(8,128)(2,1)S(1)}, u32[]{:S(2)}, u32[]{:S(2)}) %collective-permute-start.2) | collective-permute-done | bytes 69664 | tf_op jit(solution)/shard_map/ppermute | solution.py:355
  13.9 0.1 pad_maximum_fusion.1.rest_0_
  13.9 0.1 collective-permute-start.3
  14.0 1.3 %collective-permute-done.3.rest_1_ = bf16[16,4352]{1,0:T(8,128)(2,1)S(1)} collective-permute-done((bf16[16,4352]{1,0:T(8,128)(2,1)S(1)}, bf16[16,4352]{1,0:T(8,128)(2,1)S(1)}, u32[]{:S(2)}, u32[]{:S(2)}) %collective-permute-start.3) | collective-permute-done | bytes 139296 | tf_op jit(solution)/shard_map/ppermute | solution.py:355
  15.4 1.5 %early.1 = (bf16[16,8192]{1,0:T(8,128)(2,1)S(1)}, f32[16,256]{1,0:T(8,128)S(1)}, f32[16,256]{1,0:T(8,128)S(1)}) custom-call(f32[9,4096]{1,0:T(8,128)S(1)} %get-tuple-element.27.cos_ref, f32[9,4096]{1,0:T(8,128)S(1)} %get-tuple-element.28.sin_ref, bf16[128,4096]{1,0:T(8,128)(2,1)S(1)} %get-tuple-element.29.square_ref, ...), custom_call_target="tpu_custom_call" | custom-call | flops 37748736 | bytes 4000000 | tf_op jit(solution)/shard_map/early/pallas_call | solution.py:392
  16.9 0.6 %collective-permute-done.4.last_ref = bf16[32,4096]{1,0:T(8,128)(2,1)S(1)} collective-permute-done((bf16[32,4096]{1,0:T(8,128)(2,1)S(1)}, bf16[32,4096]{1,0:T(8,128)(2,1)S(1)}, u32[]{:S(2)}, u32[]{:S(2)}) %collective-permute-start.4) | collective-permute-done | bytes 262176 | tf_op jit(solution)/shard_map/ppermute | solution.py:355
  17.5 1.4 %final.1 = (f32[8,512]{1,0:T(8,128)S(1)}, f32[8,512]{1,0:T(8,128)S(1)}) custom-call(bf16[16,8192]{1,0:T(8,128)(2,1)S(1)} %get-tuple-element.32.weighted_ref, f32[16,256]{1,0:T(8,128)S(1)} %get-tuple-element.33.extra_ref, f32[16,256]{1,0:T(8,128)S(1)} %get-tuple-element.34.rows_ref, f32[9,4096]{1,0:T(8,128)S(1)} %get-tuple-element.27.cos_ref, ...), custom_call_target="tpu_custom_call" | custom-call | flops 37748736 | bytes 4000000 | tf_op jit(solution)/shard_map/final/pallas_call | solution.py:409
  18.9 2.7 %collective-permute-start.5 = (f32[8,512]{1,0:T(8,128)S(1)}, f32[8,512]{1,0:T(8,128)S(1)}, u32[]{:S(2)}, u32[]{:S(2)}) collective-permute-start(f32[8,512]{1,0:T(8,128)S(1)} %get-tuple-element.36), channel_id=1, source_target_pairs={{0,4},{1,5},{2,6},{3,7},{4,0},{5,1},{6,2},{7,3},{8,12},{9,13},{10,... | collective-permute-start | bytes 49160 | tf_op jit(solution)/shard_map/ppermute | solution.py:355
  21.6 2.0 %collective-permute-done.5.recv_ref = f32[8,512]{1,0:T(8,128)S(1)} collective-permute-done((f32[8,512]{1,0:T(8,128)S(1)}, f32[8,512]{1,0:T(8,128)S(1)}, u32[]{:S(2)}, u32[]{:S(2)}) %collective-permute-start.5) | collective-permute-done | bytes 16416 | tf_op jit(solution)/shard_map/ppermute | solution.py:355
  23.6 0.7 %place.1 = f32[9,8,64]{2,1,0:T(8,128)} custom-call(f32[8,512]{1,0:T(8,128)S(1)} %get-tuple-element.35.keep_ref, f32[8,512]{1,0:T(8,128)S(1)} %collective-permute-done.5.recv_ref), custom_call_target="tpu_custom_call" | custom-call | tf_op jit(solution)/shard_map/place/pallas_call | solution.py:420
  (2 shorter events, 0.1 us)
Async XLA Ops:
  1.6 7.9 %collective-permute-start.1 = (bf16[16,4096]{1,0:T(8,128)(2,1)S(1)}, bf16[16,4096]{1,0:T(8,128)(2,1)S(1)}, u32[]{:S(2)}, u32[]{:S(2)}) collective-permute-start(bf16[16,4096]{1,0:T(8,128)(2,1)S(1)} %get-tuple-element.22.rest_2_), channel_id=1, source_target_pairs={{0,1},{1,0},{2,3},{3,2},{4,5},{5,4},{6,7},{7,6},{8,9},{9,8},{10,11... | collective-permute-start | bytes 393224 | tf_op jit(solution)/shard_map/ppermute | solution.py:355
  4.6 4.8 %collective-permute-start = (bf16[4,4352]{1,0:T(4,128)(2,1)S(1)}, bf16[4,4352]{1,0:T(4,128)(2,1)S(1)}, u32[]{:S(2)}, u32[]{:S(2)}) collective-permute-start(bf16[4,4352]{1,0:T(4,128)(2,1)S(1)} %get-tuple-element.21), channel_id=1, source_target_pairs={{0,4},{1,5},{2,6},{3,7},{4,0},{5,1},{6,2},{7,3},{8,12},{9,13},{10,... | collective-permute-start | bytes 104456 | tf_op jit(solution)/shard_map/ppermute | solution.py:355
  9.5 4.4 %collective-permute-start.2 = (bf16[8,4352]{1,0:T(8,128)(2,1)S(1)}, bf16[8,4352]{1,0:T(8,128)(2,1)S(1)}, u32[]{:S(2)}, u32[]{:S(2)}) collective-permute-start(bf16[8,4352]{1,0:T(8,128)(2,1)S(1)} %pad_maximum_fusion.2), channel_id=1, source_target_pairs={{0,16},{8,24},{16,0},{24,8},{1,17},{9,25},{17,1},{25,9},{2,18},{10... | collective-permute-start | bytes 208904 | tf_op jit(solution)/shard_map/ppermute | solution.py:355
  11.1 6.4 %collective-permute-start.4 = (bf16[32,4096]{1,0:T(8,128)(2,1)S(1)}, bf16[32,4096]{1,0:T(8,128)(2,1)S(1)}, u32[]{:S(2)}, u32[]{:S(2)}) collective-permute-start(bf16[32,4096]{1,0:T(8,128)(2,1)S(1)} %pad_maximum_fusion), channel_id=1, source_target_pairs={{0,2},{1,3},{2,0},{3,1},{4,6},{5,7},{6,4},{7,5},{8,10},{9,11},{10,... | collective-permute-start | bytes 786440 | tf_op jit(solution)/shard_map/ppermute | solution.py:355
  13.9 1.4 %collective-permute-start.3 = (bf16[16,4352]{1,0:T(8,128)(2,1)S(1)}, bf16[16,4352]{1,0:T(8,128)(2,1)S(1)}, u32[]{:S(2)}, u32[]{:S(2)}) collective-permute-start(bf16[16,4352]{1,0:T(8,128)(2,1)S(1)} %pad_maximum_fusion.1.rest_0_), channel_id=1, source_target_pairs={{0,8},{8,0},{16,24},{24,16},{1,9},{9,1},{17,25},{25,17},{2,10},{10... | collective-permute-start | bytes 417800 | tf_op jit(solution)/shard_map/ppermute | solution.py:355
  18.9 4.7 %collective-permute-start.5 = (f32[8,512]{1,0:T(8,128)S(1)}, f32[8,512]{1,0:T(8,128)S(1)}, u32[]{:S(2)}, u32[]{:S(2)}) collective-permute-start(f32[8,512]{1,0:T(8,128)S(1)} %get-tuple-element.36), channel_id=1, source_target_pairs={{0,4},{1,5},{2,6},{3,7},{4,0},{5,1},{6,2},{7,3},{8,12},{9,13},{10,... | collective-permute-start | bytes 49160 | tf_op jit(solution)/shard_map/ppermute | solution.py:355

commit v11 on v10

--- a/solution.py
+++ b/solution.py
@@ -364,6 +364,12 @@
         bit *= 2
     last = swap(joined(planes), "blk", bit)
 
+    parts, weights = [part, across], []
+    for n in range(ng.bit_length() - 2, -1, -1):
+        part = joined(parts)
+        parts = [part, swap(part, "grp", 1 << n)]
+        weights.append((1 << n, 2 << len(weights)))
+
     cos_part, sin_part, square = pl.pallas_call(
         table_kernel,
         out_shape=[
@@ -377,13 +383,6 @@
         cost_estimate=pl.CostEstimate(flops=4_000_000, bytes_accessed=2_000_000, transcendentals=0),
         name="tables",
     )(curves, noise, angle)
-
-    across, planes[-1], cos_part = lax.optimization_barrier((across, planes[-1], cos_part))
-    parts, weights = [part, across], []
-    for n in range(ng.bit_length() - 2, -1, -1):
-        part = joined(parts)
-        parts = [part, swap(part, "grp", 1 << n)]
-        weights.append((1 << n, 2 << len(weights)))
 
     count = 2 * ng * n_part
     early = half // 2 * n_proj

time: 24.5 us -> 24.3 us (level)
  starting transfers between devices: 11.6 us -> 10.7 us
  waiting for transfers between devices: 6.78 us -> 7.5 us
    ppermute x6, starting transfers between devices: 11.6 us -> 10.7 us  [swap(): return lax.ppermute(value, axis, [(i, i ^ bit) for i in range(size)])]
    ppermute x6, waiting for transfers between devices: 6.78 us -> 7.5 us  [swap(): return lax.ppermute(value, axis, [(i, i ^ bit) for i in range(size)])]
  transfers between devices with their start and end apart: 6 -> 6, of which waited for: 5 -> 6; matrix products, arithmetic and copies ran while one was open for 0% -> 1% of each run, Pallas kernels for 9% -> 9%
where the time goes in v11:
time: 24.3 us; the launch traced here: 24.2 us
  starting transfers between devices  10.7 us (44%)
  waiting for transfers between devices  7.5 us (31%)
  Pallas kernels  5.81 us (24%)
    ppermute x6, starting transfers between devices, swap(): return lax.ppermute(value, axis, [(i, i ^ bit) for i in range(size)])  10.7 us
    ppermute x6, waiting for transfers between devices, swap(): return lax.ppermute(value, axis, [(i, i ^ bit) for i in range(size)])  7.5 us
    pallas_call x1, Pallas kernels, per_device(): pl.pallas_call(pack_kernel, out_shape=[vmem_out((2 * n_proj, wide), BF16)...  1.58 us
    pallas_call x1, Pallas kernels, per_device(): pl.pallas_call(functools.partial(early_kernel, len(parts), ng, weights, b...  1.52 us
    pallas_call x1, Pallas kernels, per_device(): pl.pallas_call(functools.partial(final_kernel, bits, n_proj, length, subs...  1.4 us
    pallas_call x1, Pallas kernels, per_device(): pl.pallas_call(functools.partial(place_kernel, half), out_shape=shape((sh...  0.72 us
    pallas_call x1, Pallas kernels, per_device(): pl.pallas_call(table_kernel, out_shape=[vmem_out((shifts, wide), F32), vm...  0.58 us
  transfers between devices with their start and end apart: 6, of which 6 were waited for; matrix products, arithmetic and copies ran while one was open for 1% of the time, Pallas kernels for 9%

profile of v11, /device:TPU:0, one launch (start us, length us, event | category | flops | bytes accessed | tf_op | source)
XLA Modules:
  0.0 24.2 jit_solution(11477477485385997824)
XLA Ops:
  0.0 1.6 %pack.1 = (bf16[16,4096]{1,0:T(8,128)(2,1)S(1)}, bf16[4,4352]{1,0:T(4,128)(2,1)S(1)}, f32[64,4000]{1,0:T(8,128)S(1)}, f32[1,4000]{1,0:T(1,128)S(1)}, f32[9,4000]{1,0:T(8,128)S(1)}) custom-call(s32[2]{0:T(128)} %class_hbm.1, s32[8]{0:T(128)} %subset_hbm.1, bf16[2,2,4000]{2,1,0:T(2,128)(2,1)} %particles_hbm.1, bf16[2,192]{1,0:T(2,128)(2,1)} %prior_hbm.1, ...), custom_call_target="tpu_custom_call" | custom-call | tf_op jit(solution)/shard_map/pack/pallas_call | solution.py:328
  1.6 4.1 %collective-permute-start = (bf16[4,4352]{1,0:T(4,128)(2,1)S(1)}, bf16[4,4352]{1,0:T(4,128)(2,1)S(1)}, u32[]{:S(2)}, u32[]{:S(2)}) collective-permute-start(bf16[4,4352]{1,0:T(4,128)(2,1)S(1)} %get-tuple-element.24), channel_id=1, source_target_pairs={{0,4},{1,5},{2,6},{3,7},{4,0},{5,1},{6,2},{7,3},{8,12},{9,13},{10,... | collective-permute-start | bytes 104456 | tf_op jit(solution)/shard_map/ppermute | solution.py:355
  5.7 1.5 %collective-permute-start.3 = (bf16[16,4096]{1,0:T(8,128)(2,1)S(1)}, bf16[16,4096]{1,0:T(8,128)(2,1)S(1)}, u32[]{:S(2)}, u32[]{:S(2)}) collective-permute-start(bf16[16,4096]{1,0:T(8,128)(2,1)S(1)} %get-tuple-element.25.rest_2_), channel_id=1, source_target_pairs={{0,1},{1,0},{2,3},{3,2},{4,5},{5,4},{6,7},{7,6},{8,9},{9,8},{10,11... | collective-permute-start | bytes 393224 | tf_op jit(solution)/shard_map/ppermute | solution.py:355
  7.2 0.8 %collective-permute-done = bf16[4,4352]{1,0:T(4,128)(2,1)S(1)} collective-permute-done((bf16[4,4352]{1,0:T(4,128)(2,1)S(1)}, bf16[4,4352]{1,0:T(4,128)(2,1)S(1)}, u32[]{:S(2)}, u32[]{:S(2)}) %collective-permute-start) | collective-permute-done | bytes 34848 | tf_op jit(solution)/shard_map/ppermute | solution.py:355
  8.0 1.8 %collective-permute-start.1 = (bf16[8,4352]{1,0:T(8,128)(2,1)S(1)}, bf16[8,4352]{1,0:T(8,128)(2,1)S(1)}, u32[]{:S(2)}, u32[]{:S(2)}) collective-permute-start(bf16[8,4352]{1,0:T(8,128)(2,1)S(1)} %pad_maximum_fusion.2), channel_id=1, source_target_pairs={{0,16},{8,24},{16,0},{24,8},{1,17},{9,25},{17,1},{25,9},{2,18},{10... | collective-permute-start | bytes 208904 | tf_op jit(solution)/shard_map/ppermute | solution.py:355
  9.8 0.9 %collective-permute-done.3.rest_3_ = bf16[16,4096]{1,0:T(8,128)(2,1)S(1)} collective-permute-done((bf16[16,4096]{1,0:T(8,128)(2,1)S(1)}, bf16[16,4096]{1,0:T(8,128)(2,1)S(1)}, u32[]{:S(2)}, u32[]{:S(2)}) %collective-permute-start.3) | collective-permute-done | bytes 131104 | tf_op jit(solution)/shard_map/ppermute | solution.py:355
  10.7 1.6 %collective-permute-start.4 = (bf16[32,4096]{1,0:T(8,128)(2,1)S(1)}, bf16[32,4096]{1,0:T(8,128)(2,1)S(1)}, u32[]{:S(2)}, u32[]{:S(2)}) collective-permute-start(bf16[32,4096]{1,0:T(8,128)(2,1)S(1)} %pad_maximum_fusion), channel_id=1, source_target_pairs={{0,2},{1,3},{2,0},{3,1},{4,6},{5,7},{6,4},{7,5},{8,10},{9,11},{10,... | collective-permute-start | bytes 786440 | tf_op jit(solution)/shard_map/ppermute | solution.py:355
  12.3 0.1 collective-permute-done.1
  12.4 0.1 pad_maximum_fusion.1.rest_0_
  12.5 0.1 collective-permute-start.2
  12.5 0.6 %tables.1 = (f32[9,4096]{1,0:T(8,128)S(1)}, f32[9,4096]{1,0:T(8,128)S(1)}, bf16[128,4096]{1,0:T(8,128)(2,1)S(1)}) custom-call(f32[64,4000]{1,0:T(8,128)S(1)} %get-tuple-element.18.curves_ref, f32[1,4000]{1,0:T(1,128)S(1)} %get-tuple-element.19.noise_ref, f32[9,4000]{1,0:T(8,128)S(1)} %get-tuple-element.20.angle_ref), custom_call_target="tpu_custom_call" | custom-call | flops 4000000 | bytes 2000000 | tf_op jit(solution)/shard_map/tables/pallas_call | solution.py:373
  13.1 0.8 %collective-permute-done.2.rest_1_ = bf16[16,4352]{1,0:T(8,128)(2,1)S(1)} collective-permute-done((bf16[16,4352]{1,0:T(8,128)(2,1)S(1)}, bf16[16,4352]{1,0:T(8,128)(2,1)S(1)}, u32[]{:S(2)}, u32[]{:S(2)}) %collective-permute-start.2) | collective-permute-done | bytes 139296 | tf_op jit(solution)/shard_map/ppermute | solution.py:355
  13.9 1.5 %early.1 = (bf16[16,8192]{1,0:T(8,128)(2,1)S(1)}, f32[16,256]{1,0:T(8,128)S(1)}, f32[16,256]{1,0:T(8,128)S(1)}) custom-call(f32[9,4096]{1,0:T(8,128)S(1)} %get-tuple-element.21.cos_ref, f32[9,4096]{1,0:T(8,128)S(1)} %get-tuple-element.22.sin_ref, bf16[128,4096]{1,0:T(8,128)(2,1)S(1)} %get-tuple-element.23.square_ref, ...), custom_call_target="tpu_custom_call" | custom-call | flops 37748736 | bytes 4000000 | tf_op jit(solution)/shard_map/early/pallas_call | solution.py:391
  15.4 2.0 %collective-permute-done.4.last_ref = bf16[32,4096]{1,0:T(8,128)(2,1)S(1)} collective-permute-done((bf16[32,4096]{1,0:T(8,128)(2,1)S(1)}, bf16[32,4096]{1,0:T(8,128)(2,1)S(1)}, u32[]{:S(2)}, u32[]{:S(2)}) %collective-permute-start.4) | collective-permute-done | bytes 262176 | tf_op jit(solution)/shard_map/ppermute | solution.py:355
  17.4 1.4 %final.1 = (f32[8,512]{1,0:T(8,128)S(1)}, f32[8,512]{1,0:T(8,128)S(1)}) custom-call(bf16[16,8192]{1,0:T(8,128)(2,1)S(1)} %get-tuple-element.26.weighted_ref, f32[16,256]{1,0:T(8,128)S(1)} %get-tuple-element.27.extra_ref, f32[16,256]{1,0:T(8,128)S(1)} %get-tuple-element.28.rows_ref, f32[9,4096]{1,0:T(8,128)S(1)} %get-tuple-element.21.cos_ref, ...), custom_call_target="tpu_custom_call" | custom-call | flops 37748736 | bytes 4000000 | tf_op jit(solution)/shard_map/final/pallas_call | solution.py:408
  18.8 1.6 %collective-permute-start.5 = (f32[8,512]{1,0:T(8,128)S(1)}, f32[8,512]{1,0:T(8,128)S(1)}, u32[]{:S(2)}, u32[]{:S(2)}) collective-permute-start(f32[8,512]{1,0:T(8,128)S(1)} %get-tuple-element.30), channel_id=1, source_target_pairs={{0,4},{1,5},{2,6},{3,7},{4,0},{5,1},{6,2},{7,3},{8,12},{9,13},{10,... | collective-permute-start | bytes 49160 | tf_op jit(solution)/shard_map/ppermute | solution.py:355
  20.4 3.1 %collective-permute-done.5.recv_ref = f32[8,512]{1,0:T(8,128)S(1)} collective-permute-done((f32[8,512]{1,0:T(8,128)S(1)}, f32[8,512]{1,0:T(8,128)S(1)}, u32[]{:S(2)}, u32[]{:S(2)}) %collective-permute-start.5) | collective-permute-done | bytes 16416 | tf_op jit(solution)/shard_map/ppermute | solution.py:355
  23.4 0.7 %place.1 = f32[9,8,64]{2,1,0:T(8,128)} custom-call(f32[8,512]{1,0:T(8,128)S(1)} %get-tuple-element.29.keep_ref, f32[8,512]{1,0:T(8,128)S(1)} %collective-permute-done.5.recv_ref), custom_call_target="tpu_custom_call" | custom-call | tf_op jit(solution)/shard_map/place/pallas_call | solution.py:419
  (2 shorter events, 0.1 us)
Async XLA Ops:
  1.6 6.4 %collective-permute-start = (bf16[4,4352]{1,0:T(4,128)(2,1)S(1)}, bf16[4,4352]{1,0:T(4,128)(2,1)S(1)}, u32[]{:S(2)}, u32[]{:S(2)}) collective-permute-start(bf16[4,4352]{1,0:T(4,128)(2,1)S(1)} %get-tuple-element.24), channel_id=1, source_target_pairs={{0,4},{1,5},{2,6},{3,7},{4,0},{5,1},{6,2},{7,3},{8,12},{9,13},{10,... | collective-permute-start | bytes 104456 | tf_op jit(solution)/shard_map/ppermute | solution.py:355
  5.7 5.0 %collective-permute-start.3 = (bf16[16,4096]{1,0:T(8,128)(2,1)S(1)}, bf16[16,4096]{1,0:T(8,128)(2,1)S(1)}, u32[]{:S(2)}, u32[]{:S(2)}) collective-permute-start(bf16[16,4096]{1,0:T(8,128)(2,1)S(1)} %get-tuple-element.25.rest_2_), channel_id=1, source_target_pairs={{0,1},{1,0},{2,3},{3,2},{4,5},{5,4},{6,7},{7,6},{8,9},{9,8},{10,11... | collective-permute-start | bytes 393224 | tf_op jit(solution)/shard_map/ppermute | solution.py:355
  8.0 4.4 %collective-permute-start.1 = (bf16[8,4352]{1,0:T(8,128)(2,1)S(1)}, bf16[8,4352]{1,0:T(8,128)(2,1)S(1)}, u32[]{:S(2)}, u32[]{:S(2)}) collective-permute-start(bf16[8,4352]{1,0:T(8,128)(2,1)S(1)} %pad_maximum_fusion.2), channel_id=1, source_target_pairs={{0,16},{8,24},{16,0},{24,8},{1,17},{9,25},{17,1},{25,9},{2,18},{10... | collective-permute-start | bytes 208904 | tf_op jit(solution)/shard_map/ppermute | solution.py:355
  10.7 6.7 %collective-permute-start.4 = (bf16[32,4096]{1,0:T(8,128)(2,1)S(1)}, bf16[32,4096]{1,0:T(8,128)(2,1)S(1)}, u32[]{:S(2)}, u32[]{:S(2)}) collective-permute-start(bf16[32,4096]{1,0:T(8,128)(2,1)S(1)} %pad_maximum_fusion), channel_id=1, source_target_pairs={{0,2},{1,3},{2,0},{3,1},{4,6},{5,7},{6,4},{7,5},{8,10},{9,11},{10,... | collective-permute-start | bytes 786440 | tf_op jit(solution)/shard_map/ppermute | solution.py:355
  12.5 1.4 %collective-permute-start.2 = (bf16[16,4352]{1,0:T(8,128)(2,1)S(1)}, bf16[16,4352]{1,0:T(8,128)(2,1)S(1)}, u32[]{:S(2)}, u32[]{:S(2)}) collective-permute-start(bf16[16,4352]{1,0:T(8,128)(2,1)S(1)} %pad_maximum_fusion.1.rest_0_), channel_id=1, source_target_pairs={{0,8},{8,0},{16,24},{24,16},{1,9},{9,1},{17,25},{25,17},{2,10},{10... | collective-permute-start | bytes 417800 | tf_op jit(solution)/shard_map/ppermute | solution.py:355
  18.8 4.7 %collective-permute-start.5 = (f32[8,512]{1,0:T(8,128)S(1)}, f32[8,512]{1,0:T(8,128)S(1)}, u32[]{:S(2)}, u32[]{:S(2)}) collective-permute-start(f32[8,512]{1,0:T(8,128)S(1)} %get-tuple-element.30), channel_id=1, source_target_pairs={{0,4},{1,5},{2,6},{3,7},{4,0},{5,1},{6,2},{7,3},{8,12},{9,13},{10,... | collective-permute-start | bytes 49160 | tf_op jit(solution)/shard_map/ppermute | solution.py:355

commit v12 on v10

--- a/solution.py
+++ b/solution.py
@@ -93,7 +93,7 @@
     row = lax.broadcasted_iota(jnp.int32, (2 * n_part, wide), 0)
     row_extra = lax.broadcasted_iota(jnp.int32, (2 * n_part, extra), 0)
     lane_extra = lax.broadcasted_iota(jnp.int32, (2 * n_part, extra), 1)
-    prior = padded(prior_ref[...].astype(F32), extra)
+    prior = padded(prior_ref[...].astype(F32), 2 * extra)
     rows = jnp.zeros((2 * n_part, wide), F32)
     rows_extra = jnp.zeros((2 * n_part, extra), F32)
     for i in range(n_part):
@@ -101,12 +101,13 @@
         both = padded(particles_ref[i].astype(F32) * curve, wide)
         rows = jnp.where(row == i, both[0:1], rows)
         rows = jnp.where(row == n_part + i, both[1:2], rows)
-        small = jnp.where(
-            lane_extra == subsets,
+        rest = jnp.where(
+            lane_extra == subsets - extra,
             class_ref[i].astype(F32),
-            jnp.broadcast_to(prior[i : i + 1], rows_extra.shape),
+            jnp.broadcast_to(prior[i : i + 1, extra:], rows_extra.shape),
         )
-        rows_extra = jnp.where(row_extra == i, small, rows_extra)
+        rows_extra = jnp.where(row_extra == i, prior[i : i + 1, :extra], rows_extra)
+        rows_extra = jnp.where(row_extra == n_part + i, rest, rows_extra)
     part_ref[:, :wide] = rows.astype(BF16)
     part_ref[:, wide:] = rows_extra.astype(BF16)
     for t in range(phase_ref.shape[0]):
@@ -149,11 +150,26 @@
     )
 
 
-def score_pieces(weighted_ref, banks, cos_ref, sin_ref, square_ref, n_proj):
+def added_rows(extra, norm, banks, n_proj, length, subsets):
+    ids_at = length // 128 * 128
+    ids = []
+    for bank in banks:
+        for first in range(0, bank.shape[0], 2 * n_proj):
+            rows = bank[first : first + 2 * n_proj, ids_at : ids_at + 128].astype(F32)
+            ids.append(rows[:n_proj])
+    ids = jnp.concatenate(ids, axis=0)[:, length - ids_at : length - ids_at + 1]
+    subset_col = lax.broadcasted_iota(jnp.int32, (ids.shape[0], subsets), 1).astype(F32)
+    subset_hot = (subset_col == ids).astype(F32).astype(BF16)
+    prior = lax.dot_general(
+        extra[:, :subsets].astype(BF16), subset_hot, NT_DIMS, preferred_element_type=F32
+    )
+    return prior - 0.5 * norm
+
+
+def score_pieces(weighted_ref, extra, banks, cos_ref, sin_ref, squares_of, length, subsets, n_proj):
     shifts, wide = cos_ref.shape
-    classes_count = square_ref.shape[0] // 2
     step = 256 if wide % 256 == 0 else 128
-    cross, table = None, None
+    cross, norm = None, None
     for at in range(0, wide, step):
         span = slice(at, at + step)
         reals, imags = [], []
@@ -162,76 +178,56 @@
                 both = bank[first : first + 2 * n_proj, span].astype(F32)
                 reals.append(both[:n_proj])
                 imags.append(both[n_proj:])
-        real, imag = jnp.concatenate(reals, axis=0), jnp.concatenate(imags, axis=0)
         real_rows, imag_rows = [], []
-        for t in range(shifts):
-            cos_part, sin_part = cos_ref[t : t + 1, span], sin_ref[t : t + 1, span]
-            real_rows.append((cos_part * real + sin_part * imag).astype(BF16))
-            imag_rows.append((cos_part * imag - sin_part * real).astype(BF16))
+        for real, imag in zip(reals, imags):
+            for t in range(shifts):
+                cos_part, sin_part = cos_ref[t : t + 1, span], sin_ref[t : t + 1, span]
+                real_rows.append(cos_part * real + sin_part * imag)
+                imag_rows.append(cos_part * imag - sin_part * real)
         terms = lax.dot_general(
             weighted_ref[:, span],
-            jnp.concatenate(real_rows, axis=0),
+            jnp.concatenate(real_rows, axis=0).astype(BF16),
             NT_DIMS,
             preferred_element_type=F32,
         ) + lax.dot_general(
             weighted_ref[:, wide + at : wide + at + step],
-            jnp.concatenate(imag_rows, axis=0),
+            jnp.concatenate(imag_rows, axis=0).astype(BF16),
             NT_DIMS,
             preferred_element_type=F32,
         )
+        real, imag = jnp.concatenate(reals, axis=0), jnp.concatenate(imags, axis=0)
         power = split_terms(real * real + imag * imag)
-        norms = lax.dot_general(
-            square_ref[:, span], power, NT_DIMS, preferred_element_type=F32
+        norms = lax.dot_general(squares_of(span), power, NT_DIMS, preferred_element_type=F32)
+        cross = terms if cross is None else cross + terms
+        norm = norms if norm is None else norm + norms
+    count, total = cross.shape[0], norm.shape[1] // 2
+    norm = norm[:count, total:] + norm[count:, :total] + norm[:count, :total]
+    added = added_rows(extra, norm, banks, n_proj, length, subsets)
+    width = shifts * n_proj
+    pieces = []
+    for n in range(total // n_proj):
+        pieces.append(
+            jnp.concatenate(
+                [cross[:, n * width : (n + 1) * width], added[:, n * n_proj : (n + 1) * n_proj]], axis=1
+            )
         )
-        cross = terms if cross is None else cross + terms
-        table = norms if table is None else table + norms
-    count = table.shape[1] // 2
-    table = (
-        table[:classes_count, count:] + table[classes_count:, :count] + table[:classes_count, :count]
-    )
-    return cross, table
-
-
-def in_lanes(values, blk, bits, n_proj, lanes):
-    if values.shape[1] < lanes:
-        zeros = jnp.zeros((values.shape[0], lanes - values.shape[1]), F32)
-        values = jnp.concatenate([values, zeros], axis=1)
-    lane = lax.broadcasted_iota(jnp.int32, values.shape, 1)
-    for bit in bits:
-        step = bit * n_proj
-        other = jnp.where(
-            (lane & step) != 0, pltpu.roll(values, step, 1), pltpu.roll(values, lanes - step, 1)
-        )
-        values = jnp.where((blk & bit) != 0, other, values)
-    return values
-
-
-def added_rows(extra, table, banks, n_proj, length, subsets):
-    ids_at = length // 128 * 128
-    ids = []
-    for bank in banks:
-        for n in range(bank.shape[0] // (2 * n_proj)):
-            rows = bank[2 * n_proj * n : 2 * n_proj * (n + 1), ids_at : ids_at + 128].astype(F32)
-            ids.append(rows[:n_proj])
-    ids = jnp.concatenate(ids, axis=0)[:, length - ids_at : length - ids_at + 1]
-    count, classes_count = extra.shape[0], table.shape[0]
-    class_col = lax.broadcasted_iota(jnp.int32, (count, classes_count), 1).astype(F32)
-    onehot = (class_col == extra[:, subsets : subsets + 1]).astype(F32)
-    norm = jnp.dot(onehot, table, precision=HIGHEST, preferred_element_type=F32)
-    subset_col = lax.broadcasted_iota(jnp.int32, (ids.shape[0], subsets), 1).astype(F32)
-    subset_hot = (subset_col == ids).astype(F32).astype(BF16)
-    prior = lax.dot_general(
-        extra[:, :subsets].astype(BF16), subset_hot, NT_DIMS, preferred_element_type=F32
-    )
-    return prior - 0.5 * norm
+    return pieces
+
+
+def store_pieces(out, pieces, first, slot, rows):
+    for n, piece in enumerate(pieces):
+        at = (first + n) * slot
+        out[:, at : at + piece.shape[1]] = piece[rows]
 
 
 def early_kernel(
-    n_parts, ng, weights, bits, n_part, n_proj, length, subsets, cos_ref, sin_ref, square_ref, *rest
+    n_parts, ng, weights, n_part, n_proj, length, subsets, cos_ref, sin_ref, square_ref, *rest
 ):
-    parts, (*banks, weighted_ref, extra_ref, rows_ref) = rest[:n_parts], rest[n_parts:]
-    blk, g = lax.axis_index("blk"), lax.axis_index("grp")
+    parts, rest = rest[:n_parts], rest[n_parts:]
+    *banks, weighted_ref, extra_ref, select_ref, rows_ref = rest
+    g = lax.axis_index("grp")
     wide = weighted_ref.shape[1] // 2
+    classes_count = square_ref.shape[0] // 2
 
     held = jnp.concatenate([part[...] for part in parts], axis=0)
     count = 2 * ng * n_part
@@ -246,42 +242,64 @@
     ordered = jnp.dot(pick, held, preferred_element_type=F32)
     weighted_ref[:, :wide] = ordered[:count, :wide].astype(BF16)
     weighted_ref[:, wide:] = ordered[count:, :wide].astype(BF16)
-    extra = ordered[:count, wide:]
+    extra = jnp.concatenate([ordered[:count, wide:], ordered[count:, wide:]], axis=1)
     extra_ref[...] = extra
-    cross, table = score_pieces(weighted_ref, banks, cos_ref, sin_ref, square_ref, n_proj)
-    added = added_rows(extra, table, banks, n_proj, length, subsets)
-    rows = jnp.concatenate([cross, added], axis=1)
-    rows_ref[...] = in_lanes(rows, blk, bits, n_proj, rows_ref.shape[1])
+    class_col = lax.broadcasted_iota(jnp.int32, (count, classes_count), 1).astype(F32)
+    onehot = (class_col == extra[:, subsets : subsets + 1]).astype(F32).astype(BF16)
+
+    def squares_of(span):
+        high = jnp.dot(onehot, square_ref[:classes_count, span], preferred_element_type=F32)
+        low = jnp.dot(onehot, square_ref[classes_count:, span], preferred_element_type=F32)
+        both = jnp.concatenate([high, low], axis=0).astype(BF16)
+        select_ref[:, span] = both
+        return both
+
+    pieces = score_pieces(
+        weighted_ref, extra, banks, cos_ref, sin_ref, squares_of, length, subsets, n_proj
+    )
+    store_pieces(rows_ref, pieces, 0, rows_ref.shape[1] // len(pieces), slice(None))
 
 
 def final_kernel(
-    bits, n_proj, length, subsets, weighted_ref, extra_ref, rows_ref, cos_ref, sin_ref, square_ref, last_ref, *outs
+    half, n_proj, length, subsets, weighted_ref, extra_ref, select_ref, rows_ref, cos_ref, sin_ref, last_ref, *outs
 ):
+    pieces = score_pieces(
+        weighted_ref,
+        extra_ref[...],
+        [last_ref],
+        cos_ref,
+        sin_ref,
+        lambda span: select_ref[:, span],
+        length,
+        subsets,
+        n_proj,
+    )
+    dest, lanes = outs[0].shape
+    held = rows_ref.shape[1]
+    for s, out in enumerate(outs):
+        rows = slice(s * dest, (s + 1) * dest)
+        out[:, :held] = rows_ref[rows, :]
+        store_pieces(out, pieces, half - len(pieces), lanes // half, rows)
+
+
+def place_kernel(half, n_proj, order, keep_ref, recv_ref, out_ref):
     blk = lax.axis_index("blk")
-    cross, table = score_pieces(weighted_ref, [last_ref], cos_ref, sin_ref, square_ref, n_proj)
-    added = added_rows(extra_ref[...], table, [last_ref], n_proj, length, subsets)
-    rows = jnp.concatenate([cross, added], axis=1)
-    dest, lanes = outs[0].shape[0], rows_ref.shape[1]
-    rows = in_lanes(rows, blk, bits, n_proj, lanes)
-    for s, out in enumerate(outs):
-        out[:, :lanes] = rows_ref[s * dest : (s + 1) * dest, :]
-        out[:, lanes:] = rows[s * dest : (s + 1) * dest]
-
-
-def place_kernel(half, keep_ref, recv_ref, out_ref):
-    blk = lax.axis_index("blk")
-    own_first, early_first = blk < half, (blk & (half // 2)) == 0
+    own_first = blk < half
     keep, recv = keep_ref[...], recv_ref[...]
-    lanes = keep.shape[1] // 2
+    slot = keep.shape[1] // half
+    shifts = out_ref.shape[0]
     parts = []
     for values in (jnp.where(own_first, keep, recv), jnp.where(own_first, recv, keep)):
-        early, late = values[:, :lanes], values[:, lanes:]
-        parts += [jnp.where(early_first, early, late), jnp.where(early_first, late, early)]
-    shifts, _, width = out_ref.shape
-    width = width // 4
+        found = [values[:, order.index(n) * slot : (order.index(n) + 1) * slot] for n in range(half)]
+        bit = 1
+        while bit < half:
+            swapped = (blk & bit) != 0
+            found = [jnp.where(swapped, found[n ^ bit], found[n]) for n in range(half)]
+            bit *= 2
+        parts += found
 
     def line(t):
-        return jnp.concatenate([part[:, t * width : (t + 1) * width] for part in parts], axis=1)
+        return jnp.concatenate([part[:, t * n_proj : (t + 1) * n_proj] for part in parts], axis=1)
 
     added = line(shifts)
     for t in range(shifts):
@@ -307,7 +325,7 @@
     classes_count = ctf_curves.shape[0]
     subsets = orient_prior.shape[1]
     wide = 128 * (length // 128 + 1)
-    extra = 128 * (subsets // 128 + 1)
+    extra = 128 * -(-(subsets + 1) // 256)
     noise = noise_weight.reshape(1, length)
     shape = jax.ShapeDtypeStruct
 
@@ -358,11 +376,15 @@
         return pieces[0] if len(pieces) == 1 else jnp.concatenate(pieces, axis=0)
 
     across = swap(part, "blk", half)
-    planes, bit = [bank], 1
-    while 2 * bit < half:
-        planes.append(swap(joined(planes), "blk", bit))
-        bit *= 2
-    last = swap(joined(planes), "blk", bit)
+    near = swap(bank, "blk", 1)
+    planes, order = [bank], [0]
+    for n in range(half.bit_length() - 2, 0, -1):
+        planes.append(swap(joined(planes), "blk", 1 << n))
+        order += [offset ^ (1 << n) for offset in order]
+    far, near = lax.optimization_barrier((joined(planes[1:]), near))
+    last = swap(jnp.pad(far, ((0, 0), (0, 3 * 128))), "blk", 1)
+    planes = [bank, near, far]
+    order = [0, 1] + order[1:] + [offset ^ 1 for offset in order[1:]]
 
     cos_part, sin_part, square = pl.pallas_call(
         table_kernel,
@@ -378,7 +400,7 @@
         name="tables",
     )(curves, noise, angle)
 
-    across, planes[-1], cos_part = lax.optimization_barrier((across, planes[-1], cos_part))
+    across, cos_part = lax.optimization_barrier((across, cos_part))
     parts, weights = [part, across], []
     for n in range(ng.bit_length() - 2, -1, -1):
         part = joined(parts)
@@ -386,39 +408,39 @@
         weights.append((1 << n, 2 << len(weights)))
 
     count = 2 * ng * n_part
-    early = half // 2 * n_proj
-    lanes = 128 * -(-(shifts + 1) * early // 128)
-    bits = [1 << n for n in range(half.bit_length() - 2)]
-    weighted, extra_rows, rows = pl.pallas_call(
-        functools.partial(
-            early_kernel, len(parts), ng, weights, bits, n_part, n_proj, length, subsets
-        ),
+    late = half // 2 - 1
+    slot = 128 * -(-(shifts + 1) * n_proj // 128)
+    weighted, extra_rows, select, rows = pl.pallas_call(
+        functools.partial(early_kernel, len(parts), ng, weights, n_part, n_proj, length, subsets),
         out_shape=[
             vmem_out((count, 2 * wide), BF16),
-            vmem_out((count, extra), F32),
-            vmem_out((count, lanes), F32),
+            vmem_out((count, 2 * extra), F32),
+            vmem_out((2 * count, wide), BF16),
+            vmem_out((count, (half - late) * slot), F32),
         ],
         in_specs=[_vmem()] * (3 + len(parts) + len(planes)),
-        out_specs=[_vmem()] * 3,
+        out_specs=[_vmem()] * 4,
         compiler_params=_params(16),
         cost_estimate=pl.CostEstimate(
-            flops=4 * count * early * shifts * wide, bytes_accessed=4_000_000, transcendentals=0
+            flops=4 * count * (half - late) * n_proj * shifts * wide,
+            bytes_accessed=4_000_000,
+            transcendentals=0,
         ),
         name="early",
     )(cos_part, sin_part, square, *parts, *planes)
     keep, give = pl.pallas_call(
-        functools.partial(final_kernel, bits, n_proj, length, subsets),
-        out_shape=[vmem_out((ng * n_part, 2 * lanes), F32)] * 2,
+        functools.partial(final_kernel, half, n_proj, length, subsets),
+        out_shape=[vmem_out((ng * n_part, half * slot), F32)] * 2,
         in_specs=[_vmem()] * 7,
         out_specs=[_vmem()] * 2,
         compiler_params=_params(16),
         cost_estimate=pl.CostEstimate(
-            flops=4 * count * early * shifts * wide, bytes_accessed=4_000_000, transcendentals=0
+            flops=4 * count * late * n_proj * shifts * wide, bytes_accessed=4_000_000, transcendentals=0
         ),
         name="final",
-    )(weighted, extra_rows, rows, cos_part, sin_part, square, last)
+    )(weighted, extra_rows, select, rows, cos_part, sin_part, last)
     scores = pl.pallas_call(
-        functools.partial(place_kernel, half),
+        functools.partial(place_kernel, half, n_proj, order),
         out_shape=shape((shifts, ng * n_part, nb * n_proj), F32),
         in_specs=[_vmem()] * 2,
         out_specs=_vmem(),

time: 24.5 us -> 24.9 us (1.016)
  Pallas kernels: 5.81 us -> 6.79 us
  waiting for transfers between devices: 6.78 us -> 6.04 us
    pallas_call x3, Pallas kernels: 3.65 us -> 4.62 us  [the longest x1 3.15 us: per_device(): pl.pallas_call(functools.partial(early_kernel, len(parts), ng, weights, n...]
    ppermute x6 -> x7, waiting for transfers between devices: 6.78 us -> 6.04 us  [swap(): return lax.ppermute(value, axis, [(i, i ^ bit) for i in range(size)])]
    ppermute x6 -> x7, starting transfers between devices: 11.6 us -> 11.7 us  [swap(): return lax.ppermute(value, axis, [(i, i ^ bit) for i in range(size)])]
  transfers between devices with their start and end apart: 6 -> 7, of which waited for: 5 -> 3; matrix products, arithmetic and copies ran while one was open for 0% -> 0% of each run, Pallas kernels for 9% -> 15%
where the time goes in v12:
time: 24.9 us; the launch traced here: 24.7 us
  starting transfers between devices  11.7 us (47%)
  Pallas kernels  6.79 us (27%)
  waiting for transfers between devices  6.04 us (24%)
    ppermute x7, starting transfers between devices, swap(): return lax.ppermute(value, axis, [(i, i ^ bit) for i in range(size)])  11.7 us
    ppermute x7, waiting for transfers between devices, swap(): return lax.ppermute(value, axis, [(i, i ^ bit) for i in range(size)])  6.04 us
    pallas_call x1, Pallas kernels, per_device(): pl.pallas_call(functools.partial(early_kernel, len(parts), ng, weights, n...  3.15 us
    pallas_call x1, Pallas kernels, per_device(): pl.pallas_call(pack_kernel, out_shape=[vmem_out((2 * n_proj, wide), BF16)...  1.58 us
    pallas_call x1, Pallas kernels, per_device(): pl.pallas_call(functools.partial(place_kernel, half, n_proj, order), out_...  0.77 us
    pallas_call x1, Pallas kernels, per_device(): pl.pallas_call(functools.partial(final_kernel, half, n_proj, length, subs...  0.7 us
    pallas_call x1, Pallas kernels, per_device(): pl.pallas_call(table_kernel, out_shape=[vmem_out((shifts, wide), F32), vm...  0.59 us
  transfers between devices with their start and end apart: 7, of which 3 were waited for; matrix products, arithmetic and copies ran while one was open for 0% of the time, Pallas kernels for 15%

profile of v12, /device:TPU:0, one launch (start us, length us, event | category | flops | bytes accessed | tf_op | source)
XLA Modules:
  0.0 24.7 jit_solution(11916352693787688779)
XLA Ops:
  0.0 1.6 %pack.1 = (bf16[16,4096]{1,0:T(8,128)(2,1)S(1)}, bf16[4,4224]{1,0:T(4,128)(2,1)S(1)}, f32[64,4000]{1,0:T(8,128)S(1)}, f32[1,4000]{1,0:T(1,128)S(1)}, f32[9,4000]{1,0:T(8,128)S(1)}) custom-call(s32[2]{0:T(128)} %class_hbm.1, s32[8]{0:T(128)} %subset_hbm.1, bf16[2,2,4000]{2,1,0:T(2,128)(2,1)} %particles_hbm.1, bf16[2,192]{1,0:T(2,128)(2,1)} %prior_hbm.1, ...), custom_call_target="tpu_custom_call" | custom-call | tf_op jit(solution)/shard_map/pack/pallas_call | solution.py:346
  1.6 4.1 %collective-permute-start = (bf16[4,4224]{1,0:T(4,128)(2,1)S(1)}, bf16[4,4224]{1,0:T(4,128)(2,1)S(1)}, u32[]{:S(2)}, u32[]{:S(2)}) collective-permute-start(bf16[4,4224]{1,0:T(4,128)(2,1)S(1)} %get-tuple-element.23), channel_id=1, source_target_pairs={{0,4},{1,5},{2,6},{3,7},{4,0},{5,1},{6,2},{7,3},{8,12},{9,13},{10,... | collective-permute-start | bytes 101384 | tf_op jit(solution)/shard_map/ppermute | solution.py:373
  5.7 1.6 %collective-permute-start.3 = (bf16[16,4096]{1,0:T(8,128)(2,1)S(1)}, bf16[16,4096]{1,0:T(8,128)(2,1)S(1)}, u32[]{:S(2)}, u32[]{:S(2)}) collective-permute-start(bf16[16,4096]{1,0:T(8,128)(2,1)S(1)} %get-tuple-element.32.rest_2_), channel_id=1, source_target_pairs={{0,2},{1,3},{2,0},{3,1},{4,6},{5,7},{6,4},{7,5},{8,10},{9,11},{10,... | collective-permute-start | bytes 393224 | tf_op jit(solution)/shard_map/ppermute | solution.py:373
  7.3 1.5 %collective-permute-start.4 = (bf16[16,4096]{1,0:T(8,128)(2,1)S(1)}, bf16[16,4096]{1,0:T(8,128)(2,1)S(1)}, u32[]{:S(2)}, u32[]{:S(2)}) collective-permute-start(bf16[16,4096]{1,0:T(8,128)(2,1)S(1)} %get-tuple-element.32.rest_2_), channel_id=1, source_target_pairs={{0,1},{1,0},{2,3},{3,2},{4,5},{5,4},{6,7},{7,6},{8,9},{9,8},{10,11... | collective-permute-start | bytes 393224 | tf_op jit(solution)/shard_map/ppermute | solution.py:373
  8.8 0.6 %tables.1 = (f32[9,4096]{1,0:T(8,128)S(1)}, f32[9,4096]{1,0:T(8,128)S(1)}, bf16[128,4096]{1,0:T(8,128)(2,1)S(1)}) custom-call(f32[64,4000]{1,0:T(8,128)S(1)} %get-tuple-element.24.curves_ref, f32[1,4000]{1,0:T(1,128)S(1)} %get-tuple-element.25.noise_ref, f32[9,4000]{1,0:T(8,128)S(1)} %get-tuple-element.26.angle_ref), custom_call_target="tpu_custom_call" | custom-call | flops 4000000 | bytes 2000000 | tf_op jit(solution)/shard_map/tables/pallas_call | solution.py:389
  9.4 0.0 collective-permute-done
  9.4 1.6 %collective-permute-start.1 = (bf16[8,4224]{1,0:T(8,128)(2,1)S(1)}, bf16[8,4224]{1,0:T(8,128)(2,1)S(1)}, u32[]{:S(2)}, u32[]{:S(2)}) collective-permute-start(bf16[8,4224]{1,0:T(8,128)(2,1)S(1)} %pad_maximum_fusion.1), channel_id=1, source_target_pairs={{0,16},{8,24},{16,0},{24,8},{1,17},{9,25},{17,1},{25,9},{2,18},{10... | collective-permute-start | bytes 202760 | tf_op jit(solution)/shard_map/ppermute | solution.py:373
  11.0 0.0 collective-permute-done.3.rest_4_
  11.0 1.2 %collective-permute-done.4.rest_3_ = bf16[16,4096]{1,0:T(8,128)(2,1)S(1)} collective-permute-done((bf16[16,4096]{1,0:T(8,128)(2,1)S(1)}, bf16[16,4096]{1,0:T(8,128)(2,1)S(1)}, u32[]{:S(2)}, u32[]{:S(2)}) %collective-permute-start.4) | collective-permute-done | bytes 131104 | tf_op jit(solution)/shard_map/ppermute | solution.py:373
  12.3 1.6 %collective-permute-start.5 = (bf16[16,4480]{1,0:T(8,128)(2,1)S(1)}, bf16[16,4480]{1,0:T(8,128)(2,1)S(1)}, u32[]{:S(2)}, u32[]{:S(2)}) collective-permute-start(bf16[16,4480]{1,0:T(8,128)(2,1)S(1)} %pad.4), channel_id=1, source_target_pairs={{0,1},{1,0},{2,3},{3,2},{4,5},{5,4},{6,7},{7,6},{8,9},{9,8},{10,11... | collective-permute-start | bytes 430088 | tf_op jit(solution)/shard_map/ppermute | solution.py:373
  13.8 0.0 collective-permute-done.1
  13.8 0.1 pad_maximum_fusion.rest_0_
  13.9 0.1 collective-permute-start.2
  14.0 1.3 %collective-permute-done.2.rest_1_ = bf16[16,4224]{1,0:T(8,128)(2,1)S(1)} collective-permute-done((bf16[16,4224]{1,0:T(8,128)(2,1)S(1)}, bf16[16,4224]{1,0:T(8,128)(2,1)S(1)}, u32[]{:S(2)}, u32[]{:S(2)}) %collective-permute-start.2) | collective-permute-done | bytes 135200 | tf_op jit(solution)/shard_map/ppermute | solution.py:373
  15.3 3.1 %early.1 = (bf16[16,8192]{1,0:T(8,128)(2,1)S(1)}, f32[16,256]{1,0:T(8,128)S(1)}, bf16[32,4096]{1,0:T(8,128)(2,1)S(1)}, f32[16,384]{1,0:T(8,128)S(1)}) custom-call(f32[9,4096]{1,0:T(8,128)S(1)} %get-tuple-element.28.cos_ref, f32[9,4096]{1,0:T(8,128)S(1)} %get-tuple-element.29.sin_ref, bf16[128,4096]{1,0:T(8,128)(2,1)S(1)} %get-tuple-element.30.square_ref, ...), custom_call_target="tpu_custom_call" | custom-call | flops 56623104 | bytes 4000000 | tf_op jit(solution)/shard_map/early/pallas_call | solution.py:413
  18.5 0.0 collective-permute-done.5.last_ref
  18.5 0.7 %final.1 = (f32[8,512]{1,0:T(8,128)S(1)}, f32[8,512]{1,0:T(8,128)S(1)}) custom-call(bf16[16,8192]{1,0:T(8,128)(2,1)S(1)} %get-tuple-element.35.weighted_ref, f32[16,256]{1,0:T(8,128)S(1)} %get-tuple-element.36.extra_ref, bf16[32,4096]{1,0:T(8,128)(2,1)S(1)} %get-tuple-element.37.select_ref, f32[16,384]{1,0:T(8,128)S(1)} %get-tuple-element.38.rows_ref, ...), custom_call_target="tpu_custom_call" | custom-call | flops 18874368 | bytes 4000000 | tf_op jit(solution)/shard_map/final/pallas_call | solution.py:431
  19.2 1.3 %collective-permute-start.6 = (f32[8,512]{1,0:T(8,128)S(1)}, f32[8,512]{1,0:T(8,128)S(1)}, u32[]{:S(2)}, u32[]{:S(2)}) collective-permute-start(f32[8,512]{1,0:T(8,128)S(1)} %get-tuple-element.40), channel_id=1, source_target_pairs={{0,4},{1,5},{2,6},{3,7},{4,0},{5,1},{6,2},{7,3},{8,12},{9,13},{10,... | collective-permute-start | bytes 49160 | tf_op jit(solution)/shard_map/ppermute | solution.py:373
  20.5 3.4 %collective-permute-done.6.recv_ref = f32[8,512]{1,0:T(8,128)S(1)} collective-permute-done((f32[8,512]{1,0:T(8,128)S(1)}, f32[8,512]{1,0:T(8,128)S(1)}, u32[]{:S(2)}, u32[]{:S(2)}) %collective-permute-start.6) | collective-permute-done | bytes 16416 | tf_op jit(solution)/shard_map/ppermute | solution.py:373
  24.0 0.8 %place.1 = f32[9,8,64]{2,1,0:T(8,128)} custom-call(f32[8,512]{1,0:T(8,128)S(1)} %get-tuple-element.39.keep_ref, f32[8,512]{1,0:T(8,128)S(1)} %collective-permute-done.6.recv_ref), custom_call_target="tpu_custom_call" | custom-call | tf_op jit(solution)/shard_map/place/pallas_call | solution.py:442
  (2 shorter events, 0.1 us)
Async XLA Ops:
  1.6 7.8 %collective-permute-start = (bf16[4,4224]{1,0:T(4,128)(2,1)S(1)}, bf16[4,4224]{1,0:T(4,128)(2,1)S(1)}, u32[]{:S(2)}, u32[]{:S(2)}) collective-permute-start(bf16[4,4224]{1,0:T(4,128)(2,1)S(1)} %get-tuple-element.23), channel_id=1, source_target_pairs={{0,4},{1,5},{2,6},{3,7},{4,0},{5,1},{6,2},{7,3},{8,12},{9,13},{10,... | collective-permute-start | bytes 101384 | tf_op jit(solution)/shard_map/ppermute | solution.py:373
  5.7 5.3 %collective-permute-start.3 = (bf16[16,4096]{1,0:T(8,128)(2,1)S(1)}, bf16[16,4096]{1,0:T(8,128)(2,1)S(1)}, u32[]{:S(2)}, u32[]{:S(2)}) collective-permute-start(bf16[16,4096]{1,0:T(8,128)(2,1)S(1)} %get-tuple-element.32.rest_2_), channel_id=1, source_target_pairs={{0,2},{1,3},{2,0},{3,1},{4,6},{5,7},{6,4},{7,5},{8,10},{9,11},{10,... | collective-permute-start | bytes 393224 | tf_op jit(solution)/shard_map/ppermute | solution.py:373
  7.3 5.0 %collective-permute-start.4 = (bf16[16,4096]{1,0:T(8,128)(2,1)S(1)}, bf16[16,4096]{1,0:T(8,128)(2,1)S(1)}, u32[]{:S(2)}, u32[]{:S(2)}) collective-permute-start(bf16[16,4096]{1,0:T(8,128)(2,1)S(1)} %get-tuple-element.32.rest_2_), channel_id=1, source_target_pairs={{0,1},{1,0},{2,3},{3,2},{4,5},{5,4},{6,7},{7,6},{8,9},{9,8},{10,11... | collective-permute-start | bytes 393224 | tf_op jit(solution)/shard_map/ppermute | solution.py:373
  9.4 4.4 %collective-permute-start.1 = (bf16[8,4224]{1,0:T(8,128)(2,1)S(1)}, bf16[8,4224]{1,0:T(8,128)(2,1)S(1)}, u32[]{:S(2)}, u32[]{:S(2)}) collective-permute-start(bf16[8,4224]{1,0:T(8,128)(2,1)S(1)} %pad_maximum_fusion.1), channel_id=1, source_target_pairs={{0,16},{8,24},{16,0},{24,8},{1,17},{9,25},{17,1},{25,9},{2,18},{10... | collective-permute-start | bytes 202760 | tf_op jit(solution)/shard_map/ppermute | solution.py:373
  12.3 6.3 %collective-permute-start.5 = (bf16[16,4480]{1,0:T(8,128)(2,1)S(1)}, bf16[16,4480]{1,0:T(8,128)(2,1)S(1)}, u32[]{:S(2)}, u32[]{:S(2)}) collective-permute-start(bf16[16,4480]{1,0:T(8,128)(2,1)S(1)} %pad.4), channel_id=1, source_target_pairs={{0,1},{1,0},{2,3},{3,2},{4,5},{5,4},{6,7},{7,6},{8,9},{9,8},{10,11... | collective-permute-start | bytes 430088 | tf_op jit(solution)/shard_map/ppermute | solution.py:373
  13.9 1.4 %collective-permute-start.2 = (bf16[16,4224]{1,0:T(8,128)(2,1)S(1)}, bf16[16,4224]{1,0:T(8,128)(2,1)S(1)}, u32[]{:S(2)}, u32[]{:S(2)}) collective-permute-start(bf16[16,4224]{1,0:T(8,128)(2,1)S(1)} %pad_maximum_fusion.rest_0_), channel_id=1, source_target_pairs={{0,8},{8,0},{16,24},{24,16},{1,9},{9,1},{17,25},{25,17},{2,10},{10... | collective-permute-start | bytes 405512 | tf_op jit(solution)/shard_map/ppermute | solution.py:373
  19.2 4.7 %collective-permute-start.6 = (f32[8,512]{1,0:T(8,128)S(1)}, f32[8,512]{1,0:T(8,128)S(1)}, u32[]{:S(2)}, u32[]{:S(2)}) collective-permute-start(f32[8,512]{1,0:T(8,128)S(1)} %get-tuple-element.40), channel_id=1, source_target_pairs={{0,4},{1,5},{2,6},{3,7},{4,0},{5,1},{6,2},{7,3},{8,12},{9,13},{10,... | collective-permute-start | bytes 49160 | tf_op jit(solution)/shard_map/ppermute | solution.py:373

commit v13 on v12

--- a/solution.py
+++ b/solution.py
@@ -166,51 +166,58 @@
     return prior - 0.5 * norm
 
 
-def score_pieces(weighted_ref, extra, banks, cos_ref, sin_ref, squares_of, length, subsets, n_proj):
+def bank_pieces(bank, span, n_proj):
+    for first in range(0, bank.shape[0], 2 * n_proj):
+        both = bank[first : first + 2 * n_proj, span].astype(F32)
+        yield both[:n_proj], both[n_proj:]
+
+
+def shifted_rows(real, imag, cos_ref, sin_ref, span):
+    real_rows, imag_rows = [], []
+    for t in range(cos_ref.shape[0]):
+        cos_part, sin_part = cos_ref[t : t + 1, span], sin_ref[t : t + 1, span]
+        real_rows.append(cos_part * real + sin_part * imag)
+        imag_rows.append(cos_part * imag - sin_part * real)
+    return (
+        jnp.concatenate(real_rows, axis=0).astype(BF16),
+        jnp.concatenate(imag_rows, axis=0).astype(BF16),
+    )
+
+
+def spans_of(wide):
+    step = 256 if wide % 256 == 0 else 128
+    return [slice(at, at + step) for at in range(0, wide, step)]
+
+
+def shift_kernel(n_proj, cos_ref, sin_ref, *rest):
+    *banks, shifted_ref, power_ref = rest
     shifts, wide = cos_ref.shape
-    step = 256 if wide % 256 == 0 else 128
-    cross, norm = None, None
-    for at in range(0, wide, step):
-        span = slice(at, at + step)
-        reals, imags = [], []
+    width = shifts * n_proj
+    for span in spans_of(wide):
+        powers, at = [], 0
         for bank in banks:
-            for first in range(0, bank.shape[0], 2 * n_proj):
-                both = bank[first : first + 2 * n_proj, span].astype(F32)
-                reals.append(both[:n_proj])
-                imags.append(both[n_proj:])
-        real_rows, imag_rows = [], []
-        for real, imag in zip(reals, imags):
-            for t in range(shifts):
-                cos_part, sin_part = cos_ref[t : t + 1, span], sin_ref[t : t + 1, span]
-                real_rows.append(cos_part * real + sin_part * imag)
-                imag_rows.append(cos_part * imag - sin_part * real)
-        terms = lax.dot_general(
-            weighted_ref[:, span],
-            jnp.concatenate(real_rows, axis=0).astype(BF16),
-            NT_DIMS,
-            preferred_element_type=F32,
-        ) + lax.dot_general(
-            weighted_ref[:, wide + at : wide + at + step],
-            jnp.concatenate(imag_rows, axis=0).astype(BF16),
-            NT_DIMS,
-            preferred_element_type=F32,
-        )
-        real, imag = jnp.concatenate(reals, axis=0), jnp.concatenate(imags, axis=0)
-        power = split_terms(real * real + imag * imag)
-        norms = lax.dot_general(squares_of(span), power, NT_DIMS, preferred_element_type=F32)
-        cross = terms if cross is None else cross + terms
-        norm = norms if norm is None else norm + norms
+            for real, imag in bank_pieces(bank, span, n_proj):
+                real_rows, imag_rows = shifted_rows(real, imag, cos_ref, sin_ref, span)
+                shifted_ref[at : at + width, span] = real_rows
+                shifted_ref[at : at + width, wide + span.start : wide + span.stop] = imag_rows
+                powers.append(real * real + imag * imag)
+                at += width
+        power_ref[:, span] = split_terms(jnp.concatenate(powers, axis=0))
+
+
+def multiply(left, right):
+    return lax.dot_general(left, right, NT_DIMS, preferred_element_type=F32)
+
+
+def pieces_of(cross, norm, extra, banks, length, subsets, n_proj):
     count, total = cross.shape[0], norm.shape[1] // 2
+    width = cross.shape[1] * n_proj // total
     norm = norm[:count, total:] + norm[count:, :total] + norm[:count, :total]
     added = added_rows(extra, norm, banks, n_proj, length, subsets)
-    width = shifts * n_proj
     pieces = []
     for n in range(total // n_proj):
-        pieces.append(
-            jnp.concatenate(
-                [cross[:, n * width : (n + 1) * width], added[:, n * n_proj : (n + 1) * n_proj]], axis=1
-            )
-        )
+        scores = cross[:, n * width : (n + 1) * width]
+        pieces.append(jnp.concatenate([scores, added[:, n * n_proj : (n + 1) * n_proj]], axis=1))
     return pieces
 
 
@@ -220,11 +227,12 @@
         out[:, at : at + piece.shape[1]] = piece[rows]
 
 
-def early_kernel(
-    n_parts, ng, weights, n_part, n_proj, length, subsets, cos_ref, sin_ref, square_ref, *rest
-):
+def early_kernel(n_parts, n_banks, ng, weights, n_part, n_proj, length, subsets, square_ref, *rest):
     parts, rest = rest[:n_parts], rest[n_parts:]
-    *banks, weighted_ref, extra_ref, select_ref, rows_ref = rest
+    groups, (weighted_ref, extra_ref, select_ref, rows_ref) = [], rest[-4:]
+    for n in n_banks:
+        groups.append((rest[0], rest[1], rest[2 : 2 + n]))
+        rest = rest[2 + n :]
     g = lax.axis_index("grp")
     wide = weighted_ref.shape[1] // 2
     classes_count = square_ref.shape[0] // 2
@@ -246,34 +254,38 @@
     extra_ref[...] = extra
     class_col = lax.broadcasted_iota(jnp.int32, (count, classes_count), 1).astype(F32)
     onehot = (class_col == extra[:, subsets : subsets + 1]).astype(F32).astype(BF16)
-
-    def squares_of(span):
-        high = jnp.dot(onehot, square_ref[:classes_count, span], preferred_element_type=F32)
-        low = jnp.dot(onehot, square_ref[classes_count:, span], preferred_element_type=F32)
-        both = jnp.concatenate([high, low], axis=0).astype(BF16)
-        select_ref[:, span] = both
-        return both
-
-    pieces = score_pieces(
-        weighted_ref, extra, banks, cos_ref, sin_ref, squares_of, length, subsets, n_proj
-    )
+    for n in range(2):
+        squares = square_ref[n * classes_count : (n + 1) * classes_count, :]
+        chosen = jnp.dot(onehot, squares, preferred_element_type=F32)
+        select_ref[n * count : (n + 1) * count, :] = chosen.astype(BF16)
+
+    pieces = []
+    for shifted_ref, power_ref, banks in groups:
+        cross = multiply(weighted_ref[...], shifted_ref[...])
+        norm = multiply(select_ref[...], power_ref[...])
+        pieces += pieces_of(cross, norm, extra, banks, length, subsets, n_proj)
     store_pieces(rows_ref, pieces, 0, rows_ref.shape[1] // len(pieces), slice(None))
 
 
 def final_kernel(
     half, n_proj, length, subsets, weighted_ref, extra_ref, select_ref, rows_ref, cos_ref, sin_ref, last_ref, *outs
 ):
-    pieces = score_pieces(
-        weighted_ref,
-        extra_ref[...],
-        [last_ref],
-        cos_ref,
-        sin_ref,
-        lambda span: select_ref[:, span],
-        length,
-        subsets,
-        n_proj,
-    )
+    shifts, wide = cos_ref.shape
+    cross, norm = None, None
+    for span in spans_of(wide):
+        terms, powers = [], []
+        for real, imag in bank_pieces(last_ref, span, n_proj):
+            real_rows, imag_rows = shifted_rows(real, imag, cos_ref, sin_ref, span)
+            terms.append(
+                multiply(weighted_ref[:, span], real_rows)
+                + multiply(weighted_ref[:, wide + span.start : wide + span.stop], imag_rows)
+            )
+            powers.append(real * real + imag * imag)
+        terms = jnp.concatenate(terms, axis=1)
+        norms = multiply(select_ref[:, span], split_terms(jnp.concatenate(powers, axis=0)))
+        cross = terms if cross is None else cross + terms
+        norm = norms if norm is None else norm + norms
+    pieces = pieces_of(cross, norm, extra_ref[...], [last_ref], length, subsets, n_proj)
     dest, lanes = outs[0].shape
     held = rows_ref.shape[1]
     for s, out in enumerate(outs):
@@ -383,7 +395,6 @@
         order += [offset ^ (1 << n) for offset in order]
     far, near = lax.optimization_barrier((joined(planes[1:]), near))
     last = swap(jnp.pad(far, ((0, 0), (0, 3 * 128))), "blk", 1)
-    planes = [bank, near, far]
     order = [0, 1] + order[1:] + [offset ^ 1 for offset in order[1:]]
 
     cos_part, sin_part, square = pl.pallas_call(
@@ -400,25 +411,44 @@
         name="tables",
     )(curves, noise, angle)
 
-    across, cos_part = lax.optimization_barrier((across, cos_part))
+    def shifted_call(banks, name):
+        total = sum(piece.shape[0] for piece in banks) // 2
+        return pl.pallas_call(
+            functools.partial(shift_kernel, n_proj),
+            out_shape=[vmem_out((shifts * total, 2 * wide), BF16), vmem_out((2 * total, wide), BF16)],
+            in_specs=[_vmem()] * (2 + len(banks)),
+            out_specs=[_vmem()] * 2,
+            compiler_params=_params(16),
+            cost_estimate=pl.CostEstimate(
+                flops=6 * total * shifts * wide, bytes_accessed=4_000_000, transcendentals=0
+            ),
+            name=name,
+        )(cos_part, sin_part, *banks)
+
+    own_rows, own_power = shifted_call([bank], "shift_own")
+
+    across, own_power = lax.optimization_barrier((across, own_power))
     parts, weights = [part, across], []
     for n in range(ng.bit_length() - 2, -1, -1):
         part = joined(parts)
         parts = [part, swap(part, "grp", 1 << n)]
         weights.append((1 << n, 2 << len(weights)))
 
+    rest_rows, rest_power = shifted_call([near, far], "shift_rest")
     count = 2 * ng * n_part
     late = half // 2 - 1
     slot = 128 * -(-(shifts + 1) * n_proj // 128)
     weighted, extra_rows, select, rows = pl.pallas_call(
-        functools.partial(early_kernel, len(parts), ng, weights, n_part, n_proj, length, subsets),
+        functools.partial(
+            early_kernel, len(parts), (1, 2), ng, weights, n_part, n_proj, length, subsets
+        ),
         out_shape=[
             vmem_out((count, 2 * wide), BF16),
             vmem_out((count, 2 * extra), F32),
             vmem_out((2 * count, wide), BF16),
             vmem_out((count, (half - late) * slot), F32),
         ],
-        in_specs=[_vmem()] * (3 + len(parts) + len(planes)),
+        in_specs=[_vmem()] * (8 + len(parts)),
         out_specs=[_vmem()] * 4,
         compiler_params=_params(16),
         cost_estimate=pl.CostEstimate(
@@ -427,7 +457,7 @@
             transcendentals=0,
         ),
         name="early",
-    )(cos_part, sin_part, square, *parts, *planes)
+    )(square, *parts, own_rows, own_power, bank, rest_rows, rest_power, near, far)
     keep, give = pl.pallas_call(
         functools.partial(final_kernel, half, n_proj, length, subsets),
         out_shape=[vmem_out((ng * n_part, half * slot), F32)] * 2,

time: 24.9 us -> 23.8 us (0.956)
  waiting for transfers between devices: 6.04 us -> 5.63 us
  Pallas kernels: 6.79 us -> 6.4 us
  starting transfers between devices: 11.7 us -> 11.4 us
    ppermute x7, waiting for transfers between devices: 6.04 us -> 5.63 us  [swap(): return lax.ppermute(value, axis, [(i, i ^ bit) for i in range(size)])]
    pallas_call x1 -> x3, Pallas kernels: 3.15 us -> 2.75 us  [the longest x1 1.81 us: per_device(): pl.pallas_call(functools.partial(early_kernel, len(parts), (1, 2), ng, we...]
    ppermute x7, starting transfers between devices: 11.7 us -> 11.4 us  [swap(): return lax.ppermute(value, axis, [(i, i ^ bit) for i in range(size)])]
  transfers between devices with their start and end apart: 7 -> 7, of which waited for: 3 -> 4; matrix products, arithmetic and copies ran while one was open for 0% -> 0% of each run, Pallas kernels for 15% -> 14%
where the time goes in v13:
time: 23.8 us; the launch traced here: 23.7 us
  starting transfers between devices  11.4 us (48%)
  Pallas kernels  6.4 us (27%)
  waiting for transfers between devices  5.63 us (24%)
    ppermute x7, starting transfers between devices, swap(): return lax.ppermute(value, axis, [(i, i ^ bit) for i in range(size)])  11.4 us
    ppermute x7, waiting for transfers between devices, swap(): return lax.ppermute(value, axis, [(i, i ^ bit) for i in range(size)])  5.63 us
    pallas_call x1, Pallas kernels, per_device(): pl.pallas_call(functools.partial(early_kernel, len(parts), (1, 2), ng, we...  1.81 us
    pallas_call x1, Pallas kernels, per_device(): pl.pallas_call(pack_kernel, out_shape=[vmem_out((2 * n_proj, wide), BF16)...  1.58 us
    pallas_call x2, Pallas kernels, shifted_call(): pl.pallas_call(functools.partial(shift_kernel, n_proj), out_shape=[vmem_o...  0.94 us
    pallas_call x1, Pallas kernels, per_device(): pl.pallas_call(functools.partial(place_kernel, half, n_proj, order), out_...  0.77 us
    pallas_call x1, Pallas kernels, per_device(): pl.pallas_call(functools.partial(final_kernel, half, n_proj, length, subs...  0.73 us
    pallas_call x1, Pallas kernels, per_device(): pl.pallas_call(table_kernel, out_shape=[vmem_out((shifts, wide), F32), vm...  0.58 us
  transfers between devices with their start and end apart: 7, of which 4 were waited for; matrix products, arithmetic and copies ran while one was open for 0% of the time, Pallas kernels for 14%

profile of v13, /device:TPU:0, one launch (start us, length us, event | category | flops | bytes accessed | tf_op | source)
XLA Modules:
  0.0 23.7 jit_solution(9509082482471005688)
XLA Ops:
  0.0 1.6 %pack.1 = (bf16[16,4096]{1,0:T(8,128)(2,1)S(1)}, bf16[4,4224]{1,0:T(4,128)(2,1)S(1)}, f32[64,4000]{1,0:T(8,128)S(1)}, f32[1,4000]{1,0:T(1,128)S(1)}, f32[9,4000]{1,0:T(8,128)S(1)}) custom-call(s32[2]{0:T(128)} %class_hbm.1, s32[8]{0:T(128)} %subset_hbm.1, bf16[2,2,4000]{2,1,0:T(2,128)(2,1)} %particles_hbm.1, bf16[2,192]{1,0:T(2,128)(2,1)} %prior_hbm.1, ...), custom_call_target="tpu_custom_call" | custom-call | tf_op jit(solution)/shard_map/pack/pallas_call | solution.py:358
  1.6 4.1 %collective-permute-start = (bf16[4,4224]{1,0:T(4,128)(2,1)S(1)}, bf16[4,4224]{1,0:T(4,128)(2,1)S(1)}, u32[]{:S(2)}, u32[]{:S(2)}) collective-permute-start(bf16[4,4224]{1,0:T(4,128)(2,1)S(1)} %get-tuple-element.31), channel_id=1, source_target_pairs={{0,4},{1,5},{2,6},{3,7},{4,0},{5,1},{6,2},{7,3},{8,12},{9,13},{10,... | collective-permute-start | bytes 101384 | tf_op jit(solution)/shard_map/ppermute | solution.py:385
  5.7 1.6 %collective-permute-start.3 = (bf16[16,4096]{1,0:T(8,128)(2,1)S(1)}, bf16[16,4096]{1,0:T(8,128)(2,1)S(1)}, u32[]{:S(2)}, u32[]{:S(2)}) collective-permute-start(bf16[16,4096]{1,0:T(8,128)(2,1)S(1)} %get-tuple-element.34.rest_0_.rest_4_), channel_id=1, source_target_pairs={{0,2},{1,3},{2,0},{3,1},{4,6},{5,7},{6,4},{7,5},{8,10},{9,11},{10,... | collective-permute-start | bytes 393224 | tf_op jit(solution)/shard_map/ppermute | solution.py:385
  7.3 1.5 %collective-permute-start.4 = (bf16[16,4096]{1,0:T(8,128)(2,1)S(1)}, bf16[16,4096]{1,0:T(8,128)(2,1)S(1)}, u32[]{:S(2)}, u32[]{:S(2)}) collective-permute-start(bf16[16,4096]{1,0:T(8,128)(2,1)S(1)} %get-tuple-element.34.rest_0_.rest_4_), channel_id=1, source_target_pairs={{0,1},{1,0},{2,3},{3,2},{4,5},{5,4},{6,7},{7,6},{8,9},{9,8},{10,11... | collective-permute-start | bytes 393224 | tf_op jit(solution)/shard_map/ppermute | solution.py:385
  8.8 0.6 %tables.1 = (f32[9,4096]{1,0:T(8,128)S(1)}, f32[9,4096]{1,0:T(8,128)S(1)}, bf16[128,4096]{1,0:T(8,128)(2,1)S(1)}) custom-call(f32[64,4000]{1,0:T(8,128)S(1)} %get-tuple-element.27.curves_ref, f32[1,4000]{1,0:T(1,128)S(1)} %get-tuple-element.28.noise_ref, f32[9,4000]{1,0:T(8,128)S(1)} %get-tuple-element.29.angle_ref), custom_call_target="tpu_custom_call" | custom-call | flops 4000000 | bytes 2000000 | tf_op jit(solution)/shard_map/tables/pallas_call | solution.py:400
  9.4 0.3 %shift_own.1 = (bf16[72,8192]{1,0:T(8,128)(2,1)S(1)}, bf16[16,4096]{1,0:T(8,128)(2,1)S(1)}) custom-call(f32[9,4096]{1,0:T(8,128)S(1)} %get-tuple-element.32.cos_ref, f32[9,4096]{1,0:T(8,128)S(1)} %get-tuple-element.33.sin_ref, bf16[16,4096]{1,0:T(8,128)(2,1)S(1)} %get-tuple-element.34.rest_0_.rest_4_), custom_call_target="tpu_custom_call" | custom-call | flops 1769472 | bytes 4000000 | tf_op jit(solution)/shard_map/shift_own/pallas_call | solution.py:416
  9.7 0.0 collective-permute-done
  9.8 1.6 %collective-permute-start.1 = (bf16[8,4224]{1,0:T(8,128)(2,1)S(1)}, bf16[8,4224]{1,0:T(8,128)(2,1)S(1)}, u32[]{:S(2)}, u32[]{:S(2)}) collective-permute-start(bf16[8,4224]{1,0:T(8,128)(2,1)S(1)} %pad_maximum_fusion.1), channel_id=1, source_target_pairs={{0,16},{8,24},{16,0},{24,8},{1,17},{9,25},{17,1},{25,9},{2,18},{10... | collective-permute-start | bytes 202760 | tf_op jit(solution)/shard_map/ppermute | solution.py:385
  11.3 0.0 collective-permute-done.3.rest_1_.rest_8_
  11.3 0.9 %collective-permute-done.4.rest_0_.rest_7_ = bf16[16,4096]{1,0:T(8,128)(2,1)S(1)} collective-permute-done((bf16[16,4096]{1,0:T(8,128)(2,1)S(1)}, bf16[16,4096]{1,0:T(8,128)(2,1)S(1)}, u32[]{:S(2)}, u32[]{:S(2)}) %collective-permute-start.4) | collective-permute-done | bytes 131104 | tf_op jit(solution)/shard_map/ppermute | solution.py:385
  12.3 1.6 %collective-permute-start.5 = (bf16[16,4480]{1,0:T(8,128)(2,1)S(1)}, bf16[16,4480]{1,0:T(8,128)(2,1)S(1)}, u32[]{:S(2)}, u32[]{:S(2)}) collective-permute-start(bf16[16,4480]{1,0:T(8,128)(2,1)S(1)} %pad.4), channel_id=1, source_target_pairs={{0,1},{1,0},{2,3},{3,2},{4,5},{5,4},{6,7},{7,6},{8,9},{9,8},{10,11... | collective-permute-start | bytes 430088 | tf_op jit(solution)/shard_map/ppermute | solution.py:385
  13.8 0.3 %collective-permute-done.1 = bf16[8,4224]{1,0:T(8,128)(2,1)S(1)} collective-permute-done((bf16[8,4224]{1,0:T(8,128)(2,1)S(1)}, bf16[8,4224]{1,0:T(8,128)(2,1)S(1)}, u32[]{:S(2)}, u32[]{:S(2)}) %collective-permute-start.1) | collective-permute-done | bytes 67616 | tf_op jit(solution)/shard_map/ppermute | solution.py:385
  14.1 0.1 pad_maximum_fusion.rest_0_
  14.2 0.1 collective-permute-start.2
  14.3 0.6 %shift_rest.1 = (bf16[144,8192]{1,0:T(8,128)(2,1)S(1)}, bf16[32,4096]{1,0:T(8,128)(2,1)S(1)}) custom-call(f32[9,4096]{1,0:T(8,128)S(1)} %get-tuple-element.32.cos_ref, f32[9,4096]{1,0:T(8,128)S(1)} %get-tuple-element.33.sin_ref, bf16[16,4096]{1,0:T(8,128)(2,1)S(1)} %collective-permute-done.4.rest_0_.rest_7_, ...), custom_call_target="tpu_custom_call" | custom-call | flops 3538944 | bytes 4000000 | tf_op jit(solution)/shard_map/shift_rest/pallas_call | solution.py:416
  14.9 0.7 %collective-permute-done.2.rest_1_ = bf16[16,4224]{1,0:T(8,128)(2,1)S(1)} collective-permute-done((bf16[16,4224]{1,0:T(8,128)(2,1)S(1)}, bf16[16,4224]{1,0:T(8,128)(2,1)S(1)}, u32[]{:S(2)}, u32[]{:S(2)}) %collective-permute-start.2) | collective-permute-done | bytes 135200 | tf_op jit(solution)/shard_map/ppermute | solution.py:385
  15.6 1.8 %early.1 = (bf16[16,8192]{1,0:T(8,128)(2,1)S(1)}, f32[16,256]{1,0:T(8,128)S(1)}, bf16[32,4096]{1,0:T(8,128)(2,1)S(1)}, f32[16,384]{1,0:T(8,128)S(1)}) custom-call(bf16[128,4096]{1,0:T(8,128)(2,1)S(1)} %get-tuple-element.30.square_ref, bf16[16,4224]{1,0:T(8,128)(2,1)S(1)} %pad_maximum_fusion.rest_0_, bf16[16,4224]{1,0:T(8,128)(2,1)S(1)} %collective-permute-done.2.rest_1_, ...), custom_call_target="tpu_custom_call" | custom-call | flops 56623104 | bytes 4000000 | tf_op jit(solution)/shard_map/early/pallas_call | solution.py:441
  17.4 0.0 collective-permute-done.5.last_ref
  17.4 0.7 %final.1 = (f32[8,512]{1,0:T(8,128)S(1)}, f32[8,512]{1,0:T(8,128)S(1)}) custom-call(bf16[16,8192]{1,0:T(8,128)(2,1)S(1)} %get-tuple-element.43.weighted_ref, f32[16,256]{1,0:T(8,128)S(1)} %get-tuple-element.44.extra_ref, bf16[32,4096]{1,0:T(8,128)(2,1)S(1)} %get-tuple-element.45.select_ref, f32[16,384]{1,0:T(8,128)S(1)} %get-tuple-element.46.rows_ref, ...), custom_call_target="tpu_custom_call" | custom-call | flops 18874368 | bytes 4000000 | tf_op jit(solution)/shard_map/final/pallas_call | solution.py:461
  18.1 1.0 %collective-permute-start.6 = (f32[8,512]{1,0:T(8,128)S(1)}, f32[8,512]{1,0:T(8,128)S(1)}, u32[]{:S(2)}, u32[]{:S(2)}) collective-permute-start(f32[8,512]{1,0:T(8,128)S(1)} %get-tuple-element.48), channel_id=1, source_target_pairs={{0,4},{1,5},{2,6},{3,7},{4,0},{5,1},{6,2},{7,3},{8,12},{9,13},{10,... | collective-permute-start | bytes 49160 | tf_op jit(solution)/shard_map/ppermute | solution.py:385
  19.2 3.7 %collective-permute-done.6.recv_ref = f32[8,512]{1,0:T(8,128)S(1)} collective-permute-done((f32[8,512]{1,0:T(8,128)S(1)}, f32[8,512]{1,0:T(8,128)S(1)}, u32[]{:S(2)}, u32[]{:S(2)}) %collective-permute-start.6) | collective-permute-done | bytes 16416 | tf_op jit(solution)/shard_map/ppermute | solution.py:385
  22.9 0.8 %place.1 = f32[9,8,64]{2,1,0:T(8,128)} custom-call(f32[8,512]{1,0:T(8,128)S(1)} %get-tuple-element.47.keep_ref, f32[8,512]{1,0:T(8,128)S(1)} %collective-permute-done.6.recv_ref), custom_call_target="tpu_custom_call" | custom-call | tf_op jit(solution)/shard_map/place/pallas_call | solution.py:472
  (2 shorter events, 0.1 us)
Async XLA Ops:
  1.6 8.1 %collective-permute-start = (bf16[4,4224]{1,0:T(4,128)(2,1)S(1)}, bf16[4,4224]{1,0:T(4,128)(2,1)S(1)}, u32[]{:S(2)}, u32[]{:S(2)}) collective-permute-start(bf16[4,4224]{1,0:T(4,128)(2,1)S(1)} %get-tuple-element.31), channel_id=1, source_target_pairs={{0,4},{1,5},{2,6},{3,7},{4,0},{5,1},{6,2},{7,3},{8,12},{9,13},{10,... | collective-permute-start | bytes 101384 | tf_op jit(solution)/shard_map/ppermute | solution.py:385
  5.7 5.6 %collective-permute-start.3 = (bf16[16,4096]{1,0:T(8,128)(2,1)S(1)}, bf16[16,4096]{1,0:T(8,128)(2,1)S(1)}, u32[]{:S(2)}, u32[]{:S(2)}) collective-permute-start(bf16[16,4096]{1,0:T(8,128)(2,1)S(1)} %get-tuple-element.34.rest_0_.rest_4_), channel_id=1, source_target_pairs={{0,2},{1,3},{2,0},{3,1},{4,6},{5,7},{6,4},{7,5},{8,10},{9,11},{10,... | collective-permute-start | bytes 393224 | tf_op jit(solution)/shard_map/ppermute | solution.py:385
  7.3 5.0 %collective-permute-start.4 = (bf16[16,4096]{1,0:T(8,128)(2,1)S(1)}, bf16[16,4096]{1,0:T(8,128)(2,1)S(1)}, u32[]{:S(2)}, u32[]{:S(2)}) collective-permute-start(bf16[16,4096]{1,0:T(8,128)(2,1)S(1)} %get-tuple-element.34.rest_0_.rest_4_), channel_id=1, source_target_pairs={{0,1},{1,0},{2,3},{3,2},{4,5},{5,4},{6,7},{7,6},{8,9},{9,8},{10,11... | collective-permute-start | bytes 393224 | tf_op jit(solution)/shard_map/ppermute | solution.py:385
  9.8 4.4 %collective-permute-start.1 = (bf16[8,4224]{1,0:T(8,128)(2,1)S(1)}, bf16[8,4224]{1,0:T(8,128)(2,1)S(1)}, u32[]{:S(2)}, u32[]{:S(2)}) collective-permute-start(bf16[8,4224]{1,0:T(8,128)(2,1)S(1)} %pad_maximum_fusion.1), channel_id=1, source_target_pairs={{0,16},{8,24},{16,0},{24,8},{1,17},{9,25},{17,1},{25,9},{2,18},{10... | collective-permute-start | bytes 202760 | tf_op jit(solution)/shard_map/ppermute | solution.py:385
  12.3 5.2 %collective-permute-start.5 = (bf16[16,4480]{1,0:T(8,128)(2,1)S(1)}, bf16[16,4480]{1,0:T(8,128)(2,1)S(1)}, u32[]{:S(2)}, u32[]{:S(2)}) collective-permute-start(bf16[16,4480]{1,0:T(8,128)(2,1)S(1)} %pad.4), channel_id=1, source_target_pairs={{0,1},{1,0},{2,3},{3,2},{4,5},{5,4},{6,7},{7,6},{8,9},{9,8},{10,11... | collective-permute-start | bytes 430088 | tf_op jit(solution)/shard_map/ppermute | solution.py:385
  14.2 1.4 %collective-permute-start.2 = (bf16[16,4224]{1,0:T(8,128)(2,1)S(1)}, bf16[16,4224]{1,0:T(8,128)(2,1)S(1)}, u32[]{:S(2)}, u32[]{:S(2)}) collective-permute-start(bf16[16,4224]{1,0:T(8,128)(2,1)S(1)} %pad_maximum_fusion.rest_0_), channel_id=1, source_target_pairs={{0,8},{8,0},{16,24},{24,16},{1,9},{9,1},{17,25},{25,17},{2,10},{10... | collective-permute-start | bytes 405512 | tf_op jit(solution)/shard_map/ppermute | solution.py:385
  18.1 4.7 %collective-permute-start.6 = (f32[8,512]{1,0:T(8,128)S(1)}, f32[8,512]{1,0:T(8,128)S(1)}, u32[]{:S(2)}, u32[]{:S(2)}) collective-permute-start(f32[8,512]{1,0:T(8,128)S(1)} %get-tuple-element.48), channel_id=1, source_target_pairs={{0,4},{1,5},{2,6},{3,7},{4,0},{5,1},{6,2},{7,3},{8,12},{9,13},{10,... | collective-permute-start | bytes 49160 | tf_op jit(solution)/shard_map/ppermute | solution.py:385

commit v14 on v13

--- a/solution.py
+++ b/solution.py
@@ -261,7 +261,7 @@
 
     pieces = []
     for shifted_ref, power_ref, banks in groups:
-        cross = multiply(weighted_ref[...], shifted_ref[...])
+        cross = multiply(shifted_ref[...], weighted_ref[...]).T
         norm = multiply(select_ref[...], power_ref[...])
         pieces += pieces_of(cross, norm, extra, banks, length, subsets, n_proj)
     store_pieces(rows_ref, pieces, 0, rows_ref.shape[1] // len(pieces), slice(None))
@@ -277,15 +277,15 @@
         for real, imag in bank_pieces(last_ref, span, n_proj):
             real_rows, imag_rows = shifted_rows(real, imag, cos_ref, sin_ref, span)
             terms.append(
-                multiply(weighted_ref[:, span], real_rows)
-                + multiply(weighted_ref[:, wide + span.start : wide + span.stop], imag_rows)
+                multiply(real_rows, weighted_ref[:, span])
+                + multiply(imag_rows, weighted_ref[:, wide + span.start : wide + span.stop])
             )
             powers.append(real * real + imag * imag)
-        terms = jnp.concatenate(terms, axis=1)
+        terms = jnp.concatenate(terms, axis=0)
         norms = multiply(select_ref[:, span], split_terms(jnp.concatenate(powers, axis=0)))
         cross = terms if cross is None else cross + terms
         norm = norms if norm is None else norm + norms
-    pieces = pieces_of(cross, norm, extra_ref[...], [last_ref], length, subsets, n_proj)
+    pieces = pieces_of(cross.T, norm, extra_ref[...], [last_ref], length, subsets, n_proj)
     dest, lanes = outs[0].shape
     held = rows_ref.shape[1]
     for s, out in enumerate(outs):

time: 23.8 us -> 23.9 us (level)
  no operation moved by 1% of the time
where the time goes in v14:
time: 23.9 us; the launch traced here: 23.7 us
  starting transfers between devices  11.5 us (48%)
  Pallas kernels  6.44 us (27%)
  waiting for transfers between devices  5.63 us (24%)
    ppermute x7, starting transfers between devices, swap(): return lax.ppermute(value, axis, [(i, i ^ bit) for i in range(size)])  11.5 us
    ppermute x7, waiting for transfers between devices, swap(): return lax.ppermute(value, axis, [(i, i ^ bit) for i in range(size)])  5.63 us
    pallas_call x1, Pallas kernels, per_device(): pl.pallas_call(functools.partial(early_kernel, len(parts), (1, 2), ng, we...  1.86 us
    pallas_call x1, Pallas kernels, per_device(): pl.pallas_call(pack_kernel, out_shape=[vmem_out((2 * n_proj, wide), BF16)...  1.58 us
    pallas_call x2, Pallas kernels, shifted_call(): pl.pallas_call(functools.partial(shift_kernel, n_proj), out_shape=[vmem_o...  0.94 us
    pallas_call x1, Pallas kernels, per_device(): pl.pallas_call(functools.partial(place_kernel, half, n_proj, order), out_...  0.77 us
    pallas_call x1, Pallas kernels, per_device(): pl.pallas_call(functools.partial(final_kernel, half, n_proj, length, subs...  0.71 us
    pallas_call x1, Pallas kernels, per_device(): pl.pallas_call(table_kernel, out_shape=[vmem_out((shifts, wide), F32), vm...  0.58 us
  transfers between devices with their start and end apart: 7, of which 4 were waited for; matrix products, arithmetic and copies ran while one was open for 0% of the time, Pallas kernels for 14%

profile of v14, /device:TPU:0, one launch (start us, length us, event | category | flops | bytes accessed | tf_op | source)
XLA Modules:
  0.0 23.7 jit_solution(8458289194677996987)
XLA Ops:
  0.0 1.6 %pack.1 = (bf16[16,4096]{1,0:T(8,128)(2,1)S(1)}, bf16[4,4224]{1,0:T(4,128)(2,1)S(1)}, f32[64,4000]{1,0:T(8,128)S(1)}, f32[1,4000]{1,0:T(1,128)S(1)}, f32[9,4000]{1,0:T(8,128)S(1)}) custom-call(s32[2]{0:T(128)} %class_hbm.1, s32[8]{0:T(128)} %subset_hbm.1, bf16[2,2,4000]{2,1,0:T(2,128)(2,1)} %particles_hbm.1, bf16[2,192]{1,0:T(2,128)(2,1)} %prior_hbm.1, ...), custom_call_target="tpu_custom_call" | custom-call | tf_op jit(solution)/shard_map/pack/pallas_call | solution.py:358
  1.6 4.1 %collective-permute-start = (bf16[4,4224]{1,0:T(4,128)(2,1)S(1)}, bf16[4,4224]{1,0:T(4,128)(2,1)S(1)}, u32[]{:S(2)}, u32[]{:S(2)}) collective-permute-start(bf16[4,4224]{1,0:T(4,128)(2,1)S(1)} %get-tuple-element.31), channel_id=1, source_target_pairs={{0,4},{1,5},{2,6},{3,7},{4,0},{5,1},{6,2},{7,3},{8,12},{9,13},{10,... | collective-permute-start | bytes 101384 | tf_op jit(solution)/shard_map/ppermute | solution.py:385
  5.7 1.6 %collective-permute-start.3 = (bf16[16,4096]{1,0:T(8,128)(2,1)S(1)}, bf16[16,4096]{1,0:T(8,128)(2,1)S(1)}, u32[]{:S(2)}, u32[]{:S(2)}) collective-permute-start(bf16[16,4096]{1,0:T(8,128)(2,1)S(1)} %get-tuple-element.34.rest_0_.rest_4_), channel_id=1, source_target_pairs={{0,2},{1,3},{2,0},{3,1},{4,6},{5,7},{6,4},{7,5},{8,10},{9,11},{10,... | collective-permute-start | bytes 393224 | tf_op jit(solution)/shard_map/ppermute | solution.py:385
  7.3 1.5 %collective-permute-start.4 = (bf16[16,4096]{1,0:T(8,128)(2,1)S(1)}, bf16[16,4096]{1,0:T(8,128)(2,1)S(1)}, u32[]{:S(2)}, u32[]{:S(2)}) collective-permute-start(bf16[16,4096]{1,0:T(8,128)(2,1)S(1)} %get-tuple-element.34.rest_0_.rest_4_), channel_id=1, source_target_pairs={{0,1},{1,0},{2,3},{3,2},{4,5},{5,4},{6,7},{7,6},{8,9},{9,8},{10,11... | collective-permute-start | bytes 393224 | tf_op jit(solution)/shard_map/ppermute | solution.py:385
  8.8 0.6 %tables.1 = (f32[9,4096]{1,0:T(8,128)S(1)}, f32[9,4096]{1,0:T(8,128)S(1)}, bf16[128,4096]{1,0:T(8,128)(2,1)S(1)}) custom-call(f32[64,4000]{1,0:T(8,128)S(1)} %get-tuple-element.27.curves_ref, f32[1,4000]{1,0:T(1,128)S(1)} %get-tuple-element.28.noise_ref, f32[9,4000]{1,0:T(8,128)S(1)} %get-tuple-element.29.angle_ref), custom_call_target="tpu_custom_call" | custom-call | flops 4000000 | bytes 2000000 | tf_op jit(solution)/shard_map/tables/pallas_call | solution.py:400
  9.4 0.3 %shift_own.1 = (bf16[72,8192]{1,0:T(8,128)(2,1)S(1)}, bf16[16,4096]{1,0:T(8,128)(2,1)S(1)}) custom-call(f32[9,4096]{1,0:T(8,128)S(1)} %get-tuple-element.32.cos_ref, f32[9,4096]{1,0:T(8,128)S(1)} %get-tuple-element.33.sin_ref, bf16[16,4096]{1,0:T(8,128)(2,1)S(1)} %get-tuple-element.34.rest_0_.rest_4_), custom_call_target="tpu_custom_call" | custom-call | flops 1769472 | bytes 4000000 | tf_op jit(solution)/shard_map/shift_own/pallas_call | solution.py:416
  9.7 0.0 collective-permute-done
  9.8 1.6 %collective-permute-start.1 = (bf16[8,4224]{1,0:T(8,128)(2,1)S(1)}, bf16[8,4224]{1,0:T(8,128)(2,1)S(1)}, u32[]{:S(2)}, u32[]{:S(2)}) collective-permute-start(bf16[8,4224]{1,0:T(8,128)(2,1)S(1)} %pad_maximum_fusion.1), channel_id=1, source_target_pairs={{0,16},{8,24},{16,0},{24,8},{1,17},{9,25},{17,1},{25,9},{2,18},{10... | collective-permute-start | bytes 202760 | tf_op jit(solution)/shard_map/ppermute | solution.py:385
  11.3 0.0 collective-permute-done.3.rest_1_.rest_8_
  11.3 0.9 %collective-permute-done.4.rest_0_.rest_7_ = bf16[16,4096]{1,0:T(8,128)(2,1)S(1)} collective-permute-done((bf16[16,4096]{1,0:T(8,128)(2,1)S(1)}, bf16[16,4096]{1,0:T(8,128)(2,1)S(1)}, u32[]{:S(2)}, u32[]{:S(2)}) %collective-permute-start.4) | collective-permute-done | bytes 131104 | tf_op jit(solution)/shard_map/ppermute | solution.py:385
  12.3 1.6 %collective-permute-start.5 = (bf16[16,4480]{1,0:T(8,128)(2,1)S(1)}, bf16[16,4480]{1,0:T(8,128)(2,1)S(1)}, u32[]{:S(2)}, u32[]{:S(2)}) collective-permute-start(bf16[16,4480]{1,0:T(8,128)(2,1)S(1)} %pad.4), channel_id=1, source_target_pairs={{0,1},{1,0},{2,3},{3,2},{4,5},{5,4},{6,7},{7,6},{8,9},{9,8},{10,11... | collective-permute-start | bytes 430088 | tf_op jit(solution)/shard_map/ppermute | solution.py:385
  13.8 0.3 %collective-permute-done.1 = bf16[8,4224]{1,0:T(8,128)(2,1)S(1)} collective-permute-done((bf16[8,4224]{1,0:T(8,128)(2,1)S(1)}, bf16[8,4224]{1,0:T(8,128)(2,1)S(1)}, u32[]{:S(2)}, u32[]{:S(2)}) %collective-permute-start.1) | collective-permute-done | bytes 67616 | tf_op jit(solution)/shard_map/ppermute | solution.py:385
  14.1 0.1 pad_maximum_fusion.rest_0_
  14.2 0.1 collective-permute-start.2
  14.3 0.6 %shift_rest.1 = (bf16[144,8192]{1,0:T(8,128)(2,1)S(1)}, bf16[32,4096]{1,0:T(8,128)(2,1)S(1)}) custom-call(f32[9,4096]{1,0:T(8,128)S(1)} %get-tuple-element.32.cos_ref, f32[9,4096]{1,0:T(8,128)S(1)} %get-tuple-element.33.sin_ref, bf16[16,4096]{1,0:T(8,128)(2,1)S(1)} %collective-permute-done.4.rest_0_.rest_7_, ...), custom_call_target="tpu_custom_call" | custom-call | flops 3538944 | bytes 4000000 | tf_op jit(solution)/shard_map/shift_rest/pallas_call | solution.py:416
  14.9 0.7 %collective-permute-done.2.rest_1_ = bf16[16,4224]{1,0:T(8,128)(2,1)S(1)} collective-permute-done((bf16[16,4224]{1,0:T(8,128)(2,1)S(1)}, bf16[16,4224]{1,0:T(8,128)(2,1)S(1)}, u32[]{:S(2)}, u32[]{:S(2)}) %collective-permute-start.2) | collective-permute-done | bytes 135200 | tf_op jit(solution)/shard_map/ppermute | solution.py:385
  15.6 1.9 %early.1 = (bf16[16,8192]{1,0:T(8,128)(2,1)S(1)}, f32[16,256]{1,0:T(8,128)S(1)}, bf16[32,4096]{1,0:T(8,128)(2,1)S(1)}, f32[16,384]{1,0:T(8,128)S(1)}) custom-call(bf16[128,4096]{1,0:T(8,128)(2,1)S(1)} %get-tuple-element.30.square_ref, bf16[16,4224]{1,0:T(8,128)(2,1)S(1)} %pad_maximum_fusion.rest_0_, bf16[16,4224]{1,0:T(8,128)(2,1)S(1)} %collective-permute-done.2.rest_1_, ...), custom_call_target="tpu_custom_call" | custom-call | flops 56623104 | bytes 4000000 | tf_op jit(solution)/shard_map/early/pallas_call | solution.py:441
  17.5 0.0 collective-permute-done.5.last_ref
  17.5 0.7 %final.1 = (f32[8,512]{1,0:T(8,128)S(1)}, f32[8,512]{1,0:T(8,128)S(1)}) custom-call(bf16[16,8192]{1,0:T(8,128)(2,1)S(1)} %get-tuple-element.43.weighted_ref, f32[16,256]{1,0:T(8,128)S(1)} %get-tuple-element.44.extra_ref, bf16[32,4096]{1,0:T(8,128)(2,1)S(1)} %get-tuple-element.45.select_ref, f32[16,384]{1,0:T(8,128)S(1)} %get-tuple-element.46.rows_ref, ...), custom_call_target="tpu_custom_call" | custom-call | flops 18874368 | bytes 4000000 | tf_op jit(solution)/shard_map/final/pallas_call | solution.py:461
  18.2 1.1 %collective-permute-start.6 = (f32[8,512]{1,0:T(8,128)S(1)}, f32[8,512]{1,0:T(8,128)S(1)}, u32[]{:S(2)}, u32[]{:S(2)}) collective-permute-start(f32[8,512]{1,0:T(8,128)S(1)} %get-tuple-element.48), channel_id=1, source_target_pairs={{0,4},{1,5},{2,6},{3,7},{4,0},{5,1},{6,2},{7,3},{8,12},{9,13},{10,... | collective-permute-start | bytes 49160 | tf_op jit(solution)/shard_map/ppermute | solution.py:385
  19.3 3.7 %collective-permute-done.6.recv_ref = f32[8,512]{1,0:T(8,128)S(1)} collective-permute-done((f32[8,512]{1,0:T(8,128)S(1)}, f32[8,512]{1,0:T(8,128)S(1)}, u32[]{:S(2)}, u32[]{:S(2)}) %collective-permute-start.6) | collective-permute-done | bytes 16416 | tf_op jit(solution)/shard_map/ppermute | solution.py:385
  23.0 0.8 %place.1 = f32[9,8,64]{2,1,0:T(8,128)} custom-call(f32[8,512]{1,0:T(8,128)S(1)} %get-tuple-element.47.keep_ref, f32[8,512]{1,0:T(8,128)S(1)} %collective-permute-done.6.recv_ref), custom_call_target="tpu_custom_call" | custom-call | tf_op jit(solution)/shard_map/place/pallas_call | solution.py:472
  (2 shorter events, 0.1 us)
Async XLA Ops:
  1.6 8.1 %collective-permute-start = (bf16[4,4224]{1,0:T(4,128)(2,1)S(1)}, bf16[4,4224]{1,0:T(4,128)(2,1)S(1)}, u32[]{:S(2)}, u32[]{:S(2)}) collective-permute-start(bf16[4,4224]{1,0:T(4,128)(2,1)S(1)} %get-tuple-element.31), channel_id=1, source_target_pairs={{0,4},{1,5},{2,6},{3,7},{4,0},{5,1},{6,2},{7,3},{8,12},{9,13},{10,... | collective-permute-start | bytes 101384 | tf_op jit(solution)/shard_map/ppermute | solution.py:385
  5.7 5.6 %collective-permute-start.3 = (bf16[16,4096]{1,0:T(8,128)(2,1)S(1)}, bf16[16,4096]{1,0:T(8,128)(2,1)S(1)}, u32[]{:S(2)}, u32[]{:S(2)}) collective-permute-start(bf16[16,4096]{1,0:T(8,128)(2,1)S(1)} %get-tuple-element.34.rest_0_.rest_4_), channel_id=1, source_target_pairs={{0,2},{1,3},{2,0},{3,1},{4,6},{5,7},{6,4},{7,5},{8,10},{9,11},{10,... | collective-permute-start | bytes 393224 | tf_op jit(solution)/shard_map/ppermute | solution.py:385
  7.3 5.0 %collective-permute-start.4 = (bf16[16,4096]{1,0:T(8,128)(2,1)S(1)}, bf16[16,4096]{1,0:T(8,128)(2,1)S(1)}, u32[]{:S(2)}, u32[]{:S(2)}) collective-permute-start(bf16[16,4096]{1,0:T(8,128)(2,1)S(1)} %get-tuple-element.34.rest_0_.rest_4_), channel_id=1, source_target_pairs={{0,1},{1,0},{2,3},{3,2},{4,5},{5,4},{6,7},{7,6},{8,9},{9,8},{10,11... | collective-permute-start | bytes 393224 | tf_op jit(solution)/shard_map/ppermute | solution.py:385
  9.8 4.4 %collective-permute-start.1 = (bf16[8,4224]{1,0:T(8,128)(2,1)S(1)}, bf16[8,4224]{1,0:T(8,128)(2,1)S(1)}, u32[]{:S(2)}, u32[]{:S(2)}) collective-permute-start(bf16[8,4224]{1,0:T(8,128)(2,1)S(1)} %pad_maximum_fusion.1), channel_id=1, source_target_pairs={{0,16},{8,24},{16,0},{24,8},{1,17},{9,25},{17,1},{25,9},{2,18},{10... | collective-permute-start | bytes 202760 | tf_op jit(solution)/shard_map/ppermute | solution.py:385
  12.3 5.2 %collective-permute-start.5 = (bf16[16,4480]{1,0:T(8,128)(2,1)S(1)}, bf16[16,4480]{1,0:T(8,128)(2,1)S(1)}, u32[]{:S(2)}, u32[]{:S(2)}) collective-permute-start(bf16[16,4480]{1,0:T(8,128)(2,1)S(1)} %pad.4), channel_id=1, source_target_pairs={{0,1},{1,0},{2,3},{3,2},{4,5},{5,4},{6,7},{7,6},{8,9},{9,8},{10,11... | collective-permute-start | bytes 430088 | tf_op jit(solution)/shard_map/ppermute | solution.py:385
  14.2 1.4 %collective-permute-start.2 = (bf16[16,4224]{1,0:T(8,128)(2,1)S(1)}, bf16[16,4224]{1,0:T(8,128)(2,1)S(1)}, u32[]{:S(2)}, u32[]{:S(2)}) collective-permute-start(bf16[16,4224]{1,0:T(8,128)(2,1)S(1)} %pad_maximum_fusion.rest_0_), channel_id=1, source_target_pairs={{0,8},{8,0},{16,24},{24,16},{1,9},{9,1},{17,25},{25,17},{2,10},{10... | collective-permute-start | bytes 405512 | tf_op jit(solution)/shard_map/ppermute | solution.py:385
  18.2 4.8 %collective-permute-start.6 = (f32[8,512]{1,0:T(8,128)S(1)}, f32[8,512]{1,0:T(8,128)S(1)}, u32[]{:S(2)}, u32[]{:S(2)}) collective-permute-start(f32[8,512]{1,0:T(8,128)S(1)} %get-tuple-element.48), channel_id=1, source_target_pairs={{0,4},{1,5},{2,6},{3,7},{4,0},{5,1},{6,2},{7,3},{8,12},{9,13},{10,... | collective-permute-start | bytes 49160 | tf_op jit(solution)/shard_map/ppermute | solution.py:385

commit v15 on v13

--- a/solution.py
+++ b/solution.py
@@ -189,10 +189,18 @@
     return [slice(at, at + step) for at in range(0, wide, step)]
 
 
-def shift_kernel(n_proj, cos_ref, sin_ref, *rest):
-    *banks, shifted_ref, power_ref = rest
+def table_of(norms):
+    classes_count, total = norms.shape[0] // 2, norms.shape[1] // 2
+    return (
+        norms[:classes_count, total:] + norms[classes_count:, :total] + norms[:classes_count, :total]
+    )
+
+
+def shift_kernel(n_proj, cos_ref, sin_ref, square_ref, *rest):
+    *banks, shifted_ref, table_ref = rest
     shifts, wide = cos_ref.shape
     width = shifts * n_proj
+    norms = None
     for span in spans_of(wide):
         powers, at = [], 0
         for bank in banks:
@@ -202,17 +210,21 @@
                 shifted_ref[at : at + width, wide + span.start : wide + span.stop] = imag_rows
                 powers.append(real * real + imag * imag)
                 at += width
-        power_ref[:, span] = split_terms(jnp.concatenate(powers, axis=0))
+        terms = multiply(square_ref[:, span], split_terms(jnp.concatenate(powers, axis=0)))
+        norms = terms if norms is None else norms + terms
+    table_ref[...] = table_of(norms)
 
 
 def multiply(left, right):
     return lax.dot_general(left, right, NT_DIMS, preferred_element_type=F32)
 
 
-def pieces_of(cross, norm, extra, banks, length, subsets, n_proj):
-    count, total = cross.shape[0], norm.shape[1] // 2
+def pieces_of(cross, table, extra, banks, length, subsets, n_proj):
+    classes_count, total = table.shape
     width = cross.shape[1] * n_proj // total
-    norm = norm[:count, total:] + norm[count:, :total] + norm[:count, :total]
+    class_col = lax.broadcasted_iota(jnp.int32, (cross.shape[0], classes_count), 1).astype(F32)
+    onehot = (class_col == extra[:, subsets : subsets + 1]).astype(F32)
+    norm = jnp.dot(onehot, table, precision=HIGHEST, preferred_element_type=F32)
     added = added_rows(extra, norm, banks, n_proj, length, subsets)
     pieces = []
     for n in range(total // n_proj):
@@ -227,15 +239,14 @@
         out[:, at : at + piece.shape[1]] = piece[rows]
 
 
-def early_kernel(n_parts, n_banks, ng, weights, n_part, n_proj, length, subsets, square_ref, *rest):
+def early_kernel(n_parts, n_banks, ng, weights, n_part, n_proj, length, subsets, *rest):
     parts, rest = rest[:n_parts], rest[n_parts:]
-    groups, (weighted_ref, extra_ref, select_ref, rows_ref) = [], rest[-4:]
+    groups, (weighted_ref, extra_ref, rows_ref) = [], rest[-3:]
     for n in n_banks:
         groups.append((rest[0], rest[1], rest[2 : 2 + n]))
         rest = rest[2 + n :]
     g = lax.axis_index("grp")
     wide = weighted_ref.shape[1] // 2
-    classes_count = square_ref.shape[0] // 2
 
     held = jnp.concatenate([part[...] for part in parts], axis=0)
     count = 2 * ng * n_part
@@ -252,23 +263,15 @@
     weighted_ref[:, wide:] = ordered[count:, :wide].astype(BF16)
     extra = jnp.concatenate([ordered[:count, wide:], ordered[count:, wide:]], axis=1)
     extra_ref[...] = extra
-    class_col = lax.broadcasted_iota(jnp.int32, (count, classes_count), 1).astype(F32)
-    onehot = (class_col == extra[:, subsets : subsets + 1]).astype(F32).astype(BF16)
-    for n in range(2):
-        squares = square_ref[n * classes_count : (n + 1) * classes_count, :]
-        chosen = jnp.dot(onehot, squares, preferred_element_type=F32)
-        select_ref[n * count : (n + 1) * count, :] = chosen.astype(BF16)
-
     pieces = []
-    for shifted_ref, power_ref, banks in groups:
+    for shifted_ref, table_ref, banks in groups:
         cross = multiply(weighted_ref[...], shifted_ref[...])
-        norm = multiply(select_ref[...], power_ref[...])
-        pieces += pieces_of(cross, norm, extra, banks, length, subsets, n_proj)
+        pieces += pieces_of(cross, table_ref[...], extra, banks, length, subsets, n_proj)
     store_pieces(rows_ref, pieces, 0, rows_ref.shape[1] // len(pieces), slice(None))
 
 
 def final_kernel(
-    half, n_proj, length, subsets, weighted_ref, extra_ref, select_ref, rows_ref, cos_ref, sin_ref, last_ref, *outs
+    half, n_proj, length, subsets, weighted_ref, extra_ref, rows_ref, cos_ref, sin_ref, square_ref, last_ref, *outs
 ):
     shifts, wide = cos_ref.shape
     cross, norm = None, None
@@ -282,10 +285,10 @@
             )
             powers.append(real * real + imag * imag)
         terms = jnp.concatenate(terms, axis=1)
-        norms = multiply(select_ref[:, span], split_terms(jnp.concatenate(powers, axis=0)))
+        norms = multiply(square_ref[:, span], split_terms(jnp.concatenate(powers, axis=0)))
         cross = terms if cross is None else cross + terms
         norm = norms if norm is None else norm + norms
-    pieces = pieces_of(cross, norm, extra_ref[...], [last_ref], length, subsets, n_proj)
+    pieces = pieces_of(cross, table_of(norm), extra_ref[...], [last_ref], length, subsets, n_proj)
     dest, lanes = outs[0].shape
     held = rows_ref.shape[1]
     for s, out in enumerate(outs):
@@ -415,41 +418,40 @@
         total = sum(piece.shape[0] for piece in banks) // 2
         return pl.pallas_call(
             functools.partial(shift_kernel, n_proj),
-            out_shape=[vmem_out((shifts * total, 2 * wide), BF16), vmem_out((2 * total, wide), BF16)],
-            in_specs=[_vmem()] * (2 + len(banks)),
+            out_shape=[vmem_out((shifts * total, 2 * wide), BF16), vmem_out((classes_count, total), F32)],
+            in_specs=[_vmem()] * (3 + len(banks)),
             out_specs=[_vmem()] * 2,
             compiler_params=_params(16),
             cost_estimate=pl.CostEstimate(
                 flops=6 * total * shifts * wide, bytes_accessed=4_000_000, transcendentals=0
             ),
             name=name,
-        )(cos_part, sin_part, *banks)
-
-    own_rows, own_power = shifted_call([bank], "shift_own")
-
-    across, own_power = lax.optimization_barrier((across, own_power))
+        )(cos_part, sin_part, square, *banks)
+
+    own_rows, own_norms = shifted_call([bank], "shift_own")
+
+    across, own_norms = lax.optimization_barrier((across, own_norms))
     parts, weights = [part, across], []
     for n in range(ng.bit_length() - 2, -1, -1):
         part = joined(parts)
         parts = [part, swap(part, "grp", 1 << n)]
         weights.append((1 << n, 2 << len(weights)))
 
-    rest_rows, rest_power = shifted_call([near, far], "shift_rest")
+    rest_rows, rest_norms = shifted_call([near, far], "shift_rest")
     count = 2 * ng * n_part
     late = half // 2 - 1
     slot = 128 * -(-(shifts + 1) * n_proj // 128)
-    weighted, extra_rows, select, rows = pl.pallas_call(
+    weighted, extra_rows, rows = pl.pallas_call(
         functools.partial(
             early_kernel, len(parts), (1, 2), ng, weights, n_part, n_proj, length, subsets
         ),
         out_shape=[
             vmem_out((count, 2 * wide), BF16),
             vmem_out((count, 2 * extra), F32),
-            vmem_out((2 * count, wide), BF16),
             vmem_out((count, (half - late) * slot), F32),
         ],
-        in_specs=[_vmem()] * (8 + len(parts)),
-        out_specs=[_vmem()] * 4,
+        in_specs=[_vmem()] * (7 + len(parts)),
+        out_specs=[_vmem()] * 3,
         compiler_params=_params(16),
         cost_estimate=pl.CostEstimate(
             flops=4 * count * (half - late) * n_proj * shifts * wide,
@@ -457,7 +459,7 @@
             transcendentals=0,
         ),
         name="early",
-    )(square, *parts, own_rows, own_power, bank, rest_rows, rest_power, near, far)
+    )(*parts, own_rows, own_norms, bank, rest_rows, rest_norms, near, far)
     keep, give = pl.pallas_call(
         functools.partial(final_kernel, half, n_proj, length, subsets),
         out_shape=[vmem_out((ng * n_part, half * slot), F32)] * 2,
@@ -468,7 +470,7 @@
             flops=4 * count * late * n_proj * shifts * wide, bytes_accessed=4_000_000, transcendentals=0
         ),
         name="final",
-    )(weighted, extra_rows, select, rows, cos_part, sin_part, last)
+    )(weighted, extra_rows, rows, cos_part, sin_part, square, last)
     scores = pl.pallas_call(
         functools.partial(place_kernel, half, n_proj, order),
         out_shape=shape((shifts, ng * n_part, nb * n_proj), F32),

time: 23.8 us -> 24.3 us (1.021)
  Pallas kernels: 6.4 us -> 7.54 us
  starting transfers between devices: 11.4 us -> 10.9 us
    pallas_call x2, Pallas kernels: 0.94 us -> 2.07 us  [shifted_call(): pl.pallas_call(functools.partial(shift_kernel, n_proj), out_shape=[vmem_o...]
    ppermute x7, starting transfers between devices: 11.4 us -> 10.9 us  [swap(): return lax.ppermute(value, axis, [(i, i ^ bit) for i in range(size)])]
    pallas_call x1, Pallas kernels: 0.73 us -> 1.13 us  [per_device(): pl.pallas_call(functools.partial(final_kernel, half, n_proj, length, subs...]
    pallas_call x1, Pallas kernels: 1.81 us -> 1.42 us  [per_device(): pl.pallas_call(functools.partial(early_kernel, len(parts), (1, 2), ng, we...]
  transfers between devices with their start and end apart: 7 -> 7, of which waited for: 4 -> 4; matrix products, arithmetic and copies ran while one was open for 0% -> 0% of each run, Pallas kernels for 14% -> 17%
where the time goes in v15:
time: 24.3 us; the launch traced here: 24.2 us
  starting transfers between devices  10.9 us (45%)
  Pallas kernels  7.54 us (31%)
  waiting for transfers between devices  5.56 us (23%)
    ppermute x7, starting transfers between devices, swap(): return lax.ppermute(value, axis, [(i, i ^ bit) for i in range(size)])  10.9 us
    ppermute x7, waiting for transfers between devices, swap(): return lax.ppermute(value, axis, [(i, i ^ bit) for i in range(size)])  5.56 us
    pallas_call x2, Pallas kernels, shifted_call(): pl.pallas_call(functools.partial(shift_kernel, n_proj), out_shape=[vmem_o...  2.07 us
    pallas_call x1, Pallas kernels, per_device(): pl.pallas_call(pack_kernel, out_shape=[vmem_out((2 * n_proj, wide), BF16)...  1.58 us
    pallas_call x1, Pallas kernels, per_device(): pl.pallas_call(functools.partial(early_kernel, len(parts), (1, 2), ng, we...  1.42 us
    pallas_call x1, Pallas kernels, per_device(): pl.pallas_call(functools.partial(final_kernel, half, n_proj, length, subs...  1.13 us
    pallas_call x1, Pallas kernels, per_device(): pl.pallas_call(functools.partial(place_kernel, half, n_proj, order), out_...  0.77 us
    pallas_call x1, Pallas kernels, per_device(): pl.pallas_call(table_kernel, out_shape=[vmem_out((shifts, wide), F32), vm...  0.58 us
  transfers between devices with their start and end apart: 7, of which 4 were waited for; matrix products, arithmetic and copies ran while one was open for 0% of the time, Pallas kernels for 17%

profile of v15, /device:TPU:0, one launch (start us, length us, event | category | flops | bytes accessed | tf_op | source)
XLA Modules:
  0.0 24.2 jit_solution(9968168780507176501)
XLA Ops:
  0.0 1.6 %pack.1 = (bf16[16,4096]{1,0:T(8,128)(2,1)S(1)}, bf16[4,4224]{1,0:T(4,128)(2,1)S(1)}, f32[64,4000]{1,0:T(8,128)S(1)}, f32[1,4000]{1,0:T(1,128)S(1)}, f32[9,4000]{1,0:T(8,128)S(1)}) custom-call(s32[2]{0:T(128)} %class_hbm.1, s32[8]{0:T(128)} %subset_hbm.1, bf16[2,2,4000]{2,1,0:T(2,128)(2,1)} %particles_hbm.1, bf16[2,192]{1,0:T(2,128)(2,1)} %prior_hbm.1, ...), custom_call_target="tpu_custom_call" | custom-call | tf_op jit(solution)/shard_map/pack/pallas_call | solution.py:361
  1.6 4.1 %collective-permute-start = (bf16[4,4224]{1,0:T(4,128)(2,1)S(1)}, bf16[4,4224]{1,0:T(4,128)(2,1)S(1)}, u32[]{:S(2)}, u32[]{:S(2)}) collective-permute-start(bf16[4,4224]{1,0:T(4,128)(2,1)S(1)} %get-tuple-element.26), channel_id=1, source_target_pairs={{0,4},{1,5},{2,6},{3,7},{4,0},{5,1},{6,2},{7,3},{8,12},{9,13},{10,... | collective-permute-start | bytes 101384 | tf_op jit(solution)/shard_map/ppermute | solution.py:388
  5.7 1.6 %collective-permute-start.3 = (bf16[16,4096]{1,0:T(8,128)(2,1)S(1)}, bf16[16,4096]{1,0:T(8,128)(2,1)S(1)}, u32[]{:S(2)}, u32[]{:S(2)}) collective-permute-start(bf16[16,4096]{1,0:T(8,128)(2,1)S(1)} %get-tuple-element.33.rest_0_.rest_4_), channel_id=1, source_target_pairs={{0,2},{1,3},{2,0},{3,1},{4,6},{5,7},{6,4},{7,5},{8,10},{9,11},{10,... | collective-permute-start | bytes 393224 | tf_op jit(solution)/shard_map/ppermute | solution.py:388
  7.3 1.5 %collective-permute-start.4 = (bf16[16,4096]{1,0:T(8,128)(2,1)S(1)}, bf16[16,4096]{1,0:T(8,128)(2,1)S(1)}, u32[]{:S(2)}, u32[]{:S(2)}) collective-permute-start(bf16[16,4096]{1,0:T(8,128)(2,1)S(1)} %get-tuple-element.33.rest_0_.rest_4_), channel_id=1, source_target_pairs={{0,1},{1,0},{2,3},{3,2},{4,5},{5,4},{6,7},{7,6},{8,9},{9,8},{10,11... | collective-permute-start | bytes 393224 | tf_op jit(solution)/shard_map/ppermute | solution.py:388
  8.8 0.6 %tables.1 = (f32[9,4096]{1,0:T(8,128)S(1)}, f32[9,4096]{1,0:T(8,128)S(1)}, bf16[128,4096]{1,0:T(8,128)(2,1)S(1)}) custom-call(f32[64,4000]{1,0:T(8,128)S(1)} %get-tuple-element.27.curves_ref, f32[1,4000]{1,0:T(1,128)S(1)} %get-tuple-element.28.noise_ref, f32[9,4000]{1,0:T(8,128)S(1)} %get-tuple-element.29.angle_ref), custom_call_target="tpu_custom_call" | custom-call | flops 4000000 | bytes 2000000 | tf_op jit(solution)/shard_map/tables/pallas_call | solution.py:403
  9.4 0.9 %shift_own.1 = (bf16[72,8192]{1,0:T(8,128)(2,1)S(1)}, f32[64,8]{1,0:T(8,128)S(1)}) custom-call(f32[9,4096]{1,0:T(8,128)S(1)} %get-tuple-element.30.cos_ref, f32[9,4096]{1,0:T(8,128)S(1)} %get-tuple-element.31.sin_ref, bf16[128,4096]{1,0:T(8,128)(2,1)S(1)} %get-tuple-element.32.square_ref, bf16[16,4096]{1,0:T(8,128)(2,1)S(1)} %get-tuple-element.33.rest_0_.rest_4_), custom_call_target="tpu_custom_call" | custom-call | flops 1769472 | bytes 4000000 | tf_op jit(solution)/shard_map/shift_own/pallas_call | solution.py:419
  10.2 0.0 collective-permute-done
  10.3 1.5 %collective-permute-start.1 = (bf16[8,4224]{1,0:T(8,128)(2,1)S(1)}, bf16[8,4224]{1,0:T(8,128)(2,1)S(1)}, u32[]{:S(2)}, u32[]{:S(2)}) collective-permute-start(bf16[8,4224]{1,0:T(8,128)(2,1)S(1)} %pad_maximum_fusion.1), channel_id=1, source_target_pairs={{0,16},{8,24},{16,0},{24,8},{1,17},{9,25},{17,1},{25,9},{2,18},{10... | collective-permute-start | bytes 202760 | tf_op jit(solution)/shard_map/ppermute | solution.py:388
  11.8 0.0 collective-permute-done.3.rest_1_.rest_8_
  11.8 0.4 %collective-permute-done.4.rest_0_.rest_7_ = bf16[16,4096]{1,0:T(8,128)(2,1)S(1)} collective-permute-done((bf16[16,4096]{1,0:T(8,128)(2,1)S(1)}, bf16[16,4096]{1,0:T(8,128)(2,1)S(1)}, u32[]{:S(2)}, u32[]{:S(2)}) %collective-permute-start.4) | collective-permute-done | bytes 131104 | tf_op jit(solution)/shard_map/ppermute | solution.py:388
  12.3 1.6 %collective-permute-start.5 = (bf16[16,4480]{1,0:T(8,128)(2,1)S(1)}, bf16[16,4480]{1,0:T(8,128)(2,1)S(1)}, u32[]{:S(2)}, u32[]{:S(2)}) collective-permute-start(bf16[16,4480]{1,0:T(8,128)(2,1)S(1)} %pad.4), channel_id=1, source_target_pairs={{0,1},{1,0},{2,3},{3,2},{4,5},{5,4},{6,7},{7,6},{8,9},{9,8},{10,11... | collective-permute-start | bytes 430088 | tf_op jit(solution)/shard_map/ppermute | solution.py:388
  13.8 0.8 %collective-permute-done.1 = bf16[8,4224]{1,0:T(8,128)(2,1)S(1)} collective-permute-done((bf16[8,4224]{1,0:T(8,128)(2,1)S(1)}, bf16[8,4224]{1,0:T(8,128)(2,1)S(1)}, u32[]{:S(2)}, u32[]{:S(2)}) %collective-permute-start.1) | collective-permute-done | bytes 67616 | tf_op jit(solution)/shard_map/ppermute | solution.py:388
  14.6 0.1 pad_maximum_fusion.rest_0_
  14.7 0.1 collective-permute-start.2
  14.8 1.2 %shift_rest.1 = (bf16[144,8192]{1,0:T(8,128)(2,1)S(1)}, f32[64,16]{1,0:T(8,128)S(1)}) custom-call(f32[9,4096]{1,0:T(8,128)S(1)} %get-tuple-element.30.cos_ref, f32[9,4096]{1,0:T(8,128)S(1)} %get-tuple-element.31.sin_ref, bf16[128,4096]{1,0:T(8,128)(2,1)S(1)} %get-tuple-element.32.square_ref, bf16[16,4096]{1,0:T(8,128)(2,1)S(1)} %collective-permute-done.4.rest_0_.rest_7_, ...), custom_call_target="tpu_custom_call" | custom-call | flops 3538944 | bytes 4000000 | tf_op jit(solution)/shard_map/shift_rest/pallas_call | solution.py:419
  16.0 0.1 collective-permute-done.2.rest_1_
  16.1 1.4 %early.1 = (bf16[16,8192]{1,0:T(8,128)(2,1)S(1)}, f32[16,256]{1,0:T(8,128)S(1)}, f32[16,384]{1,0:T(8,128)S(1)}) custom-call(bf16[16,4224]{1,0:T(8,128)(2,1)S(1)} %pad_maximum_fusion.rest_0_, bf16[16,4224]{1,0:T(8,128)(2,1)S(1)} %collective-permute-done.2.rest_1_, bf16[72,8192]{1,0:T(8,128)(2,1)S(1)} %get-tuple-element.36.rest_2_, ...), custom_call_target="tpu_custom_call" | custom-call | flops 56623104 | bytes 4000000 | tf_op jit(solution)/shard_map/early/pallas_call | solution.py:444
  17.5 0.0 collective-permute-done.5.last_ref
  17.5 1.1 %final.1 = (f32[8,512]{1,0:T(8,128)S(1)}, f32[8,512]{1,0:T(8,128)S(1)}) custom-call(bf16[16,8192]{1,0:T(8,128)(2,1)S(1)} %get-tuple-element.42.weighted_ref, f32[16,256]{1,0:T(8,128)S(1)} %get-tuple-element.43.extra_ref, f32[16,384]{1,0:T(8,128)S(1)} %get-tuple-element.44.rows_ref, f32[9,4096]{1,0:T(8,128)S(1)} %get-tuple-element.30.cos_ref, ...), custom_call_target="tpu_custom_call" | custom-call | flops 18874368 | bytes 4000000 | tf_op jit(solution)/shard_map/final/pallas_call | solution.py:463
  18.7 0.5 %collective-permute-start.6 = (f32[8,512]{1,0:T(8,128)S(1)}, f32[8,512]{1,0:T(8,128)S(1)}, u32[]{:S(2)}, u32[]{:S(2)}) collective-permute-start(f32[8,512]{1,0:T(8,128)S(1)} %get-tuple-element.46), channel_id=1, source_target_pairs={{0,4},{1,5},{2,6},{3,7},{4,0},{5,1},{6,2},{7,3},{8,12},{9,13},{10,... | collective-permute-start | bytes 49160 | tf_op jit(solution)/shard_map/ppermute | solution.py:388
  19.2 4.2 %collective-permute-done.6.recv_ref = f32[8,512]{1,0:T(8,128)S(1)} collective-permute-done((f32[8,512]{1,0:T(8,128)S(1)}, f32[8,512]{1,0:T(8,128)S(1)}, u32[]{:S(2)}, u32[]{:S(2)}) %collective-permute-start.6) | collective-permute-done | bytes 16416 | tf_op jit(solution)/shard_map/ppermute | solution.py:388
  23.4 0.8 %place.1 = f32[9,8,64]{2,1,0:T(8,128)} custom-call(f32[8,512]{1,0:T(8,128)S(1)} %get-tuple-element.45.keep_ref, f32[8,512]{1,0:T(8,128)S(1)} %collective-permute-done.6.recv_ref), custom_call_target="tpu_custom_call" | custom-call | tf_op jit(solution)/shard_map/place/pallas_call | solution.py:474
  (2 shorter events, 0.1 us)
Async XLA Ops:
  1.6 8.6 %collective-permute-start = (bf16[4,4224]{1,0:T(4,128)(2,1)S(1)}, bf16[4,4224]{1,0:T(4,128)(2,1)S(1)}, u32[]{:S(2)}, u32[]{:S(2)}) collective-permute-start(bf16[4,4224]{1,0:T(4,128)(2,1)S(1)} %get-tuple-element.26), channel_id=1, source_target_pairs={{0,4},{1,5},{2,6},{3,7},{4,0},{5,1},{6,2},{7,3},{8,12},{9,13},{10,... | collective-permute-start | bytes 101384 | tf_op jit(solution)/shard_map/ppermute | solution.py:388
  5.7 6.1 %collective-permute-start.3 = (bf16[16,4096]{1,0:T(8,128)(2,1)S(1)}, bf16[16,4096]{1,0:T(8,128)(2,1)S(1)}, u32[]{:S(2)}, u32[]{:S(2)}) collective-permute-start(bf16[16,4096]{1,0:T(8,128)(2,1)S(1)} %get-tuple-element.33.rest_0_.rest_4_), channel_id=1, source_target_pairs={{0,2},{1,3},{2,0},{3,1},{4,6},{5,7},{6,4},{7,5},{8,10},{9,11},{10,... | collective-permute-start | bytes 393224 | tf_op jit(solution)/shard_map/ppermute | solution.py:388
  7.3 5.0 %collective-permute-start.4 = (bf16[16,4096]{1,0:T(8,128)(2,1)S(1)}, bf16[16,4096]{1,0:T(8,128)(2,1)S(1)}, u32[]{:S(2)}, u32[]{:S(2)}) collective-permute-start(bf16[16,4096]{1,0:T(8,128)(2,1)S(1)} %get-tuple-element.33.rest_0_.rest_4_), channel_id=1, source_target_pairs={{0,1},{1,0},{2,3},{3,2},{4,5},{5,4},{6,7},{7,6},{8,9},{9,8},{10,11... | collective-permute-start | bytes 393224 | tf_op jit(solution)/shard_map/ppermute | solution.py:388
  10.3 4.4 %collective-permute-start.1 = (bf16[8,4224]{1,0:T(8,128)(2,1)S(1)}, bf16[8,4224]{1,0:T(8,128)(2,1)S(1)}, u32[]{:S(2)}, u32[]{:S(2)}) collective-permute-start(bf16[8,4224]{1,0:T(8,128)(2,1)S(1)} %pad_maximum_fusion.1), channel_id=1, source_target_pairs={{0,16},{8,24},{16,0},{24,8},{1,17},{9,25},{17,1},{25,9},{2,18},{10... | collective-permute-start | bytes 202760 | tf_op jit(solution)/shard_map/ppermute | solution.py:388
  12.3 5.3 %collective-permute-start.5 = (bf16[16,4480]{1,0:T(8,128)(2,1)S(1)}, bf16[16,4480]{1,0:T(8,128)(2,1)S(1)}, u32[]{:S(2)}, u32[]{:S(2)}) collective-permute-start(bf16[16,4480]{1,0:T(8,128)(2,1)S(1)} %pad.4), channel_id=1, source_target_pairs={{0,1},{1,0},{2,3},{3,2},{4,5},{5,4},{6,7},{7,6},{8,9},{9,8},{10,11... | collective-permute-start | bytes 430088 | tf_op jit(solution)/shard_map/ppermute | solution.py:388
  14.7 1.4 %collective-permute-start.2 = (bf16[16,4224]{1,0:T(8,128)(2,1)S(1)}, bf16[16,4224]{1,0:T(8,128)(2,1)S(1)}, u32[]{:S(2)}, u32[]{:S(2)}) collective-permute-start(bf16[16,4224]{1,0:T(8,128)(2,1)S(1)} %pad_maximum_fusion.rest_0_), channel_id=1, source_target_pairs={{0,8},{8,0},{16,24},{24,16},{1,9},{9,1},{17,25},{25,17},{2,10},{10... | collective-permute-start | bytes 405512 | tf_op jit(solution)/shard_map/ppermute | solution.py:388
  18.7 4.7 %collective-permute-start.6 = (f32[8,512]{1,0:T(8,128)S(1)}, f32[8,512]{1,0:T(8,128)S(1)}, u32[]{:S(2)}, u32[]{:S(2)}) collective-permute-start(f32[8,512]{1,0:T(8,128)S(1)} %get-tuple-element.46), channel_id=1, source_target_pairs={{0,4},{1,5},{2,6},{3,7},{4,0},{5,1},{6,2},{7,3},{8,12},{9,13},{10,... | collective-permute-start | bytes 49160 | tf_op jit(solution)/shard_map/ppermute | solution.py:388

commit v16 on v13

--- a/solution.py
+++ b/solution.py
@@ -46,11 +46,16 @@
     proj_ref,
     sems,
 ):
+    n_proj, n_class = proj_hbm.shape[0], curves_hbm.shape[0]
     pairs = [
-        (proj_hbm, proj_ref),
+        (proj_hbm.at[: n_proj // 2], proj_ref.at[: n_proj // 2]),
+        (proj_hbm.at[n_proj // 2 :], proj_ref.at[n_proj // 2 :]),
         (subset_hbm, subset_ref),
         (class_hbm, class_ref),
-        (curves_hbm, curves_ref),
+        (curves_hbm.at[: n_class // 4], curves_ref.at[: n_class // 4]),
+        (curves_hbm.at[n_class // 4 : n_class // 2], curves_ref.at[n_class // 4 : n_class // 2]),
+        (curves_hbm.at[n_class // 2 : 3 * n_class // 4], curves_ref.at[n_class // 2 : 3 * n_class // 4]),
+        (curves_hbm.at[3 * n_class // 4 :], curves_ref.at[3 * n_class // 4 :]),
         (particles_hbm, particles_ref),
         (noise_hbm, noise_ref),
         (prior_hbm, prior_ref),
@@ -60,7 +65,7 @@
     copies = [pltpu.make_async_copy(a, b, sems.at[n]) for n, (a, b) in enumerate(pairs)]
     for copy in copies:
         copy.start()
-    n_part, n_proj = particles_ref.shape[0], proj_ref.shape[0]
+    n_part = particles_ref.shape[0]
     length = proj_ref.shape[2]
     wide = bank_ref.shape[1]
 
@@ -70,7 +75,7 @@
 
     row = lax.broadcasted_iota(jnp.int32, (n_proj, wide), 0)
     lane = lax.broadcasted_iota(jnp.int32, (n_proj, wide), 1)
-    for copy in copies[:2]:
+    for copy in copies[:3]:
         copy.wait()
     real = jnp.zeros((n_proj, wide), F32)
     imag = jnp.zeros((n_proj, wide), F32)
@@ -86,30 +91,26 @@
     real = jnp.concatenate([real[:, : wide - 128], ends], axis=1)
     bank_ref[...] = jnp.concatenate([real, imag], axis=0).astype(BF16)
 
-    for copy in copies[2:]:
+    for copy in copies[3:]:
         copy.wait()
     subsets = prior_ref.shape[1]
-    extra = part_ref.shape[1] - wide
-    row = lax.broadcasted_iota(jnp.int32, (2 * n_part, wide), 0)
-    row_extra = lax.broadcasted_iota(jnp.int32, (2 * n_part, extra), 0)
-    lane_extra = lax.broadcasted_iota(jnp.int32, (2 * n_part, extra), 1)
-    prior = padded(prior_ref[...].astype(F32), 2 * extra)
-    rows = jnp.zeros((2 * n_part, wide), F32)
-    rows_extra = jnp.zeros((2 * n_part, extra), F32)
+    extra = part_ref.shape[1] - 2 * wide
+    row = lax.broadcasted_iota(jnp.int32, (n_part, wide), 0)
+    row_extra = lax.broadcasted_iota(jnp.int32, (n_part, extra), 0)
+    lane_extra = lax.broadcasted_iota(jnp.int32, (n_part, extra), 1)
+    real = jnp.zeros((n_part, wide), F32)
+    imag = jnp.zeros((n_part, wide), F32)
+    small = padded(prior_ref[...].astype(F32), extra)
     for i in range(n_part):
         curve = curves_ref[pl.ds(class_ref[i], 1), :] * noise_ref[...]
         both = padded(particles_ref[i].astype(F32) * curve, wide)
-        rows = jnp.where(row == i, both[0:1], rows)
-        rows = jnp.where(row == n_part + i, both[1:2], rows)
-        rest = jnp.where(
-            lane_extra == subsets - extra,
-            class_ref[i].astype(F32),
-            jnp.broadcast_to(prior[i : i + 1, extra:], rows_extra.shape),
-        )
-        rows_extra = jnp.where(row_extra == i, prior[i : i + 1, :extra], rows_extra)
-        rows_extra = jnp.where(row_extra == n_part + i, rest, rows_extra)
-    part_ref[:, :wide] = rows.astype(BF16)
-    part_ref[:, wide:] = rows_extra.astype(BF16)
+        real = jnp.where(row == i, both[0:1], real)
+        imag = jnp.where(row == i, both[1:2], imag)
+        place = (row_extra == i) & (lane_extra == subsets)
+        small = jnp.where(place, class_ref[i].astype(F32), small)
+    part_ref[:, :wide] = real.astype(BF16)
+    part_ref[:, wide : 2 * wide] = imag.astype(BF16)
+    part_ref[:, 2 * wide :] = small.astype(BF16)
     for t in range(phase_ref.shape[0]):
         angle_ref[t : t + 1, :] = phase_ref[pl.ds(trans_ref[t], 1), :]
 
@@ -227,31 +228,21 @@
         out[:, at : at + piece.shape[1]] = piece[rows]
 
 
-def early_kernel(n_parts, n_banks, ng, weights, n_part, n_proj, length, subsets, square_ref, *rest):
+def rows_of(parts, span):
+    return jnp.concatenate([part[:, span] for part in parts], axis=0)
+
+
+def early_kernel(n_parts, n_banks, n_proj, length, subsets, square_ref, *rest):
     parts, rest = rest[:n_parts], rest[n_parts:]
-    groups, (weighted_ref, extra_ref, select_ref, rows_ref) = [], rest[-4:]
+    groups, (select_ref, rows_ref) = [], rest[-2:]
     for n in n_banks:
         groups.append((rest[0], rest[1], rest[2 : 2 + n]))
         rest = rest[2 + n :]
-    g = lax.axis_index("grp")
-    wide = weighted_ref.shape[1] // 2
+    wide = select_ref.shape[1]
     classes_count = square_ref.shape[0] // 2
-
-    held = jnp.concatenate([part[...] for part in parts], axis=0)
-    count = 2 * ng * n_part
-    out_row = lax.broadcasted_iota(jnp.int32, (2 * count, held.shape[0]), 0)
-    in_row = lax.broadcasted_iota(jnp.int32, (2 * count, held.shape[0]), 1)
-    kind, rest_row = out_row // count, out_row % count
-    source, rest_row = rest_row // (ng * n_part), rest_row % (ng * n_part)
-    away, i = rest_row // n_part ^ g, rest_row % n_part
-    for bit, weight in weights:
-        source += jnp.where(away & bit != 0, weight, 0)
-    pick = (in_row == source * (2 * n_part) + kind * n_part + i).astype(F32).astype(BF16)
-    ordered = jnp.dot(pick, held, preferred_element_type=F32)
-    weighted_ref[:, :wide] = ordered[:count, :wide].astype(BF16)
-    weighted_ref[:, wide:] = ordered[count:, :wide].astype(BF16)
-    extra = jnp.concatenate([ordered[:count, wide:], ordered[count:, wide:]], axis=1)
-    extra_ref[...] = extra
+    weighted = rows_of(parts, slice(2 * wide))
+    extra = rows_of(parts, slice(2 * wide, None)).astype(F32)
+    count = extra.shape[0]
     class_col = lax.broadcasted_iota(jnp.int32, (count, classes_count), 1).astype(F32)
     onehot = (class_col == extra[:, subsets : subsets + 1]).astype(F32).astype(BF16)
     for n in range(2):
@@ -261,15 +252,16 @@
 
     pieces = []
     for shifted_ref, power_ref, banks in groups:
-        cross = multiply(weighted_ref[...], shifted_ref[...])
+        cross = multiply(weighted, shifted_ref[...])
         norm = multiply(select_ref[...], power_ref[...])
         pieces += pieces_of(cross, norm, extra, banks, length, subsets, n_proj)
     store_pieces(rows_ref, pieces, 0, rows_ref.shape[1] // len(pieces), slice(None))
 
 
 def final_kernel(
-    half, n_proj, length, subsets, weighted_ref, extra_ref, select_ref, rows_ref, cos_ref, sin_ref, last_ref, *outs
+    half, n_parts, bits, n_proj, length, subsets, select_ref, rows_ref, cos_ref, sin_ref, last_ref, *rest
 ):
+    parts, outs = rest[:n_parts], rest[n_parts:]
     shifts, wide = cos_ref.shape
     cross, norm = None, None
     for span in spans_of(wide):
@@ -277,21 +269,45 @@
         for real, imag in bank_pieces(last_ref, span, n_proj):
             real_rows, imag_rows = shifted_rows(real, imag, cos_ref, sin_ref, span)
             terms.append(
-                multiply(weighted_ref[:, span], real_rows)
-                + multiply(weighted_ref[:, wide + span.start : wide + span.stop], imag_rows)
+                multiply(rows_of(parts, span), real_rows)
+                + multiply(rows_of(parts, slice(wide + span.start, wide + span.stop)), imag_rows)
             )
             powers.append(real * real + imag * imag)
         terms = jnp.concatenate(terms, axis=1)
         norms = multiply(select_ref[:, span], split_terms(jnp.concatenate(powers, axis=0)))
         cross = terms if cross is None else cross + terms
         norm = norms if norm is None else norm + norms
-    pieces = pieces_of(cross, norm, extra_ref[...], [last_ref], length, subsets, n_proj)
+    extra = rows_of(parts, slice(2 * wide, None)).astype(F32)
+    pieces = pieces_of(cross, norm, extra, [last_ref], length, subsets, n_proj)
     dest, lanes = outs[0].shape
-    held = rows_ref.shape[1]
-    for s, out in enumerate(outs):
-        rows = slice(s * dest, (s + 1) * dest)
-        out[:, :held] = rows_ref[rows, :]
-        store_pieces(out, pieces, half - len(pieces), lanes // half, rows)
+    slot = lanes // half
+    ng = 1 << len(bits)
+    n_part = dest // ng
+    g = lax.axis_index("grp")
+    row = lax.broadcasted_iota(jnp.int32, (dest, slot), 0)
+
+    def in_rows(values, d):
+        found = []
+        for away in range(ng):
+            source = d
+            for n, bit in enumerate(bits):
+                source += (2 << n) if away & bit else 0
+            found.append(values[source * n_part : (source + 1) * n_part])
+        values = jnp.concatenate(found, axis=0)
+        for bit in bits:
+            step = bit * n_part
+            other = jnp.where(
+                (row & step) != 0, pltpu.roll(values, step, 0), pltpu.roll(values, dest - step, 0)
+            )
+            values = jnp.where((g & bit) != 0, other, values)
+        return values
+
+    zeros = jnp.zeros((2 * dest, slot - pieces[0].shape[1]), F32)
+    held = [rows_ref[:, at : at + slot] for at in range(0, rows_ref.shape[1], slot)]
+    held += [jnp.concatenate([piece, zeros], axis=1) for piece in pieces]
+    for d, out in enumerate(outs):
+        for n, values in enumerate(held):
+            out[:, n * slot : (n + 1) * slot] = in_rows(values, d)
 
 
 def place_kernel(half, n_proj, order, keep_ref, recv_ref, out_ref):
@@ -337,7 +353,7 @@
     classes_count = ctf_curves.shape[0]
     subsets = orient_prior.shape[1]
     wide = 128 * (length // 128 + 1)
-    extra = 128 * -(-(subsets + 1) // 256)
+    extra = 128 * (subsets // 128 + 1)
     noise = noise_weight.reshape(1, length)
     shape = jax.ShapeDtypeStruct
 
@@ -359,7 +375,7 @@
         pack_kernel,
         out_shape=[
             vmem_out((2 * n_proj, wide), BF16),
-            vmem_out((2 * n_part, wide + extra), BF16),
+            vmem_out((n_part, 2 * wide + extra), BF16),
             vmem_out(ctf_curves.shape, F32),
             vmem_out(noise.shape, F32),
             vmem_out(shift_phase.shape, F32),
@@ -374,7 +390,7 @@
             pltpu.VMEM(orient_prior.shape, BF16),
             pltpu.VMEM(shift_phase.shape, F32),
             pltpu.VMEM(projections.shape, BF16),
-            pltpu.SemaphoreType.DMA((len(operands),)),
+            pltpu.SemaphoreType.DMA((len(operands) + 4,)),
         ],
         compiler_params=_params(16),
         name="pack",
@@ -428,28 +444,24 @@
     own_rows, own_power = shifted_call([bank], "shift_own")
 
     across, own_power = lax.optimization_barrier((across, own_power))
-    parts, weights = [part, across], []
-    for n in range(ng.bit_length() - 2, -1, -1):
+    parts = [part, across]
+    bits = [1 << n for n in range(ng.bit_length() - 2, -1, -1)]
+    for bit in bits:
         part = joined(parts)
-        parts = [part, swap(part, "grp", 1 << n)]
-        weights.append((1 << n, 2 << len(weights)))
+        parts = [part, swap(part, "grp", bit)]
 
     rest_rows, rest_power = shifted_call([near, far], "shift_rest")
     count = 2 * ng * n_part
     late = half // 2 - 1
     slot = 128 * -(-(shifts + 1) * n_proj // 128)
-    weighted, extra_rows, select, rows = pl.pallas_call(
-        functools.partial(
-            early_kernel, len(parts), (1, 2), ng, weights, n_part, n_proj, length, subsets
-        ),
+    select, rows = pl.pallas_call(
+        functools.partial(early_kernel, len(parts), (1, 2), n_proj, length, subsets),
         out_shape=[
-            vmem_out((count, 2 * wide), BF16),
-            vmem_out((count, 2 * extra), F32),
             vmem_out((2 * count, wide), BF16),
             vmem_out((count, (half - late) * slot), F32),
         ],
         in_specs=[_vmem()] * (8 + len(parts)),
-        out_specs=[_vmem()] * 4,
+        out_specs=[_vmem()] * 2,
         compiler_params=_params(16),
         cost_estimate=pl.CostEstimate(
             flops=4 * count * (half - late) * n_proj * shifts * wide,
@@ -459,16 +471,16 @@
         name="early",
     )(square, *parts, own_rows, own_power, bank, rest_rows, rest_power, near, far)
     keep, give = pl.pallas_call(
-        functools.partial(final_kernel, half, n_proj, length, subsets),
+        functools.partial(final_kernel, half, len(parts), bits, n_proj, length, subsets),
         out_shape=[vmem_out((ng * n_part, half * slot), F32)] * 2,
-        in_specs=[_vmem()] * 7,
+        in_specs=[_vmem()] * (5 + len(parts)),
         out_specs=[_vmem()] * 2,
         compiler_params=_params(16),
         cost_estimate=pl.CostEstimate(
             flops=4 * count * late * n_proj * shifts * wide, bytes_accessed=4_000_000, transcendentals=0
         ),
         name="final",
-    )(weighted, extra_rows, select, rows, cos_part, sin_part, last)
+    )(select, rows, cos_part, sin_part, last, *parts)
     scores = pl.pallas_call(
         functools.partial(place_kernel, half, n_proj, order),
         out_shape=shape((shifts, ng * n_part, nb * n_proj), F32),

time: 23.8 us -> 23.9 us (level)
  transfers between devices with their start and end apart: 7 -> 7, of which waited for: 4 -> 5; matrix products, arithmetic and copies ran while one was open for 0% -> 1% of each run, Pallas kernels for 14% -> 13%
where the time goes in v16:
time: 23.9 us; the launch traced here: 23.7 us
  starting transfers between devices  11.4 us (48%)
  Pallas kernels  6.24 us (26%)
  waiting for transfers between devices  5.82 us (24%)
    ppermute x7, starting transfers between devices, swap(): return lax.ppermute(value, axis, [(i, i ^ bit) for i in range(size)])  11.4 us
    ppermute x7, waiting for transfers between devices, swap(): return lax.ppermute(value, axis, [(i, i ^ bit) for i in range(size)])  5.82 us
    pallas_call x1, Pallas kernels, per_device(): pl.pallas_call(pack_kernel, out_shape=[vmem_out((2 * n_proj, wide), BF16)...  1.62 us
    pallas_call x1, Pallas kernels, per_device(): pl.pallas_call(functools.partial(early_kernel, len(parts), (1, 2), n_proj...  1.61 us
    pallas_call x2, Pallas kernels, shifted_call(): pl.pallas_call(functools.partial(shift_kernel, n_proj), out_shape=[vmem_o...  0.94 us
    pallas_call x1, Pallas kernels, per_device(): pl.pallas_call(functools.partial(place_kernel, half, n_proj, order), out_...  0.77 us
    pallas_call x1, Pallas kernels, per_device(): pl.pallas_call(functools.partial(final_kernel, half, len(parts), bits, n_...  0.72 us
    pallas_call x1, Pallas kernels, per_device(): pl.pallas_call(table_kernel, out_shape=[vmem_out((shifts, wide), F32), vm...  0.59 us
  transfers between devices with their start and end apart: 7, of which 5 were waited for; matrix products, arithmetic and copies ran while one was open for 1% of the time, Pallas kernels for 13%

profile of v16, /device:TPU:0, one launch (start us, length us, event | category | flops | bytes accessed | tf_op | source)
XLA Modules:
  0.0 23.7 jit_solution(17415313096196498986)
XLA Ops:
  0.0 1.6 %pack.1 = (bf16[16,4096]{1,0:T(8,128)(2,1)S(1)}, bf16[2,8448]{1,0:T(2,128)(2,1)S(1)}, f32[64,4000]{1,0:T(8,128)S(1)}, f32[1,4000]{1,0:T(1,128)S(1)}, f32[9,4000]{1,0:T(8,128)S(1)}) custom-call(s32[2]{0:T(128)} %class_hbm.1, s32[8]{0:T(128)} %subset_hbm.1, bf16[2,2,4000]{2,1,0:T(2,128)(2,1)} %particles_hbm.1, bf16[2,192]{1,0:T(2,128)(2,1)} %prior_hbm.1, ...), custom_call_target="tpu_custom_call" | custom-call | tf_op jit(solution)/shard_map/pack/pallas_call | solution.py:374
  1.6 4.1 %collective-permute-start = (bf16[2,8448]{1,0:T(2,128)(2,1)S(1)}, bf16[2,8448]{1,0:T(2,128)(2,1)S(1)}, u32[]{:S(2)}, u32[]{:S(2)}) collective-permute-start(bf16[2,8448]{1,0:T(2,128)(2,1)S(1)} %get-tuple-element.29), channel_id=1, source_target_pairs={{0,4},{1,5},{2,6},{3,7},{4,0},{5,1},{6,2},{7,3},{8,12},{9,13},{10,... | collective-permute-start | bytes 101384 | tf_op jit(solution)/shard_map/ppermute | solution.py:401
  5.7 1.6 %collective-permute-start.3 = (bf16[16,4096]{1,0:T(8,128)(2,1)S(1)}, bf16[16,4096]{1,0:T(8,128)(2,1)S(1)}, u32[]{:S(2)}, u32[]{:S(2)}) collective-permute-start(bf16[16,4096]{1,0:T(8,128)(2,1)S(1)} %get-tuple-element.32.rest_0_.rest_4_), channel_id=1, source_target_pairs={{0,2},{1,3},{2,0},{3,1},{4,6},{5,7},{6,4},{7,5},{8,10},{9,11},{10,... | collective-permute-start | bytes 393224 | tf_op jit(solution)/shard_map/ppermute | solution.py:401
  7.3 1.5 %collective-permute-start.4 = (bf16[16,4096]{1,0:T(8,128)(2,1)S(1)}, bf16[16,4096]{1,0:T(8,128)(2,1)S(1)}, u32[]{:S(2)}, u32[]{:S(2)}) collective-permute-start(bf16[16,4096]{1,0:T(8,128)(2,1)S(1)} %get-tuple-element.32.rest_0_.rest_4_), channel_id=1, source_target_pairs={{0,1},{1,0},{2,3},{3,2},{4,5},{5,4},{6,7},{7,6},{8,9},{9,8},{10,11... | collective-permute-start | bytes 393224 | tf_op jit(solution)/shard_map/ppermute | solution.py:401
  8.8 0.6 %tables.1 = (f32[9,4096]{1,0:T(8,128)S(1)}, f32[9,4096]{1,0:T(8,128)S(1)}, bf16[128,4096]{1,0:T(8,128)(2,1)S(1)}) custom-call(f32[64,4000]{1,0:T(8,128)S(1)} %get-tuple-element.25.curves_ref, f32[1,4000]{1,0:T(1,128)S(1)} %get-tuple-element.26.noise_ref, f32[9,4000]{1,0:T(8,128)S(1)} %get-tuple-element.27.angle_ref), custom_call_target="tpu_custom_call" | custom-call | flops 4000000 | bytes 2000000 | tf_op jit(solution)/shard_map/tables/pallas_call | solution.py:416
  9.4 0.3 %shift_own.1 = (bf16[72,8192]{1,0:T(8,128)(2,1)S(1)}, bf16[16,4096]{1,0:T(8,128)(2,1)S(1)}) custom-call(f32[9,4096]{1,0:T(8,128)S(1)} %get-tuple-element.30.cos_ref, f32[9,4096]{1,0:T(8,128)S(1)} %get-tuple-element.31.sin_ref, bf16[16,4096]{1,0:T(8,128)(2,1)S(1)} %get-tuple-element.32.rest_0_.rest_4_), custom_call_target="tpu_custom_call" | custom-call | flops 1769472 | bytes 4000000 | tf_op jit(solution)/shard_map/shift_own/pallas_call | solution.py:432
  9.8 0.0 collective-permute-done
  9.8 0.1 pad_maximum_fusion.1
  9.8 1.6 %collective-permute-start.1 = (bf16[4,8448]{1,0:T(4,128)(2,1)S(1)}, bf16[4,8448]{1,0:T(4,128)(2,1)S(1)}, u32[]{:S(2)}, u32[]{:S(2)}) collective-permute-start(bf16[4,8448]{1,0:T(4,128)(2,1)S(1)} %pad_maximum_fusion.1), channel_id=1, source_target_pairs={{0,16},{8,24},{16,0},{24,8},{1,17},{9,25},{17,1},{25,9},{2,18},{10... | collective-permute-start | bytes 202760 | tf_op jit(solution)/shard_map/ppermute | solution.py:401
  11.4 0.0 collective-permute-done.3.rest_1_.rest_8_
  11.4 0.9 %collective-permute-done.4.rest_0_.rest_7_ = bf16[16,4096]{1,0:T(8,128)(2,1)S(1)} collective-permute-done((bf16[16,4096]{1,0:T(8,128)(2,1)S(1)}, bf16[16,4096]{1,0:T(8,128)(2,1)S(1)}, u32[]{:S(2)}, u32[]{:S(2)}) %collective-permute-start.4) | collective-permute-done | bytes 131104 | tf_op jit(solution)/shard_map/ppermute | solution.py:401
  12.3 1.6 %collective-permute-start.5 = (bf16[16,4480]{1,0:T(8,128)(2,1)S(1)}, bf16[16,4480]{1,0:T(8,128)(2,1)S(1)}, u32[]{:S(2)}, u32[]{:S(2)}) collective-permute-start(bf16[16,4480]{1,0:T(8,128)(2,1)S(1)} %pad.4), channel_id=1, source_target_pairs={{0,1},{1,0},{2,3},{3,2},{4,5},{5,4},{6,7},{7,6},{8,9},{9,8},{10,11... | collective-permute-start | bytes 430088 | tf_op jit(solution)/shard_map/ppermute | solution.py:401
  13.9 0.3 %collective-permute-done.1 = bf16[4,8448]{1,0:T(4,128)(2,1)S(1)} collective-permute-done((bf16[4,8448]{1,0:T(4,128)(2,1)S(1)}, bf16[4,8448]{1,0:T(4,128)(2,1)S(1)}, u32[]{:S(2)}, u32[]{:S(2)}) %collective-permute-start.1) | collective-permute-done | bytes 67616 | tf_op jit(solution)/shard_map/ppermute | solution.py:401
  14.2 0.1 pad_maximum_fusion.rest_0_
  14.3 0.1 collective-permute-start.2
  14.4 0.6 %shift_rest.1 = (bf16[144,8192]{1,0:T(8,128)(2,1)S(1)}, bf16[32,4096]{1,0:T(8,128)(2,1)S(1)}) custom-call(f32[9,4096]{1,0:T(8,128)S(1)} %get-tuple-element.30.cos_ref, f32[9,4096]{1,0:T(8,128)S(1)} %get-tuple-element.31.sin_ref, bf16[16,4096]{1,0:T(8,128)(2,1)S(1)} %collective-permute-done.4.rest_0_.rest_7_, ...), custom_call_target="tpu_custom_call" | custom-call | flops 3538944 | bytes 4000000 | tf_op jit(solution)/shard_map/shift_rest/pallas_call | solution.py:432
  15.0 0.7 %collective-permute-done.2.rest_1_ = bf16[8,8448]{1,0:T(8,128)(2,1)S(1)} collective-permute-done((bf16[8,8448]{1,0:T(8,128)(2,1)S(1)}, bf16[8,8448]{1,0:T(8,128)(2,1)S(1)}, u32[]{:S(2)}, u32[]{:S(2)}) %collective-permute-start.2) | collective-permute-done | bytes 135200 | tf_op jit(solution)/shard_map/ppermute | solution.py:401
  15.7 1.6 %early.1 = (bf16[32,4096]{1,0:T(8,128)(2,1)S(1)}, f32[16,384]{1,0:T(8,128)S(1)}) custom-call(bf16[128,4096]{1,0:T(8,128)(2,1)S(1)} %get-tuple-element.28.square_ref, bf16[8,8448]{1,0:T(8,128)(2,1)S(1)} %pad_maximum_fusion.rest_0_, bf16[8,8448]{1,0:T(8,128)(2,1)S(1)} %collective-permute-done.2.rest_1_, bf16[72,8192]{1,0:T(8,128)(2,1)S(1)} %get-tuple-element.35.rest_2_, ...), custom_call_target="tpu_custom_call" | custom-call | flops 56623104 | bytes 4000000 | tf_op jit(solution)/shard_map/early/pallas_call | solution.py:457
  17.3 0.1 collective-permute-done.5.last_ref
  17.5 0.7 %final.1 = (f32[8,512]{1,0:T(8,128)S(1)}, f32[8,512]{1,0:T(8,128)S(1)}) custom-call(bf16[32,4096]{1,0:T(8,128)(2,1)S(1)} %get-tuple-element.41.select_ref, f32[16,384]{1,0:T(8,128)S(1)} %get-tuple-element.42.rows_ref, f32[9,4096]{1,0:T(8,128)S(1)} %get-tuple-element.30.cos_ref, f32[9,4096]{1,0:T(8,128)S(1)} %get-tuple-element.31.sin_ref, ...), custom_call_target="tpu_custom_call" | custom-call | flops 18874368 | bytes 4000000 | tf_op jit(solution)/shard_map/final/pallas_call | solution.py:473
  18.2 1.0 %collective-permute-start.6 = (f32[8,512]{1,0:T(8,128)S(1)}, f32[8,512]{1,0:T(8,128)S(1)}, u32[]{:S(2)}, u32[]{:S(2)}) collective-permute-start(f32[8,512]{1,0:T(8,128)S(1)} %get-tuple-element.44), channel_id=1, source_target_pairs={{0,4},{1,5},{2,6},{3,7},{4,0},{5,1},{6,2},{7,3},{8,12},{9,13},{10,... | collective-permute-start | bytes 49160 | tf_op jit(solution)/shard_map/ppermute | solution.py:401
  19.2 3.8 %collective-permute-done.6.recv_ref = f32[8,512]{1,0:T(8,128)S(1)} collective-permute-done((f32[8,512]{1,0:T(8,128)S(1)}, f32[8,512]{1,0:T(8,128)S(1)}, u32[]{:S(2)}, u32[]{:S(2)}) %collective-permute-start.6) | collective-permute-done | bytes 16416 | tf_op jit(solution)/shard_map/ppermute | solution.py:401
  23.0 0.8 %place.1 = f32[9,8,64]{2,1,0:T(8,128)} custom-call(f32[8,512]{1,0:T(8,128)S(1)} %get-tuple-element.43.keep_ref, f32[8,512]{1,0:T(8,128)S(1)} %collective-permute-done.6.recv_ref), custom_call_target="tpu_custom_call" | custom-call | tf_op jit(solution)/shard_map/place/pallas_call | solution.py:484
  (1 shorter events, 0.0 us)
Async XLA Ops:
  1.6 8.1 %collective-permute-start = (bf16[2,8448]{1,0:T(2,128)(2,1)S(1)}, bf16[2,8448]{1,0:T(2,128)(2,1)S(1)}, u32[]{:S(2)}, u32[]{:S(2)}) collective-permute-start(bf16[2,8448]{1,0:T(2,128)(2,1)S(1)} %get-tuple-element.29), channel_id=1, source_target_pairs={{0,4},{1,5},{2,6},{3,7},{4,0},{5,1},{6,2},{7,3},{8,12},{9,13},{10,... | collective-permute-start | bytes 101384 | tf_op jit(solution)/shard_map/ppermute | solution.py:401
  5.7 5.7 %collective-permute-start.3 = (bf16[16,4096]{1,0:T(8,128)(2,1)S(1)}, bf16[16,4096]{1,0:T(8,128)(2,1)S(1)}, u32[]{:S(2)}, u32[]{:S(2)}) collective-permute-start(bf16[16,4096]{1,0:T(8,128)(2,1)S(1)} %get-tuple-element.32.rest_0_.rest_4_), channel_id=1, source_target_pairs={{0,2},{1,3},{2,0},{3,1},{4,6},{5,7},{6,4},{7,5},{8,10},{9,11},{10,... | collective-permute-start | bytes 393224 | tf_op jit(solution)/shard_map/ppermute | solution.py:401
  7.3 5.0 %collective-permute-start.4 = (bf16[16,4096]{1,0:T(8,128)(2,1)S(1)}, bf16[16,4096]{1,0:T(8,128)(2,1)S(1)}, u32[]{:S(2)}, u32[]{:S(2)}) collective-permute-start(bf16[16,4096]{1,0:T(8,128)(2,1)S(1)} %get-tuple-element.32.rest_0_.rest_4_), channel_id=1, source_target_pairs={{0,1},{1,0},{2,3},{3,2},{4,5},{5,4},{6,7},{7,6},{8,9},{9,8},{10,11... | collective-permute-start | bytes 393224 | tf_op jit(solution)/shard_map/ppermute | solution.py:401
  9.8 4.4 %collective-permute-start.1 = (bf16[4,8448]{1,0:T(4,128)(2,1)S(1)}, bf16[4,8448]{1,0:T(4,128)(2,1)S(1)}, u32[]{:S(2)}, u32[]{:S(2)}) collective-permute-start(bf16[4,8448]{1,0:T(4,128)(2,1)S(1)} %pad_maximum_fusion.1), channel_id=1, source_target_pairs={{0,16},{8,24},{16,0},{24,8},{1,17},{9,25},{17,1},{25,9},{2,18},{10... | collective-permute-start | bytes 202760 | tf_op jit(solution)/shard_map/ppermute | solution.py:401
  12.3 5.2 %collective-permute-start.5 = (bf16[16,4480]{1,0:T(8,128)(2,1)S(1)}, bf16[16,4480]{1,0:T(8,128)(2,1)S(1)}, u32[]{:S(2)}, u32[]{:S(2)}) collective-permute-start(bf16[16,4480]{1,0:T(8,128)(2,1)S(1)} %pad.4), channel_id=1, source_target_pairs={{0,1},{1,0},{2,3},{3,2},{4,5},{5,4},{6,7},{7,6},{8,9},{9,8},{10,11... | collective-permute-start | bytes 430088 | tf_op jit(solution)/shard_map/ppermute | solution.py:401
  14.3 1.4 %collective-permute-start.2 = (bf16[8,8448]{1,0:T(8,128)(2,1)S(1)}, bf16[8,8448]{1,0:T(8,128)(2,1)S(1)}, u32[]{:S(2)}, u32[]{:S(2)}) collective-permute-start(bf16[8,8448]{1,0:T(8,128)(2,1)S(1)} %pad_maximum_fusion.rest_0_), channel_id=1, source_target_pairs={{0,8},{8,0},{16,24},{24,16},{1,9},{9,1},{17,25},{25,17},{2,10},{10... | collective-permute-start | bytes 405512 | tf_op jit(solution)/shard_map/ppermute | solution.py:401
  18.2 4.8 %collective-permute-start.6 = (f32[8,512]{1,0:T(8,128)S(1)}, f32[8,512]{1,0:T(8,128)S(1)}, u32[]{:S(2)}, u32[]{:S(2)}) collective-permute-start(f32[8,512]{1,0:T(8,128)S(1)} %get-tuple-element.44), channel_id=1, source_target_pairs={{0,4},{1,5},{2,6},{3,7},{4,0},{5,1},{6,2},{7,3},{8,12},{9,13},{10,... | collective-permute-start | bytes 49160 | tf_op jit(solution)/shard_map/ppermute | solution.py:401

commit v17 on v16

--- a/solution.py
+++ b/solution.py
@@ -210,15 +210,19 @@
     return lax.dot_general(left, right, NT_DIMS, preferred_element_type=F32)
 
 
+def added(total, terms):
+    return terms if total is None else total + terms
+
+
 def pieces_of(cross, norm, extra, banks, length, subsets, n_proj):
     count, total = cross.shape[0], norm.shape[1] // 2
     width = cross.shape[1] * n_proj // total
     norm = norm[:count, total:] + norm[count:, :total] + norm[:count, :total]
-    added = added_rows(extra, norm, banks, n_proj, length, subsets)
+    offset = added_rows(extra, norm, banks, n_proj, length, subsets)
     pieces = []
     for n in range(total // n_proj):
         scores = cross[:, n * width : (n + 1) * width]
-        pieces.append(jnp.concatenate([scores, added[:, n * n_proj : (n + 1) * n_proj]], axis=1))
+        pieces.append(jnp.concatenate([scores, offset[:, n * n_proj : (n + 1) * n_proj]], axis=1))
     return pieces
 
 
@@ -240,7 +244,6 @@
         rest = rest[2 + n :]
     wide = select_ref.shape[1]
     classes_count = square_ref.shape[0] // 2
-    weighted = rows_of(parts, slice(2 * wide))
     extra = rows_of(parts, slice(2 * wide, None)).astype(F32)
     count = extra.shape[0]
     class_col = lax.broadcasted_iota(jnp.int32, (count, classes_count), 1).astype(F32)
@@ -252,9 +255,14 @@
 
     pieces = []
     for shifted_ref, power_ref, banks in groups:
-        cross = multiply(weighted, shifted_ref[...])
+        cross, turned = None, None
+        for at in range(0, wide, 512):
+            span = slice(at, min(at + 512, wide))
+            other = slice(wide + span.start, wide + span.stop)
+            cross = added(cross, multiply(rows_of(parts, span), shifted_ref[:, span]))
+            turned = added(turned, multiply(shifted_ref[:, other], rows_of(parts, other)))
         norm = multiply(select_ref[...], power_ref[...])
-        pieces += pieces_of(cross, norm, extra, banks, length, subsets, n_proj)
+        pieces += pieces_of(cross + turned.T, norm, extra, banks, length, subsets, n_proj)
     store_pieces(rows_ref, pieces, 0, rows_ref.shape[1] // len(pieces), slice(None))
 
 
@@ -263,24 +271,25 @@
 ):
     parts, outs = rest[:n_parts], rest[n_parts:]
     shifts, wide = cos_ref.shape
-    cross, norm = None, None
+    cross, turned, norm = None, None, None
     for span in spans_of(wide):
-        terms, powers = [], []
+        terms, others, powers = [], [], []
         for real, imag in bank_pieces(last_ref, span, n_proj):
             real_rows, imag_rows = shifted_rows(real, imag, cos_ref, sin_ref, span)
-            terms.append(
-                multiply(rows_of(parts, span), real_rows)
-                + multiply(rows_of(parts, slice(wide + span.start, wide + span.stop)), imag_rows)
-            )
+            terms.append(multiply(rows_of(parts, span), real_rows))
+            other = slice(wide + span.start, wide + span.stop)
+            others.append(multiply(imag_rows, rows_of(parts, other)))
             powers.append(real * real + imag * imag)
-        terms = jnp.concatenate(terms, axis=1)
-        norms = multiply(select_ref[:, span], split_terms(jnp.concatenate(powers, axis=0)))
-        cross = terms if cross is None else cross + terms
-        norm = norms if norm is None else norm + norms
+        cross = added(cross, jnp.concatenate(terms, axis=1))
+        turned = added(turned, jnp.concatenate(others, axis=0))
+        power = split_terms(jnp.concatenate(powers, axis=0))
+        norm = added(norm, multiply(select_ref[:, span], power))
+    cross = cross + turned.T
     extra = rows_of(parts, slice(2 * wide, None)).astype(F32)
     pieces = pieces_of(cross, norm, extra, [last_ref], length, subsets, n_proj)
     dest, lanes = outs[0].shape
-    slot = lanes // half
+    slot = rows_ref.shape[1] // (half - len(pieces))
+    width = pieces[0].shape[1]
     ng = 1 << len(bits)
     n_part = dest // ng
     g = lax.axis_index("grp")
@@ -305,17 +314,18 @@
     zeros = jnp.zeros((2 * dest, slot - pieces[0].shape[1]), F32)
     held = [rows_ref[:, at : at + slot] for at in range(0, rows_ref.shape[1], slot)]
     held += [jnp.concatenate([piece, zeros], axis=1) for piece in pieces]
+    padding = [jnp.zeros((dest, lanes - half * width), F32)] if lanes > half * width else []
     for d, out in enumerate(outs):
-        for n, values in enumerate(held):
-            out[:, n * slot : (n + 1) * slot] = in_rows(values, d)
+        rows = [in_rows(values, d)[:, :width] for values in held]
+        out[...] = jnp.concatenate(rows + padding, axis=1)
 
 
 def place_kernel(half, n_proj, order, keep_ref, recv_ref, out_ref):
     blk = lax.axis_index("blk")
     own_first = blk < half
     keep, recv = keep_ref[...], recv_ref[...]
-    slot = keep.shape[1] // half
     shifts = out_ref.shape[0]
+    slot = (shifts + 1) * n_proj
     parts = []
     for values in (jnp.where(own_first, keep, recv), jnp.where(own_first, recv, keep)):
         found = [values[:, order.index(n) * slot : (order.index(n) + 1) * slot] for n in range(half)]
@@ -454,6 +464,7 @@
     count = 2 * ng * n_part
     late = half // 2 - 1
     slot = 128 * -(-(shifts + 1) * n_proj // 128)
+    lanes = 128 * -(-(shifts + 1) * n_proj * half // 128)
     select, rows = pl.pallas_call(
         functools.partial(early_kernel, len(parts), (1, 2), n_proj, length, subsets),
         out_shape=[
@@ -472,7 +483,7 @@
     )(square, *parts, own_rows, own_power, bank, rest_rows, rest_power, near, far)
     keep, give = pl.pallas_call(
         functools.partial(final_kernel, half, len(parts), bits, n_proj, length, subsets),
-        out_shape=[vmem_out((ng * n_part, half * slot), F32)] * 2,
+        out_shape=[vmem_out((ng * n_part, lanes), F32)] * 2,
         in_specs=[_vmem()] * (5 + len(parts)),
         out_specs=[_vmem()] * 2,
         compiler_params=_params(16),

time: 23.9 us -> 23.9 us (level)
  waiting for transfers between devices: 5.82 us -> 6.2 us
  starting transfers between devices: 11.4 us -> 11.1 us
    ppermute x7, waiting for transfers between devices: 5.82 us -> 6.2 us  [swap(): return lax.ppermute(value, axis, [(i, i ^ bit) for i in range(size)])]
    ppermute x7, starting transfers between devices: 11.4 us -> 11.1 us  [swap(): return lax.ppermute(value, axis, [(i, i ^ bit) for i in range(size)])]
  transfers between devices with their start and end apart: 7 -> 7, of which waited for: 5 -> 5; matrix products, arithmetic and copies ran while one was open for 1% -> 1% of each run, Pallas kernels for 13% -> 12%
where the time goes in v17:
time: 23.9 us; the launch traced here: 23.8 us
  starting transfers between devices  11.1 us (46%)
  Pallas kernels  6.23 us (26%)
  waiting for transfers between devices  6.2 us (26%)
    ppermute x7, starting transfers between devices, swap(): return lax.ppermute(value, axis, [(i, i ^ bit) for i in range(size)])  11.1 us
    ppermute x7, waiting for transfers between devices, swap(): return lax.ppermute(value, axis, [(i, i ^ bit) for i in range(size)])  6.2 us
    pallas_call x1, Pallas kernels, per_device(): pl.pallas_call(pack_kernel, out_shape=[vmem_out((2 * n_proj, wide), BF16)...  1.62 us
    pallas_call x1, Pallas kernels, per_device(): pl.pallas_call(functools.partial(early_kernel, len(parts), (1, 2), n_proj...  1.38 us
    pallas_call x2, Pallas kernels, shifted_call(): pl.pallas_call(functools.partial(shift_kernel, n_proj), out_shape=[vmem_o...  0.94 us
    pallas_call x1, Pallas kernels, per_device(): pl.pallas_call(functools.partial(place_kernel, half, n_proj, order), out_...  0.91 us
    pallas_call x1, Pallas kernels, per_device(): pl.pallas_call(functools.partial(final_kernel, half, len(parts), bits, n_...  0.8 us
    pallas_call x1, Pallas kernels, per_device(): pl.pallas_call(table_kernel, out_shape=[vmem_out((shifts, wide), F32), vm...  0.59 us
  transfers between devices with their start and end apart: 7, of which 5 were waited for; matrix products, arithmetic and copies ran while one was open for 1% of the time, Pallas kernels for 12%

profile of v17, /device:TPU:0, one launch (start us, length us, event | category | flops | bytes accessed | tf_op | source)
XLA Modules:
  0.0 23.8 jit_solution(8250183015466599362)
XLA Ops:
  0.0 1.6 %pack.1 = (bf16[16,4096]{1,0:T(8,128)(2,1)S(1)}, bf16[2,8448]{1,0:T(2,128)(2,1)S(1)}, f32[64,4000]{1,0:T(8,128)S(1)}, f32[1,4000]{1,0:T(1,128)S(1)}, f32[9,4000]{1,0:T(8,128)S(1)}) custom-call(s32[2]{0:T(128)} %class_hbm.1, s32[8]{0:T(128)} %subset_hbm.1, bf16[2,2,4000]{2,1,0:T(2,128)(2,1)} %particles_hbm.1, bf16[2,192]{1,0:T(2,128)(2,1)} %prior_hbm.1, ...), custom_call_target="tpu_custom_call" | custom-call | tf_op jit(solution)/shard_map/pack/pallas_call | solution.py:384
  1.6 4.1 %collective-permute-start = (bf16[2,8448]{1,0:T(2,128)(2,1)S(1)}, bf16[2,8448]{1,0:T(2,128)(2,1)S(1)}, u32[]{:S(2)}, u32[]{:S(2)}) collective-permute-start(bf16[2,8448]{1,0:T(2,128)(2,1)S(1)} %get-tuple-element.29), channel_id=1, source_target_pairs={{0,4},{1,5},{2,6},{3,7},{4,0},{5,1},{6,2},{7,3},{8,12},{9,13},{10,... | collective-permute-start | bytes 101384 | tf_op jit(solution)/shard_map/ppermute | solution.py:411
  5.7 1.6 %collective-permute-start.3 = (bf16[16,4096]{1,0:T(8,128)(2,1)S(1)}, bf16[16,4096]{1,0:T(8,128)(2,1)S(1)}, u32[]{:S(2)}, u32[]{:S(2)}) collective-permute-start(bf16[16,4096]{1,0:T(8,128)(2,1)S(1)} %get-tuple-element.32.rest_0_.rest_4_), channel_id=1, source_target_pairs={{0,2},{1,3},{2,0},{3,1},{4,6},{5,7},{6,4},{7,5},{8,10},{9,11},{10,... | collective-permute-start | bytes 393224 | tf_op jit(solution)/shard_map/ppermute | solution.py:411
  7.3 1.5 %collective-permute-start.4 = (bf16[16,4096]{1,0:T(8,128)(2,1)S(1)}, bf16[16,4096]{1,0:T(8,128)(2,1)S(1)}, u32[]{:S(2)}, u32[]{:S(2)}) collective-permute-start(bf16[16,4096]{1,0:T(8,128)(2,1)S(1)} %get-tuple-element.32.rest_0_.rest_4_), channel_id=1, source_target_pairs={{0,1},{1,0},{2,3},{3,2},{4,5},{5,4},{6,7},{7,6},{8,9},{9,8},{10,11... | collective-permute-start | bytes 393224 | tf_op jit(solution)/shard_map/ppermute | solution.py:411
  8.8 0.6 %tables.1 = (f32[9,4096]{1,0:T(8,128)S(1)}, f32[9,4096]{1,0:T(8,128)S(1)}, bf16[128,4096]{1,0:T(8,128)(2,1)S(1)}) custom-call(f32[64,4000]{1,0:T(8,128)S(1)} %get-tuple-element.25.curves_ref, f32[1,4000]{1,0:T(1,128)S(1)} %get-tuple-element.26.noise_ref, f32[9,4000]{1,0:T(8,128)S(1)} %get-tuple-element.27.angle_ref), custom_call_target="tpu_custom_call" | custom-call | flops 4000000 | bytes 2000000 | tf_op jit(solution)/shard_map/tables/pallas_call | solution.py:426
  9.4 0.3 %shift_own.1 = (bf16[72,8192]{1,0:T(8,128)(2,1)S(1)}, bf16[16,4096]{1,0:T(8,128)(2,1)S(1)}) custom-call(f32[9,4096]{1,0:T(8,128)S(1)} %get-tuple-element.30.cos_ref, f32[9,4096]{1,0:T(8,128)S(1)} %get-tuple-element.31.sin_ref, bf16[16,4096]{1,0:T(8,128)(2,1)S(1)} %get-tuple-element.32.rest_0_.rest_4_), custom_call_target="tpu_custom_call" | custom-call | flops 1769472 | bytes 4000000 | tf_op jit(solution)/shard_map/shift_own/pallas_call | solution.py:442
  9.8 0.0 collective-permute-done
  9.8 0.1 pad_maximum_fusion.1
  9.8 1.6 %collective-permute-start.1 = (bf16[4,8448]{1,0:T(4,128)(2,1)S(1)}, bf16[4,8448]{1,0:T(4,128)(2,1)S(1)}, u32[]{:S(2)}, u32[]{:S(2)}) collective-permute-start(bf16[4,8448]{1,0:T(4,128)(2,1)S(1)} %pad_maximum_fusion.1), channel_id=1, source_target_pairs={{0,16},{8,24},{16,0},{24,8},{1,17},{9,25},{17,1},{25,9},{2,18},{10... | collective-permute-start | bytes 202760 | tf_op jit(solution)/shard_map/ppermute | solution.py:411
  11.4 0.0 collective-permute-done.3.rest_1_.rest_8_
  11.4 0.9 %collective-permute-done.4.rest_0_.rest_7_ = bf16[16,4096]{1,0:T(8,128)(2,1)S(1)} collective-permute-done((bf16[16,4096]{1,0:T(8,128)(2,1)S(1)}, bf16[16,4096]{1,0:T(8,128)(2,1)S(1)}, u32[]{:S(2)}, u32[]{:S(2)}) %collective-permute-start.4) | collective-permute-done | bytes 131104 | tf_op jit(solution)/shard_map/ppermute | solution.py:411
  12.3 1.6 %collective-permute-start.5 = (bf16[16,4480]{1,0:T(8,128)(2,1)S(1)}, bf16[16,4480]{1,0:T(8,128)(2,1)S(1)}, u32[]{:S(2)}, u32[]{:S(2)}) collective-permute-start(bf16[16,4480]{1,0:T(8,128)(2,1)S(1)} %pad.4), channel_id=1, source_target_pairs={{0,1},{1,0},{2,3},{3,2},{4,5},{5,4},{6,7},{7,6},{8,9},{9,8},{10,11... | collective-permute-start | bytes 430088 | tf_op jit(solution)/shard_map/ppermute | solution.py:411
  13.9 0.3 %collective-permute-done.1 = bf16[4,8448]{1,0:T(4,128)(2,1)S(1)} collective-permute-done((bf16[4,8448]{1,0:T(4,128)(2,1)S(1)}, bf16[4,8448]{1,0:T(4,128)(2,1)S(1)}, u32[]{:S(2)}, u32[]{:S(2)}) %collective-permute-start.1) | collective-permute-done | bytes 67616 | tf_op jit(solution)/shard_map/ppermute | solution.py:411
  14.2 0.1 pad_maximum_fusion.rest_0_
  14.3 0.1 collective-permute-start.2
  14.4 0.6 %shift_rest.1 = (bf16[144,8192]{1,0:T(8,128)(2,1)S(1)}, bf16[32,4096]{1,0:T(8,128)(2,1)S(1)}) custom-call(f32[9,4096]{1,0:T(8,128)S(1)} %get-tuple-element.30.cos_ref, f32[9,4096]{1,0:T(8,128)S(1)} %get-tuple-element.31.sin_ref, bf16[16,4096]{1,0:T(8,128)(2,1)S(1)} %collective-permute-done.4.rest_0_.rest_7_, ...), custom_call_target="tpu_custom_call" | custom-call | flops 3538944 | bytes 4000000 | tf_op jit(solution)/shard_map/shift_rest/pallas_call | solution.py:442
  15.0 0.7 %collective-permute-done.2.rest_1_ = bf16[8,8448]{1,0:T(8,128)(2,1)S(1)} collective-permute-done((bf16[8,8448]{1,0:T(8,128)(2,1)S(1)}, bf16[8,8448]{1,0:T(8,128)(2,1)S(1)}, u32[]{:S(2)}, u32[]{:S(2)}) %collective-permute-start.2) | collective-permute-done | bytes 135200 | tf_op jit(solution)/shard_map/ppermute | solution.py:411
  15.7 1.4 %early.1 = (bf16[32,4096]{1,0:T(8,128)(2,1)S(1)}, f32[16,384]{1,0:T(8,128)S(1)}) custom-call(bf16[128,4096]{1,0:T(8,128)(2,1)S(1)} %get-tuple-element.28.square_ref, bf16[8,8448]{1,0:T(8,128)(2,1)S(1)} %pad_maximum_fusion.rest_0_, bf16[8,8448]{1,0:T(8,128)(2,1)S(1)} %collective-permute-done.2.rest_1_, bf16[72,8192]{1,0:T(8,128)(2,1)S(1)} %get-tuple-element.35.rest_2_, ...), custom_call_target="tpu_custom_call" | custom-call | flops 56623104 | bytes 4000000 | tf_op jit(solution)/shard_map/early/pallas_call | solution.py:468
  17.1 0.3 %collective-permute-done.5.last_ref = bf16[16,4480]{1,0:T(8,128)(2,1)S(1)} collective-permute-done((bf16[16,4480]{1,0:T(8,128)(2,1)S(1)}, bf16[16,4480]{1,0:T(8,128)(2,1)S(1)}, u32[]{:S(2)}, u32[]{:S(2)}) %collective-permute-start.5) | collective-permute-done | bytes 143392 | tf_op jit(solution)/shard_map/ppermute | solution.py:411
  17.5 0.8 %final.1 = (f32[8,384]{1,0:T(8,128)S(1)}, f32[8,384]{1,0:T(8,128)S(1)}) custom-call(bf16[32,4096]{1,0:T(8,128)(2,1)S(1)} %get-tuple-element.41.select_ref, f32[16,384]{1,0:T(8,128)S(1)} %get-tuple-element.42.rows_ref, f32[9,4096]{1,0:T(8,128)S(1)} %get-tuple-element.30.cos_ref, f32[9,4096]{1,0:T(8,128)S(1)} %get-tuple-element.31.sin_ref, ...), custom_call_target="tpu_custom_call" | custom-call | flops 18874368 | bytes 4000000 | tf_op jit(solution)/shard_map/final/pallas_call | solution.py:484
  18.3 0.7 %collective-permute-start.6 = (f32[8,384]{1,0:T(8,128)S(1)}, f32[8,384]{1,0:T(8,128)S(1)}, u32[]{:S(2)}, u32[]{:S(2)}) collective-permute-start(f32[8,384]{1,0:T(8,128)S(1)} %get-tuple-element.44), channel_id=1, source_target_pairs={{0,4},{1,5},{2,6},{3,7},{4,0},{5,1},{6,2},{7,3},{8,12},{9,13},{10,... | collective-permute-start | bytes 36872 | tf_op jit(solution)/shard_map/ppermute | solution.py:411
  18.9 4.0 %collective-permute-done.6.recv_ref = f32[8,384]{1,0:T(8,128)S(1)} collective-permute-done((f32[8,384]{1,0:T(8,128)S(1)}, f32[8,384]{1,0:T(8,128)S(1)}, u32[]{:S(2)}, u32[]{:S(2)}) %collective-permute-start.6) | collective-permute-done | bytes 12320 | tf_op jit(solution)/shard_map/ppermute | solution.py:411
  22.9 0.9 %place.1 = f32[9,8,64]{2,1,0:T(8,128)} custom-call(f32[8,384]{1,0:T(8,128)S(1)} %get-tuple-element.43.keep_ref, f32[8,384]{1,0:T(8,128)S(1)} %collective-permute-done.6.recv_ref), custom_call_target="tpu_custom_call" | custom-call | tf_op jit(solution)/shard_map/place/pallas_call | solution.py:495
  (1 shorter events, 0.0 us)
Async XLA Ops:
  1.6 8.1 %collective-permute-start = (bf16[2,8448]{1,0:T(2,128)(2,1)S(1)}, bf16[2,8448]{1,0:T(2,128)(2,1)S(1)}, u32[]{:S(2)}, u32[]{:S(2)}) collective-permute-start(bf16[2,8448]{1,0:T(2,128)(2,1)S(1)} %get-tuple-element.29), channel_id=1, source_target_pairs={{0,4},{1,5},{2,6},{3,7},{4,0},{5,1},{6,2},{7,3},{8,12},{9,13},{10,... | collective-permute-start | bytes 101384 | tf_op jit(solution)/shard_map/ppermute | solution.py:411
  5.7 5.7 %collective-permute-start.3 = (bf16[16,4096]{1,0:T(8,128)(2,1)S(1)}, bf16[16,4096]{1,0:T(8,128)(2,1)S(1)}, u32[]{:S(2)}, u32[]{:S(2)}) collective-permute-start(bf16[16,4096]{1,0:T(8,128)(2,1)S(1)} %get-tuple-element.32.rest_0_.rest_4_), channel_id=1, source_target_pairs={{0,2},{1,3},{2,0},{3,1},{4,6},{5,7},{6,4},{7,5},{8,10},{9,11},{10,... | collective-permute-start | bytes 393224 | tf_op jit(solution)/shard_map/ppermute | solution.py:411
  7.3 5.0 %collective-permute-start.4 = (bf16[16,4096]{1,0:T(8,128)(2,1)S(1)}, bf16[16,4096]{1,0:T(8,128)(2,1)S(1)}, u32[]{:S(2)}, u32[]{:S(2)}) collective-permute-start(bf16[16,4096]{1,0:T(8,128)(2,1)S(1)} %get-tuple-element.32.rest_0_.rest_4_), channel_id=1, source_target_pairs={{0,1},{1,0},{2,3},{3,2},{4,5},{5,4},{6,7},{7,6},{8,9},{9,8},{10,11... | collective-permute-start | bytes 393224 | tf_op jit(solution)/shard_map/ppermute | solution.py:411
  9.8 4.4 %collective-permute-start.1 = (bf16[4,8448]{1,0:T(4,128)(2,1)S(1)}, bf16[4,8448]{1,0:T(4,128)(2,1)S(1)}, u32[]{:S(2)}, u32[]{:S(2)}) collective-permute-start(bf16[4,8448]{1,0:T(4,128)(2,1)S(1)} %pad_maximum_fusion.1), channel_id=1, source_target_pairs={{0,16},{8,24},{16,0},{24,8},{1,17},{9,25},{17,1},{25,9},{2,18},{10... | collective-permute-start | bytes 202760 | tf_op jit(solution)/shard_map/ppermute | solution.py:411
  12.3 5.2 %collective-permute-start.5 = (bf16[16,4480]{1,0:T(8,128)(2,1)S(1)}, bf16[16,4480]{1,0:T(8,128)(2,1)S(1)}, u32[]{:S(2)}, u32[]{:S(2)}) collective-permute-start(bf16[16,4480]{1,0:T(8,128)(2,1)S(1)} %pad.4), channel_id=1, source_target_pairs={{0,1},{1,0},{2,3},{3,2},{4,5},{5,4},{6,7},{7,6},{8,9},{9,8},{10,11... | collective-permute-start | bytes 430088 | tf_op jit(solution)/shard_map/ppermute | solution.py:411
  14.3 1.4 %collective-permute-start.2 = (bf16[8,8448]{1,0:T(8,128)(2,1)S(1)}, bf16[8,8448]{1,0:T(8,128)(2,1)S(1)}, u32[]{:S(2)}, u32[]{:S(2)}) collective-permute-start(bf16[8,8448]{1,0:T(8,128)(2,1)S(1)} %pad_maximum_fusion.rest_0_), channel_id=1, source_target_pairs={{0,8},{8,0},{16,24},{24,16},{1,9},{9,1},{17,25},{25,17},{2,10},{10... | collective-permute-start | bytes 405512 | tf_op jit(solution)/shard_map/ppermute | solution.py:411
  18.3 4.6 %collective-permute-start.6 = (f32[8,384]{1,0:T(8,128)S(1)}, f32[8,384]{1,0:T(8,128)S(1)}, u32[]{:S(2)}, u32[]{:S(2)}) collective-permute-start(f32[8,384]{1,0:T(8,128)S(1)} %get-tuple-element.44), channel_id=1, source_target_pairs={{0,4},{1,5},{2,6},{3,7},{4,0},{5,1},{6,2},{7,3},{8,12},{9,13},{10,... | collective-permute-start | bytes 36872 | tf_op jit(solution)/shard_map/ppermute | solution.py:411

commit v18 on v17

--- a/solution.py
+++ b/solution.py
@@ -323,7 +323,9 @@
 def place_kernel(half, n_proj, order, keep_ref, recv_ref, out_ref):
     blk = lax.axis_index("blk")
     own_first = blk < half
-    keep, recv = keep_ref[...], recv_ref[...]
+    dest = keep_ref.shape[0]
+    keep = keep_ref[...]
+    recv = jnp.where(own_first, recv_ref[dest:], recv_ref[:dest])
     shifts = out_ref.shape[0]
     slot = (shifts + 1) * n_proj
     parts = []
@@ -492,6 +494,8 @@
         ),
         name="final",
     )(select, rows, cos_part, sin_part, last, *parts)
+    couples = [[b, b + half] for b in range(half)]
+    recv = lax.all_gather(give, "blk", axis_index_groups=couples, axis=0, tiled=True)
     scores = pl.pallas_call(
         functools.partial(place_kernel, half, n_proj, order),
         out_shape=shape((shifts, ng * n_part, nb * n_proj), F32),
@@ -499,7 +503,7 @@
         out_specs=_vmem(),
         compiler_params=_params(4),
         name="place",
-    )(keep, swap(give, "blk", half))
+    )(keep, recv)
     return scores.transpose(1, 0, 2)
 
 

time: 23.9 us -> 24.6 us (1.029)
  blocking collectives: 0 us -> 5.31 us
  waiting for transfers between devices: 6.2 us -> 2.25 us
  starting transfers between devices: 11.1 us -> 10.4 us
    all_gather x0 -> x1, blocking collectives: none -> 5.31 us  [per_device(): lax.all_gather(give, 'blk', axis_index_groups=couples, axis=0, tiled=True)]
    ppermute x7 -> x6, waiting for transfers between devices: 6.2 us -> 2.25 us  [swap(): return lax.ppermute(value, axis, [(i, i ^ bit) for i in range(size)])]
    ppermute x7 -> x6, starting transfers between devices: 11.1 us -> 10.4 us  [swap(): return lax.ppermute(value, axis, [(i, i ^ bit) for i in range(size)])]
  transfers between devices with their start and end apart: 7 -> 6, of which waited for: 5 -> 4; matrix products, arithmetic and copies ran while one was open for 1% -> 1% of each run, Pallas kernels for 12% -> 12%
where the time goes in v18:
time: 24.6 us; the launch traced here: 24.5 us
  starting transfers between devices  10.4 us (42%)
  Pallas kernels  6.23 us (25%)
  blocking collectives  5.31 us (22%)
  waiting for transfers between devices  2.25 us (9%)
    ppermute x6, starting transfers between devices, swap(): return lax.ppermute(value, axis, [(i, i ^ bit) for i in range(size)])  10.4 us
    all_gather x1, blocking collectives, per_device(): lax.all_gather(give, 'blk', axis_index_groups=couples, axis=0, tiled=True)  5.31 us
    ppermute x6, waiting for transfers between devices, swap(): return lax.ppermute(value, axis, [(i, i ^ bit) for i in range(size)])  2.25 us
    pallas_call x1, Pallas kernels, per_device(): pl.pallas_call(pack_kernel, out_shape=[vmem_out((2 * n_proj, wide), BF16)...  1.62 us
    pallas_call x1, Pallas kernels, per_device(): pl.pallas_call(functools.partial(early_kernel, len(parts), (1, 2), n_proj...  1.38 us
    pallas_call x2, Pallas kernels, shifted_call(): pl.pallas_call(functools.partial(shift_kernel, n_proj), out_shape=[vmem_o...  0.94 us
    pallas_call x1, Pallas kernels, per_device(): pl.pallas_call(functools.partial(place_kernel, half, n_proj, order), out_...  0.91 us
    pallas_call x1, Pallas kernels, per_device(): pl.pallas_call(functools.partial(final_kernel, half, len(parts), bits, n_...  0.8 us
  transfers between devices with their start and end apart: 6, of which 4 were waited for; matrix products, arithmetic and copies ran while one was open for 1% of the time, Pallas kernels for 12%

profile of v18, /device:TPU:0, one launch (start us, length us, event | category | flops | bytes accessed | tf_op | source)
XLA Modules:
  0.0 24.5 jit_solution(12271009897994321038)
XLA Ops:
  0.0 1.6 %pack.1 = (bf16[16,4096]{1,0:T(8,128)(2,1)S(1)}, bf16[2,8448]{1,0:T(2,128)(2,1)S(1)}, f32[64,4000]{1,0:T(8,128)S(1)}, f32[1,4000]{1,0:T(1,128)S(1)}, f32[9,4000]{1,0:T(8,128)S(1)}) custom-call(s32[2]{0:T(128)} %class_hbm.1, s32[8]{0:T(128)} %subset_hbm.1, bf16[2,2,4000]{2,1,0:T(2,128)(2,1)} %particles_hbm.1, bf16[2,192]{1,0:T(2,128)(2,1)} %prior_hbm.1, ...), custom_call_target="tpu_custom_call" | custom-call | tf_op jit(solution)/shard_map/pack/pallas_call | solution.py:386
  1.6 4.1 %collective-permute-start = (bf16[2,8448]{1,0:T(2,128)(2,1)S(1)}, bf16[2,8448]{1,0:T(2,128)(2,1)S(1)}, u32[]{:S(2)}, u32[]{:S(2)}) collective-permute-start(bf16[2,8448]{1,0:T(2,128)(2,1)S(1)} %get-tuple-element.29), channel_id=1, source_target_pairs={{0,4},{1,5},{2,6},{3,7},{4,0},{5,1},{6,2},{7,3},{8,12},{9,13},{10,... | collective-permute-start | bytes 101384 | tf_op jit(solution)/shard_map/ppermute | solution.py:413
  5.7 1.6 %collective-permute-start.3 = (bf16[16,4096]{1,0:T(8,128)(2,1)S(1)}, bf16[16,4096]{1,0:T(8,128)(2,1)S(1)}, u32[]{:S(2)}, u32[]{:S(2)}) collective-permute-start(bf16[16,4096]{1,0:T(8,128)(2,1)S(1)} %get-tuple-element.32.rest_0_.rest_4_), channel_id=1, source_target_pairs={{0,2},{1,3},{2,0},{3,1},{4,6},{5,7},{6,4},{7,5},{8,10},{9,11},{10,... | collective-permute-start | bytes 393224 | tf_op jit(solution)/shard_map/ppermute | solution.py:413
  7.3 1.5 %collective-permute-start.4 = (bf16[16,4096]{1,0:T(8,128)(2,1)S(1)}, bf16[16,4096]{1,0:T(8,128)(2,1)S(1)}, u32[]{:S(2)}, u32[]{:S(2)}) collective-permute-start(bf16[16,4096]{1,0:T(8,128)(2,1)S(1)} %get-tuple-element.32.rest_0_.rest_4_), channel_id=1, source_target_pairs={{0,1},{1,0},{2,3},{3,2},{4,5},{5,4},{6,7},{7,6},{8,9},{9,8},{10,11... | collective-permute-start | bytes 393224 | tf_op jit(solution)/shard_map/ppermute | solution.py:413
  8.8 0.6 %tables.1 = (f32[9,4096]{1,0:T(8,128)S(1)}, f32[9,4096]{1,0:T(8,128)S(1)}, bf16[128,4096]{1,0:T(8,128)(2,1)S(1)}) custom-call(f32[64,4000]{1,0:T(8,128)S(1)} %get-tuple-element.25.curves_ref, f32[1,4000]{1,0:T(1,128)S(1)} %get-tuple-element.26.noise_ref, f32[9,4000]{1,0:T(8,128)S(1)} %get-tuple-element.27.angle_ref), custom_call_target="tpu_custom_call" | custom-call | flops 4000000 | bytes 2000000 | tf_op jit(solution)/shard_map/tables/pallas_call | solution.py:428
  9.4 0.3 %shift_own.1 = (bf16[72,8192]{1,0:T(8,128)(2,1)S(1)}, bf16[16,4096]{1,0:T(8,128)(2,1)S(1)}) custom-call(f32[9,4096]{1,0:T(8,128)S(1)} %get-tuple-element.30.cos_ref, f32[9,4096]{1,0:T(8,128)S(1)} %get-tuple-element.31.sin_ref, bf16[16,4096]{1,0:T(8,128)(2,1)S(1)} %get-tuple-element.32.rest_0_.rest_4_), custom_call_target="tpu_custom_call" | custom-call | flops 1769472 | bytes 4000000 | tf_op jit(solution)/shard_map/shift_own/pallas_call | solution.py:444
  9.8 0.0 collective-permute-done
  9.8 0.1 pad_maximum_fusion.1
  9.8 1.6 %collective-permute-start.1 = (bf16[4,8448]{1,0:T(4,128)(2,1)S(1)}, bf16[4,8448]{1,0:T(4,128)(2,1)S(1)}, u32[]{:S(2)}, u32[]{:S(2)}) collective-permute-start(bf16[4,8448]{1,0:T(4,128)(2,1)S(1)} %pad_maximum_fusion.1), channel_id=1, source_target_pairs={{0,16},{8,24},{16,0},{24,8},{1,17},{9,25},{17,1},{25,9},{2,18},{10... | collective-permute-start | bytes 202760 | tf_op jit(solution)/shard_map/ppermute | solution.py:413
  11.4 0.0 collective-permute-done.3.rest_1_.rest_8_
  11.4 0.9 %collective-permute-done.4.rest_0_.rest_7_ = bf16[16,4096]{1,0:T(8,128)(2,1)S(1)} collective-permute-done((bf16[16,4096]{1,0:T(8,128)(2,1)S(1)}, bf16[16,4096]{1,0:T(8,128)(2,1)S(1)}, u32[]{:S(2)}, u32[]{:S(2)}) %collective-permute-start.4) | collective-permute-done | bytes 131104 | tf_op jit(solution)/shard_map/ppermute | solution.py:413
  12.3 1.6 %collective-permute-start.5 = (bf16[16,4480]{1,0:T(8,128)(2,1)S(1)}, bf16[16,4480]{1,0:T(8,128)(2,1)S(1)}, u32[]{:S(2)}, u32[]{:S(2)}) collective-permute-start(bf16[16,4480]{1,0:T(8,128)(2,1)S(1)} %pad.4), channel_id=1, source_target_pairs={{0,1},{1,0},{2,3},{3,2},{4,5},{5,4},{6,7},{7,6},{8,9},{9,8},{10,11... | collective-permute-start | bytes 430088 | tf_op jit(solution)/shard_map/ppermute | solution.py:413
  13.9 0.3 %collective-permute-done.1 = bf16[4,8448]{1,0:T(4,128)(2,1)S(1)} collective-permute-done((bf16[4,8448]{1,0:T(4,128)(2,1)S(1)}, bf16[4,8448]{1,0:T(4,128)(2,1)S(1)}, u32[]{:S(2)}, u32[]{:S(2)}) %collective-permute-start.1) | collective-permute-done | bytes 67616 | tf_op jit(solution)/shard_map/ppermute | solution.py:413
  14.2 0.1 pad_maximum_fusion.rest_0_
  14.3 0.1 collective-permute-start.2
  14.4 0.6 %shift_rest.1 = (bf16[144,8192]{1,0:T(8,128)(2,1)S(1)}, bf16[32,4096]{1,0:T(8,128)(2,1)S(1)}) custom-call(f32[9,4096]{1,0:T(8,128)S(1)} %get-tuple-element.30.cos_ref, f32[9,4096]{1,0:T(8,128)S(1)} %get-tuple-element.31.sin_ref, bf16[16,4096]{1,0:T(8,128)(2,1)S(1)} %collective-permute-done.4.rest_0_.rest_7_, ...), custom_call_target="tpu_custom_call" | custom-call | flops 3538944 | bytes 4000000 | tf_op jit(solution)/shard_map/shift_rest/pallas_call | solution.py:444
  15.0 0.7 %collective-permute-done.2.rest_1_ = bf16[8,8448]{1,0:T(8,128)(2,1)S(1)} collective-permute-done((bf16[8,8448]{1,0:T(8,128)(2,1)S(1)}, bf16[8,8448]{1,0:T(8,128)(2,1)S(1)}, u32[]{:S(2)}, u32[]{:S(2)}) %collective-permute-start.2) | collective-permute-done | bytes 135200 | tf_op jit(solution)/shard_map/ppermute | solution.py:413
  15.7 1.4 %early.1 = (bf16[32,4096]{1,0:T(8,128)(2,1)S(1)}, f32[16,384]{1,0:T(8,128)S(1)}) custom-call(bf16[128,4096]{1,0:T(8,128)(2,1)S(1)} %get-tuple-element.28.square_ref, bf16[8,8448]{1,0:T(8,128)(2,1)S(1)} %pad_maximum_fusion.rest_0_, bf16[8,8448]{1,0:T(8,128)(2,1)S(1)} %collective-permute-done.2.rest_1_, bf16[72,8192]{1,0:T(8,128)(2,1)S(1)} %get-tuple-element.35.rest_2_, ...), custom_call_target="tpu_custom_call" | custom-call | flops 56623104 | bytes 4000000 | tf_op jit(solution)/shard_map/early/pallas_call | solution.py:470
  17.1 0.3 %collective-permute-done.5.last_ref = bf16[16,4480]{1,0:T(8,128)(2,1)S(1)} collective-permute-done((bf16[16,4480]{1,0:T(8,128)(2,1)S(1)}, bf16[16,4480]{1,0:T(8,128)(2,1)S(1)}, u32[]{:S(2)}, u32[]{:S(2)}) %collective-permute-start.5) | collective-permute-done | bytes 143392 | tf_op jit(solution)/shard_map/ppermute | solution.py:413
  17.5 0.8 %final.1 = (f32[8,384]{1,0:T(8,128)S(1)}, f32[8,384]{1,0:T(8,128)S(1)}) custom-call(bf16[32,4096]{1,0:T(8,128)(2,1)S(1)} %get-tuple-element.41.select_ref, f32[16,384]{1,0:T(8,128)S(1)} %get-tuple-element.42.rows_ref, f32[9,4096]{1,0:T(8,128)S(1)} %get-tuple-element.30.cos_ref, f32[9,4096]{1,0:T(8,128)S(1)} %get-tuple-element.31.sin_ref, ...), custom_call_target="tpu_custom_call" | custom-call | flops 18874368 | bytes 4000000 | tf_op jit(solution)/shard_map/final/pallas_call | solution.py:486
  18.3 5.3 %all_gather.3.recv_ref = f32[16,384]{1,0:T(8,128)S(1)} all-gather(f32[8,384]{1,0:T(8,128)S(1)} %get-tuple-element.44), channel_id=1, replica_groups={{0,4},{1,5},{2,6},{3,7},{8,12},{9,13},{10,14},{11,15},{16,20},{17,21},{..., dimensions={0}, use_global_device_ids=true | all-gather | bytes 36864 | tf_op jit(solution)/shard_map/all_gather | solution.py:498
  23.6 0.9 %place.1 = f32[9,8,64]{2,1,0:T(8,128)} custom-call(f32[8,384]{1,0:T(8,128)S(1)} %get-tuple-element.43.keep_ref, f32[16,384]{1,0:T(8,128)S(1)} %all_gather.3.recv_ref), custom_call_target="tpu_custom_call" | custom-call | tf_op jit(solution)/shard_map/place/pallas_call | solution.py:499
  (1 shorter events, 0.0 us)
Async XLA Ops:
  1.6 8.1 %collective-permute-start = (bf16[2,8448]{1,0:T(2,128)(2,1)S(1)}, bf16[2,8448]{1,0:T(2,128)(2,1)S(1)}, u32[]{:S(2)}, u32[]{:S(2)}) collective-permute-start(bf16[2,8448]{1,0:T(2,128)(2,1)S(1)} %get-tuple-element.29), channel_id=1, source_target_pairs={{0,4},{1,5},{2,6},{3,7},{4,0},{5,1},{6,2},{7,3},{8,12},{9,13},{10,... | collective-permute-start | bytes 101384 | tf_op jit(solution)/shard_map/ppermute | solution.py:413
  5.7 5.7 %collective-permute-start.3 = (bf16[16,4096]{1,0:T(8,128)(2,1)S(1)}, bf16[16,4096]{1,0:T(8,128)(2,1)S(1)}, u32[]{:S(2)}, u32[]{:S(2)}) collective-permute-start(bf16[16,4096]{1,0:T(8,128)(2,1)S(1)} %get-tuple-element.32.rest_0_.rest_4_), channel_id=1, source_target_pairs={{0,2},{1,3},{2,0},{3,1},{4,6},{5,7},{6,4},{7,5},{8,10},{9,11},{10,... | collective-permute-start | bytes 393224 | tf_op jit(solution)/shard_map/ppermute | solution.py:413
  7.3 5.0 %collective-permute-start.4 = (bf16[16,4096]{1,0:T(8,128)(2,1)S(1)}, bf16[16,4096]{1,0:T(8,128)(2,1)S(1)}, u32[]{:S(2)}, u32[]{:S(2)}) collective-permute-start(bf16[16,4096]{1,0:T(8,128)(2,1)S(1)} %get-tuple-element.32.rest_0_.rest_4_), channel_id=1, source_target_pairs={{0,1},{1,0},{2,3},{3,2},{4,5},{5,4},{6,7},{7,6},{8,9},{9,8},{10,11... | collective-permute-start | bytes 393224 | tf_op jit(solution)/shard_map/ppermute | solution.py:413
  9.8 4.4 %collective-permute-start.1 = (bf16[4,8448]{1,0:T(4,128)(2,1)S(1)}, bf16[4,8448]{1,0:T(4,128)(2,1)S(1)}, u32[]{:S(2)}, u32[]{:S(2)}) collective-permute-start(bf16[4,8448]{1,0:T(4,128)(2,1)S(1)} %pad_maximum_fusion.1), channel_id=1, source_target_pairs={{0,16},{8,24},{16,0},{24,8},{1,17},{9,25},{17,1},{25,9},{2,18},{10... | collective-permute-start | bytes 202760 | tf_op jit(solution)/shard_map/ppermute | solution.py:413
  12.3 5.2 %collective-permute-start.5 = (bf16[16,4480]{1,0:T(8,128)(2,1)S(1)}, bf16[16,4480]{1,0:T(8,128)(2,1)S(1)}, u32[]{:S(2)}, u32[]{:S(2)}) collective-permute-start(bf16[16,4480]{1,0:T(8,128)(2,1)S(1)} %pad.4), channel_id=1, source_target_pairs={{0,1},{1,0},{2,3},{3,2},{4,5},{5,4},{6,7},{7,6},{8,9},{9,8},{10,11... | collective-permute-start | bytes 430088 | tf_op jit(solution)/shard_map/ppermute | solution.py:413
  14.3 1.4 %collective-permute-start.2 = (bf16[8,8448]{1,0:T(8,128)(2,1)S(1)}, bf16[8,8448]{1,0:T(8,128)(2,1)S(1)}, u32[]{:S(2)}, u32[]{:S(2)}) collective-permute-start(bf16[8,8448]{1,0:T(8,128)(2,1)S(1)} %pad_maximum_fusion.rest_0_), channel_id=1, source_target_pairs={{0,8},{8,0},{16,24},{24,16},{1,9},{9,1},{17,25},{25,17},{2,10},{10... | collective-permute-start | bytes 405512 | tf_op jit(solution)/shard_map/ppermute | solution.py:413

commit v19 on v17

--- a/solution.py
+++ b/solution.py
@@ -91,7 +91,11 @@
     real = jnp.concatenate([real[:, : wide - 128], ends], axis=1)
     bank_ref[...] = jnp.concatenate([real, imag], axis=0).astype(BF16)
 
-    for copy in copies[3:]:
+    for copy in copies[-2:]:
+        copy.wait()
+    for t in range(phase_ref.shape[0]):
+        angle_ref[t : t + 1, :] = phase_ref[pl.ds(trans_ref[t], 1), :]
+    for copy in copies[3:-2]:
         copy.wait()
     subsets = prior_ref.shape[1]
     extra = part_ref.shape[1] - 2 * wide
@@ -111,8 +115,6 @@
     part_ref[:, :wide] = real.astype(BF16)
     part_ref[:, wide : 2 * wide] = imag.astype(BF16)
     part_ref[:, 2 * wide :] = small.astype(BF16)
-    for t in range(phase_ref.shape[0]):
-        angle_ref[t : t + 1, :] = phase_ref[pl.ds(trans_ref[t], 1), :]
 
 
 def sine_cosine(x):
@@ -247,11 +249,13 @@
     extra = rows_of(parts, slice(2 * wide, None)).astype(F32)
     count = extra.shape[0]
     class_col = lax.broadcasted_iota(jnp.int32, (count, classes_count), 1).astype(F32)
-    onehot = (class_col == extra[:, subsets : subsets + 1]).astype(F32).astype(BF16)
-    for n in range(2):
-        squares = square_ref[n * classes_count : (n + 1) * classes_count, :]
-        chosen = jnp.dot(onehot, squares, preferred_element_type=F32)
-        select_ref[n * count : (n + 1) * count, :] = chosen.astype(BF16)
+    onehot = (class_col == extra[:, subsets : subsets + 1]).astype(F32)
+    nothing = jnp.zeros_like(onehot)
+    pick = jnp.concatenate(
+        [jnp.concatenate([onehot, nothing], axis=1), jnp.concatenate([nothing, onehot], axis=1)], axis=0
+    ).astype(BF16)
+    chosen = jnp.dot(pick, square_ref[...], preferred_element_type=F32)
+    select_ref[...] = chosen.astype(BF16)
 
     pieces = []
     for shifted_ref, power_ref, banks in groups:
@@ -269,7 +273,7 @@
 def final_kernel(
     half, n_parts, bits, n_proj, length, subsets, select_ref, rows_ref, cos_ref, sin_ref, last_ref, *rest
 ):
-    parts, outs = rest[:n_parts], rest[n_parts:]
+    parts, (late_ref, give_ref) = rest[:n_parts], rest[n_parts:]
     shifts, wide = cos_ref.shape
     cross, turned, norm = None, None, None
     for span in spans_of(wide):
@@ -287,61 +291,77 @@
     cross = cross + turned.T
     extra = rows_of(parts, slice(2 * wide, None)).astype(F32)
     pieces = pieces_of(cross, norm, extra, [last_ref], length, subsets, n_proj)
-    dest, lanes = outs[0].shape
-    slot = rows_ref.shape[1] // (half - len(pieces))
+    slot = late_ref.shape[1] // len(pieces)
+    zeros = jnp.zeros((extra.shape[0], slot - pieces[0].shape[1]), F32)
+    late = [jnp.concatenate([piece, zeros], axis=1) for piece in pieces]
+    late_ref[...] = jnp.concatenate(late, axis=1)
+    dest, lanes = give_ref.shape
     width = pieces[0].shape[1]
+    rows = [in_rows(values, 1, bits, dest)[:, :width] for values in slots_of(rows_ref, slot) + late]
+    if lanes > half * width:
+        rows.append(jnp.zeros((dest, lanes - half * width), F32))
+    give_ref[...] = jnp.concatenate(rows, axis=1)
+
+
+def slots_of(rows_ref, slot):
+    return [rows_ref[:, at : at + slot] for at in range(0, rows_ref.shape[1], slot)]
+
+
+def in_rows(values, d, bits, dest):
     ng = 1 << len(bits)
     n_part = dest // ng
     g = lax.axis_index("grp")
-    row = lax.broadcasted_iota(jnp.int32, (dest, slot), 0)
-
-    def in_rows(values, d):
-        found = []
-        for away in range(ng):
-            source = d
-            for n, bit in enumerate(bits):
-                source += (2 << n) if away & bit else 0
-            found.append(values[source * n_part : (source + 1) * n_part])
-        values = jnp.concatenate(found, axis=0)
-        for bit in bits:
-            step = bit * n_part
-            other = jnp.where(
-                (row & step) != 0, pltpu.roll(values, step, 0), pltpu.roll(values, dest - step, 0)
-            )
-            values = jnp.where((g & bit) != 0, other, values)
-        return values
-
-    zeros = jnp.zeros((2 * dest, slot - pieces[0].shape[1]), F32)
-    held = [rows_ref[:, at : at + slot] for at in range(0, rows_ref.shape[1], slot)]
-    held += [jnp.concatenate([piece, zeros], axis=1) for piece in pieces]
-    padding = [jnp.zeros((dest, lanes - half * width), F32)] if lanes > half * width else []
-    for d, out in enumerate(outs):
-        rows = [in_rows(values, d)[:, :width] for values in held]
-        out[...] = jnp.concatenate(rows + padding, axis=1)
+    row = lax.broadcasted_iota(jnp.int32, (dest, values.shape[1]), 0)
+    found = []
+    for away in range(ng):
+        source = d
+        for n, bit in enumerate(bits):
+            source += (2 << n) if away & bit else 0
+        found.append(values[source * n_part : (source + 1) * n_part])
+    values = jnp.concatenate(found, axis=0)
+    for bit in bits:
+        step = bit * n_part
+        other = jnp.where(
+            (row & step) != 0, pltpu.roll(values, step, 0), pltpu.roll(values, dest - step, 0)
+        )
+        values = jnp.where((g & bit) != 0, other, values)
+    return values
+
+
+def by_shift(pieces, order, n_proj, shifts):
+    blk = lax.axis_index("blk")
+    half = len(order)
+    found = [pieces[order.index(n)] for n in range(half)]
+    bit = 1
+    while bit < half:
+        swapped = (blk & bit) != 0
+        found = [jnp.where(swapped, found[n ^ bit], found[n]) for n in range(half)]
+        bit *= 2
+
+    def line(t):
+        return jnp.concatenate([piece[:, t * n_proj : (t + 1) * n_proj] for piece in found], axis=1)
+
+    offset = line(shifts)
+    return [line(t) + offset for t in range(shifts)]
+
+
+def keep_kernel(slot, n_proj, order, bits, rows_ref, late_ref, out_ref):
+    shifts, dest, _ = out_ref.shape
+    pieces = [in_rows(values, 0, bits, dest) for values in slots_of(rows_ref, slot) + slots_of(late_ref, slot)]
+    for t, line in enumerate(by_shift(pieces, order, n_proj, shifts)):
+        out_ref[t] = line
 
 
 def place_kernel(half, n_proj, order, keep_ref, recv_ref, out_ref):
-    blk = lax.axis_index("blk")
-    own_first = blk < half
-    keep, recv = keep_ref[...], recv_ref[...]
+    own_first = lax.axis_index("blk") < half
     shifts = out_ref.shape[0]
-    slot = (shifts + 1) * n_proj
-    parts = []
-    for values in (jnp.where(own_first, keep, recv), jnp.where(own_first, recv, keep)):
-        found = [values[:, order.index(n) * slot : (order.index(n) + 1) * slot] for n in range(half)]
-        bit = 1
-        while bit < half:
-            swapped = (blk & bit) != 0
-            found = [jnp.where(swapped, found[n ^ bit], found[n]) for n in range(half)]
-            bit *= 2
-        parts += found
-
-    def line(t):
-        return jnp.concatenate([part[:, t * n_proj : (t + 1) * n_proj] for part in parts], axis=1)
-
-    added = line(shifts)
-    for t in range(shifts):
-        out_ref[t] = line(t) + added
+    width = (shifts + 1) * n_proj
+    recv = recv_ref[...]
+    pieces = [recv[:, n * width : (n + 1) * width] for n in range(half)]
+    for t, line in enumerate(by_shift(pieces, order, n_proj, shifts)):
+        keep = keep_ref[t]
+        low, high = jnp.where(own_first, keep, line), jnp.where(own_first, line, keep)
+        out_ref[t] = jnp.concatenate([low, high], axis=1)
 
 
 def per_device(
@@ -457,7 +477,8 @@
     parts = [part, across]
     bits = [1 << n for n in range(ng.bit_length() - 2, -1, -1)]
     for bit in bits:
-        part = joined(parts)
+        rows = parts[0].shape[0]
+        part = lax.dynamic_update_slice(jnp.pad(parts[0], ((0, rows), (0, 0))), parts[1], (rows, 0))
         parts = [part, swap(part, "grp", bit)]
 
     rest_rows, rest_power = shifted_call([near, far], "shift_rest")
@@ -481,9 +502,9 @@
         ),
         name="early",
     )(square, *parts, own_rows, own_power, bank, rest_rows, rest_power, near, far)
-    keep, give = pl.pallas_call(
+    late_rows, give = pl.pallas_call(
         functools.partial(final_kernel, half, len(parts), bits, n_proj, length, subsets),
-        out_shape=[vmem_out((ng * n_part, lanes), F32)] * 2,
+        out_shape=[vmem_out((count, late * slot), F32), vmem_out((ng * n_part, lanes), F32)],
         in_specs=[_vmem()] * (5 + len(parts)),
         out_specs=[_vmem()] * 2,
         compiler_params=_params(16),
@@ -492,6 +513,15 @@
         ),
         name="final",
     )(select, rows, cos_part, sin_part, last, *parts)
+    recv = swap(give, "blk", half)
+    keep = pl.pallas_call(
+        functools.partial(keep_kernel, slot, n_proj, order, bits),
+        out_shape=vmem_out((shifts, ng * n_part, half * n_proj), F32),
+        in_specs=[_vmem()] * 2,
+        out_specs=_vmem(),
+        compiler_params=_params(4),
+        name="keep",
+    )(rows, late_rows)
     scores = pl.pallas_call(
         functools.partial(place_kernel, half, n_proj, order),
         out_shape=shape((shifts, ng * n_part, nb * n_proj), F32),
@@ -499,7 +529,7 @@
         out_specs=_vmem(),
         compiler_params=_params(4),
         name="place",
-    )(keep, swap(give, "blk", half))
+    )(keep, recv)
     return scores.transpose(1, 0, 2)
 
 

time: 23.9 us -> 24 us (level)
  waiting for transfers between devices: 6.2 us -> 5.89 us
    ppermute x7, waiting for transfers between devices: 6.2 us -> 5.89 us  [swap(): return lax.ppermute(value, axis, [(i, i ^ bit) for i in range(size)])]
  transfers between devices with their start and end apart: 7 -> 7, of which waited for: 5 -> 5; matrix products, arithmetic and copies ran while one was open for 1% -> 1% of each run, Pallas kernels for 12% -> 13%
where the time goes in v19:
time: 24 us; the launch traced here: 23.8 us
  starting transfers between devices  11.2 us (47%)
  Pallas kernels  6.46 us (27%)
  waiting for transfers between devices  5.89 us (25%)
    ppermute x7, starting transfers between devices, swap(): return lax.ppermute(value, axis, [(i, i ^ bit) for i in range(size)])  11.2 us
    ppermute x7, waiting for transfers between devices, swap(): return lax.ppermute(value, axis, [(i, i ^ bit) for i in range(size)])  5.89 us
    pallas_call x1, Pallas kernels, per_device(): pl.pallas_call(pack_kernel, out_shape=[vmem_out((2 * n_proj, wide), BF16)...  1.65 us
    pallas_call x1, Pallas kernels, per_device(): pl.pallas_call(functools.partial(early_kernel, len(parts), (1, 2), n_proj...  1.47 us
    pallas_call x2, Pallas kernels, shifted_call(): pl.pallas_call(functools.partial(shift_kernel, n_proj), out_shape=[vmem_o...  0.94 us
    pallas_call x1, Pallas kernels, per_device(): pl.pallas_call(functools.partial(place_kernel, half, n_proj, order), out_...  0.93 us
    pallas_call x1, Pallas kernels, per_device(): pl.pallas_call(functools.partial(final_kernel, half, len(parts), bits, n_...  0.76 us
    pallas_call x1, Pallas kernels, per_device(): pl.pallas_call(table_kernel, out_shape=[vmem_out((shifts, wide), F32), vm...  0.59 us
  transfers between devices with their start and end apart: 7, of which 5 were waited for; matrix products, arithmetic and copies ran while one was open for 1% of the time, Pallas kernels for 13%

profile of v19, /device:TPU:0, one launch (start us, length us, event | category | flops | bytes accessed | tf_op | source)
XLA Modules:
  0.0 23.8 jit_solution(13391940393436341207)
XLA Ops:
  0.0 1.7 %pack.1 = (bf16[16,4096]{1,0:T(8,128)(2,1)S(1)}, bf16[2,8448]{1,0:T(2,128)(2,1)S(1)}, f32[64,4000]{1,0:T(8,128)S(1)}, f32[1,4000]{1,0:T(1,128)S(1)}, f32[9,4000]{1,0:T(8,128)S(1)}) custom-call(s32[2]{0:T(128)} %class_hbm.1, s32[8]{0:T(128)} %subset_hbm.1, bf16[2,2,4000]{2,1,0:T(2,128)(2,1)} %particles_hbm.1, bf16[2,192]{1,0:T(2,128)(2,1)} %prior_hbm.1, ...), custom_call_target="tpu_custom_call" | custom-call | tf_op jit(solution)/shard_map/pack/pallas_call | solution.py:404
  1.7 4.1 %collective-permute-start = (bf16[2,8448]{1,0:T(2,128)(2,1)S(1)}, bf16[2,8448]{1,0:T(2,128)(2,1)S(1)}, u32[]{:S(2)}, u32[]{:S(2)}) collective-permute-start(bf16[2,8448]{1,0:T(2,128)(2,1)S(1)} %get-tuple-element.29), channel_id=1, source_target_pairs={{0,4},{1,5},{2,6},{3,7},{4,0},{5,1},{6,2},{7,3},{8,12},{9,13},{10,... | collective-permute-start | bytes 101384 | tf_op jit(solution)/shard_map/ppermute | solution.py:431
  5.8 1.6 %collective-permute-start.3 = (bf16[16,4096]{1,0:T(8,128)(2,1)S(1)}, bf16[16,4096]{1,0:T(8,128)(2,1)S(1)}, u32[]{:S(2)}, u32[]{:S(2)}) collective-permute-start(bf16[16,4096]{1,0:T(8,128)(2,1)S(1)} %get-tuple-element.32.rest_0_.rest_4_), channel_id=1, source_target_pairs={{0,2},{1,3},{2,0},{3,1},{4,6},{5,7},{6,4},{7,5},{8,10},{9,11},{10,... | collective-permute-start | bytes 393224 | tf_op jit(solution)/shard_map/ppermute | solution.py:431
  7.3 1.5 %collective-permute-start.4 = (bf16[16,4096]{1,0:T(8,128)(2,1)S(1)}, bf16[16,4096]{1,0:T(8,128)(2,1)S(1)}, u32[]{:S(2)}, u32[]{:S(2)}) collective-permute-start(bf16[16,4096]{1,0:T(8,128)(2,1)S(1)} %get-tuple-element.32.rest_0_.rest_4_), channel_id=1, source_target_pairs={{0,1},{1,0},{2,3},{3,2},{4,5},{5,4},{6,7},{7,6},{8,9},{9,8},{10,11... | collective-permute-start | bytes 393224 | tf_op jit(solution)/shard_map/ppermute | solution.py:431
  8.9 0.6 %tables.1 = (f32[9,4096]{1,0:T(8,128)S(1)}, f32[9,4096]{1,0:T(8,128)S(1)}, bf16[128,4096]{1,0:T(8,128)(2,1)S(1)}) custom-call(f32[64,4000]{1,0:T(8,128)S(1)} %get-tuple-element.25.curves_ref, f32[1,4000]{1,0:T(1,128)S(1)} %get-tuple-element.26.noise_ref, f32[9,4000]{1,0:T(8,128)S(1)} %get-tuple-element.27.angle_ref), custom_call_target="tpu_custom_call" | custom-call | flops 4000000 | bytes 2000000 | tf_op jit(solution)/shard_map/tables/pallas_call | solution.py:446
  9.5 0.3 %shift_own.1 = (bf16[72,8192]{1,0:T(8,128)(2,1)S(1)}, bf16[16,4096]{1,0:T(8,128)(2,1)S(1)}) custom-call(f32[9,4096]{1,0:T(8,128)S(1)} %get-tuple-element.30.cos_ref, f32[9,4096]{1,0:T(8,128)S(1)} %get-tuple-element.31.sin_ref, bf16[16,4096]{1,0:T(8,128)(2,1)S(1)} %get-tuple-element.32.rest_0_.rest_4_), custom_call_target="tpu_custom_call" | custom-call | flops 1769472 | bytes 4000000 | tf_op jit(solution)/shard_map/shift_own/pallas_call | solution.py:462
  9.8 0.0 collective-permute-done
  9.8 0.1 pad_maximum_fusion.1
  9.9 1.6 %collective-permute-start.1 = (bf16[4,8448]{1,0:T(4,128)(2,1)S(1)}, bf16[4,8448]{1,0:T(4,128)(2,1)S(1)}, u32[]{:S(2)}, u32[]{:S(2)}) collective-permute-start(bf16[4,8448]{1,0:T(4,128)(2,1)S(1)} %pad_maximum_fusion.1), channel_id=1, source_target_pairs={{0,16},{8,24},{16,0},{24,8},{1,17},{9,25},{17,1},{25,9},{2,18},{10... | collective-permute-start | bytes 202760 | tf_op jit(solution)/shard_map/ppermute | solution.py:431
  11.4 0.0 collective-permute-done.3.rest_1_.rest_8_
  11.4 0.9 %collective-permute-done.4.rest_0_.rest_7_ = bf16[16,4096]{1,0:T(8,128)(2,1)S(1)} collective-permute-done((bf16[16,4096]{1,0:T(8,128)(2,1)S(1)}, bf16[16,4096]{1,0:T(8,128)(2,1)S(1)}, u32[]{:S(2)}, u32[]{:S(2)}) %collective-permute-start.4) | collective-permute-done | bytes 131104 | tf_op jit(solution)/shard_map/ppermute | solution.py:431
  12.3 1.6 %collective-permute-start.5 = (bf16[16,4480]{1,0:T(8,128)(2,1)S(1)}, bf16[16,4480]{1,0:T(8,128)(2,1)S(1)}, u32[]{:S(2)}, u32[]{:S(2)}) collective-permute-start(bf16[16,4480]{1,0:T(8,128)(2,1)S(1)} %pad.8), channel_id=1, source_target_pairs={{0,1},{1,0},{2,3},{3,2},{4,5},{5,4},{6,7},{7,6},{8,9},{9,8},{10,11... | collective-permute-start | bytes 430088 | tf_op jit(solution)/shard_map/ppermute | solution.py:431
  13.9 0.3 %collective-permute-done.1 = bf16[4,8448]{1,0:T(4,128)(2,1)S(1)} collective-permute-done((bf16[4,8448]{1,0:T(4,128)(2,1)S(1)}, bf16[4,8448]{1,0:T(4,128)(2,1)S(1)}, u32[]{:S(2)}, u32[]{:S(2)}) %collective-permute-start.1) | collective-permute-done | bytes 67616 | tf_op jit(solution)/shard_map/ppermute | solution.py:431
  14.2 0.1 pad_maximum_fusion.rest_0_
  14.4 0.1 collective-permute-start.2
  14.4 0.6 %shift_rest.1 = (bf16[144,8192]{1,0:T(8,128)(2,1)S(1)}, bf16[32,4096]{1,0:T(8,128)(2,1)S(1)}) custom-call(f32[9,4096]{1,0:T(8,128)S(1)} %get-tuple-element.30.cos_ref, f32[9,4096]{1,0:T(8,128)S(1)} %get-tuple-element.31.sin_ref, bf16[16,4096]{1,0:T(8,128)(2,1)S(1)} %collective-permute-done.4.rest_0_.rest_7_, ...), custom_call_target="tpu_custom_call" | custom-call | flops 3538944 | bytes 4000000 | tf_op jit(solution)/shard_map/shift_rest/pallas_call | solution.py:462
  15.1 0.7 %collective-permute-done.2.rest_1_ = bf16[8,8448]{1,0:T(8,128)(2,1)S(1)} collective-permute-done((bf16[8,8448]{1,0:T(8,128)(2,1)S(1)}, bf16[8,8448]{1,0:T(8,128)(2,1)S(1)}, u32[]{:S(2)}, u32[]{:S(2)}) %collective-permute-start.2) | collective-permute-done | bytes 135200 | tf_op jit(solution)/shard_map/ppermute | solution.py:431
  15.8 1.5 %early.1 = (bf16[32,4096]{1,0:T(8,128)(2,1)S(1)}, f32[16,384]{1,0:T(8,128)S(1)}) custom-call(bf16[128,4096]{1,0:T(8,128)(2,1)S(1)} %get-tuple-element.28.square_ref, bf16[8,8448]{1,0:T(8,128)(2,1)S(1)} %pad_maximum_fusion.rest_0_, bf16[8,8448]{1,0:T(8,128)(2,1)S(1)} %collective-permute-done.2.rest_1_, bf16[72,8192]{1,0:T(8,128)(2,1)S(1)} %get-tuple-element.35.rest_2_, ...), custom_call_target="tpu_custom_call" | custom-call | flops 56623104 | bytes 4000000 | tf_op jit(solution)/shard_map/early/pallas_call | solution.py:489
  17.3 0.2 collective-permute-done.5.last_ref
  17.5 0.8 %final.1 = (f32[16,128]{1,0:T(8,128)S(1)}, f32[8,384]{1,0:T(8,128)S(1)}) custom-call(bf16[32,4096]{1,0:T(8,128)(2,1)S(1)} %get-tuple-element.42.select_ref, f32[16,384]{1,0:T(8,128)S(1)} %get-tuple-element.41.rows_ref, f32[9,4096]{1,0:T(8,128)S(1)} %get-tuple-element.30.cos_ref, f32[9,4096]{1,0:T(8,128)S(1)} %get-tuple-element.31.sin_ref, ...), custom_call_target="tpu_custom_call" | custom-call | flops 18874368 | bytes 4000000 | tf_op jit(solution)/shard_map/final/pallas_call | solution.py:505
  18.3 0.8 %collective-permute-start.6 = (f32[8,384]{1,0:T(8,128)S(1)}, f32[8,384]{1,0:T(8,128)S(1)}, u32[]{:S(2)}, u32[]{:S(2)}) collective-permute-start(f32[8,384]{1,0:T(8,128)S(1)} %get-tuple-element.44), channel_id=1, source_target_pairs={{0,4},{1,5},{2,6},{3,7},{4,0},{5,1},{6,2},{7,3},{8,12},{9,13},{10,... | collective-permute-start | bytes 36872 | tf_op jit(solution)/shard_map/ppermute | solution.py:431
  19.1 0.1 keep.1.keep_ref
  19.2 3.7 %collective-permute-done.6.recv_ref = f32[8,384]{1,0:T(8,128)S(1)} collective-permute-done((f32[8,384]{1,0:T(8,128)S(1)}, f32[8,384]{1,0:T(8,128)S(1)}, u32[]{:S(2)}, u32[]{:S(2)}) %collective-permute-start.6) | collective-permute-done | bytes 12320 | tf_op jit(solution)/shard_map/ppermute | solution.py:431
  22.9 0.9 %place.1 = f32[9,8,64]{2,1,0:T(8,128)} custom-call(f32[9,8,32]{2,1,0:T(8,128)S(1)} %keep.1.keep_ref, f32[8,384]{1,0:T(8,128)S(1)} %collective-permute-done.6.recv_ref), custom_call_target="tpu_custom_call" | custom-call | tf_op jit(solution)/shard_map/place/pallas_call | solution.py:525
  (1 shorter events, 0.0 us)
Async XLA Ops:
  1.7 8.1 %collective-permute-start = (bf16[2,8448]{1,0:T(2,128)(2,1)S(1)}, bf16[2,8448]{1,0:T(2,128)(2,1)S(1)}, u32[]{:S(2)}, u32[]{:S(2)}) collective-permute-start(bf16[2,8448]{1,0:T(2,128)(2,1)S(1)} %get-tuple-element.29), channel_id=1, source_target_pairs={{0,4},{1,5},{2,6},{3,7},{4,0},{5,1},{6,2},{7,3},{8,12},{9,13},{10,... | collective-permute-start | bytes 101384 | tf_op jit(solution)/shard_map/ppermute | solution.py:431
  5.8 5.7 %collective-permute-start.3 = (bf16[16,4096]{1,0:T(8,128)(2,1)S(1)}, bf16[16,4096]{1,0:T(8,128)(2,1)S(1)}, u32[]{:S(2)}, u32[]{:S(2)}) collective-permute-start(bf16[16,4096]{1,0:T(8,128)(2,1)S(1)} %get-tuple-element.32.rest_0_.rest_4_), channel_id=1, source_target_pairs={{0,2},{1,3},{2,0},{3,1},{4,6},{5,7},{6,4},{7,5},{8,10},{9,11},{10,... | collective-permute-start | bytes 393224 | tf_op jit(solution)/shard_map/ppermute | solution.py:431
  7.3 5.0 %collective-permute-start.4 = (bf16[16,4096]{1,0:T(8,128)(2,1)S(1)}, bf16[16,4096]{1,0:T(8,128)(2,1)S(1)}, u32[]{:S(2)}, u32[]{:S(2)}) collective-permute-start(bf16[16,4096]{1,0:T(8,128)(2,1)S(1)} %get-tuple-element.32.rest_0_.rest_4_), channel_id=1, source_target_pairs={{0,1},{1,0},{2,3},{3,2},{4,5},{5,4},{6,7},{7,6},{8,9},{9,8},{10,11... | collective-permute-start | bytes 393224 | tf_op jit(solution)/shard_map/ppermute | solution.py:431
  9.9 4.4 %collective-permute-start.1 = (bf16[4,8448]{1,0:T(4,128)(2,1)S(1)}, bf16[4,8448]{1,0:T(4,128)(2,1)S(1)}, u32[]{:S(2)}, u32[]{:S(2)}) collective-permute-start(bf16[4,8448]{1,0:T(4,128)(2,1)S(1)} %pad_maximum_fusion.1), channel_id=1, source_target_pairs={{0,16},{8,24},{16,0},{24,8},{1,17},{9,25},{17,1},{25,9},{2,18},{10... | collective-permute-start | bytes 202760 | tf_op jit(solution)/shard_map/ppermute | solution.py:431
  12.3 5.2 %collective-permute-start.5 = (bf16[16,4480]{1,0:T(8,128)(2,1)S(1)}, bf16[16,4480]{1,0:T(8,128)(2,1)S(1)}, u32[]{:S(2)}, u32[]{:S(2)}) collective-permute-start(bf16[16,4480]{1,0:T(8,128)(2,1)S(1)} %pad.8), channel_id=1, source_target_pairs={{0,1},{1,0},{2,3},{3,2},{4,5},{5,4},{6,7},{7,6},{8,9},{9,8},{10,11... | collective-permute-start | bytes 430088 | tf_op jit(solution)/shard_map/ppermute | solution.py:431
  14.4 1.4 %collective-permute-start.2 = (bf16[8,8448]{1,0:T(8,128)(2,1)S(1)}, bf16[8,8448]{1,0:T(8,128)(2,1)S(1)}, u32[]{:S(2)}, u32[]{:S(2)}) collective-permute-start(bf16[8,8448]{1,0:T(8,128)(2,1)S(1)} %pad_maximum_fusion.rest_0_), channel_id=1, source_target_pairs={{0,8},{8,0},{16,24},{24,16},{1,9},{9,1},{17,25},{25,17},{2,10},{10... | collective-permute-start | bytes 405512 | tf_op jit(solution)/shard_map/ppermute | solution.py:431
  18.3 4.7 %collective-permute-start.6 = (f32[8,384]{1,0:T(8,128)S(1)}, f32[8,384]{1,0:T(8,128)S(1)}, u32[]{:S(2)}, u32[]{:S(2)}) collective-permute-start(f32[8,384]{1,0:T(8,128)S(1)} %get-tuple-element.44), channel_id=1, source_target_pairs={{0,4},{1,5},{2,6},{3,7},{4,0},{5,1},{6,2},{7,3},{8,12},{9,13},{10,... | collective-permute-start | bytes 36872 | tf_op jit(solution)/shard_map/ppermute | solution.py:431

commit v20 on v19

--- a/solution.py
+++ b/solution.py
@@ -91,11 +91,7 @@
     real = jnp.concatenate([real[:, : wide - 128], ends], axis=1)
     bank_ref[...] = jnp.concatenate([real, imag], axis=0).astype(BF16)
 
-    for copy in copies[-2:]:
-        copy.wait()
-    for t in range(phase_ref.shape[0]):
-        angle_ref[t : t + 1, :] = phase_ref[pl.ds(trans_ref[t], 1), :]
-    for copy in copies[3:-2]:
+    for copy in copies[3:]:
         copy.wait()
     subsets = prior_ref.shape[1]
     extra = part_ref.shape[1] - 2 * wide
@@ -115,6 +111,8 @@
     part_ref[:, :wide] = real.astype(BF16)
     part_ref[:, wide : 2 * wide] = imag.astype(BF16)
     part_ref[:, 2 * wide :] = small.astype(BF16)
+    for t in range(phase_ref.shape[0]):
+        angle_ref[t : t + 1, :] = phase_ref[pl.ds(trans_ref[t], 1), :]
 
 
 def sine_cosine(x):
@@ -249,13 +247,11 @@
     extra = rows_of(parts, slice(2 * wide, None)).astype(F32)
     count = extra.shape[0]
     class_col = lax.broadcasted_iota(jnp.int32, (count, classes_count), 1).astype(F32)
-    onehot = (class_col == extra[:, subsets : subsets + 1]).astype(F32)
-    nothing = jnp.zeros_like(onehot)
-    pick = jnp.concatenate(
-        [jnp.concatenate([onehot, nothing], axis=1), jnp.concatenate([nothing, onehot], axis=1)], axis=0
-    ).astype(BF16)
-    chosen = jnp.dot(pick, square_ref[...], preferred_element_type=F32)
-    select_ref[...] = chosen.astype(BF16)
+    onehot = (class_col == extra[:, subsets : subsets + 1]).astype(F32).astype(BF16)
+    for n in range(2):
+        squares = square_ref[n * classes_count : (n + 1) * classes_count, :]
+        chosen = jnp.dot(onehot, squares, preferred_element_type=F32)
+        select_ref[n * count : (n + 1) * count, :] = chosen.astype(BF16)
 
     pieces = []
     for shifted_ref, power_ref, banks in groups:
@@ -271,24 +267,23 @@
 
 
 def final_kernel(
-    half, n_parts, bits, n_proj, length, subsets, select_ref, rows_ref, cos_ref, sin_ref, last_ref, *rest
+    order, n_parts, bits, n_proj, length, subsets, select_ref, rows_ref, cos_ref, sin_ref, last_ref, *rest
 ):
     parts, (late_ref, give_ref) = rest[:n_parts], rest[n_parts:]
     shifts, wide = cos_ref.shape
-    cross, turned, norm = None, None, None
+    cross, norm = None, None
     for span in spans_of(wide):
-        terms, others, powers = [], [], []
+        terms, powers = [], []
         for real, imag in bank_pieces(last_ref, span, n_proj):
             real_rows, imag_rows = shifted_rows(real, imag, cos_ref, sin_ref, span)
-            terms.append(multiply(rows_of(parts, span), real_rows))
             other = slice(wide + span.start, wide + span.stop)
-            others.append(multiply(imag_rows, rows_of(parts, other)))
+            terms.append(
+                multiply(rows_of(parts, span), real_rows) + multiply(rows_of(parts, other), imag_rows)
+            )
             powers.append(real * real + imag * imag)
         cross = added(cross, jnp.concatenate(terms, axis=1))
-        turned = added(turned, jnp.concatenate(others, axis=0))
         power = split_terms(jnp.concatenate(powers, axis=0))
         norm = added(norm, multiply(select_ref[:, span], power))
-    cross = cross + turned.T
     extra = rows_of(parts, slice(2 * wide, None)).astype(F32)
     pieces = pieces_of(cross, norm, extra, [last_ref], length, subsets, n_proj)
     slot = late_ref.shape[1] // len(pieces)
@@ -297,9 +292,10 @@
     late_ref[...] = jnp.concatenate(late, axis=1)
     dest, lanes = give_ref.shape
     width = pieces[0].shape[1]
-    rows = [in_rows(values, 1, bits, dest)[:, :width] for values in slots_of(rows_ref, slot) + late]
-    if lanes > half * width:
-        rows.append(jnp.zeros((dest, lanes - half * width), F32))
+    rows = [in_rows(values, 1, bits, dest) for values in slots_of(rows_ref, slot) + late]
+    rows = [values[:, :width] for values in in_order(rows, order)]
+    if lanes > len(rows) * width:
+        rows.append(jnp.zeros((dest, lanes - len(rows) * width), F32))
     give_ref[...] = jnp.concatenate(rows, axis=1)
 
 
@@ -328,18 +324,21 @@
     return values
 
 
-def by_shift(pieces, order, n_proj, shifts):
+def in_order(pieces, order):
     blk = lax.axis_index("blk")
-    half = len(order)
-    found = [pieces[order.index(n)] for n in range(half)]
+    found = [pieces[order.index(n)] for n in range(len(order))]
     bit = 1
-    while bit < half:
+    while bit < len(order):
         swapped = (blk & bit) != 0
-        found = [jnp.where(swapped, found[n ^ bit], found[n]) for n in range(half)]
+        found = [jnp.where(swapped, found[n ^ bit], found[n]) for n in range(len(order))]
         bit *= 2
-
+    return found
+
+
+def by_shift(pieces, n_proj, shifts):
     def line(t):
-        return jnp.concatenate([piece[:, t * n_proj : (t + 1) * n_proj] for piece in found], axis=1)
+        one = [piece[:, t * n_proj : (t + 1) * n_proj] for piece in pieces]
+        return jnp.concatenate(one + one, axis=1)
 
     offset = line(shifts)
     return [line(t) + offset for t in range(shifts)]
@@ -348,20 +347,18 @@
 def keep_kernel(slot, n_proj, order, bits, rows_ref, late_ref, out_ref):
     shifts, dest, _ = out_ref.shape
     pieces = [in_rows(values, 0, bits, dest) for values in slots_of(rows_ref, slot) + slots_of(late_ref, slot)]
-    for t, line in enumerate(by_shift(pieces, order, n_proj, shifts)):
+    for t, line in enumerate(by_shift(in_order(pieces, order), n_proj, shifts)):
         out_ref[t] = line
 
 
-def place_kernel(half, n_proj, order, keep_ref, recv_ref, out_ref):
-    own_first = lax.axis_index("blk") < half
-    shifts = out_ref.shape[0]
+def place_kernel(half, n_proj, keep_ref, recv_ref, out_ref):
+    shifts, dest, total = out_ref.shape
     width = (shifts + 1) * n_proj
-    recv = recv_ref[...]
-    pieces = [recv[:, n * width : (n + 1) * width] for n in range(half)]
-    for t, line in enumerate(by_shift(pieces, order, n_proj, shifts)):
-        keep = keep_ref[t]
-        low, high = jnp.where(own_first, keep, line), jnp.where(own_first, line, keep)
-        out_ref[t] = jnp.concatenate([low, high], axis=1)
+    lower = lax.broadcasted_iota(jnp.int32, (dest, total), 1) < total // 2
+    own = lower == (lax.axis_index("blk") < half)
+    pieces = [recv_ref[:, n * width : (n + 1) * width] for n in range(half)]
+    for t, line in enumerate(by_shift(pieces, n_proj, shifts)):
+        out_ref[t] = jnp.where(own, keep_ref[t], line)
 
 
 def per_device(
@@ -477,8 +474,7 @@
     parts = [part, across]
     bits = [1 << n for n in range(ng.bit_length() - 2, -1, -1)]
     for bit in bits:
-        rows = parts[0].shape[0]
-        part = lax.dynamic_update_slice(jnp.pad(parts[0], ((0, rows), (0, 0))), parts[1], (rows, 0))
+        part = joined(parts)
         parts = [part, swap(part, "grp", bit)]
 
     rest_rows, rest_power = shifted_call([near, far], "shift_rest")
@@ -503,7 +499,7 @@
         name="early",
     )(square, *parts, own_rows, own_power, bank, rest_rows, rest_power, near, far)
     late_rows, give = pl.pallas_call(
-        functools.partial(final_kernel, half, len(parts), bits, n_proj, length, subsets),
+        functools.partial(final_kernel, order, len(parts), bits, n_proj, length, subsets),
         out_shape=[vmem_out((count, late * slot), F32), vmem_out((ng * n_part, lanes), F32)],
         in_specs=[_vmem()] * (5 + len(parts)),
         out_specs=[_vmem()] * 2,
@@ -516,14 +512,14 @@
     recv = swap(give, "blk", half)
     keep = pl.pallas_call(
         functools.partial(keep_kernel, slot, n_proj, order, bits),
-        out_shape=vmem_out((shifts, ng * n_part, half * n_proj), F32),
+        out_shape=vmem_out((shifts, ng * n_part, nb * n_proj), F32),
         in_specs=[_vmem()] * 2,
         out_specs=_vmem(),
         compiler_params=_params(4),
         name="keep",
     )(rows, late_rows)
     scores = pl.pallas_call(
-        functools.partial(place_kernel, half, n_proj, order),
+        functools.partial(place_kernel, half, n_proj),
         out_shape=shape((shifts, ng * n_part, nb * n_proj), F32),
         in_specs=[_vmem()] * 2,
         out_specs=_vmem(),

time: 24 us -> 23.8 us (level)
  Pallas kernels: 6.46 us -> 6.2 us
where the time goes in v20:
time: 23.8 us; the launch traced here: 23.6 us
  starting transfers between devices  11.1 us (47%)
  Pallas kernels  6.2 us (26%)
  waiting for transfers between devices  6.06 us (25%)
    ppermute x7, starting transfers between devices, swap(): return lax.ppermute(value, axis, [(i, i ^ bit) for i in range(size)])  11.1 us
    ppermute x7, waiting for transfers between devices, swap(): return lax.ppermute(value, axis, [(i, i ^ bit) for i in range(size)])  6.06 us
    pallas_call x1, Pallas kernels, per_device(): pl.pallas_call(pack_kernel, out_shape=[vmem_out((2 * n_proj, wide), BF16)...  1.62 us
    pallas_call x1, Pallas kernels, per_device(): pl.pallas_call(functools.partial(early_kernel, len(parts), (1, 2), n_proj...  1.38 us
    pallas_call x2, Pallas kernels, shifted_call(): pl.pallas_call(functools.partial(shift_kernel, n_proj), out_shape=[vmem_o...  0.94 us
    pallas_call x1, Pallas kernels, per_device(): pl.pallas_call(functools.partial(final_kernel, order, len(parts), bits, n...  0.81 us
    pallas_call x1, Pallas kernels, per_device(): pl.pallas_call(functools.partial(place_kernel, half, n_proj), out_shape=s...  0.73 us
    pallas_call x1, Pallas kernels, per_device(): pl.pallas_call(table_kernel, out_shape=[vmem_out((shifts, wide), F32), vm...  0.59 us
  transfers between devices with their start and end apart: 7, of which 5 were waited for; matrix products, arithmetic and copies ran while one was open for 1% of the time, Pallas kernels for 13%

profile of v20, /device:TPU:0, one launch (start us, length us, event | category | flops | bytes accessed | tf_op | source)
XLA Modules:
  0.0 23.6 jit_solution(15009872128321240387)
XLA Ops:
  0.0 1.6 %pack.1 = (bf16[16,4096]{1,0:T(8,128)(2,1)S(1)}, bf16[2,8448]{1,0:T(2,128)(2,1)S(1)}, f32[64,4000]{1,0:T(8,128)S(1)}, f32[1,4000]{1,0:T(1,128)S(1)}, f32[9,4000]{1,0:T(8,128)S(1)}) custom-call(s32[2]{0:T(128)} %class_hbm.1, s32[8]{0:T(128)} %subset_hbm.1, bf16[2,2,4000]{2,1,0:T(2,128)(2,1)} %particles_hbm.1, bf16[2,192]{1,0:T(2,128)(2,1)} %prior_hbm.1, ...), custom_call_target="tpu_custom_call" | custom-call | tf_op jit(solution)/shard_map/pack/pallas_call | solution.py:401
  1.6 4.1 %collective-permute-start = (bf16[2,8448]{1,0:T(2,128)(2,1)S(1)}, bf16[2,8448]{1,0:T(2,128)(2,1)S(1)}, u32[]{:S(2)}, u32[]{:S(2)}) collective-permute-start(bf16[2,8448]{1,0:T(2,128)(2,1)S(1)} %get-tuple-element.29), channel_id=1, source_target_pairs={{0,4},{1,5},{2,6},{3,7},{4,0},{5,1},{6,2},{7,3},{8,12},{9,13},{10,... | collective-permute-start | bytes 101384 | tf_op jit(solution)/shard_map/ppermute | solution.py:428
  5.7 1.6 %collective-permute-start.3 = (bf16[16,4096]{1,0:T(8,128)(2,1)S(1)}, bf16[16,4096]{1,0:T(8,128)(2,1)S(1)}, u32[]{:S(2)}, u32[]{:S(2)}) collective-permute-start(bf16[16,4096]{1,0:T(8,128)(2,1)S(1)} %get-tuple-element.32.rest_0_.rest_4_), channel_id=1, source_target_pairs={{0,2},{1,3},{2,0},{3,1},{4,6},{5,7},{6,4},{7,5},{8,10},{9,11},{10,... | collective-permute-start | bytes 393224 | tf_op jit(solution)/shard_map/ppermute | solution.py:428
  7.3 1.5 %collective-permute-start.4 = (bf16[16,4096]{1,0:T(8,128)(2,1)S(1)}, bf16[16,4096]{1,0:T(8,128)(2,1)S(1)}, u32[]{:S(2)}, u32[]{:S(2)}) collective-permute-start(bf16[16,4096]{1,0:T(8,128)(2,1)S(1)} %get-tuple-element.32.rest_0_.rest_4_), channel_id=1, source_target_pairs={{0,1},{1,0},{2,3},{3,2},{4,5},{5,4},{6,7},{7,6},{8,9},{9,8},{10,11... | collective-permute-start | bytes 393224 | tf_op jit(solution)/shard_map/ppermute | solution.py:428
  8.8 0.6 %tables.1 = (f32[9,4096]{1,0:T(8,128)S(1)}, f32[9,4096]{1,0:T(8,128)S(1)}, bf16[128,4096]{1,0:T(8,128)(2,1)S(1)}) custom-call(f32[64,4000]{1,0:T(8,128)S(1)} %get-tuple-element.25.curves_ref, f32[1,4000]{1,0:T(1,128)S(1)} %get-tuple-element.26.noise_ref, f32[9,4000]{1,0:T(8,128)S(1)} %get-tuple-element.27.angle_ref), custom_call_target="tpu_custom_call" | custom-call | flops 4000000 | bytes 2000000 | tf_op jit(solution)/shard_map/tables/pallas_call | solution.py:443
  9.4 0.3 %shift_own.1 = (bf16[72,8192]{1,0:T(8,128)(2,1)S(1)}, bf16[16,4096]{1,0:T(8,128)(2,1)S(1)}) custom-call(f32[9,4096]{1,0:T(8,128)S(1)} %get-tuple-element.30.cos_ref, f32[9,4096]{1,0:T(8,128)S(1)} %get-tuple-element.31.sin_ref, bf16[16,4096]{1,0:T(8,128)(2,1)S(1)} %get-tuple-element.32.rest_0_.rest_4_), custom_call_target="tpu_custom_call" | custom-call | flops 1769472 | bytes 4000000 | tf_op jit(solution)/shard_map/shift_own/pallas_call | solution.py:459
  9.8 0.0 collective-permute-done
  9.8 0.1 pad_maximum_fusion.1
  9.8 1.6 %collective-permute-start.1 = (bf16[4,8448]{1,0:T(4,128)(2,1)S(1)}, bf16[4,8448]{1,0:T(4,128)(2,1)S(1)}, u32[]{:S(2)}, u32[]{:S(2)}) collective-permute-start(bf16[4,8448]{1,0:T(4,128)(2,1)S(1)} %pad_maximum_fusion.1), channel_id=1, source_target_pairs={{0,16},{8,24},{16,0},{24,8},{1,17},{9,25},{17,1},{25,9},{2,18},{10... | collective-permute-start | bytes 202760 | tf_op jit(solution)/shard_map/ppermute | solution.py:428
  11.4 0.0 collective-permute-done.3.rest_1_.rest_8_
  11.4 0.9 %collective-permute-done.4.rest_0_.rest_7_ = bf16[16,4096]{1,0:T(8,128)(2,1)S(1)} collective-permute-done((bf16[16,4096]{1,0:T(8,128)(2,1)S(1)}, bf16[16,4096]{1,0:T(8,128)(2,1)S(1)}, u32[]{:S(2)}, u32[]{:S(2)}) %collective-permute-start.4) | collective-permute-done | bytes 131104 | tf_op jit(solution)/shard_map/ppermute | solution.py:428
  12.3 1.6 %collective-permute-start.5 = (bf16[16,4480]{1,0:T(8,128)(2,1)S(1)}, bf16[16,4480]{1,0:T(8,128)(2,1)S(1)}, u32[]{:S(2)}, u32[]{:S(2)}) collective-permute-start(bf16[16,4480]{1,0:T(8,128)(2,1)S(1)} %pad.4), channel_id=1, source_target_pairs={{0,1},{1,0},{2,3},{3,2},{4,5},{5,4},{6,7},{7,6},{8,9},{9,8},{10,11... | collective-permute-start | bytes 430088 | tf_op jit(solution)/shard_map/ppermute | solution.py:428
  13.9 0.3 %collective-permute-done.1 = bf16[4,8448]{1,0:T(4,128)(2,1)S(1)} collective-permute-done((bf16[4,8448]{1,0:T(4,128)(2,1)S(1)}, bf16[4,8448]{1,0:T(4,128)(2,1)S(1)}, u32[]{:S(2)}, u32[]{:S(2)}) %collective-permute-start.1) | collective-permute-done | bytes 67616 | tf_op jit(solution)/shard_map/ppermute | solution.py:428
  14.2 0.1 pad_maximum_fusion.rest_0_
  14.3 0.1 collective-permute-start.2
  14.4 0.6 %shift_rest.1 = (bf16[144,8192]{1,0:T(8,128)(2,1)S(1)}, bf16[32,4096]{1,0:T(8,128)(2,1)S(1)}) custom-call(f32[9,4096]{1,0:T(8,128)S(1)} %get-tuple-element.30.cos_ref, f32[9,4096]{1,0:T(8,128)S(1)} %get-tuple-element.31.sin_ref, bf16[16,4096]{1,0:T(8,128)(2,1)S(1)} %collective-permute-done.4.rest_0_.rest_7_, ...), custom_call_target="tpu_custom_call" | custom-call | flops 3538944 | bytes 4000000 | tf_op jit(solution)/shard_map/shift_rest/pallas_call | solution.py:459
  15.0 0.7 %collective-permute-done.2.rest_1_ = bf16[8,8448]{1,0:T(8,128)(2,1)S(1)} collective-permute-done((bf16[8,8448]{1,0:T(8,128)(2,1)S(1)}, bf16[8,8448]{1,0:T(8,128)(2,1)S(1)}, u32[]{:S(2)}, u32[]{:S(2)}) %collective-permute-start.2) | collective-permute-done | bytes 135200 | tf_op jit(solution)/shard_map/ppermute | solution.py:428
  15.7 1.4 %early.1 = (bf16[32,4096]{1,0:T(8,128)(2,1)S(1)}, f32[16,384]{1,0:T(8,128)S(1)}) custom-call(bf16[128,4096]{1,0:T(8,128)(2,1)S(1)} %get-tuple-element.28.square_ref, bf16[8,8448]{1,0:T(8,128)(2,1)S(1)} %pad_maximum_fusion.rest_0_, bf16[8,8448]{1,0:T(8,128)(2,1)S(1)} %collective-permute-done.2.rest_1_, bf16[72,8192]{1,0:T(8,128)(2,1)S(1)} %get-tuple-element.35.rest_2_, ...), custom_call_target="tpu_custom_call" | custom-call | flops 56623104 | bytes 4000000 | tf_op jit(solution)/shard_map/early/pallas_call | solution.py:485
  17.1 0.3 %collective-permute-done.5.last_ref = bf16[16,4480]{1,0:T(8,128)(2,1)S(1)} collective-permute-done((bf16[16,4480]{1,0:T(8,128)(2,1)S(1)}, bf16[16,4480]{1,0:T(8,128)(2,1)S(1)}, u32[]{:S(2)}, u32[]{:S(2)}) %collective-permute-start.5) | collective-permute-done | bytes 143392 | tf_op jit(solution)/shard_map/ppermute | solution.py:428
  17.5 0.8 %final.1 = (f32[16,128]{1,0:T(8,128)S(1)}, f32[8,384]{1,0:T(8,128)S(1)}) custom-call(bf16[32,4096]{1,0:T(8,128)(2,1)S(1)} %get-tuple-element.42.select_ref, f32[16,384]{1,0:T(8,128)S(1)} %get-tuple-element.41.rows_ref, f32[9,4096]{1,0:T(8,128)S(1)} %get-tuple-element.30.cos_ref, f32[9,4096]{1,0:T(8,128)S(1)} %get-tuple-element.31.sin_ref, ...), custom_call_target="tpu_custom_call" | custom-call | flops 18874368 | bytes 4000000 | tf_op jit(solution)/shard_map/final/pallas_call | solution.py:501
  18.3 0.7 %collective-permute-start.6 = (f32[8,384]{1,0:T(8,128)S(1)}, f32[8,384]{1,0:T(8,128)S(1)}, u32[]{:S(2)}, u32[]{:S(2)}) collective-permute-start(f32[8,384]{1,0:T(8,128)S(1)} %get-tuple-element.44), channel_id=1, source_target_pairs={{0,4},{1,5},{2,6},{3,7},{4,0},{5,1},{6,2},{7,3},{8,12},{9,13},{10,... | collective-permute-start | bytes 36872 | tf_op jit(solution)/shard_map/ppermute | solution.py:428
  18.9 0.1 keep.1.keep_ref
  19.1 3.8 %collective-permute-done.6.recv_ref = f32[8,384]{1,0:T(8,128)S(1)} collective-permute-done((f32[8,384]{1,0:T(8,128)S(1)}, f32[8,384]{1,0:T(8,128)S(1)}, u32[]{:S(2)}, u32[]{:S(2)}) %collective-permute-start.6) | collective-permute-done | bytes 12320 | tf_op jit(solution)/shard_map/ppermute | solution.py:428
  22.9 0.7 %place.1 = f32[9,8,64]{2,1,0:T(8,128)} custom-call(f32[9,8,64]{2,1,0:T(8,128)S(1)} %keep.1.keep_ref, f32[8,384]{1,0:T(8,128)S(1)} %collective-permute-done.6.recv_ref), custom_call_target="tpu_custom_call" | custom-call | tf_op jit(solution)/shard_map/place/pallas_call | solution.py:521
  (1 shorter events, 0.0 us)
Async XLA Ops:
  1.6 8.1 %collective-permute-start = (bf16[2,8448]{1,0:T(2,128)(2,1)S(1)}, bf16[2,8448]{1,0:T(2,128)(2,1)S(1)}, u32[]{:S(2)}, u32[]{:S(2)}) collective-permute-start(bf16[2,8448]{1,0:T(2,128)(2,1)S(1)} %get-tuple-element.29), channel_id=1, source_target_pairs={{0,4},{1,5},{2,6},{3,7},{4,0},{5,1},{6,2},{7,3},{8,12},{9,13},{10,... | collective-permute-start | bytes 101384 | tf_op jit(solution)/shard_map/ppermute | solution.py:428
  5.7 5.7 %collective-permute-start.3 = (bf16[16,4096]{1,0:T(8,128)(2,1)S(1)}, bf16[16,4096]{1,0:T(8,128)(2,1)S(1)}, u32[]{:S(2)}, u32[]{:S(2)}) collective-permute-start(bf16[16,4096]{1,0:T(8,128)(2,1)S(1)} %get-tuple-element.32.rest_0_.rest_4_), channel_id=1, source_target_pairs={{0,2},{1,3},{2,0},{3,1},{4,6},{5,7},{6,4},{7,5},{8,10},{9,11},{10,... | collective-permute-start | bytes 393224 | tf_op jit(solution)/shard_map/ppermute | solution.py:428
  7.3 5.0 %collective-permute-start.4 = (bf16[16,4096]{1,0:T(8,128)(2,1)S(1)}, bf16[16,4096]{1,0:T(8,128)(2,1)S(1)}, u32[]{:S(2)}, u32[]{:S(2)}) collective-permute-start(bf16[16,4096]{1,0:T(8,128)(2,1)S(1)} %get-tuple-element.32.rest_0_.rest_4_), channel_id=1, source_target_pairs={{0,1},{1,0},{2,3},{3,2},{4,5},{5,4},{6,7},{7,6},{8,9},{9,8},{10,11... | collective-permute-start | bytes 393224 | tf_op jit(solution)/shard_map/ppermute | solution.py:428
  9.8 4.4 %collective-permute-start.1 = (bf16[4,8448]{1,0:T(4,128)(2,1)S(1)}, bf16[4,8448]{1,0:T(4,128)(2,1)S(1)}, u32[]{:S(2)}, u32[]{:S(2)}) collective-permute-start(bf16[4,8448]{1,0:T(4,128)(2,1)S(1)} %pad_maximum_fusion.1), channel_id=1, source_target_pairs={{0,16},{8,24},{16,0},{24,8},{1,17},{9,25},{17,1},{25,9},{2,18},{10... | collective-permute-start | bytes 202760 | tf_op jit(solution)/shard_map/ppermute | solution.py:428
  12.3 5.2 %collective-permute-start.5 = (bf16[16,4480]{1,0:T(8,128)(2,1)S(1)}, bf16[16,4480]{1,0:T(8,128)(2,1)S(1)}, u32[]{:S(2)}, u32[]{:S(2)}) collective-permute-start(bf16[16,4480]{1,0:T(8,128)(2,1)S(1)} %pad.4), channel_id=1, source_target_pairs={{0,1},{1,0},{2,3},{3,2},{4,5},{5,4},{6,7},{7,6},{8,9},{9,8},{10,11... | collective-permute-start | bytes 430088 | tf_op jit(solution)/shard_map/ppermute | solution.py:428
  14.3 1.4 %collective-permute-start.2 = (bf16[8,8448]{1,0:T(8,128)(2,1)S(1)}, bf16[8,8448]{1,0:T(8,128)(2,1)S(1)}, u32[]{:S(2)}, u32[]{:S(2)}) collective-permute-start(bf16[8,8448]{1,0:T(8,128)(2,1)S(1)} %pad_maximum_fusion.rest_0_), channel_id=1, source_target_pairs={{0,8},{8,0},{16,24},{24,16},{1,9},{9,1},{17,25},{25,17},{2,10},{10... | collective-permute-start | bytes 405512 | tf_op jit(solution)/shard_map/ppermute | solution.py:428
  18.3 4.6 %collective-permute-start.6 = (f32[8,384]{1,0:T(8,128)S(1)}, f32[8,384]{1,0:T(8,128)S(1)}, u32[]{:S(2)}, u32[]{:S(2)}) collective-permute-start(f32[8,384]{1,0:T(8,128)S(1)} %get-tuple-element.44), channel_id=1, source_target_pairs={{0,4},{1,5},{2,6},{3,7},{4,0},{5,1},{6,2},{7,3},{8,12},{9,13},{10,... | collective-permute-start | bytes 36872 | tf_op jit(solution)/shard_map/ppermute | solution.py:428

commit v21 on v20

--- a/solution.py
+++ b/solution.py
@@ -46,16 +46,12 @@
     proj_ref,
     sems,
 ):
-    n_proj, n_class = proj_hbm.shape[0], curves_hbm.shape[0]
+    n_proj = proj_hbm.shape[0]
     pairs = [
-        (proj_hbm.at[: n_proj // 2], proj_ref.at[: n_proj // 2]),
-        (proj_hbm.at[n_proj // 2 :], proj_ref.at[n_proj // 2 :]),
+        (proj_hbm, proj_ref),
+        (curves_hbm, curves_ref),
         (subset_hbm, subset_ref),
         (class_hbm, class_ref),
-        (curves_hbm.at[: n_class // 4], curves_ref.at[: n_class // 4]),
-        (curves_hbm.at[n_class // 4 : n_class // 2], curves_ref.at[n_class // 4 : n_class // 2]),
-        (curves_hbm.at[n_class // 2 : 3 * n_class // 4], curves_ref.at[n_class // 2 : 3 * n_class // 4]),
-        (curves_hbm.at[3 * n_class // 4 :], curves_ref.at[3 * n_class // 4 :]),
         (particles_hbm, particles_ref),
         (noise_hbm, noise_ref),
         (prior_hbm, prior_ref),
@@ -75,8 +71,8 @@
 
     row = lax.broadcasted_iota(jnp.int32, (n_proj, wide), 0)
     lane = lax.broadcasted_iota(jnp.int32, (n_proj, wide), 1)
-    for copy in copies[:3]:
-        copy.wait()
+    copies[0].wait()
+    copies[2].wait()
     real = jnp.zeros((n_proj, wide), F32)
     imag = jnp.zeros((n_proj, wide), F32)
     for j in range(n_proj):
@@ -91,6 +87,7 @@
     real = jnp.concatenate([real[:, : wide - 128], ends], axis=1)
     bank_ref[...] = jnp.concatenate([real, imag], axis=0).astype(BF16)
 
+    copies[1].wait()
     for copy in copies[3:]:
         copy.wait()
     subsets = prior_ref.shape[1]
@@ -417,7 +414,7 @@
             pltpu.VMEM(orient_prior.shape, BF16),
             pltpu.VMEM(shift_phase.shape, F32),
             pltpu.VMEM(projections.shape, BF16),
-            pltpu.SemaphoreType.DMA((len(operands) + 4,)),
+            pltpu.SemaphoreType.DMA((len(operands),)),
         ],
         compiler_params=_params(16),
         name="pack",
@@ -474,7 +471,7 @@
     parts = [part, across]
     bits = [1 << n for n in range(ng.bit_length() - 2, -1, -1)]
     for bit in bits:
-        part = joined(parts)
+        part = lax.optimization_barrier(joined(parts))
         parts = [part, swap(part, "grp", bit)]
 
     rest_rows, rest_power = shifted_call([near, far], "shift_rest")

time: 23.8 us -> 23.7 us (level)
  no operation moved by 1% of the time
where the time goes in v21:
time: 23.7 us; the launch traced here: 23.6 us
  starting transfers between devices  11 us (46%)
  Pallas kernels  6.17 us (26%)
  waiting for transfers between devices  6.15 us (26%)
    ppermute x7, starting transfers between devices, swap(): return lax.ppermute(value, axis, [(i, i ^ bit) for i in range(size)])  11 us
    ppermute x7, waiting for transfers between devices, swap(): return lax.ppermute(value, axis, [(i, i ^ bit) for i in range(size)])  6.15 us
    pallas_call x1, Pallas kernels, per_device(): pl.pallas_call(pack_kernel, out_shape=[vmem_out((2 * n_proj, wide), BF16)...  1.59 us
    pallas_call x1, Pallas kernels, per_device(): pl.pallas_call(functools.partial(early_kernel, len(parts), (1, 2), n_proj...  1.38 us
    pallas_call x2, Pallas kernels, shifted_call(): pl.pallas_call(functools.partial(shift_kernel, n_proj), out_shape=[vmem_o...  0.94 us
    pallas_call x1, Pallas kernels, per_device(): pl.pallas_call(functools.partial(final_kernel, order, len(parts), bits, n...  0.81 us
    pallas_call x1, Pallas kernels, per_device(): pl.pallas_call(functools.partial(place_kernel, half, n_proj), out_shape=s...  0.73 us
    pallas_call x1, Pallas kernels, per_device(): pl.pallas_call(table_kernel, out_shape=[vmem_out((shifts, wide), F32), vm...  0.59 us
  transfers between devices with their start and end apart: 7, of which 5 were waited for; matrix products, arithmetic and copies ran while one was open for 1% of the time, Pallas kernels for 13%

profile of v21, /device:TPU:0, one launch (start us, length us, event | category | flops | bytes accessed | tf_op | source)
XLA Modules:
  0.0 23.6 jit_solution(18324672862615184680)
XLA Ops:
  0.0 1.6 %pack.1 = (bf16[16,4096]{1,0:T(8,128)(2,1)S(1)}, bf16[2,8448]{1,0:T(2,128)(2,1)S(1)}, f32[64,4000]{1,0:T(8,128)S(1)}, f32[1,4000]{1,0:T(1,128)S(1)}, f32[9,4000]{1,0:T(8,128)S(1)}) custom-call(s32[2]{0:T(128)} %class_hbm.1, s32[8]{0:T(128)} %subset_hbm.1, bf16[2,2,4000]{2,1,0:T(2,128)(2,1)} %particles_hbm.1, bf16[2,192]{1,0:T(2,128)(2,1)} %prior_hbm.1, ...), custom_call_target="tpu_custom_call" | custom-call | tf_op jit(solution)/shard_map/pack/pallas_call | solution.py:398
  1.6 4.1 %collective-permute-start = (bf16[2,8448]{1,0:T(2,128)(2,1)S(1)}, bf16[2,8448]{1,0:T(2,128)(2,1)S(1)}, u32[]{:S(2)}, u32[]{:S(2)}) collective-permute-start(bf16[2,8448]{1,0:T(2,128)(2,1)S(1)} %get-tuple-element.29), channel_id=1, source_target_pairs={{0,4},{1,5},{2,6},{3,7},{4,0},{5,1},{6,2},{7,3},{8,12},{9,13},{10,... | collective-permute-start | bytes 101384 | tf_op jit(solution)/shard_map/ppermute | solution.py:425
  5.7 1.6 %collective-permute-start.3 = (bf16[16,4096]{1,0:T(8,128)(2,1)S(1)}, bf16[16,4096]{1,0:T(8,128)(2,1)S(1)}, u32[]{:S(2)}, u32[]{:S(2)}) collective-permute-start(bf16[16,4096]{1,0:T(8,128)(2,1)S(1)} %get-tuple-element.32.rest_0_.rest_4_), channel_id=1, source_target_pairs={{0,2},{1,3},{2,0},{3,1},{4,6},{5,7},{6,4},{7,5},{8,10},{9,11},{10,... | collective-permute-start | bytes 393224 | tf_op jit(solution)/shard_map/ppermute | solution.py:425
  7.3 1.5 %collective-permute-start.4 = (bf16[16,4096]{1,0:T(8,128)(2,1)S(1)}, bf16[16,4096]{1,0:T(8,128)(2,1)S(1)}, u32[]{:S(2)}, u32[]{:S(2)}) collective-permute-start(bf16[16,4096]{1,0:T(8,128)(2,1)S(1)} %get-tuple-element.32.rest_0_.rest_4_), channel_id=1, source_target_pairs={{0,1},{1,0},{2,3},{3,2},{4,5},{5,4},{6,7},{7,6},{8,9},{9,8},{10,11... | collective-permute-start | bytes 393224 | tf_op jit(solution)/shard_map/ppermute | solution.py:425
  8.8 0.6 %tables.1 = (f32[9,4096]{1,0:T(8,128)S(1)}, f32[9,4096]{1,0:T(8,128)S(1)}, bf16[128,4096]{1,0:T(8,128)(2,1)S(1)}) custom-call(f32[64,4000]{1,0:T(8,128)S(1)} %get-tuple-element.25.curves_ref, f32[1,4000]{1,0:T(1,128)S(1)} %get-tuple-element.26.noise_ref, f32[9,4000]{1,0:T(8,128)S(1)} %get-tuple-element.27.angle_ref), custom_call_target="tpu_custom_call" | custom-call | flops 4000000 | bytes 2000000 | tf_op jit(solution)/shard_map/tables/pallas_call | solution.py:440
  9.4 0.3 %shift_own.1 = (bf16[72,8192]{1,0:T(8,128)(2,1)S(1)}, bf16[16,4096]{1,0:T(8,128)(2,1)S(1)}) custom-call(f32[9,4096]{1,0:T(8,128)S(1)} %get-tuple-element.30.cos_ref, f32[9,4096]{1,0:T(8,128)S(1)} %get-tuple-element.31.sin_ref, bf16[16,4096]{1,0:T(8,128)(2,1)S(1)} %get-tuple-element.32.rest_0_.rest_4_), custom_call_target="tpu_custom_call" | custom-call | flops 1769472 | bytes 4000000 | tf_op jit(solution)/shard_map/shift_own/pallas_call | solution.py:456
  9.7 0.0 collective-permute-done
  9.7 0.1 pad_maximum_fusion.1
  9.8 1.6 %collective-permute-start.1 = (bf16[4,8448]{1,0:T(4,128)(2,1)S(1)}, bf16[4,8448]{1,0:T(4,128)(2,1)S(1)}, u32[]{:S(2)}, u32[]{:S(2)}) collective-permute-start(bf16[4,8448]{1,0:T(4,128)(2,1)S(1)} %pad_maximum_fusion.1), channel_id=1, source_target_pairs={{0,16},{8,24},{16,0},{24,8},{1,17},{9,25},{17,1},{25,9},{2,18},{10... | collective-permute-start | bytes 202760 | tf_op jit(solution)/shard_map/ppermute | solution.py:425
  11.4 0.0 collective-permute-done.3.rest_1_.rest_8_
  11.4 0.9 %collective-permute-done.4.rest_0_.rest_7_ = bf16[16,4096]{1,0:T(8,128)(2,1)S(1)} collective-permute-done((bf16[16,4096]{1,0:T(8,128)(2,1)S(1)}, bf16[16,4096]{1,0:T(8,128)(2,1)S(1)}, u32[]{:S(2)}, u32[]{:S(2)}) %collective-permute-start.4) | collective-permute-done | bytes 131104 | tf_op jit(solution)/shard_map/ppermute | solution.py:425
  12.3 1.6 %collective-permute-start.5 = (bf16[16,4480]{1,0:T(8,128)(2,1)S(1)}, bf16[16,4480]{1,0:T(8,128)(2,1)S(1)}, u32[]{:S(2)}, u32[]{:S(2)}) collective-permute-start(bf16[16,4480]{1,0:T(8,128)(2,1)S(1)} %pad.4), channel_id=1, source_target_pairs={{0,1},{1,0},{2,3},{3,2},{4,5},{5,4},{6,7},{7,6},{8,9},{9,8},{10,11... | collective-permute-start | bytes 430088 | tf_op jit(solution)/shard_map/ppermute | solution.py:425
  13.8 0.3 %collective-permute-done.1 = bf16[4,8448]{1,0:T(4,128)(2,1)S(1)} collective-permute-done((bf16[4,8448]{1,0:T(4,128)(2,1)S(1)}, bf16[4,8448]{1,0:T(4,128)(2,1)S(1)}, u32[]{:S(2)}, u32[]{:S(2)}) %collective-permute-start.1) | collective-permute-done | bytes 67616 | tf_op jit(solution)/shard_map/ppermute | solution.py:425
  14.2 0.1 pad_maximum_fusion.rest_0_
  14.2 0.1 collective-permute-start.2
  14.3 0.6 %shift_rest.1 = (bf16[144,8192]{1,0:T(8,128)(2,1)S(1)}, bf16[32,4096]{1,0:T(8,128)(2,1)S(1)}) custom-call(f32[9,4096]{1,0:T(8,128)S(1)} %get-tuple-element.30.cos_ref, f32[9,4096]{1,0:T(8,128)S(1)} %get-tuple-element.31.sin_ref, bf16[16,4096]{1,0:T(8,128)(2,1)S(1)} %collective-permute-done.4.rest_0_.rest_7_, ...), custom_call_target="tpu_custom_call" | custom-call | flops 3538944 | bytes 4000000 | tf_op jit(solution)/shard_map/shift_rest/pallas_call | solution.py:456
  14.9 0.7 %collective-permute-done.2.rest_1_ = bf16[8,8448]{1,0:T(8,128)(2,1)S(1)} collective-permute-done((bf16[8,8448]{1,0:T(8,128)(2,1)S(1)}, bf16[8,8448]{1,0:T(8,128)(2,1)S(1)}, u32[]{:S(2)}, u32[]{:S(2)}) %collective-permute-start.2) | collective-permute-done | bytes 135200 | tf_op jit(solution)/shard_map/ppermute | solution.py:425
  15.7 1.4 %early.1 = (bf16[32,4096]{1,0:T(8,128)(2,1)S(1)}, f32[16,384]{1,0:T(8,128)S(1)}) custom-call(bf16[128,4096]{1,0:T(8,128)(2,1)S(1)} %get-tuple-element.28.square_ref, bf16[8,8448]{1,0:T(8,128)(2,1)S(1)} %pad_maximum_fusion.rest_0_, bf16[8,8448]{1,0:T(8,128)(2,1)S(1)} %collective-permute-done.2.rest_1_, bf16[72,8192]{1,0:T(8,128)(2,1)S(1)} %get-tuple-element.35.rest_2_, ...), custom_call_target="tpu_custom_call" | custom-call | flops 56623104 | bytes 4000000 | tf_op jit(solution)/shard_map/early/pallas_call | solution.py:482
  17.0 0.4 %collective-permute-done.5.last_ref = bf16[16,4480]{1,0:T(8,128)(2,1)S(1)} collective-permute-done((bf16[16,4480]{1,0:T(8,128)(2,1)S(1)}, bf16[16,4480]{1,0:T(8,128)(2,1)S(1)}, u32[]{:S(2)}, u32[]{:S(2)}) %collective-permute-start.5) | collective-permute-done | bytes 143392 | tf_op jit(solution)/shard_map/ppermute | solution.py:425
  17.4 0.8 %final.1 = (f32[16,128]{1,0:T(8,128)S(1)}, f32[8,384]{1,0:T(8,128)S(1)}) custom-call(bf16[32,4096]{1,0:T(8,128)(2,1)S(1)} %get-tuple-element.42.select_ref, f32[16,384]{1,0:T(8,128)S(1)} %get-tuple-element.41.rows_ref, f32[9,4096]{1,0:T(8,128)S(1)} %get-tuple-element.30.cos_ref, f32[9,4096]{1,0:T(8,128)S(1)} %get-tuple-element.31.sin_ref, ...), custom_call_target="tpu_custom_call" | custom-call | flops 18874368 | bytes 4000000 | tf_op jit(solution)/shard_map/final/pallas_call | solution.py:498
  18.2 0.6 %collective-permute-start.6 = (f32[8,384]{1,0:T(8,128)S(1)}, f32[8,384]{1,0:T(8,128)S(1)}, u32[]{:S(2)}, u32[]{:S(2)}) collective-permute-start(f32[8,384]{1,0:T(8,128)S(1)} %get-tuple-element.44), channel_id=1, source_target_pairs={{0,4},{1,5},{2,6},{3,7},{4,0},{5,1},{6,2},{7,3},{8,12},{9,13},{10,... | collective-permute-start | bytes 36872 | tf_op jit(solution)/shard_map/ppermute | solution.py:425
  18.9 0.1 keep.1.keep_ref
  19.0 3.9 %collective-permute-done.6.recv_ref = f32[8,384]{1,0:T(8,128)S(1)} collective-permute-done((f32[8,384]{1,0:T(8,128)S(1)}, f32[8,384]{1,0:T(8,128)S(1)}, u32[]{:S(2)}, u32[]{:S(2)}) %collective-permute-start.6) | collective-permute-done | bytes 12320 | tf_op jit(solution)/shard_map/ppermute | solution.py:425
  22.9 0.7 %place.1 = f32[9,8,64]{2,1,0:T(8,128)} custom-call(f32[9,8,64]{2,1,0:T(8,128)S(1)} %keep.1.keep_ref, f32[8,384]{1,0:T(8,128)S(1)} %collective-permute-done.6.recv_ref), custom_call_target="tpu_custom_call" | custom-call | tf_op jit(solution)/shard_map/place/pallas_call | solution.py:518
  (1 shorter events, 0.0 us)
Async XLA Ops:
  1.6 8.1 %collective-permute-start = (bf16[2,8448]{1,0:T(2,128)(2,1)S(1)}, bf16[2,8448]{1,0:T(2,128)(2,1)S(1)}, u32[]{:S(2)}, u32[]{:S(2)}) collective-permute-start(bf16[2,8448]{1,0:T(2,128)(2,1)S(1)} %get-tuple-element.29), channel_id=1, source_target_pairs={{0,4},{1,5},{2,6},{3,7},{4,0},{5,1},{6,2},{7,3},{8,12},{9,13},{10,... | collective-permute-start | bytes 101384 | tf_op jit(solution)/shard_map/ppermute | solution.py:425
  5.7 5.7 %collective-permute-start.3 = (bf16[16,4096]{1,0:T(8,128)(2,1)S(1)}, bf16[16,4096]{1,0:T(8,128)(2,1)S(1)}, u32[]{:S(2)}, u32[]{:S(2)}) collective-permute-start(bf16[16,4096]{1,0:T(8,128)(2,1)S(1)} %get-tuple-element.32.rest_0_.rest_4_), channel_id=1, source_target_pairs={{0,2},{1,3},{2,0},{3,1},{4,6},{5,7},{6,4},{7,5},{8,10},{9,11},{10,... | collective-permute-start | bytes 393224 | tf_op jit(solution)/shard_map/ppermute | solution.py:425
  7.3 5.0 %collective-permute-start.4 = (bf16[16,4096]{1,0:T(8,128)(2,1)S(1)}, bf16[16,4096]{1,0:T(8,128)(2,1)S(1)}, u32[]{:S(2)}, u32[]{:S(2)}) collective-permute-start(bf16[16,4096]{1,0:T(8,128)(2,1)S(1)} %get-tuple-element.32.rest_0_.rest_4_), channel_id=1, source_target_pairs={{0,1},{1,0},{2,3},{3,2},{4,5},{5,4},{6,7},{7,6},{8,9},{9,8},{10,11... | collective-permute-start | bytes 393224 | tf_op jit(solution)/shard_map/ppermute | solution.py:425
  9.8 4.4 %collective-permute-start.1 = (bf16[4,8448]{1,0:T(4,128)(2,1)S(1)}, bf16[4,8448]{1,0:T(4,128)(2,1)S(1)}, u32[]{:S(2)}, u32[]{:S(2)}) collective-permute-start(bf16[4,8448]{1,0:T(4,128)(2,1)S(1)} %pad_maximum_fusion.1), channel_id=1, source_target_pairs={{0,16},{8,24},{16,0},{24,8},{1,17},{9,25},{17,1},{25,9},{2,18},{10... | collective-permute-start | bytes 202760 | tf_op jit(solution)/shard_map/ppermute | solution.py:425
  12.3 5.2 %collective-permute-start.5 = (bf16[16,4480]{1,0:T(8,128)(2,1)S(1)}, bf16[16,4480]{1,0:T(8,128)(2,1)S(1)}, u32[]{:S(2)}, u32[]{:S(2)}) collective-permute-start(bf16[16,4480]{1,0:T(8,128)(2,1)S(1)} %pad.4), channel_id=1, source_target_pairs={{0,1},{1,0},{2,3},{3,2},{4,5},{5,4},{6,7},{7,6},{8,9},{9,8},{10,11... | collective-permute-start | bytes 430088 | tf_op jit(solution)/shard_map/ppermute | solution.py:425
  14.2 1.4 %collective-permute-start.2 = (bf16[8,8448]{1,0:T(8,128)(2,1)S(1)}, bf16[8,8448]{1,0:T(8,128)(2,1)S(1)}, u32[]{:S(2)}, u32[]{:S(2)}) collective-permute-start(bf16[8,8448]{1,0:T(8,128)(2,1)S(1)} %pad_maximum_fusion.rest_0_), channel_id=1, source_target_pairs={{0,8},{8,0},{16,24},{24,16},{1,9},{9,1},{17,25},{25,17},{2,10},{10... | collective-permute-start | bytes 405512 | tf_op jit(solution)/shard_map/ppermute | solution.py:425
  18.2 4.6 %collective-permute-start.6 = (f32[8,384]{1,0:T(8,128)S(1)}, f32[8,384]{1,0:T(8,128)S(1)}, u32[]{:S(2)}, u32[]{:S(2)}) collective-permute-start(f32[8,384]{1,0:T(8,128)S(1)} %get-tuple-element.44), channel_id=1, source_target_pairs={{0,4},{1,5},{2,6},{3,7},{4,0},{5,1},{6,2},{7,3},{8,12},{9,13},{10,... | collective-permute-start | bytes 36872 | tf_op jit(solution)/shard_map/ppermute | solution.py:425

commit v22 on v21

--- a/solution.py
+++ b/solution.py
@@ -223,19 +223,17 @@
     return pieces
 
 
-def store_pieces(out, pieces, first, slot, rows):
-    for n, piece in enumerate(pieces):
-        at = (first + n) * slot
-        out[:, at : at + piece.shape[1]] = piece[rows]
-
-
 def rows_of(parts, span):
     return jnp.concatenate([part[:, span] for part in parts], axis=0)
 
 
-def early_kernel(n_parts, n_banks, n_proj, length, subsets, square_ref, *rest):
+def rows_of(parts, span):
+    return jnp.concatenate([part[:, span] for part in parts], axis=0)
+
+
+def score_kernel(order, bits, n_parts, n_banks, n_proj, length, subsets, square_ref, *rest):
     parts, rest = rest[:n_parts], rest[n_parts:]
-    groups, (select_ref, rows_ref) = [], rest[-2:]
+    groups, (rows_ref, give_ref, select_ref) = [], rest[-3:]
     for n in n_banks:
         groups.append((rest[0], rest[1], rest[2 : 2 + n]))
         rest = rest[2 + n :]
@@ -260,36 +258,14 @@
             turned = added(turned, multiply(shifted_ref[:, other], rows_of(parts, other)))
         norm = multiply(select_ref[...], power_ref[...])
         pieces += pieces_of(cross + turned.T, norm, extra, banks, length, subsets, n_proj)
-    store_pieces(rows_ref, pieces, 0, rows_ref.shape[1] // len(pieces), slice(None))
-
-
-def final_kernel(
-    order, n_parts, bits, n_proj, length, subsets, select_ref, rows_ref, cos_ref, sin_ref, last_ref, *rest
-):
-    parts, (late_ref, give_ref) = rest[:n_parts], rest[n_parts:]
-    shifts, wide = cos_ref.shape
-    cross, norm = None, None
-    for span in spans_of(wide):
-        terms, powers = [], []
-        for real, imag in bank_pieces(last_ref, span, n_proj):
-            real_rows, imag_rows = shifted_rows(real, imag, cos_ref, sin_ref, span)
-            other = slice(wide + span.start, wide + span.stop)
-            terms.append(
-                multiply(rows_of(parts, span), real_rows) + multiply(rows_of(parts, other), imag_rows)
-            )
-            powers.append(real * real + imag * imag)
-        cross = added(cross, jnp.concatenate(terms, axis=1))
-        power = split_terms(jnp.concatenate(powers, axis=0))
-        norm = added(norm, multiply(select_ref[:, span], power))
-    extra = rows_of(parts, slice(2 * wide, None)).astype(F32)
-    pieces = pieces_of(cross, norm, extra, [last_ref], length, subsets, n_proj)
-    slot = late_ref.shape[1] // len(pieces)
-    zeros = jnp.zeros((extra.shape[0], slot - pieces[0].shape[1]), F32)
-    late = [jnp.concatenate([piece, zeros], axis=1) for piece in pieces]
-    late_ref[...] = jnp.concatenate(late, axis=1)
+
+    slot = rows_ref.shape[1] // len(order)
+    width = pieces[0].shape[1]
+    zeros = jnp.zeros((count, slot - width), F32)
+    pieces = [jnp.concatenate([piece, zeros], axis=1) for piece in pieces]
+    rows_ref[...] = jnp.concatenate(pieces, axis=1)
     dest, lanes = give_ref.shape
-    width = pieces[0].shape[1]
-    rows = [in_rows(values, 1, bits, dest) for values in slots_of(rows_ref, slot) + late]
+    rows = [in_rows(values, 1, bits, dest) for values in pieces]
     rows = [values[:, :width] for values in in_order(rows, order)]
     if lanes > len(rows) * width:
         rows.append(jnp.zeros((dest, lanes - len(rows) * width), F32))
@@ -341,9 +317,9 @@
     return [line(t) + offset for t in range(shifts)]
 
 
-def keep_kernel(slot, n_proj, order, bits, rows_ref, late_ref, out_ref):
+def keep_kernel(slot, n_proj, order, bits, rows_ref, out_ref):
     shifts, dest, _ = out_ref.shape
-    pieces = [in_rows(values, 0, bits, dest) for values in slots_of(rows_ref, slot) + slots_of(late_ref, slot)]
+    pieces = [in_rows(values, 0, bits, dest) for values in slots_of(rows_ref, slot)]
     for t, line in enumerate(by_shift(in_order(pieces, order), n_proj, shifts)):
         out_ref[t] = line
 
@@ -433,8 +409,8 @@
     for n in range(half.bit_length() - 2, 0, -1):
         planes.append(swap(joined(planes), "blk", 1 << n))
         order += [offset ^ (1 << n) for offset in order]
-    far, near = lax.optimization_barrier((joined(planes[1:]), near))
-    last = swap(jnp.pad(far, ((0, 0), (0, 3 * 128))), "blk", 1)
+    far = joined(planes[1:])
+    last = swap(bank, "blk", 3) if half == 4 else swap(far, "blk", 1)
     order = [0, 1] + order[1:] + [offset ^ 1 for offset in order[1:]]
 
     cos_part, sin_part, square = pl.pallas_call(
@@ -465,56 +441,42 @@
             name=name,
         )(cos_part, sin_part, *banks)
 
-    own_rows, own_power = shifted_call([bank], "shift_own")
-
-    across, own_power = lax.optimization_barrier((across, own_power))
+    early_rows, early_power = shifted_call([bank, near, far], "shift")
+
     parts = [part, across]
     bits = [1 << n for n in range(ng.bit_length() - 2, -1, -1)]
     for bit in bits:
+        if bit == 1:
+            parts[1], early_power, last = lax.optimization_barrier((parts[1], early_power, last))
         part = lax.optimization_barrier(joined(parts))
         parts = [part, swap(part, "grp", bit)]
 
-    rest_rows, rest_power = shifted_call([near, far], "shift_rest")
+    last_rows, last_power = shifted_call([last], "shift_last")
+
     count = 2 * ng * n_part
-    late = half // 2 - 1
     slot = 128 * -(-(shifts + 1) * n_proj // 128)
     lanes = 128 * -(-(shifts + 1) * n_proj * half // 128)
-    select, rows = pl.pallas_call(
-        functools.partial(early_kernel, len(parts), (1, 2), n_proj, length, subsets),
-        out_shape=[
-            vmem_out((2 * count, wide), BF16),
-            vmem_out((count, (half - late) * slot), F32),
-        ],
-        in_specs=[_vmem()] * (8 + len(parts)),
+    rows, give = pl.pallas_call(
+        functools.partial(score_kernel, order, bits, len(parts), (3, 1), n_proj, length, subsets),
+        out_shape=[vmem_out((count, half * slot), F32), vmem_out((ng * n_part, lanes), F32)],
+        in_specs=[_vmem()] * (9 + len(parts)),
         out_specs=[_vmem()] * 2,
-        compiler_params=_params(16),
+        scratch_shapes=[pltpu.VMEM((2 * count, wide), BF16)],
+        compiler_params=_params(24),
         cost_estimate=pl.CostEstimate(
-            flops=4 * count * (half - late) * n_proj * shifts * wide,
-            bytes_accessed=4_000_000,
-            transcendentals=0,
+            flops=4 * count * half * n_proj * shifts * wide, bytes_accessed=4_000_000, transcendentals=0
         ),
-        name="early",
-    )(square, *parts, own_rows, own_power, bank, rest_rows, rest_power, near, far)
-    late_rows, give = pl.pallas_call(
-        functools.partial(final_kernel, order, len(parts), bits, n_proj, length, subsets),
-        out_shape=[vmem_out((count, late * slot), F32), vmem_out((ng * n_part, lanes), F32)],
-        in_specs=[_vmem()] * (5 + len(parts)),
-        out_specs=[_vmem()] * 2,
-        compiler_params=_params(16),
-        cost_estimate=pl.CostEstimate(
-            flops=4 * count * late * n_proj * shifts * wide, bytes_accessed=4_000_000, transcendentals=0
-        ),
-        name="final",
-    )(select, rows, cos_part, sin_part, last, *parts)
+        name="score",
+    )(square, *parts, early_rows, early_power, bank, near, far, last_rows, last_power, last)
     recv = swap(give, "blk", half)
     keep = pl.pallas_call(
         functools.partial(keep_kernel, slot, n_proj, order, bits),
         out_shape=vmem_out((shifts, ng * n_part, nb * n_proj), F32),
-        in_specs=[_vmem()] * 2,
+        in_specs=[_vmem()],
         out_specs=_vmem(),
         compiler_params=_params(4),
         name="keep",
-    )(rows, late_rows)
+    )(rows)
     scores = pl.pallas_call(
         functools.partial(place_kernel, half, n_proj),
         out_shape=shape((shifts, ng * n_part, nb * n_proj), F32),

time: 23.7 us -> 23.7 us (level)
  waiting for transfers between devices: 6.15 us -> 7.63 us
  starting transfers between devices: 11 us -> 9.64 us
    ppermute x7, waiting for transfers between devices: 6.15 us -> 7.63 us  [swap(): return lax.ppermute(value, axis, [(i, i ^ bit) for i in range(size)])]
    ppermute x7, starting transfers between devices: 11 us -> 9.64 us  [swap(): return lax.ppermute(value, axis, [(i, i ^ bit) for i in range(size)])]
    pallas_call x2 -> x1, Pallas kernels: 2.18 us -> 1.8 us  [per_device(): pl.pallas_call(functools.partial(score_kernel, order, bits, len(parts), (...]
    pallas_call x2, Pallas kernels: 0.94 us -> 1.27 us  [shifted_call(): pl.pallas_call(functools.partial(shift_kernel, n_proj), out_shape=[vmem_o...]
  transfers between devices with their start and end apart: 7 -> 7, of which waited for: 5 -> 4; matrix products, arithmetic and copies ran while one was open for 1% -> 0% of each run, Pallas kernels for 13% -> 8%
where the time goes in v22:
time: 23.7 us; the launch traced here: 23.6 us
  starting transfers between devices  9.64 us (41%)
  waiting for transfers between devices  7.63 us (32%)
  Pallas kernels  6.1 us (26%)
    ppermute x7, starting transfers between devices, swap(): return lax.ppermute(value, axis, [(i, i ^ bit) for i in range(size)])  9.64 us
    ppermute x7, waiting for transfers between devices, swap(): return lax.ppermute(value, axis, [(i, i ^ bit) for i in range(size)])  7.63 us
    pallas_call x1, Pallas kernels, per_device(): pl.pallas_call(functools.partial(score_kernel, order, bits, len(parts), (...  1.8 us
    pallas_call x1, Pallas kernels, per_device(): pl.pallas_call(pack_kernel, out_shape=[vmem_out((2 * n_proj, wide), BF16)...  1.59 us
    pallas_call x2, Pallas kernels, shifted_call(): pl.pallas_call(functools.partial(shift_kernel, n_proj), out_shape=[vmem_o...  1.27 us
    pallas_call x1, Pallas kernels, per_device(): pl.pallas_call(functools.partial(place_kernel, half, n_proj), out_shape=s...  0.73 us
    pallas_call x1, Pallas kernels, per_device(): pl.pallas_call(table_kernel, out_shape=[vmem_out((shifts, wide), F32), vm...  0.58 us
  transfers between devices with their start and end apart: 7, of which 4 were waited for; matrix products, arithmetic and copies ran while one was open for 0% of the time, Pallas kernels for 8%

profile of v22, /device:TPU:0, one launch (start us, length us, event | category | flops | bytes accessed | tf_op | source)
XLA Modules:
  0.0 23.6 jit_solution(7130708844925708512)
XLA Ops:
  0.0 1.6 %pack.1 = (bf16[16,4096]{1,0:T(8,128)(2,1)S(1)}, bf16[2,8448]{1,0:T(2,128)(2,1)S(1)}, f32[64,4000]{1,0:T(8,128)S(1)}, f32[1,4000]{1,0:T(1,128)S(1)}, f32[9,4000]{1,0:T(8,128)S(1)}) custom-call(s32[2]{0:T(128)} %class_hbm.1, s32[8]{0:T(128)} %subset_hbm.1, bf16[2,2,4000]{2,1,0:T(2,128)(2,1)} %particles_hbm.1, bf16[2,192]{1,0:T(2,128)(2,1)} %prior_hbm.1, ...), custom_call_target="tpu_custom_call" | custom-call | tf_op jit(solution)/shard_map/pack/pallas_call | solution.py:374
  1.6 4.1 %collective-permute-start = (bf16[2,8448]{1,0:T(2,128)(2,1)S(1)}, bf16[2,8448]{1,0:T(2,128)(2,1)S(1)}, u32[]{:S(2)}, u32[]{:S(2)}) collective-permute-start(bf16[2,8448]{1,0:T(2,128)(2,1)S(1)} %get-tuple-element.26), channel_id=1, source_target_pairs={{0,4},{1,5},{2,6},{3,7},{4,0},{5,1},{6,2},{7,3},{8,12},{9,13},{10,... | collective-permute-start | bytes 101384 | tf_op jit(solution)/shard_map/ppermute | solution.py:401
  5.7 1.5 %collective-permute-start.2 = (bf16[16,4096]{1,0:T(8,128)(2,1)S(1)}, bf16[16,4096]{1,0:T(8,128)(2,1)S(1)}, u32[]{:S(2)}, u32[]{:S(2)}) collective-permute-start(bf16[16,4096]{1,0:T(8,128)(2,1)S(1)} %get-tuple-element.29.rest_0_.rest_4_), channel_id=1, source_target_pairs={{0,1},{1,0},{2,3},{3,2},{4,5},{5,4},{6,7},{7,6},{8,9},{9,8},{10,11... | collective-permute-start | bytes 393224 | tf_op jit(solution)/shard_map/ppermute | solution.py:401
  7.2 1.6 %collective-permute-start.3 = (bf16[16,4096]{1,0:T(8,128)(2,1)S(1)}, bf16[16,4096]{1,0:T(8,128)(2,1)S(1)}, u32[]{:S(2)}, u32[]{:S(2)}) collective-permute-start(bf16[16,4096]{1,0:T(8,128)(2,1)S(1)} %get-tuple-element.29.rest_0_.rest_4_), channel_id=1, source_target_pairs={{0,2},{1,3},{2,0},{3,1},{4,6},{5,7},{6,4},{7,5},{8,10},{9,11},{10,... | collective-permute-start | bytes 393224 | tf_op jit(solution)/shard_map/ppermute | solution.py:401
  8.8 0.4 %collective-permute-start.4 = (bf16[16,4096]{1,0:T(8,128)(2,1)S(1)}, bf16[16,4096]{1,0:T(8,128)(2,1)S(1)}, u32[]{:S(2)}, u32[]{:S(2)}) collective-permute-start(bf16[16,4096]{1,0:T(8,128)(2,1)S(1)} %get-tuple-element.29.rest_0_.rest_4_), channel_id=1, source_target_pairs={{0,3},{1,2},{2,1},{3,0},{4,7},{5,6},{6,5},{7,4},{8,11},{9,10},{10,... | collective-permute-start | bytes 393224 | tf_op jit(solution)/shard_map/ppermute | solution.py:401
  9.2 0.0 collective-permute-done
  9.2 0.1 pad_maximum_fusion.1
  9.3 1.6 %collective-permute-start.1 = (bf16[4,8448]{1,0:T(4,128)(2,1)S(1)}, bf16[4,8448]{1,0:T(4,128)(2,1)S(1)}, u32[]{:S(2)}, u32[]{:S(2)}) collective-permute-start(bf16[4,8448]{1,0:T(4,128)(2,1)S(1)} %pad_maximum_fusion.1), channel_id=1, source_target_pairs={{0,16},{8,24},{16,0},{24,8},{1,17},{9,25},{17,1},{25,9},{2,18},{10... | collective-permute-start | bytes 202760 | tf_op jit(solution)/shard_map/ppermute | solution.py:401
  10.8 0.6 %tables.1 = (f32[9,4096]{1,0:T(8,128)S(1)}, f32[9,4096]{1,0:T(8,128)S(1)}, bf16[128,4096]{1,0:T(8,128)(2,1)S(1)}) custom-call(f32[64,4000]{1,0:T(8,128)S(1)} %get-tuple-element.22.curves_ref, f32[1,4000]{1,0:T(1,128)S(1)} %get-tuple-element.23.noise_ref, f32[9,4000]{1,0:T(8,128)S(1)} %get-tuple-element.24.angle_ref), custom_call_target="tpu_custom_call" | custom-call | flops 4000000 | bytes 2000000 | tf_op jit(solution)/shard_map/tables/pallas_call | solution.py:416
  11.4 0.0 collective-permute-done.2.rest_1_.rest_5_
  11.4 1.9 %collective-permute-done.3.rest_2_.rest_6_ = bf16[16,4096]{1,0:T(8,128)(2,1)S(1)} collective-permute-done((bf16[16,4096]{1,0:T(8,128)(2,1)S(1)}, bf16[16,4096]{1,0:T(8,128)(2,1)S(1)}, u32[]{:S(2)}, u32[]{:S(2)}) %collective-permute-start.3) | collective-permute-done | bytes 131104 | tf_op jit(solution)/shard_map/ppermute | solution.py:401
  13.3 0.9 %shift.1 = (bf16[216,8192]{1,0:T(8,128)(2,1)S(1)}, bf16[48,4096]{1,0:T(8,128)(2,1)S(1)}) custom-call(f32[9,4096]{1,0:T(8,128)S(1)} %get-tuple-element.27.cos_ref, f32[9,4096]{1,0:T(8,128)S(1)} %get-tuple-element.28.sin_ref, bf16[16,4096]{1,0:T(8,128)(2,1)S(1)} %get-tuple-element.29.rest_0_.rest_4_, ...), custom_call_target="tpu_custom_call" | custom-call | flops 5308416 | bytes 4000000 | tf_op jit(solution)/shard_map/shift/pallas_call | solution.py:432
  14.2 0.0 collective-permute-done.1
  14.3 0.7 %collective-permute-done.4.rest_0_.rest_9_ = bf16[16,4096]{1,0:T(8,128)(2,1)S(1)} collective-permute-done((bf16[16,4096]{1,0:T(8,128)(2,1)S(1)}, bf16[16,4096]{1,0:T(8,128)(2,1)S(1)}, u32[]{:S(2)}, u32[]{:S(2)}) %collective-permute-start.4) | collective-permute-done | bytes 131104 | tf_op jit(solution)/shard_map/ppermute | solution.py:401
  14.9 0.1 pad_maximum_fusion.rest_0_
  15.0 0.1 collective-permute-start.5
  15.1 0.3 %shift_last.1 = (bf16[72,8192]{1,0:T(8,128)(2,1)S(1)}, bf16[16,4096]{1,0:T(8,128)(2,1)S(1)}) custom-call(f32[9,4096]{1,0:T(8,128)S(1)} %get-tuple-element.27.cos_ref, f32[9,4096]{1,0:T(8,128)S(1)} %get-tuple-element.28.sin_ref, bf16[16,4096]{1,0:T(8,128)(2,1)S(1)} %collective-permute-done.4.rest_0_.rest_9_), custom_call_target="tpu_custom_call" | custom-call | flops 1769472 | bytes 4000000 | tf_op jit(solution)/shard_map/shift_last/pallas_call | solution.py:432
  15.4 1.0 %collective-permute-done.5.rest_1_ = bf16[8,8448]{1,0:T(8,128)(2,1)S(1)} collective-permute-done((bf16[8,8448]{1,0:T(8,128)(2,1)S(1)}, bf16[8,8448]{1,0:T(8,128)(2,1)S(1)}, u32[]{:S(2)}, u32[]{:S(2)}) %collective-permute-start.5) | collective-permute-done | bytes 135200 | tf_op jit(solution)/shard_map/ppermute | solution.py:401
  16.4 1.8 %score.1 = (f32[16,512]{1,0:T(8,128)S(1)}, f32[8,384]{1,0:T(8,128)S(1)}) custom-call(bf16[128,4096]{1,0:T(8,128)(2,1)S(1)} %get-tuple-element.25.square_ref, bf16[8,8448]{1,0:T(8,128)(2,1)S(1)} %pad_maximum_fusion.rest_0_, bf16[8,8448]{1,0:T(8,128)(2,1)S(1)} %collective-permute-done.5.rest_1_, bf16[216,8192]{1,0:T(8,128)(2,1)S(1)} %get-tuple-element.32.rest_2_, ...), custom_call_target="tpu_custom_call" | custom-call | flops 75497472 | bytes 4000000 | tf_op jit(solution)/shard_map/score/pallas_call | solution.py:459
  18.2 0.4 %collective-permute-start.6 = (f32[8,384]{1,0:T(8,128)S(1)}, f32[8,384]{1,0:T(8,128)S(1)}, u32[]{:S(2)}, u32[]{:S(2)}) collective-permute-start(f32[8,384]{1,0:T(8,128)S(1)} %get-tuple-element.38), channel_id=1, source_target_pairs={{0,4},{1,5},{2,6},{3,7},{4,0},{5,1},{6,2},{7,3},{8,12},{9,13},{10,... | collective-permute-start | bytes 36872 | tf_op jit(solution)/shard_map/ppermute | solution.py:401
  18.7 0.1 keep.1.keep_ref
  18.8 4.1 %collective-permute-done.6.recv_ref = f32[8,384]{1,0:T(8,128)S(1)} collective-permute-done((f32[8,384]{1,0:T(8,128)S(1)}, f32[8,384]{1,0:T(8,128)S(1)}, u32[]{:S(2)}, u32[]{:S(2)}) %collective-permute-start.6) | collective-permute-done | bytes 12320 | tf_op jit(solution)/shard_map/ppermute | solution.py:401
  22.9 0.7 %place.1 = f32[9,8,64]{2,1,0:T(8,128)} custom-call(f32[9,8,64]{2,1,0:T(8,128)S(1)} %keep.1.keep_ref, f32[8,384]{1,0:T(8,128)S(1)} %collective-permute-done.6.recv_ref), custom_call_target="tpu_custom_call" | custom-call | tf_op jit(solution)/shard_map/place/pallas_call | solution.py:480
Async XLA Ops:
  1.6 7.6 %collective-permute-start = (bf16[2,8448]{1,0:T(2,128)(2,1)S(1)}, bf16[2,8448]{1,0:T(2,128)(2,1)S(1)}, u32[]{:S(2)}, u32[]{:S(2)}) collective-permute-start(bf16[2,8448]{1,0:T(2,128)(2,1)S(1)} %get-tuple-element.26), channel_id=1, source_target_pairs={{0,4},{1,5},{2,6},{3,7},{4,0},{5,1},{6,2},{7,3},{8,12},{9,13},{10,... | collective-permute-start | bytes 101384 | tf_op jit(solution)/shard_map/ppermute | solution.py:401
  5.7 5.7 %collective-permute-start.2 = (bf16[16,4096]{1,0:T(8,128)(2,1)S(1)}, bf16[16,4096]{1,0:T(8,128)(2,1)S(1)}, u32[]{:S(2)}, u32[]{:S(2)}) collective-permute-start(bf16[16,4096]{1,0:T(8,128)(2,1)S(1)} %get-tuple-element.29.rest_0_.rest_4_), channel_id=1, source_target_pairs={{0,1},{1,0},{2,3},{3,2},{4,5},{5,4},{6,7},{7,6},{8,9},{9,8},{10,11... | collective-permute-start | bytes 393224 | tf_op jit(solution)/shard_map/ppermute | solution.py:401
  7.2 6.1 %collective-permute-start.3 = (bf16[16,4096]{1,0:T(8,128)(2,1)S(1)}, bf16[16,4096]{1,0:T(8,128)(2,1)S(1)}, u32[]{:S(2)}, u32[]{:S(2)}) collective-permute-start(bf16[16,4096]{1,0:T(8,128)(2,1)S(1)} %get-tuple-element.29.rest_0_.rest_4_), channel_id=1, source_target_pairs={{0,2},{1,3},{2,0},{3,1},{4,6},{5,7},{6,4},{7,5},{8,10},{9,11},{10,... | collective-permute-start | bytes 393224 | tf_op jit(solution)/shard_map/ppermute | solution.py:401
  8.8 6.1 %collective-permute-start.4 = (bf16[16,4096]{1,0:T(8,128)(2,1)S(1)}, bf16[16,4096]{1,0:T(8,128)(2,1)S(1)}, u32[]{:S(2)}, u32[]{:S(2)}) collective-permute-start(bf16[16,4096]{1,0:T(8,128)(2,1)S(1)} %get-tuple-element.29.rest_0_.rest_4_), channel_id=1, source_target_pairs={{0,3},{1,2},{2,1},{3,0},{4,7},{5,6},{6,5},{7,4},{8,11},{9,10},{10,... | collective-permute-start | bytes 393224 | tf_op jit(solution)/shard_map/ppermute | solution.py:401
  9.3 5.0 %collective-permute-start.1 = (bf16[4,8448]{1,0:T(4,128)(2,1)S(1)}, bf16[4,8448]{1,0:T(4,128)(2,1)S(1)}, u32[]{:S(2)}, u32[]{:S(2)}) collective-permute-start(bf16[4,8448]{1,0:T(4,128)(2,1)S(1)} %pad_maximum_fusion.1), channel_id=1, source_target_pairs={{0,16},{8,24},{16,0},{24,8},{1,17},{9,25},{17,1},{25,9},{2,18},{10... | collective-permute-start | bytes 202760 | tf_op jit(solution)/shard_map/ppermute | solution.py:401
  15.0 1.4 %collective-permute-start.5 = (bf16[8,8448]{1,0:T(8,128)(2,1)S(1)}, bf16[8,8448]{1,0:T(8,128)(2,1)S(1)}, u32[]{:S(2)}, u32[]{:S(2)}) collective-permute-start(bf16[8,8448]{1,0:T(8,128)(2,1)S(1)} %pad_maximum_fusion.rest_0_), channel_id=1, source_target_pairs={{0,8},{8,0},{16,24},{24,16},{1,9},{9,1},{17,25},{25,17},{2,10},{10... | collective-permute-start | bytes 405512 | tf_op jit(solution)/shard_map/ppermute | solution.py:401
  18.2 4.6 %collective-permute-start.6 = (f32[8,384]{1,0:T(8,128)S(1)}, f32[8,384]{1,0:T(8,128)S(1)}, u32[]{:S(2)}, u32[]{:S(2)}) collective-permute-start(f32[8,384]{1,0:T(8,128)S(1)} %get-tuple-element.38), channel_id=1, source_target_pairs={{0,4},{1,5},{2,6},{3,7},{4,0},{5,1},{6,2},{7,3},{8,12},{9,13},{10,... | collective-permute-start | bytes 36872 | tf_op jit(solution)/shard_map/ppermute | solution.py:401

commit v23 on v22

--- a/solution.py
+++ b/solution.py
@@ -411,7 +411,7 @@
         order += [offset ^ (1 << n) for offset in order]
     far = joined(planes[1:])
     last = swap(bank, "blk", 3) if half == 4 else swap(far, "blk", 1)
-    order = [0, 1] + order[1:] + [offset ^ 1 for offset in order[1:]]
+    order = order + [1] + [offset ^ 1 for offset in order[1:]]
 
     cos_part, sin_part, square = pl.pallas_call(
         table_kernel,
@@ -441,7 +441,7 @@
             name=name,
         )(cos_part, sin_part, *banks)
 
-    early_rows, early_power = shifted_call([bank, near, far], "shift")
+    early_rows, early_power = shifted_call([bank, far, near], "shift")
 
     parts = [part, across]
     bits = [1 << n for n in range(ng.bit_length() - 2, -1, -1)]
@@ -467,7 +467,7 @@
             flops=4 * count * half * n_proj * shifts * wide, bytes_accessed=4_000_000, transcendentals=0
         ),
         name="score",
-    )(square, *parts, early_rows, early_power, bank, near, far, last_rows, last_power, last)
+    )(square, *parts, early_rows, early_power, bank, far, near, last_rows, last_power, last)
     recv = swap(give, "blk", half)
     keep = pl.pallas_call(
         functools.partial(keep_kernel, slot, n_proj, order, bits),

time: 23.7 us -> 24.8 us (1.046)
  waiting for transfers between devices: 7.63 us -> 9.09 us
  starting transfers between devices: 9.64 us -> 9.23 us
    ppermute x7, waiting for transfers between devices: 7.63 us -> 9.09 us  [swap(): return lax.ppermute(value, axis, [(i, i ^ bit) for i in range(size)])]
    ppermute x7, starting transfers between devices: 9.64 us -> 9.23 us  [swap(): return lax.ppermute(value, axis, [(i, i ^ bit) for i in range(size)])]
  transfers between devices with their start and end apart: 7 -> 7, of which waited for: 4 -> 3; matrix products, arithmetic and copies ran while one was open for 0% -> 0% of each run, Pallas kernels for 8% -> 8%
where the time goes in v23:
time: 24.8 us; the launch traced here: 24.7 us
  starting transfers between devices  9.23 us (37%)
  waiting for transfers between devices  9.09 us (37%)
  Pallas kernels  6.11 us (25%)
    ppermute x7, starting transfers between devices, swap(): return lax.ppermute(value, axis, [(i, i ^ bit) for i in range(size)])  9.23 us
    ppermute x7, waiting for transfers between devices, swap(): return lax.ppermute(value, axis, [(i, i ^ bit) for i in range(size)])  9.09 us
    pallas_call x1, Pallas kernels, per_device(): pl.pallas_call(functools.partial(score_kernel, order, bits, len(parts), (...  1.8 us
    pallas_call x1, Pallas kernels, per_device(): pl.pallas_call(pack_kernel, out_shape=[vmem_out((2 * n_proj, wide), BF16)...  1.59 us
    pallas_call x2, Pallas kernels, shifted_call(): pl.pallas_call(functools.partial(shift_kernel, n_proj), out_shape=[vmem_o...  1.27 us
    pallas_call x1, Pallas kernels, per_device(): pl.pallas_call(functools.partial(place_kernel, half, n_proj), out_shape=s...  0.73 us
    pallas_call x1, Pallas kernels, per_device(): pl.pallas_call(table_kernel, out_shape=[vmem_out((shifts, wide), F32), vm...  0.58 us
  transfers between devices with their start and end apart: 7, of which 3 were waited for; matrix products, arithmetic and copies ran while one was open for 0% of the time, Pallas kernels for 8%

profile of v23, /device:TPU:0, one launch (start us, length us, event | category | flops | bytes accessed | tf_op | source)
XLA Modules:
  0.0 24.7 jit_solution(2613218882621843563)
XLA Ops:
  0.0 1.6 %pack.1 = (bf16[16,4096]{1,0:T(8,128)(2,1)S(1)}, bf16[2,8448]{1,0:T(2,128)(2,1)S(1)}, f32[64,4000]{1,0:T(8,128)S(1)}, f32[1,4000]{1,0:T(1,128)S(1)}, f32[9,4000]{1,0:T(8,128)S(1)}) custom-call(s32[2]{0:T(128)} %class_hbm.1, s32[8]{0:T(128)} %subset_hbm.1, bf16[2,2,4000]{2,1,0:T(2,128)(2,1)} %particles_hbm.1, bf16[2,192]{1,0:T(2,128)(2,1)} %prior_hbm.1, ...), custom_call_target="tpu_custom_call" | custom-call | tf_op jit(solution)/shard_map/pack/pallas_call | solution.py:374
  1.6 4.1 %collective-permute-start = (bf16[2,8448]{1,0:T(2,128)(2,1)S(1)}, bf16[2,8448]{1,0:T(2,128)(2,1)S(1)}, u32[]{:S(2)}, u32[]{:S(2)}) collective-permute-start(bf16[2,8448]{1,0:T(2,128)(2,1)S(1)} %get-tuple-element.26), channel_id=1, source_target_pairs={{0,4},{1,5},{2,6},{3,7},{4,0},{5,1},{6,2},{7,3},{8,12},{9,13},{10,... | collective-permute-start | bytes 101384 | tf_op jit(solution)/shard_map/ppermute | solution.py:401
  5.7 1.6 %collective-permute-start.2 = (bf16[16,4096]{1,0:T(8,128)(2,1)S(1)}, bf16[16,4096]{1,0:T(8,128)(2,1)S(1)}, u32[]{:S(2)}, u32[]{:S(2)}) collective-permute-start(bf16[16,4096]{1,0:T(8,128)(2,1)S(1)} %get-tuple-element.29.rest_0_.rest_4_), channel_id=1, source_target_pairs={{0,2},{1,3},{2,0},{3,1},{4,6},{5,7},{6,4},{7,5},{8,10},{9,11},{10,... | collective-permute-start | bytes 393224 | tf_op jit(solution)/shard_map/ppermute | solution.py:401
  7.3 1.5 %collective-permute-start.3 = (bf16[16,4096]{1,0:T(8,128)(2,1)S(1)}, bf16[16,4096]{1,0:T(8,128)(2,1)S(1)}, u32[]{:S(2)}, u32[]{:S(2)}) collective-permute-start(bf16[16,4096]{1,0:T(8,128)(2,1)S(1)} %get-tuple-element.29.rest_0_.rest_4_), channel_id=1, source_target_pairs={{0,1},{1,0},{2,3},{3,2},{4,5},{5,4},{6,7},{7,6},{8,9},{9,8},{10,11... | collective-permute-start | bytes 393224 | tf_op jit(solution)/shard_map/ppermute | solution.py:401
  8.8 0.4 %collective-permute-start.4 = (bf16[16,4096]{1,0:T(8,128)(2,1)S(1)}, bf16[16,4096]{1,0:T(8,128)(2,1)S(1)}, u32[]{:S(2)}, u32[]{:S(2)}) collective-permute-start(bf16[16,4096]{1,0:T(8,128)(2,1)S(1)} %get-tuple-element.29.rest_0_.rest_4_), channel_id=1, source_target_pairs={{0,3},{1,2},{2,1},{3,0},{4,7},{5,6},{6,5},{7,4},{8,11},{9,10},{10,... | collective-permute-start | bytes 393224 | tf_op jit(solution)/shard_map/ppermute | solution.py:401
  9.2 0.0 collective-permute-done
  9.2 0.1 pad_maximum_fusion.1
  9.3 1.6 %collective-permute-start.1 = (bf16[4,8448]{1,0:T(4,128)(2,1)S(1)}, bf16[4,8448]{1,0:T(4,128)(2,1)S(1)}, u32[]{:S(2)}, u32[]{:S(2)}) collective-permute-start(bf16[4,8448]{1,0:T(4,128)(2,1)S(1)} %pad_maximum_fusion.1), channel_id=1, source_target_pairs={{0,16},{8,24},{16,0},{24,8},{1,17},{9,25},{17,1},{25,9},{2,18},{10... | collective-permute-start | bytes 202760 | tf_op jit(solution)/shard_map/ppermute | solution.py:401
  10.8 0.6 %tables.1 = (f32[9,4096]{1,0:T(8,128)S(1)}, f32[9,4096]{1,0:T(8,128)S(1)}, bf16[128,4096]{1,0:T(8,128)(2,1)S(1)}) custom-call(f32[64,4000]{1,0:T(8,128)S(1)} %get-tuple-element.22.curves_ref, f32[1,4000]{1,0:T(1,128)S(1)} %get-tuple-element.23.noise_ref, f32[9,4000]{1,0:T(8,128)S(1)} %get-tuple-element.24.angle_ref), custom_call_target="tpu_custom_call" | custom-call | flops 4000000 | bytes 2000000 | tf_op jit(solution)/shard_map/tables/pallas_call | solution.py:416
  11.4 0.0 collective-permute-done.2.rest_1_.rest_5_
  11.4 3.6 %collective-permute-done.3.rest_2_.rest_6_ = bf16[16,4096]{1,0:T(8,128)(2,1)S(1)} collective-permute-done((bf16[16,4096]{1,0:T(8,128)(2,1)S(1)}, bf16[16,4096]{1,0:T(8,128)(2,1)S(1)}, u32[]{:S(2)}, u32[]{:S(2)}) %collective-permute-start.3) | collective-permute-done | bytes 131104 | tf_op jit(solution)/shard_map/ppermute | solution.py:401
  15.1 0.9 %shift.1 = (bf16[216,8192]{1,0:T(8,128)(2,1)S(1)}, bf16[48,4096]{1,0:T(8,128)(2,1)S(1)}) custom-call(f32[9,4096]{1,0:T(8,128)S(1)} %get-tuple-element.27.cos_ref, f32[9,4096]{1,0:T(8,128)S(1)} %get-tuple-element.28.sin_ref, bf16[16,4096]{1,0:T(8,128)(2,1)S(1)} %get-tuple-element.29.rest_0_.rest_4_, ...), custom_call_target="tpu_custom_call" | custom-call | flops 5308416 | bytes 4000000 | tf_op jit(solution)/shard_map/shift/pallas_call | solution.py:432
  16.0 0.0 collective-permute-done.1
  16.0 0.0 collective-permute-done.4.rest_0_.rest_9_
  16.0 0.1 pad_maximum_fusion.rest_0_
  16.1 0.1 collective-permute-start.5
  16.2 0.3 %shift_last.1 = (bf16[72,8192]{1,0:T(8,128)(2,1)S(1)}, bf16[16,4096]{1,0:T(8,128)(2,1)S(1)}) custom-call(f32[9,4096]{1,0:T(8,128)S(1)} %get-tuple-element.27.cos_ref, f32[9,4096]{1,0:T(8,128)S(1)} %get-tuple-element.28.sin_ref, bf16[16,4096]{1,0:T(8,128)(2,1)S(1)} %collective-permute-done.4.rest_0_.rest_9_), custom_call_target="tpu_custom_call" | custom-call | flops 1769472 | bytes 4000000 | tf_op jit(solution)/shard_map/shift_last/pallas_call | solution.py:432
  16.5 1.0 %collective-permute-done.5.rest_1_ = bf16[8,8448]{1,0:T(8,128)(2,1)S(1)} collective-permute-done((bf16[8,8448]{1,0:T(8,128)(2,1)S(1)}, bf16[8,8448]{1,0:T(8,128)(2,1)S(1)}, u32[]{:S(2)}, u32[]{:S(2)}) %collective-permute-start.5) | collective-permute-done | bytes 135200 | tf_op jit(solution)/shard_map/ppermute | solution.py:401
  17.5 1.8 %score.1 = (f32[16,512]{1,0:T(8,128)S(1)}, f32[8,384]{1,0:T(8,128)S(1)}) custom-call(bf16[128,4096]{1,0:T(8,128)(2,1)S(1)} %get-tuple-element.25.square_ref, bf16[8,8448]{1,0:T(8,128)(2,1)S(1)} %pad_maximum_fusion.rest_0_, bf16[8,8448]{1,0:T(8,128)(2,1)S(1)} %collective-permute-done.5.rest_1_, bf16[216,8192]{1,0:T(8,128)(2,1)S(1)} %get-tuple-element.32.rest_2_, ...), custom_call_target="tpu_custom_call" | custom-call | flops 75497472 | bytes 4000000 | tf_op jit(solution)/shard_map/score/pallas_call | solution.py:459
  19.3 0.0 collective-permute-start.6
  19.3 0.1 keep.1.keep_ref
  19.5 4.4 %collective-permute-done.6.recv_ref = f32[8,384]{1,0:T(8,128)S(1)} collective-permute-done((f32[8,384]{1,0:T(8,128)S(1)}, f32[8,384]{1,0:T(8,128)S(1)}, u32[]{:S(2)}, u32[]{:S(2)}) %collective-permute-start.6) | collective-permute-done | bytes 12320 | tf_op jit(solution)/shard_map/ppermute | solution.py:401
  23.9 0.7 %place.1 = f32[9,8,64]{2,1,0:T(8,128)} custom-call(f32[9,8,64]{2,1,0:T(8,128)S(1)} %keep.1.keep_ref, f32[8,384]{1,0:T(8,128)S(1)} %collective-permute-done.6.recv_ref), custom_call_target="tpu_custom_call" | custom-call | tf_op jit(solution)/shard_map/place/pallas_call | solution.py:480
Async XLA Ops:
  1.6 7.6 %collective-permute-start = (bf16[2,8448]{1,0:T(2,128)(2,1)S(1)}, bf16[2,8448]{1,0:T(2,128)(2,1)S(1)}, u32[]{:S(2)}, u32[]{:S(2)}) collective-permute-start(bf16[2,8448]{1,0:T(2,128)(2,1)S(1)} %get-tuple-element.26), channel_id=1, source_target_pairs={{0,4},{1,5},{2,6},{3,7},{4,0},{5,1},{6,2},{7,3},{8,12},{9,13},{10,... | collective-permute-start | bytes 101384 | tf_op jit(solution)/shard_map/ppermute | solution.py:401
  5.7 5.7 %collective-permute-start.2 = (bf16[16,4096]{1,0:T(8,128)(2,1)S(1)}, bf16[16,4096]{1,0:T(8,128)(2,1)S(1)}, u32[]{:S(2)}, u32[]{:S(2)}) collective-permute-start(bf16[16,4096]{1,0:T(8,128)(2,1)S(1)} %get-tuple-element.29.rest_0_.rest_4_), channel_id=1, source_target_pairs={{0,2},{1,3},{2,0},{3,1},{4,6},{5,7},{6,4},{7,5},{8,10},{9,11},{10,... | collective-permute-start | bytes 393224 | tf_op jit(solution)/shard_map/ppermute | solution.py:401
  7.3 7.8 %collective-permute-start.3 = (bf16[16,4096]{1,0:T(8,128)(2,1)S(1)}, bf16[16,4096]{1,0:T(8,128)(2,1)S(1)}, u32[]{:S(2)}, u32[]{:S(2)}) collective-permute-start(bf16[16,4096]{1,0:T(8,128)(2,1)S(1)} %get-tuple-element.29.rest_0_.rest_4_), channel_id=1, source_target_pairs={{0,1},{1,0},{2,3},{3,2},{4,5},{5,4},{6,7},{7,6},{8,9},{9,8},{10,11... | collective-permute-start | bytes 393224 | tf_op jit(solution)/shard_map/ppermute | solution.py:401
  8.8 7.2 %collective-permute-start.4 = (bf16[16,4096]{1,0:T(8,128)(2,1)S(1)}, bf16[16,4096]{1,0:T(8,128)(2,1)S(1)}, u32[]{:S(2)}, u32[]{:S(2)}) collective-permute-start(bf16[16,4096]{1,0:T(8,128)(2,1)S(1)} %get-tuple-element.29.rest_0_.rest_4_), channel_id=1, source_target_pairs={{0,3},{1,2},{2,1},{3,0},{4,7},{5,6},{6,5},{7,4},{8,11},{9,10},{10,... | collective-permute-start | bytes 393224 | tf_op jit(solution)/shard_map/ppermute | solution.py:401
  9.3 6.7 %collective-permute-start.1 = (bf16[4,8448]{1,0:T(4,128)(2,1)S(1)}, bf16[4,8448]{1,0:T(4,128)(2,1)S(1)}, u32[]{:S(2)}, u32[]{:S(2)}) collective-permute-start(bf16[4,8448]{1,0:T(4,128)(2,1)S(1)} %pad_maximum_fusion.1), channel_id=1, source_target_pairs={{0,16},{8,24},{16,0},{24,8},{1,17},{9,25},{17,1},{25,9},{2,18},{10... | collective-permute-start | bytes 202760 | tf_op jit(solution)/shard_map/ppermute | solution.py:401
  16.1 1.4 %collective-permute-start.5 = (bf16[8,8448]{1,0:T(8,128)(2,1)S(1)}, bf16[8,8448]{1,0:T(8,128)(2,1)S(1)}, u32[]{:S(2)}, u32[]{:S(2)}) collective-permute-start(bf16[8,8448]{1,0:T(8,128)(2,1)S(1)} %pad_maximum_fusion.rest_0_), channel_id=1, source_target_pairs={{0,8},{8,0},{16,24},{24,16},{1,9},{9,1},{17,25},{25,17},{2,10},{10... | collective-permute-start | bytes 405512 | tf_op jit(solution)/shard_map/ppermute | solution.py:401
  19.3 4.6 %collective-permute-start.6 = (f32[8,384]{1,0:T(8,128)S(1)}, f32[8,384]{1,0:T(8,128)S(1)}, u32[]{:S(2)}, u32[]{:S(2)}) collective-permute-start(f32[8,384]{1,0:T(8,128)S(1)} %get-tuple-element.38), channel_id=1, source_target_pairs={{0,4},{1,5},{2,6},{3,7},{4,0},{5,1},{6,2},{7,3},{8,12},{9,13},{10,... | collective-permute-start | bytes 36872 | tf_op jit(solution)/shard_map/ppermute | solution.py:401

commit v24 on v21

--- a/solution.py
+++ b/solution.py
@@ -182,8 +182,8 @@
     )
 
 
-def spans_of(wide):
-    step = 256 if wide % 256 == 0 else 128
+def spans_of(wide, step=256):
+    step = step if wide % step == 0 else 128
     return [slice(at, at + step) for at in range(0, wide, step)]
 
 
@@ -269,7 +269,7 @@
     parts, (late_ref, give_ref) = rest[:n_parts], rest[n_parts:]
     shifts, wide = cos_ref.shape
     cross, norm = None, None
-    for span in spans_of(wide):
+    for span in spans_of(wide, 512):
         terms, powers = [], []
         for real, imag in bank_pieces(last_ref, span, n_proj):
             real_rows, imag_rows = shifted_rows(real, imag, cos_ref, sin_ref, span)

time: 23.7 us -> 23.7 us (level)
  no operation moved by 1% of the time
where the time goes in v24:
time: 23.7 us; the launch traced here: 23.6 us
  starting transfers between devices  11 us (46%)
  Pallas kernels  6.19 us (26%)
  waiting for transfers between devices  6.15 us (26%)
    ppermute x7, starting transfers between devices, swap(): return lax.ppermute(value, axis, [(i, i ^ bit) for i in range(size)])  11 us
    ppermute x7, waiting for transfers between devices, swap(): return lax.ppermute(value, axis, [(i, i ^ bit) for i in range(size)])  6.15 us
    pallas_call x1, Pallas kernels, per_device(): pl.pallas_call(pack_kernel, out_shape=[vmem_out((2 * n_proj, wide), BF16)...  1.59 us
    pallas_call x1, Pallas kernels, per_device(): pl.pallas_call(functools.partial(early_kernel, len(parts), (1, 2), n_proj...  1.38 us
    pallas_call x2, Pallas kernels, shifted_call(): pl.pallas_call(functools.partial(shift_kernel, n_proj), out_shape=[vmem_o...  0.94 us
    pallas_call x1, Pallas kernels, per_device(): pl.pallas_call(functools.partial(final_kernel, order, len(parts), bits, n...  0.83 us
    pallas_call x1, Pallas kernels, per_device(): pl.pallas_call(functools.partial(place_kernel, half, n_proj), out_shape=s...  0.73 us
    pallas_call x1, Pallas kernels, per_device(): pl.pallas_call(table_kernel, out_shape=[vmem_out((shifts, wide), F32), vm...  0.59 us
  transfers between devices with their start and end apart: 7, of which 5 were waited for; matrix products, arithmetic and copies ran while one was open for 1% of the time, Pallas kernels for 13%

profile of v24, /device:TPU:0, one launch (start us, length us, event | category | flops | bytes accessed | tf_op | source)
XLA Modules:
  0.0 23.6 jit_solution(17749434185121184012)
XLA Ops:
  0.0 1.6 %pack.1 = (bf16[16,4096]{1,0:T(8,128)(2,1)S(1)}, bf16[2,8448]{1,0:T(2,128)(2,1)S(1)}, f32[64,4000]{1,0:T(8,128)S(1)}, f32[1,4000]{1,0:T(1,128)S(1)}, f32[9,4000]{1,0:T(8,128)S(1)}) custom-call(s32[2]{0:T(128)} %class_hbm.1, s32[8]{0:T(128)} %subset_hbm.1, bf16[2,2,4000]{2,1,0:T(2,128)(2,1)} %particles_hbm.1, bf16[2,192]{1,0:T(2,128)(2,1)} %prior_hbm.1, ...), custom_call_target="tpu_custom_call" | custom-call | tf_op jit(solution)/shard_map/pack/pallas_call | solution.py:398
  1.6 4.1 %collective-permute-start = (bf16[2,8448]{1,0:T(2,128)(2,1)S(1)}, bf16[2,8448]{1,0:T(2,128)(2,1)S(1)}, u32[]{:S(2)}, u32[]{:S(2)}) collective-permute-start(bf16[2,8448]{1,0:T(2,128)(2,1)S(1)} %get-tuple-element.29), channel_id=1, source_target_pairs={{0,4},{1,5},{2,6},{3,7},{4,0},{5,1},{6,2},{7,3},{8,12},{9,13},{10,... | collective-permute-start | bytes 101384 | tf_op jit(solution)/shard_map/ppermute | solution.py:425
  5.7 1.6 %collective-permute-start.3 = (bf16[16,4096]{1,0:T(8,128)(2,1)S(1)}, bf16[16,4096]{1,0:T(8,128)(2,1)S(1)}, u32[]{:S(2)}, u32[]{:S(2)}) collective-permute-start(bf16[16,4096]{1,0:T(8,128)(2,1)S(1)} %get-tuple-element.32.rest_0_.rest_4_), channel_id=1, source_target_pairs={{0,2},{1,3},{2,0},{3,1},{4,6},{5,7},{6,4},{7,5},{8,10},{9,11},{10,... | collective-permute-start | bytes 393224 | tf_op jit(solution)/shard_map/ppermute | solution.py:425
  7.3 1.5 %collective-permute-start.4 = (bf16[16,4096]{1,0:T(8,128)(2,1)S(1)}, bf16[16,4096]{1,0:T(8,128)(2,1)S(1)}, u32[]{:S(2)}, u32[]{:S(2)}) collective-permute-start(bf16[16,4096]{1,0:T(8,128)(2,1)S(1)} %get-tuple-element.32.rest_0_.rest_4_), channel_id=1, source_target_pairs={{0,1},{1,0},{2,3},{3,2},{4,5},{5,4},{6,7},{7,6},{8,9},{9,8},{10,11... | collective-permute-start | bytes 393224 | tf_op jit(solution)/shard_map/ppermute | solution.py:425
  8.8 0.6 %tables.1 = (f32[9,4096]{1,0:T(8,128)S(1)}, f32[9,4096]{1,0:T(8,128)S(1)}, bf16[128,4096]{1,0:T(8,128)(2,1)S(1)}) custom-call(f32[64,4000]{1,0:T(8,128)S(1)} %get-tuple-element.25.curves_ref, f32[1,4000]{1,0:T(1,128)S(1)} %get-tuple-element.26.noise_ref, f32[9,4000]{1,0:T(8,128)S(1)} %get-tuple-element.27.angle_ref), custom_call_target="tpu_custom_call" | custom-call | flops 4000000 | bytes 2000000 | tf_op jit(solution)/shard_map/tables/pallas_call | solution.py:440
  9.4 0.3 %shift_own.1 = (bf16[72,8192]{1,0:T(8,128)(2,1)S(1)}, bf16[16,4096]{1,0:T(8,128)(2,1)S(1)}) custom-call(f32[9,4096]{1,0:T(8,128)S(1)} %get-tuple-element.30.cos_ref, f32[9,4096]{1,0:T(8,128)S(1)} %get-tuple-element.31.sin_ref, bf16[16,4096]{1,0:T(8,128)(2,1)S(1)} %get-tuple-element.32.rest_0_.rest_4_), custom_call_target="tpu_custom_call" | custom-call | flops 1769472 | bytes 4000000 | tf_op jit(solution)/shard_map/shift_own/pallas_call | solution.py:456
  9.7 0.0 collective-permute-done
  9.7 0.1 pad_maximum_fusion.1
  9.8 1.6 %collective-permute-start.1 = (bf16[4,8448]{1,0:T(4,128)(2,1)S(1)}, bf16[4,8448]{1,0:T(4,128)(2,1)S(1)}, u32[]{:S(2)}, u32[]{:S(2)}) collective-permute-start(bf16[4,8448]{1,0:T(4,128)(2,1)S(1)} %pad_maximum_fusion.1), channel_id=1, source_target_pairs={{0,16},{8,24},{16,0},{24,8},{1,17},{9,25},{17,1},{25,9},{2,18},{10... | collective-permute-start | bytes 202760 | tf_op jit(solution)/shard_map/ppermute | solution.py:425
  11.4 0.0 collective-permute-done.3.rest_1_.rest_8_
  11.4 0.9 %collective-permute-done.4.rest_0_.rest_7_ = bf16[16,4096]{1,0:T(8,128)(2,1)S(1)} collective-permute-done((bf16[16,4096]{1,0:T(8,128)(2,1)S(1)}, bf16[16,4096]{1,0:T(8,128)(2,1)S(1)}, u32[]{:S(2)}, u32[]{:S(2)}) %collective-permute-start.4) | collective-permute-done | bytes 131104 | tf_op jit(solution)/shard_map/ppermute | solution.py:425
  12.3 1.6 %collective-permute-start.5 = (bf16[16,4480]{1,0:T(8,128)(2,1)S(1)}, bf16[16,4480]{1,0:T(8,128)(2,1)S(1)}, u32[]{:S(2)}, u32[]{:S(2)}) collective-permute-start(bf16[16,4480]{1,0:T(8,128)(2,1)S(1)} %pad.4), channel_id=1, source_target_pairs={{0,1},{1,0},{2,3},{3,2},{4,5},{5,4},{6,7},{7,6},{8,9},{9,8},{10,11... | collective-permute-start | bytes 430088 | tf_op jit(solution)/shard_map/ppermute | solution.py:425
  13.8 0.3 %collective-permute-done.1 = bf16[4,8448]{1,0:T(4,128)(2,1)S(1)} collective-permute-done((bf16[4,8448]{1,0:T(4,128)(2,1)S(1)}, bf16[4,8448]{1,0:T(4,128)(2,1)S(1)}, u32[]{:S(2)}, u32[]{:S(2)}) %collective-permute-start.1) | collective-permute-done | bytes 67616 | tf_op jit(solution)/shard_map/ppermute | solution.py:425
  14.2 0.1 pad_maximum_fusion.rest_0_
  14.2 0.1 collective-permute-start.2
  14.3 0.6 %shift_rest.1 = (bf16[144,8192]{1,0:T(8,128)(2,1)S(1)}, bf16[32,4096]{1,0:T(8,128)(2,1)S(1)}) custom-call(f32[9,4096]{1,0:T(8,128)S(1)} %get-tuple-element.30.cos_ref, f32[9,4096]{1,0:T(8,128)S(1)} %get-tuple-element.31.sin_ref, bf16[16,4096]{1,0:T(8,128)(2,1)S(1)} %collective-permute-done.4.rest_0_.rest_7_, ...), custom_call_target="tpu_custom_call" | custom-call | flops 3538944 | bytes 4000000 | tf_op jit(solution)/shard_map/shift_rest/pallas_call | solution.py:456
  14.9 0.7 %collective-permute-done.2.rest_1_ = bf16[8,8448]{1,0:T(8,128)(2,1)S(1)} collective-permute-done((bf16[8,8448]{1,0:T(8,128)(2,1)S(1)}, bf16[8,8448]{1,0:T(8,128)(2,1)S(1)}, u32[]{:S(2)}, u32[]{:S(2)}) %collective-permute-start.2) | collective-permute-done | bytes 135200 | tf_op jit(solution)/shard_map/ppermute | solution.py:425
  15.7 1.4 %early.1 = (bf16[32,4096]{1,0:T(8,128)(2,1)S(1)}, f32[16,384]{1,0:T(8,128)S(1)}) custom-call(bf16[128,4096]{1,0:T(8,128)(2,1)S(1)} %get-tuple-element.28.square_ref, bf16[8,8448]{1,0:T(8,128)(2,1)S(1)} %pad_maximum_fusion.rest_0_, bf16[8,8448]{1,0:T(8,128)(2,1)S(1)} %collective-permute-done.2.rest_1_, bf16[72,8192]{1,0:T(8,128)(2,1)S(1)} %get-tuple-element.35.rest_2_, ...), custom_call_target="tpu_custom_call" | custom-call | flops 56623104 | bytes 4000000 | tf_op jit(solution)/shard_map/early/pallas_call | solution.py:482
  17.0 0.4 %collective-permute-done.5.last_ref = bf16[16,4480]{1,0:T(8,128)(2,1)S(1)} collective-permute-done((bf16[16,4480]{1,0:T(8,128)(2,1)S(1)}, bf16[16,4480]{1,0:T(8,128)(2,1)S(1)}, u32[]{:S(2)}, u32[]{:S(2)}) %collective-permute-start.5) | collective-permute-done | bytes 143392 | tf_op jit(solution)/shard_map/ppermute | solution.py:425
  17.4 0.8 %final.1 = (f32[16,128]{1,0:T(8,128)S(1)}, f32[8,384]{1,0:T(8,128)S(1)}) custom-call(bf16[32,4096]{1,0:T(8,128)(2,1)S(1)} %get-tuple-element.42.select_ref, f32[16,384]{1,0:T(8,128)S(1)} %get-tuple-element.41.rows_ref, f32[9,4096]{1,0:T(8,128)S(1)} %get-tuple-element.30.cos_ref, f32[9,4096]{1,0:T(8,128)S(1)} %get-tuple-element.31.sin_ref, ...), custom_call_target="tpu_custom_call" | custom-call | flops 18874368 | bytes 4000000 | tf_op jit(solution)/shard_map/final/pallas_call | solution.py:498
  18.3 0.6 %collective-permute-start.6 = (f32[8,384]{1,0:T(8,128)S(1)}, f32[8,384]{1,0:T(8,128)S(1)}, u32[]{:S(2)}, u32[]{:S(2)}) collective-permute-start(f32[8,384]{1,0:T(8,128)S(1)} %get-tuple-element.44), channel_id=1, source_target_pairs={{0,4},{1,5},{2,6},{3,7},{4,0},{5,1},{6,2},{7,3},{8,12},{9,13},{10,... | collective-permute-start | bytes 36872 | tf_op jit(solution)/shard_map/ppermute | solution.py:425
  18.9 0.1 keep.1.keep_ref
  19.0 3.9 %collective-permute-done.6.recv_ref = f32[8,384]{1,0:T(8,128)S(1)} collective-permute-done((f32[8,384]{1,0:T(8,128)S(1)}, f32[8,384]{1,0:T(8,128)S(1)}, u32[]{:S(2)}, u32[]{:S(2)}) %collective-permute-start.6) | collective-permute-done | bytes 12320 | tf_op jit(solution)/shard_map/ppermute | solution.py:425
  22.9 0.7 %place.1 = f32[9,8,64]{2,1,0:T(8,128)} custom-call(f32[9,8,64]{2,1,0:T(8,128)S(1)} %keep.1.keep_ref, f32[8,384]{1,0:T(8,128)S(1)} %collective-permute-done.6.recv_ref), custom_call_target="tpu_custom_call" | custom-call | tf_op jit(solution)/shard_map/place/pallas_call | solution.py:518
  (1 shorter events, 0.0 us)
Async XLA Ops:
  1.6 8.1 %collective-permute-start = (bf16[2,8448]{1,0:T(2,128)(2,1)S(1)}, bf16[2,8448]{1,0:T(2,128)(2,1)S(1)}, u32[]{:S(2)}, u32[]{:S(2)}) collective-permute-start(bf16[2,8448]{1,0:T(2,128)(2,1)S(1)} %get-tuple-element.29), channel_id=1, source_target_pairs={{0,4},{1,5},{2,6},{3,7},{4,0},{5,1},{6,2},{7,3},{8,12},{9,13},{10,... | collective-permute-start | bytes 101384 | tf_op jit(solution)/shard_map/ppermute | solution.py:425
  5.7 5.7 %collective-permute-start.3 = (bf16[16,4096]{1,0:T(8,128)(2,1)S(1)}, bf16[16,4096]{1,0:T(8,128)(2,1)S(1)}, u32[]{:S(2)}, u32[]{:S(2)}) collective-permute-start(bf16[16,4096]{1,0:T(8,128)(2,1)S(1)} %get-tuple-element.32.rest_0_.rest_4_), channel_id=1, source_target_pairs={{0,2},{1,3},{2,0},{3,1},{4,6},{5,7},{6,4},{7,5},{8,10},{9,11},{10,... | collective-permute-start | bytes 393224 | tf_op jit(solution)/shard_map/ppermute | solution.py:425
  7.3 5.0 %collective-permute-start.4 = (bf16[16,4096]{1,0:T(8,128)(2,1)S(1)}, bf16[16,4096]{1,0:T(8,128)(2,1)S(1)}, u32[]{:S(2)}, u32[]{:S(2)}) collective-permute-start(bf16[16,4096]{1,0:T(8,128)(2,1)S(1)} %get-tuple-element.32.rest_0_.rest_4_), channel_id=1, source_target_pairs={{0,1},{1,0},{2,3},{3,2},{4,5},{5,4},{6,7},{7,6},{8,9},{9,8},{10,11... | collective-permute-start | bytes 393224 | tf_op jit(solution)/shard_map/ppermute | solution.py:425
  9.8 4.4 %collective-permute-start.1 = (bf16[4,8448]{1,0:T(4,128)(2,1)S(1)}, bf16[4,8448]{1,0:T(4,128)(2,1)S(1)}, u32[]{:S(2)}, u32[]{:S(2)}) collective-permute-start(bf16[4,8448]{1,0:T(4,128)(2,1)S(1)} %pad_maximum_fusion.1), channel_id=1, source_target_pairs={{0,16},{8,24},{16,0},{24,8},{1,17},{9,25},{17,1},{25,9},{2,18},{10... | collective-permute-start | bytes 202760 | tf_op jit(solution)/shard_map/ppermute | solution.py:425
  12.3 5.2 %collective-permute-start.5 = (bf16[16,4480]{1,0:T(8,128)(2,1)S(1)}, bf16[16,4480]{1,0:T(8,128)(2,1)S(1)}, u32[]{:S(2)}, u32[]{:S(2)}) collective-permute-start(bf16[16,4480]{1,0:T(8,128)(2,1)S(1)} %pad.4), channel_id=1, source_target_pairs={{0,1},{1,0},{2,3},{3,2},{4,5},{5,4},{6,7},{7,6},{8,9},{9,8},{10,11... | collective-permute-start | bytes 430088 | tf_op jit(solution)/shard_map/ppermute | solution.py:425
  14.2 1.4 %collective-permute-start.2 = (bf16[8,8448]{1,0:T(8,128)(2,1)S(1)}, bf16[8,8448]{1,0:T(8,128)(2,1)S(1)}, u32[]{:S(2)}, u32[]{:S(2)}) collective-permute-start(bf16[8,8448]{1,0:T(8,128)(2,1)S(1)} %pad_maximum_fusion.rest_0_), channel_id=1, source_target_pairs={{0,8},{8,0},{16,24},{24,16},{1,9},{9,1},{17,25},{25,17},{2,10},{10... | collective-permute-start | bytes 405512 | tf_op jit(solution)/shard_map/ppermute | solution.py:425
  18.3 4.6 %collective-permute-start.6 = (f32[8,384]{1,0:T(8,128)S(1)}, f32[8,384]{1,0:T(8,128)S(1)}, u32[]{:S(2)}, u32[]{:S(2)}) collective-permute-start(f32[8,384]{1,0:T(8,128)S(1)} %get-tuple-element.44), channel_id=1, source_target_pairs={{0,4},{1,5},{2,6},{3,7},{4,0},{5,1},{6,2},{7,3},{8,12},{9,13},{10,... | collective-permute-start | bytes 36872 | tf_op jit(solution)/shard_map/ppermute | solution.py:425

commit v25 on v21

--- a/solution.py
+++ b/solution.py
@@ -66,6 +66,8 @@
     wide = bank_ref.shape[1]
 
     def padded(values, width):
+        if values.shape[1] == width:
+            return values
         zeros = jnp.zeros((values.shape[0], width - values.shape[1]), values.dtype)
         return jnp.concatenate([values, zeros], axis=1)
 
@@ -79,12 +81,13 @@
         both = padded(proj_ref[j].astype(F32), wide)
         real = jnp.where(row == j, both[0:1], real)
         imag = jnp.where(row == j, both[1:2], imag)
-    last = slice(wide - 128, wide)
+    start = length // 128 * 128
+    last = slice(start, start + 128)
     ends = real[:, last]
     for j in range(n_proj):
         here = (row[:, last] == j) & (lane[:, last] == length)
         ends = jnp.where(here, subset_ref[j].astype(F32), ends)
-    real = jnp.concatenate([real[:, : wide - 128], ends], axis=1)
+    real = jnp.concatenate([real[:, :start], ends, real[:, start + 128 :]][: 3 if start + 128 < wide else 2], axis=1)
     bank_ref[...] = jnp.concatenate([real, imag], axis=0).astype(BF16)
 
     copies[1].wait()
@@ -94,17 +97,19 @@
     extra = part_ref.shape[1] - 2 * wide
     row = lax.broadcasted_iota(jnp.int32, (n_part, wide), 0)
     row_extra = lax.broadcasted_iota(jnp.int32, (n_part, extra), 0)
-    lane_extra = lax.broadcasted_iota(jnp.int32, (n_part, extra), 1)
     real = jnp.zeros((n_part, wide), F32)
     imag = jnp.zeros((n_part, wide), F32)
-    small = padded(prior_ref[...].astype(F32), extra)
+    small = jnp.zeros((n_part, extra), F32)
+    prior = prior_ref[...].astype(F32)
+    middle = (subsets + 1) // 2
     for i in range(n_part):
         curve = curves_ref[pl.ds(class_ref[i], 1), :] * noise_ref[...]
-        both = padded(particles_ref[i].astype(F32) * curve, wide)
-        real = jnp.where(row == i, both[0:1], real)
-        imag = jnp.where(row == i, both[1:2], imag)
-        place = (row_extra == i) & (lane_extra == subsets)
-        small = jnp.where(place, class_ref[i].astype(F32), small)
+        both = particles_ref[i].astype(F32) * curve
+        first = padded(jnp.concatenate([both[0:1], prior[i : i + 1, :middle]], axis=1), wide)
+        second = padded(jnp.concatenate([both[1:2], prior[i : i + 1, middle:]], axis=1), wide)
+        real = jnp.where(row == i, first, real)
+        imag = jnp.where(row == i, second, imag)
+        small = jnp.where(row_extra == i, class_ref[i].astype(F32), small)
     part_ref[:, :wide] = real.astype(BF16)
     part_ref[:, wide : 2 * wide] = imag.astype(BF16)
     part_ref[:, 2 * wide :] = small.astype(BF16)
@@ -233,6 +238,14 @@
     return jnp.concatenate([part[:, span] for part in parts], axis=0)
 
 
+def extra_of(parts, wide, length, subsets):
+    start, middle = length // 128 * 128, (subsets + 1) // 2
+    at = length - start
+    first = rows_of(parts, slice(start, wide)).astype(F32)[:, at : at + middle]
+    second = rows_of(parts, slice(wide + start, 2 * wide)).astype(F32)[:, at : at + subsets - middle]
+    return jnp.concatenate([first, second, rows_of(parts, slice(2 * wide, None)).astype(F32)], axis=1)
+
+
 def early_kernel(n_parts, n_banks, n_proj, length, subsets, square_ref, *rest):
     parts, rest = rest[:n_parts], rest[n_parts:]
     groups, (select_ref, rows_ref) = [], rest[-2:]
@@ -241,7 +254,7 @@
         rest = rest[2 + n :]
     wide = select_ref.shape[1]
     classes_count = square_ref.shape[0] // 2
-    extra = rows_of(parts, slice(2 * wide, None)).astype(F32)
+    extra = extra_of(parts, wide, length, subsets)
     count = extra.shape[0]
     class_col = lax.broadcasted_iota(jnp.int32, (count, classes_count), 1).astype(F32)
     onehot = (class_col == extra[:, subsets : subsets + 1]).astype(F32).astype(BF16)
@@ -281,7 +294,7 @@
         cross = added(cross, jnp.concatenate(terms, axis=1))
         power = split_terms(jnp.concatenate(powers, axis=0))
         norm = added(norm, multiply(select_ref[:, span], power))
-    extra = rows_of(parts, slice(2 * wide, None)).astype(F32)
+    extra = extra_of(parts, wide, length, subsets)
     pieces = pieces_of(cross, norm, extra, [last_ref], length, subsets, n_proj)
     slot = late_ref.shape[1] // len(pieces)
     zeros = jnp.zeros((extra.shape[0], slot - pieces[0].shape[1]), F32)
@@ -376,8 +389,8 @@
     shifts = shift_phase.shape[0]
     classes_count = ctf_curves.shape[0]
     subsets = orient_prior.shape[1]
-    wide = 128 * (length // 128 + 1)
-    extra = 128 * (subsets // 128 + 1)
+    wide = 128 * -(-(length + (subsets + 1) // 2) // 128)
+    extra = 128
     noise = noise_weight.reshape(1, length)
     shape = jax.ShapeDtypeStruct
 
@@ -434,7 +447,7 @@
         planes.append(swap(joined(planes), "blk", 1 << n))
         order += [offset ^ (1 << n) for offset in order]
     far, near = lax.optimization_barrier((joined(planes[1:]), near))
-    last = swap(jnp.pad(far, ((0, 0), (0, 3 * 128))), "blk", 1)
+    last = swap(jnp.pad(far, ((0, 0), (0, 2 * 128))), "blk", 1)
     order = [0, 1] + order[1:] + [offset ^ 1 for offset in order[1:]]
 
     cos_part, sin_part, square = pl.pallas_call(

time: 23.7 us -> 23.7 us (level)
  no operation moved by 1% of the time
where the time goes in v25:
time: 23.7 us; the launch traced here: 23.6 us
  starting transfers between devices  11.2 us (47%)
  Pallas kernels  6.22 us (26%)
  waiting for transfers between devices  5.96 us (25%)
    ppermute x7, starting transfers between devices, swap(): return lax.ppermute(value, axis, [(i, i ^ bit) for i in range(size)])  11.2 us
    ppermute x7, waiting for transfers between devices, swap(): return lax.ppermute(value, axis, [(i, i ^ bit) for i in range(size)])  5.96 us
    pallas_call x1, Pallas kernels, per_device(): pl.pallas_call(pack_kernel, out_shape=[vmem_out((2 * n_proj, wide), BF16)...  1.61 us
    pallas_call x1, Pallas kernels, per_device(): pl.pallas_call(functools.partial(early_kernel, len(parts), (1, 2), n_proj...  1.44 us
    pallas_call x2, Pallas kernels, shifted_call(): pl.pallas_call(functools.partial(shift_kernel, n_proj), out_shape=[vmem_o...  0.94 us
    pallas_call x1, Pallas kernels, per_device(): pl.pallas_call(functools.partial(final_kernel, order, len(parts), bits, n...  0.78 us
    pallas_call x1, Pallas kernels, per_device(): pl.pallas_call(functools.partial(place_kernel, half, n_proj), out_shape=s...  0.73 us
    pallas_call x1, Pallas kernels, per_device(): pl.pallas_call(table_kernel, out_shape=[vmem_out((shifts, wide), F32), vm...  0.58 us
  transfers between devices with their start and end apart: 7, of which 5 were waited for; matrix products, arithmetic and copies ran while one was open for 1% of the time, Pallas kernels for 13%

profile of v25, /device:TPU:0, one launch (start us, length us, event | category | flops | bytes accessed | tf_op | source)
XLA Modules:
  0.0 23.6 jit_solution(7458462844909558098)
XLA Ops:
  0.0 1.6 %pack.1 = (bf16[16,4096]{1,0:T(8,128)(2,1)S(1)}, bf16[2,8320]{1,0:T(2,128)(2,1)S(1)}, f32[64,4000]{1,0:T(8,128)S(1)}, f32[1,4000]{1,0:T(1,128)S(1)}, f32[9,4000]{1,0:T(8,128)S(1)}) custom-call(s32[2]{0:T(128)} %class_hbm.1, s32[8]{0:T(128)} %subset_hbm.1, bf16[2,2,4000]{2,1,0:T(2,128)(2,1)} %particles_hbm.1, bf16[2,192]{1,0:T(2,128)(2,1)} %prior_hbm.1, ...), custom_call_target="tpu_custom_call" | custom-call | tf_op jit(solution)/shard_map/pack/pallas_call | solution.py:411
  1.6 4.1 %collective-permute-start = (bf16[2,8320]{1,0:T(2,128)(2,1)S(1)}, bf16[2,8320]{1,0:T(2,128)(2,1)S(1)}, u32[]{:S(2)}, u32[]{:S(2)}) collective-permute-start(bf16[2,8320]{1,0:T(2,128)(2,1)S(1)} %get-tuple-element.29), channel_id=1, source_target_pairs={{0,4},{1,5},{2,6},{3,7},{4,0},{5,1},{6,2},{7,3},{8,12},{9,13},{10,... | collective-permute-start | bytes 99848 | tf_op jit(solution)/shard_map/ppermute | solution.py:438
  5.7 1.6 %collective-permute-start.3 = (bf16[16,4096]{1,0:T(8,128)(2,1)S(1)}, bf16[16,4096]{1,0:T(8,128)(2,1)S(1)}, u32[]{:S(2)}, u32[]{:S(2)}) collective-permute-start(bf16[16,4096]{1,0:T(8,128)(2,1)S(1)} %get-tuple-element.32.rest_0_.rest_4_), channel_id=1, source_target_pairs={{0,2},{1,3},{2,0},{3,1},{4,6},{5,7},{6,4},{7,5},{8,10},{9,11},{10,... | collective-permute-start | bytes 393224 | tf_op jit(solution)/shard_map/ppermute | solution.py:438
  7.3 1.5 %collective-permute-start.4 = (bf16[16,4096]{1,0:T(8,128)(2,1)S(1)}, bf16[16,4096]{1,0:T(8,128)(2,1)S(1)}, u32[]{:S(2)}, u32[]{:S(2)}) collective-permute-start(bf16[16,4096]{1,0:T(8,128)(2,1)S(1)} %get-tuple-element.32.rest_0_.rest_4_), channel_id=1, source_target_pairs={{0,1},{1,0},{2,3},{3,2},{4,5},{5,4},{6,7},{7,6},{8,9},{9,8},{10,11... | collective-permute-start | bytes 393224 | tf_op jit(solution)/shard_map/ppermute | solution.py:438
  8.8 0.6 %tables.1 = (f32[9,4096]{1,0:T(8,128)S(1)}, f32[9,4096]{1,0:T(8,128)S(1)}, bf16[128,4096]{1,0:T(8,128)(2,1)S(1)}) custom-call(f32[64,4000]{1,0:T(8,128)S(1)} %get-tuple-element.25.curves_ref, f32[1,4000]{1,0:T(1,128)S(1)} %get-tuple-element.26.noise_ref, f32[9,4000]{1,0:T(8,128)S(1)} %get-tuple-element.27.angle_ref), custom_call_target="tpu_custom_call" | custom-call | flops 4000000 | bytes 2000000 | tf_op jit(solution)/shard_map/tables/pallas_call | solution.py:453
  9.4 0.3 %shift_own.1 = (bf16[72,8192]{1,0:T(8,128)(2,1)S(1)}, bf16[16,4096]{1,0:T(8,128)(2,1)S(1)}) custom-call(f32[9,4096]{1,0:T(8,128)S(1)} %get-tuple-element.30.cos_ref, f32[9,4096]{1,0:T(8,128)S(1)} %get-tuple-element.31.sin_ref, bf16[16,4096]{1,0:T(8,128)(2,1)S(1)} %get-tuple-element.32.rest_0_.rest_4_), custom_call_target="tpu_custom_call" | custom-call | flops 1769472 | bytes 4000000 | tf_op jit(solution)/shard_map/shift_own/pallas_call | solution.py:469
  9.7 0.0 collective-permute-done
  9.7 0.1 pad_maximum_fusion.1
  9.8 1.6 %collective-permute-start.1 = (bf16[4,8320]{1,0:T(4,128)(2,1)S(1)}, bf16[4,8320]{1,0:T(4,128)(2,1)S(1)}, u32[]{:S(2)}, u32[]{:S(2)}) collective-permute-start(bf16[4,8320]{1,0:T(4,128)(2,1)S(1)} %pad_maximum_fusion.1), channel_id=1, source_target_pairs={{0,16},{8,24},{16,0},{24,8},{1,17},{9,25},{17,1},{25,9},{2,18},{10... | collective-permute-start | bytes 199688 | tf_op jit(solution)/shard_map/ppermute | solution.py:438
  11.4 0.0 collective-permute-done.3.rest_1_.rest_8_
  11.4 0.9 %collective-permute-done.4.rest_0_.rest_7_ = bf16[16,4096]{1,0:T(8,128)(2,1)S(1)} collective-permute-done((bf16[16,4096]{1,0:T(8,128)(2,1)S(1)}, bf16[16,4096]{1,0:T(8,128)(2,1)S(1)}, u32[]{:S(2)}, u32[]{:S(2)}) %collective-permute-start.4) | collective-permute-done | bytes 131104 | tf_op jit(solution)/shard_map/ppermute | solution.py:438
  12.3 1.6 %collective-permute-start.5 = (bf16[16,4352]{1,0:T(8,128)(2,1)S(1)}, bf16[16,4352]{1,0:T(8,128)(2,1)S(1)}, u32[]{:S(2)}, u32[]{:S(2)}) collective-permute-start(bf16[16,4352]{1,0:T(8,128)(2,1)S(1)} %pad.4), channel_id=1, source_target_pairs={{0,1},{1,0},{2,3},{3,2},{4,5},{5,4},{6,7},{7,6},{8,9},{9,8},{10,11... | collective-permute-start | bytes 417800 | tf_op jit(solution)/shard_map/ppermute | solution.py:438
  13.9 0.3 %collective-permute-done.1 = bf16[4,8320]{1,0:T(4,128)(2,1)S(1)} collective-permute-done((bf16[4,8320]{1,0:T(4,128)(2,1)S(1)}, bf16[4,8320]{1,0:T(4,128)(2,1)S(1)}, u32[]{:S(2)}, u32[]{:S(2)}) %collective-permute-start.1) | collective-permute-done | bytes 66592 | tf_op jit(solution)/shard_map/ppermute | solution.py:438
  14.2 0.1 pad_maximum_fusion.rest_0_
  14.2 0.1 collective-permute-start.2
  14.3 0.6 %shift_rest.1 = (bf16[144,8192]{1,0:T(8,128)(2,1)S(1)}, bf16[32,4096]{1,0:T(8,128)(2,1)S(1)}) custom-call(f32[9,4096]{1,0:T(8,128)S(1)} %get-tuple-element.30.cos_ref, f32[9,4096]{1,0:T(8,128)S(1)} %get-tuple-element.31.sin_ref, bf16[16,4096]{1,0:T(8,128)(2,1)S(1)} %collective-permute-done.4.rest_0_.rest_7_, ...), custom_call_target="tpu_custom_call" | custom-call | flops 3538944 | bytes 4000000 | tf_op jit(solution)/shard_map/shift_rest/pallas_call | solution.py:469
  14.9 0.7 %collective-permute-done.2.rest_1_ = bf16[8,8320]{1,0:T(8,128)(2,1)S(1)} collective-permute-done((bf16[8,8320]{1,0:T(8,128)(2,1)S(1)}, bf16[8,8320]{1,0:T(8,128)(2,1)S(1)}, u32[]{:S(2)}, u32[]{:S(2)}) %collective-permute-start.2) | collective-permute-done | bytes 133152 | tf_op jit(solution)/shard_map/ppermute | solution.py:438
  15.7 1.4 %early.1 = (bf16[32,4096]{1,0:T(8,128)(2,1)S(1)}, f32[16,384]{1,0:T(8,128)S(1)}) custom-call(bf16[128,4096]{1,0:T(8,128)(2,1)S(1)} %get-tuple-element.28.square_ref, bf16[8,8320]{1,0:T(8,128)(2,1)S(1)} %pad_maximum_fusion.rest_0_, bf16[8,8320]{1,0:T(8,128)(2,1)S(1)} %collective-permute-done.2.rest_1_, bf16[72,8192]{1,0:T(8,128)(2,1)S(1)} %get-tuple-element.35.rest_2_, ...), custom_call_target="tpu_custom_call" | custom-call | flops 56623104 | bytes 4000000 | tf_op jit(solution)/shard_map/early/pallas_call | solution.py:495
  17.1 0.3 %collective-permute-done.5.last_ref = bf16[16,4352]{1,0:T(8,128)(2,1)S(1)} collective-permute-done((bf16[16,4352]{1,0:T(8,128)(2,1)S(1)}, bf16[16,4352]{1,0:T(8,128)(2,1)S(1)}, u32[]{:S(2)}, u32[]{:S(2)}) %collective-permute-start.5) | collective-permute-done | bytes 139296 | tf_op jit(solution)/shard_map/ppermute | solution.py:438
  17.4 0.8 %final.1 = (f32[16,128]{1,0:T(8,128)S(1)}, f32[8,384]{1,0:T(8,128)S(1)}) custom-call(bf16[32,4096]{1,0:T(8,128)(2,1)S(1)} %get-tuple-element.42.select_ref, f32[16,384]{1,0:T(8,128)S(1)} %get-tuple-element.41.rows_ref, f32[9,4096]{1,0:T(8,128)S(1)} %get-tuple-element.30.cos_ref, f32[9,4096]{1,0:T(8,128)S(1)} %get-tuple-element.31.sin_ref, ...), custom_call_target="tpu_custom_call" | custom-call | flops 18874368 | bytes 4000000 | tf_op jit(solution)/shard_map/final/pallas_call | solution.py:511
  18.2 0.7 %collective-permute-start.6 = (f32[8,384]{1,0:T(8,128)S(1)}, f32[8,384]{1,0:T(8,128)S(1)}, u32[]{:S(2)}, u32[]{:S(2)}) collective-permute-start(f32[8,384]{1,0:T(8,128)S(1)} %get-tuple-element.44), channel_id=1, source_target_pairs={{0,4},{1,5},{2,6},{3,7},{4,0},{5,1},{6,2},{7,3},{8,12},{9,13},{10,... | collective-permute-start | bytes 36872 | tf_op jit(solution)/shard_map/ppermute | solution.py:438
  18.9 0.1 keep.1.keep_ref
  19.1 3.8 %collective-permute-done.6.recv_ref = f32[8,384]{1,0:T(8,128)S(1)} collective-permute-done((f32[8,384]{1,0:T(8,128)S(1)}, f32[8,384]{1,0:T(8,128)S(1)}, u32[]{:S(2)}, u32[]{:S(2)}) %collective-permute-start.6) | collective-permute-done | bytes 12320 | tf_op jit(solution)/shard_map/ppermute | solution.py:438
  22.8 0.7 %place.1 = f32[9,8,64]{2,1,0:T(8,128)} custom-call(f32[9,8,64]{2,1,0:T(8,128)S(1)} %keep.1.keep_ref, f32[8,384]{1,0:T(8,128)S(1)} %collective-permute-done.6.recv_ref), custom_call_target="tpu_custom_call" | custom-call | tf_op jit(solution)/shard_map/place/pallas_call | solution.py:531
  (1 shorter events, 0.0 us)
Async XLA Ops:
  1.6 8.1 %collective-permute-start = (bf16[2,8320]{1,0:T(2,128)(2,1)S(1)}, bf16[2,8320]{1,0:T(2,128)(2,1)S(1)}, u32[]{:S(2)}, u32[]{:S(2)}) collective-permute-start(bf16[2,8320]{1,0:T(2,128)(2,1)S(1)} %get-tuple-element.29), channel_id=1, source_target_pairs={{0,4},{1,5},{2,6},{3,7},{4,0},{5,1},{6,2},{7,3},{8,12},{9,13},{10,... | collective-permute-start | bytes 99848 | tf_op jit(solution)/shard_map/ppermute | solution.py:438
  5.7 5.7 %collective-permute-start.3 = (bf16[16,4096]{1,0:T(8,128)(2,1)S(1)}, bf16[16,4096]{1,0:T(8,128)(2,1)S(1)}, u32[]{:S(2)}, u32[]{:S(2)}) collective-permute-start(bf16[16,4096]{1,0:T(8,128)(2,1)S(1)} %get-tuple-element.32.rest_0_.rest_4_), channel_id=1, source_target_pairs={{0,2},{1,3},{2,0},{3,1},{4,6},{5,7},{6,4},{7,5},{8,10},{9,11},{10,... | collective-permute-start | bytes 393224 | tf_op jit(solution)/shard_map/ppermute | solution.py:438
  7.3 5.0 %collective-permute-start.4 = (bf16[16,4096]{1,0:T(8,128)(2,1)S(1)}, bf16[16,4096]{1,0:T(8,128)(2,1)S(1)}, u32[]{:S(2)}, u32[]{:S(2)}) collective-permute-start(bf16[16,4096]{1,0:T(8,128)(2,1)S(1)} %get-tuple-element.32.rest_0_.rest_4_), channel_id=1, source_target_pairs={{0,1},{1,0},{2,3},{3,2},{4,5},{5,4},{6,7},{7,6},{8,9},{9,8},{10,11... | collective-permute-start | bytes 393224 | tf_op jit(solution)/shard_map/ppermute | solution.py:438
  9.8 4.3 %collective-permute-start.1 = (bf16[4,8320]{1,0:T(4,128)(2,1)S(1)}, bf16[4,8320]{1,0:T(4,128)(2,1)S(1)}, u32[]{:S(2)}, u32[]{:S(2)}) collective-permute-start(bf16[4,8320]{1,0:T(4,128)(2,1)S(1)} %pad_maximum_fusion.1), channel_id=1, source_target_pairs={{0,16},{8,24},{16,0},{24,8},{1,17},{9,25},{17,1},{25,9},{2,18},{10... | collective-permute-start | bytes 199688 | tf_op jit(solution)/shard_map/ppermute | solution.py:438
  12.3 5.1 %collective-permute-start.5 = (bf16[16,4352]{1,0:T(8,128)(2,1)S(1)}, bf16[16,4352]{1,0:T(8,128)(2,1)S(1)}, u32[]{:S(2)}, u32[]{:S(2)}) collective-permute-start(bf16[16,4352]{1,0:T(8,128)(2,1)S(1)} %pad.4), channel_id=1, source_target_pairs={{0,1},{1,0},{2,3},{3,2},{4,5},{5,4},{6,7},{7,6},{8,9},{9,8},{10,11... | collective-permute-start | bytes 417800 | tf_op jit(solution)/shard_map/ppermute | solution.py:438
  14.2 1.4 %collective-permute-start.2 = (bf16[8,8320]{1,0:T(8,128)(2,1)S(1)}, bf16[8,8320]{1,0:T(8,128)(2,1)S(1)}, u32[]{:S(2)}, u32[]{:S(2)}) collective-permute-start(bf16[8,8320]{1,0:T(8,128)(2,1)S(1)} %pad_maximum_fusion.rest_0_), channel_id=1, source_target_pairs={{0,8},{8,0},{16,24},{24,16},{1,9},{9,1},{17,25},{25,17},{2,10},{10... | collective-permute-start | bytes 399368 | tf_op jit(solution)/shard_map/ppermute | solution.py:438
  18.2 4.6 %collective-permute-start.6 = (f32[8,384]{1,0:T(8,128)S(1)}, f32[8,384]{1,0:T(8,128)S(1)}, u32[]{:S(2)}, u32[]{:S(2)}) collective-permute-start(f32[8,384]{1,0:T(8,128)S(1)} %get-tuple-element.44), channel_id=1, source_target_pairs={{0,4},{1,5},{2,6},{3,7},{4,0},{5,1},{6,2},{7,3},{8,12},{9,13},{10,... | collective-permute-start | bytes 36872 | tf_op jit(solution)/shard_map/ppermute | solution.py:438

commit v26 on v25

--- a/solution.py
+++ b/solution.py
@@ -266,8 +266,8 @@
     pieces = []
     for shifted_ref, power_ref, banks in groups:
         cross, turned = None, None
-        for at in range(0, wide, 512):
-            span = slice(at, min(at + 512, wide))
+        for at in range(0, wide, 1024):
+            span = slice(at, min(at + 1024, wide))
             other = slice(wide + span.start, wide + span.stop)
             cross = added(cross, multiply(rows_of(parts, span), shifted_ref[:, span]))
             turned = added(turned, multiply(shifted_ref[:, other], rows_of(parts, other)))

time: 23.7 us -> 23.7 us (level)
  waiting for transfers between devices: 5.96 us -> 5.4 us
  Pallas kernels: 6.22 us -> 6.52 us
    ppermute x7, waiting for transfers between devices: 5.96 us -> 5.4 us  [swap(): return lax.ppermute(value, axis, [(i, i ^ bit) for i in range(size)])]
    pallas_call x1, Pallas kernels: 1.44 us -> 1.74 us  [per_device(): pl.pallas_call(functools.partial(early_kernel, len(parts), (1, 2), n_proj...]
    ppermute x7, starting transfers between devices: 11.2 us -> 11.4 us  [swap(): return lax.ppermute(value, axis, [(i, i ^ bit) for i in range(size)])]
  transfers between devices with their start and end apart: 7 -> 7, of which waited for: 5 -> 4; matrix products, arithmetic and copies ran while one was open for 1% -> 1% of each run, Pallas kernels for 13% -> 14%
where the time goes in v26:
time: 23.7 us; the launch traced here: 23.6 us
  starting transfers between devices  11.4 us (48%)
  Pallas kernels  6.52 us (28%)
  waiting for transfers between devices  5.4 us (23%)
    ppermute x7, starting transfers between devices, swap(): return lax.ppermute(value, axis, [(i, i ^ bit) for i in range(size)])  11.4 us
    ppermute x7, waiting for transfers between devices, swap(): return lax.ppermute(value, axis, [(i, i ^ bit) for i in range(size)])  5.4 us
    pallas_call x1, Pallas kernels, per_device(): pl.pallas_call(functools.partial(early_kernel, len(parts), (1, 2), n_proj...  1.74 us
    pallas_call x1, Pallas kernels, per_device(): pl.pallas_call(pack_kernel, out_shape=[vmem_out((2 * n_proj, wide), BF16)...  1.61 us
    pallas_call x2, Pallas kernels, shifted_call(): pl.pallas_call(functools.partial(shift_kernel, n_proj), out_shape=[vmem_o...  0.94 us
    pallas_call x1, Pallas kernels, per_device(): pl.pallas_call(functools.partial(final_kernel, order, len(parts), bits, n...  0.79 us
    pallas_call x1, Pallas kernels, per_device(): pl.pallas_call(functools.partial(place_kernel, half, n_proj), out_shape=s...  0.73 us
    pallas_call x1, Pallas kernels, per_device(): pl.pallas_call(table_kernel, out_shape=[vmem_out((shifts, wide), F32), vm...  0.58 us
  transfers between devices with their start and end apart: 7, of which 4 were waited for; matrix products, arithmetic and copies ran while one was open for 1% of the time, Pallas kernels for 14%

profile of v26, /device:TPU:0, one launch (start us, length us, event | category | flops | bytes accessed | tf_op | source)
XLA Modules:
  0.0 23.6 jit_solution(7995937844856926573)
XLA Ops:
  0.0 1.6 %pack.1 = (bf16[16,4096]{1,0:T(8,128)(2,1)S(1)}, bf16[2,8320]{1,0:T(2,128)(2,1)S(1)}, f32[64,4000]{1,0:T(8,128)S(1)}, f32[1,4000]{1,0:T(1,128)S(1)}, f32[9,4000]{1,0:T(8,128)S(1)}) custom-call(s32[2]{0:T(128)} %class_hbm.1, s32[8]{0:T(128)} %subset_hbm.1, bf16[2,2,4000]{2,1,0:T(2,128)(2,1)} %particles_hbm.1, bf16[2,192]{1,0:T(2,128)(2,1)} %prior_hbm.1, ...), custom_call_target="tpu_custom_call" | custom-call | tf_op jit(solution)/shard_map/pack/pallas_call | solution.py:411
  1.6 4.1 %collective-permute-start = (bf16[2,8320]{1,0:T(2,128)(2,1)S(1)}, bf16[2,8320]{1,0:T(2,128)(2,1)S(1)}, u32[]{:S(2)}, u32[]{:S(2)}) collective-permute-start(bf16[2,8320]{1,0:T(2,128)(2,1)S(1)} %get-tuple-element.29), channel_id=1, source_target_pairs={{0,4},{1,5},{2,6},{3,7},{4,0},{5,1},{6,2},{7,3},{8,12},{9,13},{10,... | collective-permute-start | bytes 99848 | tf_op jit(solution)/shard_map/ppermute | solution.py:438
  5.7 1.6 %collective-permute-start.3 = (bf16[16,4096]{1,0:T(8,128)(2,1)S(1)}, bf16[16,4096]{1,0:T(8,128)(2,1)S(1)}, u32[]{:S(2)}, u32[]{:S(2)}) collective-permute-start(bf16[16,4096]{1,0:T(8,128)(2,1)S(1)} %get-tuple-element.32.rest_0_.rest_4_), channel_id=1, source_target_pairs={{0,2},{1,3},{2,0},{3,1},{4,6},{5,7},{6,4},{7,5},{8,10},{9,11},{10,... | collective-permute-start | bytes 393224 | tf_op jit(solution)/shard_map/ppermute | solution.py:438
  7.3 1.5 %collective-permute-start.4 = (bf16[16,4096]{1,0:T(8,128)(2,1)S(1)}, bf16[16,4096]{1,0:T(8,128)(2,1)S(1)}, u32[]{:S(2)}, u32[]{:S(2)}) collective-permute-start(bf16[16,4096]{1,0:T(8,128)(2,1)S(1)} %get-tuple-element.32.rest_0_.rest_4_), channel_id=1, source_target_pairs={{0,1},{1,0},{2,3},{3,2},{4,5},{5,4},{6,7},{7,6},{8,9},{9,8},{10,11... | collective-permute-start | bytes 393224 | tf_op jit(solution)/shard_map/ppermute | solution.py:438
  8.8 0.6 %tables.1 = (f32[9,4096]{1,0:T(8,128)S(1)}, f32[9,4096]{1,0:T(8,128)S(1)}, bf16[128,4096]{1,0:T(8,128)(2,1)S(1)}) custom-call(f32[64,4000]{1,0:T(8,128)S(1)} %get-tuple-element.25.curves_ref, f32[1,4000]{1,0:T(1,128)S(1)} %get-tuple-element.26.noise_ref, f32[9,4000]{1,0:T(8,128)S(1)} %get-tuple-element.27.angle_ref), custom_call_target="tpu_custom_call" | custom-call | flops 4000000 | bytes 2000000 | tf_op jit(solution)/shard_map/tables/pallas_call | solution.py:453
  9.4 0.3 %shift_own.1 = (bf16[72,8192]{1,0:T(8,128)(2,1)S(1)}, bf16[16,4096]{1,0:T(8,128)(2,1)S(1)}) custom-call(f32[9,4096]{1,0:T(8,128)S(1)} %get-tuple-element.30.cos_ref, f32[9,4096]{1,0:T(8,128)S(1)} %get-tuple-element.31.sin_ref, bf16[16,4096]{1,0:T(8,128)(2,1)S(1)} %get-tuple-element.32.rest_0_.rest_4_), custom_call_target="tpu_custom_call" | custom-call | flops 1769472 | bytes 4000000 | tf_op jit(solution)/shard_map/shift_own/pallas_call | solution.py:469
  9.7 0.0 collective-permute-done
  9.7 0.1 pad_maximum_fusion.1
  9.8 1.6 %collective-permute-start.1 = (bf16[4,8320]{1,0:T(4,128)(2,1)S(1)}, bf16[4,8320]{1,0:T(4,128)(2,1)S(1)}, u32[]{:S(2)}, u32[]{:S(2)}) collective-permute-start(bf16[4,8320]{1,0:T(4,128)(2,1)S(1)} %pad_maximum_fusion.1), channel_id=1, source_target_pairs={{0,16},{8,24},{16,0},{24,8},{1,17},{9,25},{17,1},{25,9},{2,18},{10... | collective-permute-start | bytes 199688 | tf_op jit(solution)/shard_map/ppermute | solution.py:438
  11.4 0.0 collective-permute-done.3.rest_1_.rest_8_
  11.4 0.9 %collective-permute-done.4.rest_0_.rest_7_ = bf16[16,4096]{1,0:T(8,128)(2,1)S(1)} collective-permute-done((bf16[16,4096]{1,0:T(8,128)(2,1)S(1)}, bf16[16,4096]{1,0:T(8,128)(2,1)S(1)}, u32[]{:S(2)}, u32[]{:S(2)}) %collective-permute-start.4) | collective-permute-done | bytes 131104 | tf_op jit(solution)/shard_map/ppermute | solution.py:438
  12.3 1.6 %collective-permute-start.5 = (bf16[16,4352]{1,0:T(8,128)(2,1)S(1)}, bf16[16,4352]{1,0:T(8,128)(2,1)S(1)}, u32[]{:S(2)}, u32[]{:S(2)}) collective-permute-start(bf16[16,4352]{1,0:T(8,128)(2,1)S(1)} %pad.4), channel_id=1, source_target_pairs={{0,1},{1,0},{2,3},{3,2},{4,5},{5,4},{6,7},{7,6},{8,9},{9,8},{10,11... | collective-permute-start | bytes 417800 | tf_op jit(solution)/shard_map/ppermute | solution.py:438
  13.9 0.3 %collective-permute-done.1 = bf16[4,8320]{1,0:T(4,128)(2,1)S(1)} collective-permute-done((bf16[4,8320]{1,0:T(4,128)(2,1)S(1)}, bf16[4,8320]{1,0:T(4,128)(2,1)S(1)}, u32[]{:S(2)}, u32[]{:S(2)}) %collective-permute-start.1) | collective-permute-done | bytes 66592 | tf_op jit(solution)/shard_map/ppermute | solution.py:438
  14.2 0.1 pad_maximum_fusion.rest_0_
  14.2 0.1 collective-permute-start.2
  14.3 0.6 %shift_rest.1 = (bf16[144,8192]{1,0:T(8,128)(2,1)S(1)}, bf16[32,4096]{1,0:T(8,128)(2,1)S(1)}) custom-call(f32[9,4096]{1,0:T(8,128)S(1)} %get-tuple-element.30.cos_ref, f32[9,4096]{1,0:T(8,128)S(1)} %get-tuple-element.31.sin_ref, bf16[16,4096]{1,0:T(8,128)(2,1)S(1)} %collective-permute-done.4.rest_0_.rest_7_, ...), custom_call_target="tpu_custom_call" | custom-call | flops 3538944 | bytes 4000000 | tf_op jit(solution)/shard_map/shift_rest/pallas_call | solution.py:469
  14.9 0.7 %collective-permute-done.2.rest_1_ = bf16[8,8320]{1,0:T(8,128)(2,1)S(1)} collective-permute-done((bf16[8,8320]{1,0:T(8,128)(2,1)S(1)}, bf16[8,8320]{1,0:T(8,128)(2,1)S(1)}, u32[]{:S(2)}, u32[]{:S(2)}) %collective-permute-start.2) | collective-permute-done | bytes 133152 | tf_op jit(solution)/shard_map/ppermute | solution.py:438
  15.7 1.7 %early.1 = (bf16[32,4096]{1,0:T(8,128)(2,1)S(1)}, f32[16,384]{1,0:T(8,128)S(1)}) custom-call(bf16[128,4096]{1,0:T(8,128)(2,1)S(1)} %get-tuple-element.28.square_ref, bf16[8,8320]{1,0:T(8,128)(2,1)S(1)} %pad_maximum_fusion.rest_0_, bf16[8,8320]{1,0:T(8,128)(2,1)S(1)} %collective-permute-done.2.rest_1_, bf16[72,8192]{1,0:T(8,128)(2,1)S(1)} %get-tuple-element.35.rest_2_, ...), custom_call_target="tpu_custom_call" | custom-call | flops 56623104 | bytes 4000000 | tf_op jit(solution)/shard_map/early/pallas_call | solution.py:495
  17.4 0.0 collective-permute-done.5.last_ref
  17.4 0.8 %final.1 = (f32[16,128]{1,0:T(8,128)S(1)}, f32[8,384]{1,0:T(8,128)S(1)}) custom-call(bf16[32,4096]{1,0:T(8,128)(2,1)S(1)} %get-tuple-element.42.select_ref, f32[16,384]{1,0:T(8,128)S(1)} %get-tuple-element.41.rows_ref, f32[9,4096]{1,0:T(8,128)S(1)} %get-tuple-element.30.cos_ref, f32[9,4096]{1,0:T(8,128)S(1)} %get-tuple-element.31.sin_ref, ...), custom_call_target="tpu_custom_call" | custom-call | flops 18874368 | bytes 4000000 | tf_op jit(solution)/shard_map/final/pallas_call | solution.py:511
  18.2 1.0 %collective-permute-start.6 = (f32[8,384]{1,0:T(8,128)S(1)}, f32[8,384]{1,0:T(8,128)S(1)}, u32[]{:S(2)}, u32[]{:S(2)}) collective-permute-start(f32[8,384]{1,0:T(8,128)S(1)} %get-tuple-element.44), channel_id=1, source_target_pairs={{0,4},{1,5},{2,6},{3,7},{4,0},{5,1},{6,2},{7,3},{8,12},{9,13},{10,... | collective-permute-start | bytes 36872 | tf_op jit(solution)/shard_map/ppermute | solution.py:438
  19.2 0.1 keep.1.keep_ref
  19.4 3.5 %collective-permute-done.6.recv_ref = f32[8,384]{1,0:T(8,128)S(1)} collective-permute-done((f32[8,384]{1,0:T(8,128)S(1)}, f32[8,384]{1,0:T(8,128)S(1)}, u32[]{:S(2)}, u32[]{:S(2)}) %collective-permute-start.6) | collective-permute-done | bytes 12320 | tf_op jit(solution)/shard_map/ppermute | solution.py:438
  22.9 0.7 %place.1 = f32[9,8,64]{2,1,0:T(8,128)} custom-call(f32[9,8,64]{2,1,0:T(8,128)S(1)} %keep.1.keep_ref, f32[8,384]{1,0:T(8,128)S(1)} %collective-permute-done.6.recv_ref), custom_call_target="tpu_custom_call" | custom-call | tf_op jit(solution)/shard_map/place/pallas_call | solution.py:531
  (1 shorter events, 0.0 us)
Async XLA Ops:
  1.6 8.1 %collective-permute-start = (bf16[2,8320]{1,0:T(2,128)(2,1)S(1)}, bf16[2,8320]{1,0:T(2,128)(2,1)S(1)}, u32[]{:S(2)}, u32[]{:S(2)}) collective-permute-start(bf16[2,8320]{1,0:T(2,128)(2,1)S(1)} %get-tuple-element.29), channel_id=1, source_target_pairs={{0,4},{1,5},{2,6},{3,7},{4,0},{5,1},{6,2},{7,3},{8,12},{9,13},{10,... | collective-permute-start | bytes 99848 | tf_op jit(solution)/shard_map/ppermute | solution.py:438
  5.7 5.7 %collective-permute-start.3 = (bf16[16,4096]{1,0:T(8,128)(2,1)S(1)}, bf16[16,4096]{1,0:T(8,128)(2,1)S(1)}, u32[]{:S(2)}, u32[]{:S(2)}) collective-permute-start(bf16[16,4096]{1,0:T(8,128)(2,1)S(1)} %get-tuple-element.32.rest_0_.rest_4_), channel_id=1, source_target_pairs={{0,2},{1,3},{2,0},{3,1},{4,6},{5,7},{6,4},{7,5},{8,10},{9,11},{10,... | collective-permute-start | bytes 393224 | tf_op jit(solution)/shard_map/ppermute | solution.py:438
  7.3 5.0 %collective-permute-start.4 = (bf16[16,4096]{1,0:T(8,128)(2,1)S(1)}, bf16[16,4096]{1,0:T(8,128)(2,1)S(1)}, u32[]{:S(2)}, u32[]{:S(2)}) collective-permute-start(bf16[16,4096]{1,0:T(8,128)(2,1)S(1)} %get-tuple-element.32.rest_0_.rest_4_), channel_id=1, source_target_pairs={{0,1},{1,0},{2,3},{3,2},{4,5},{5,4},{6,7},{7,6},{8,9},{9,8},{10,11... | collective-permute-start | bytes 393224 | tf_op jit(solution)/shard_map/ppermute | solution.py:438
  9.8 4.3 %collective-permute-start.1 = (bf16[4,8320]{1,0:T(4,128)(2,1)S(1)}, bf16[4,8320]{1,0:T(4,128)(2,1)S(1)}, u32[]{:S(2)}, u32[]{:S(2)}) collective-permute-start(bf16[4,8320]{1,0:T(4,128)(2,1)S(1)} %pad_maximum_fusion.1), channel_id=1, source_target_pairs={{0,16},{8,24},{16,0},{24,8},{1,17},{9,25},{17,1},{25,9},{2,18},{10... | collective-permute-start | bytes 199688 | tf_op jit(solution)/shard_map/ppermute | solution.py:438
  12.3 5.1 %collective-permute-start.5 = (bf16[16,4352]{1,0:T(8,128)(2,1)S(1)}, bf16[16,4352]{1,0:T(8,128)(2,1)S(1)}, u32[]{:S(2)}, u32[]{:S(2)}) collective-permute-start(bf16[16,4352]{1,0:T(8,128)(2,1)S(1)} %pad.4), channel_id=1, source_target_pairs={{0,1},{1,0},{2,3},{3,2},{4,5},{5,4},{6,7},{7,6},{8,9},{9,8},{10,11... | collective-permute-start | bytes 417800 | tf_op jit(solution)/shard_map/ppermute | solution.py:438
  14.2 1.4 %collective-permute-start.2 = (bf16[8,8320]{1,0:T(8,128)(2,1)S(1)}, bf16[8,8320]{1,0:T(8,128)(2,1)S(1)}, u32[]{:S(2)}, u32[]{:S(2)}) collective-permute-start(bf16[8,8320]{1,0:T(8,128)(2,1)S(1)} %pad_maximum_fusion.rest_0_), channel_id=1, source_target_pairs={{0,8},{8,0},{16,24},{24,16},{1,9},{9,1},{17,25},{25,17},{2,10},{10... | collective-permute-start | bytes 399368 | tf_op jit(solution)/shard_map/ppermute | solution.py:438
  18.2 4.6 %collective-permute-start.6 = (f32[8,384]{1,0:T(8,128)S(1)}, f32[8,384]{1,0:T(8,128)S(1)}, u32[]{:S(2)}, u32[]{:S(2)}) collective-permute-start(f32[8,384]{1,0:T(8,128)S(1)} %get-tuple-element.44), channel_id=1, source_target_pairs={{0,4},{1,5},{2,6},{3,7},{4,0},{5,1},{6,2},{7,3},{8,12},{9,13},{10,... | collective-permute-start | bytes 36872 | tf_op jit(solution)/shard_map/ppermute | solution.py:438
